TPU v7x, 32 devices: a whole 2x2x4 slice. The times are simulated.
32 devices in a mesh: rows: 4 (over y, x), cols: 8 (over z, core).
Axes of the slice: x: 2, y: 2, z: 4, core: 2. Of those that a mesh axis runs over, the one named last changes fastest.
Arguments:
- dosage: int32 [512, 12288], P('cols', 'rows'), may hold values from 0 to 2
- present: int32 [512, 12288], P('cols', 'rows'), may hold values from 0 to 1, as said below
- components: float32 [32, 12288], P(None, 'rows'), may hold values from -8 to 8
Outputs:
- kinship: float32 [12288, 12288], P('rows', 'cols')
Inputs may be any that keep to these rules, and one draw needn't show every extreme that they name: `present`: markers whose index is a multiple of 8 are observed for every person.
All inputs are finite; a program needn't handle non-finite values.
Results may differ from a plain program's by a relative error of at most 0.0036.
Values may be sent and summed in bfloat16 or wider, within the bound.
No kernel may reach another device: no remote copies, remote signals or barrier semaphores. Data moves between devices by JAX's collectives and lax.ppermute only.
A program may use at most 128 MiB of HBM per device.

v0:
```python
import jax
import jax.numpy as jnp
from jax import lax
from jax.sharding import PartitionSpec as P


def broadcast(block, axis, holder):
    block = jnp.where(lax.axis_index(axis) == holder, block, jnp.zeros_like(block))
    return lax.psum(block, axis)


def solve_normal(gram, moment):
    width = gram.shape[0]
    index_col = jnp.arange(width, dtype=jnp.int32)[:, None]
    columns = []
    for j in range(width):
        column = gram[:, j, :]
        if j > 0:
            stacked = jnp.stack(columns, axis=1)
            column = column - jnp.sum(stacked * stacked[j][None, :, :], axis=1)
        pivot = jnp.sqrt(column[j])
        columns.append(jnp.where(index_col >= j, column / pivot[None, :], jnp.zeros_like(column)))
    factor = jnp.stack(columns, axis=1)
    forward = []
    for j in range(width):
        value = moment[j]
        for k in range(j):
            value = value - factor[j, k] * forward[k]
        forward.append(value / factor[j, j])
    backward = [None] * width
    for j in range(width - 1, -1, -1):
        value = forward[j]
        for k in range(j + 1, width):
            value = value - factor[k, j] * backward[k]
        backward[j] = value / factor[j, j]
    return jnp.stack(backward, axis=0)


def per_device(dosage, present, components):
    people = components.shape[1]
    design = jnp.concatenate([jnp.ones((1, people), jnp.float32), components], axis=0)
    width = design.shape[0]
    observed = present.astype(jnp.float32)
    counts = dosage.astype(jnp.float32)
    target = 0.5 * counts * observed
    outer_rows = (design[:, None, :] * design[None, :, :]).reshape(width * width, people)
    gram_part = jnp.dot(
        outer_rows, observed.T, precision=lax.Precision.HIGHEST, preferred_element_type=jnp.float32
    )
    moment_part = jnp.dot(
        design, target.T, precision=lax.Precision.HIGHEST, preferred_element_type=jnp.float32
    )
    gram_flat, moment = lax.psum((gram_part, moment_part), "rows")
    markers_here = observed.shape[0]
    gram = gram_flat.reshape(width, width, markers_here)
    coef = solve_normal(gram, moment)
    fitted = jnp.dot(
        coef.T, design, precision=lax.Precision.HIGHEST, preferred_element_type=jnp.float32
    )
    freq = jnp.clip(fitted, 0.01, 0.99)
    resid = observed * (counts - 2.0 * freq)
    sdev = observed * jnp.sqrt(freq * (1.0 - freq))
    panel = jnp.stack([resid, sdev]).astype(jnp.bfloat16)
    ratio = lax.axis_size("cols") // lax.axis_size("rows")
    column_width = people // ratio
    col_index = lax.axis_index("cols")
    col_start = col_index % ratio * column_width
    owner = col_index // ratio
    contract = (((0,), (0,)), ((), ()))
    full_rows = lax.all_gather(panel, "cols", axis=1, tiled=True)
    own_part = lax.dynamic_slice_in_dim(full_rows, col_start, column_width, 2)
    full_cols = broadcast(own_part, "rows", owner)
    numer = lax.dot_general(
        full_rows[0], full_cols[0], contract, preferred_element_type=jnp.float32
    )
    denom = lax.dot_general(
        full_rows[1], full_cols[1], contract, preferred_element_type=jnp.float32
    )
    return numer / (4.0 * denom)


def solution(mesh):
    placed = (P("cols", "rows"), P("cols", "rows"), P(None, "rows"))
    return jax.shard_map(
        per_device, mesh=mesh, in_specs=placed, out_specs=P("rows", "cols"), check_vma=False
    )
```

profile of v0, /device:TPU:0, one launch (start us, length us, event | category | flops | bytes accessed | tf_op | source)
XLA Modules:
  0.0 309.3 jit_solution(9560483943132380442)
XLA Ops:
  6.5 1.0 concatenate.3
  7.6 8.0 %broadcast_multiply_fusion = f32[33,33,3072]{2,1,0:T(8,128)} fusion(f32[33,3072]{1,0:T(8,128)S(1)} %concatenate.3), kind=kLoop, calls=%fused_computation.1 | loop fusion | flops 3345408 | bytes 13787136 | tf_op jit(solution)/shard_map/mul | solution.py:46
  15.6 10.6 %mul.11354 = f32[1089,3072]{1,0:T(8,128)} reshape(f32[33,33,3072]{2,1,0:T(8,128)} %broadcast_multiply_fusion) | data formatting | bytes 26763264 | tf_op jit(solution)/shard_map/mul | solution.py:46
  26.2 13.6 %fusion.8 = f32[1089,64]{1,0:T(8,128)S(1)} fusion(f32[1089,3072]{1,0:T(8,128)} %mul.11354, s32[64,3072]{1,0:T(8,128)S(1)} %copy-done), kind=kOutput, calls=%fused_computation.537 | convolution fusion | flops 2569469952 | bytes 14446848 | tf_op jit(solution)/shard_map/dot_general | solution.py:47
  39.9 1.0 copy.5
  41.3 0.8 fusion.4
  42.7 18.2 %psum.21 = f32[33,64]{1,0:T(8,128)S(1)} all-reduce(f32[33,64]{1,0:T(8,128)S(1)} %fusion.4), channel_id=1, replica_groups=mesh['rows'=4,'cols'=8] {'rows'}, use_global_device_ids=true, to_apply=%region_0.0 | all-reduce | flops 2112 | bytes 16896 | tf_op jit(solution)/shard_map/psum | solution.py:53
  60.9 30.4 %all-reduce.4.cloned.1.call-done = f32[33,33,64]{2,0,1:T(8,128)} async-done(((f32[33,33,64]{2,0,1:T(8,128)}), f32[33,33,64]{2,0,1:T(8,128)}) %all-reduce.4.cloned.1.call-update) | async-done | bytes 278800 | tf_op jit(solution)/shard_map/psum | solution.py:53
  95.3 0.8 constant_dynamic-update-slice_fusion.79
  96.9 0.8 constant_dynamic-update-slice_fusion.514
  98.7 0.8 constant_dynamic-update-slice_fusion.513
  100.4 0.8 constant_dynamic-update-slice_fusion.512
  102.1 0.8 constant_dynamic-update-slice_fusion.511
  103.8 0.8 constant_dynamic-update-slice_fusion.510
  105.4 0.8 constant_dynamic-update-slice_fusion.509
  107.1 0.8 constant_dynamic-update-slice_fusion.508
  108.8 0.8 constant_dynamic-update-slice_fusion.507
  119.6 1.3 fusion.11
  120.8 0.9 pad_maximum_fusion
  122.1 64.7 %all-gather.2.cloned.1.call-done = bf16[2,512,3072]{2,1,0:T(8,128)(2,1)} async-done(((bf16[2,64,3072]{2,1,0:T(8,128)(2,1)}), bf16[2,512,3072]{2,1,0:T(8,128)(2,1)}) %all-gather.2.cloned.1.call-update) | async-done | bytes 6291472 | tf_op jit(solution)/shard_map/all_gather | solution.py:70
  186.8 4.1 %dynamic-slice_select_fusion = bf16[2,512,1536]{2,1,0:T(8,128)(2,1)} fusion(bf16[2,512,3072]{2,1,0:T(8,128)(2,1)} %all-gather.2.cloned.1.call-done, s32[]{:T(128)S(6)} %select_n.281, pred[]{:T(512)S(6)} %eq.5), kind=kLoop, calls=%fused_computation.6 | loop fusion | flops 1572864 | bytes 6291461 | tf_op jit(solution)/shard_map/jit(_where)/select_n | solution.py:8
  190.9 86.0 %all-reduce.6.cloned.1.call-done = bf16[2,512,1536]{2,1,0:T(8,128)(2,1)} async-done(((bf16[2,512,1536]{2,1,0:T(8,128)(2,1)}), bf16[2,512,1536]{2,1,0:T(8,128)(2,1)}) %all-reduce.6.cloned.1.call-update) | async-done | bytes 3145744 | tf_op jit(solution)/shard_map/psum | solution.py:9
  276.9 11.7 %fusion = f32[3072,1536]{1,0:T(8,128)} fusion(bf16[2,512,3072]{2,1,0:T(8,128)(2,1)} %all-gather.2.cloned.1.call-done, bf16[2,512,1536]{2,1,0:T(8,128)(2,1)} %all-reduce.6.cloned.1.call-done), kind=kOutput, calls=%fused_computation.5 | convolution fusion | flops 4831838208 | bytes 23592960 | tf_op jit(solution)/shard_map/dot_general | solution.py:73
  288.6 14.1 %multiply_divide_fusion = f32[3072,1536]{1,0:T(8,128)} fusion(f32[3072,1536]{1,0:T(8,128)} %fusion, bf16[2,512,3072]{2,1,0:T(8,128)(2,1)} %all-gather.2.cloned.1.call-done, bf16[2,512,1536]{2,1,0:T(8,128)(2,1)S(1)} %copy-done.4), kind=kOutput, calls=%fused_computation | convolution fusion | flops 4841275392 | bytes 42467328 | tf_op jit(solution)/shard_map/dot_general | solution.py:76
  (305 shorter events, 21.0 us)
Async XLA Ops:
  6.5 84.8 %all-reduce.4.cloned.1.call-start = ((), (), s32[]{:S(2)}) async-start(), calls=%async_computation | async-start | bytes 1351680 | tf_op jit(solution)/shard_map/psum | solution.py:53
  15.6 10.6 %copy-start = (s32[64,3072]{1,0:T(8,128)S(1)}, s32[64,3072]{1,0:T(8,128)}, u32[]{:S(2)}) copy-start(s32[64,3072]{1,0:T(8,128)} %param.4) | copy-start | bytes 2359300
  26.2 15.1 %copy-start.1 = (f32[32,3072]{1,0:T(8,128)S(1)}, f32[32,3072]{1,0:T(8,128)}, u32[]{:S(2)}) copy-start(f32[32,3072]{1,0:T(8,128)} %param.5) | copy-start | bytes 1179652
  26.2 15.1 %copy-start.2 = (s32[64,3072]{1,0:T(8,128)S(1)}, s32[64,3072]{1,0:T(8,128)}, u32[]{:S(2)}) copy-start(s32[64,3072]{1,0:T(8,128)} %param.3) | copy-start | bytes 2359300
  40.9 145.9 %all-gather.2.cloned.1.call-start = ((), (), s32[]{:S(2)}) async-start(), calls=%async_computation.1 | async-start | bytes 7077888 | tf_op jit(solution)/shard_map/all_gather | solution.py:70
  91.3 18.4 %copy-start.3 = (f32[33,33,64]{2,0,1:T(8,128)S(1)}, f32[33,33,64]{2,0,1:T(8,128)}, u32[]{:S(2)}) copy-start(f32[33,33,64]{2,0,1:T(8,128)} %all-reduce.4.cloned.1.call-done) | copy-start | bytes 836356
  121.8 155.1 %all-reduce.6.cloned.1.call-start = ((), (), s32[]{:S(2)}) async-start(), calls=%async_computation.2 | async-start | bytes 6291456 | tf_op jit(solution)/shard_map/psum | solution.py:9
  276.9 11.7 %copy-start.4 = (bf16[2,512,1536]{2,1,0:T(8,128)(2,1)S(1)}, bf16[2,512,1536]{2,1,0:T(8,128)(2,1)}, u32[]{:S(2)}) copy-start(bf16[2,512,1536]{2,1,0:T(8,128)(2,1)} %all-reduce.6.cloned.1.call-done) | copy-start | bytes 9437188
Sparse Core Ops, SparseCore 0:
  41.0 50.2 all-reduce.3
  121.9 64.8 all-gather.1
  191.0 85.8 all-reduce.5
where the time goes:
time: 311 us; the launch traced here: 309 us
  waiting for transfers between devices  181 us (58%)
  matrix products  41.5 us (13%)
  other arithmetic  37.9 us (12%)
  blocking collectives  18.2 us (6%)
  local copies, waits for them, and re-layouts  15.7 us (5%)
  between operations  14.6 us (5%)
    psum x1, waiting for transfers between devices, broadcast(): return lax.psum(block, axis)  86 us
    all_gather x1, waiting for transfers between devices, per_device(): full_rows = lax.all_gather(panel, 'cols', axis=1, tiled=True)  64.7 us
    psum x1, waiting for transfers between devices, per_device(): gram_flat, moment = lax.psum((gram_part, moment_part), 'rows')  30.4 us
    psum x1, blocking collectives, per_device(): gram_flat, moment = lax.psum((gram_part, moment_part), 'rows')  18.2 us
    dot_general x1, matrix products, per_device(): lax.dot_general(full_rows[1], full_cols[1], contract, preferred_element_t...  14.1 us
    dot_general x1, matrix products, per_device(): jnp.dot(outer_rows, observed.T, precision=lax.Precision.HIGHEST, preferre...  13.6 us
    dot_general x1, matrix products, per_device(): lax.dot_general(full_rows[0], full_cols[0], contract, preferred_element_t...  11.7 us
    mul x1, local copies, waits for them, and re-layouts, per_device(): design[:, None, :] * design[None, :, :]  10.6 us
  transfers between devices with their start and end apart: 3, of which 3 were waited for; matrix products, arithmetic and copies ran while one was open for 1% of the time, Pallas kernels for 0%

commit v1 on v0

v1 whole, which is shorter than its diff:
```python
import functools

import jax
import jax.numpy as jnp
from jax import lax
from jax.experimental import pallas as pl
from jax.experimental.pallas import tpu as pltpu
from jax.sharding import PartitionSpec as P

F32, BF16 = jnp.float32, jnp.bfloat16
VMEM_LIMIT = 56 * 1024 * 1024
SUB = 8


def split3(x):
    high = x.astype(BF16)
    rest = x - high.astype(F32)
    mid = rest.astype(BF16)
    low = (rest - mid.astype(F32)).astype(BF16)
    return high, mid, low


def group_starts(comps):
    starts, at = [], 0
    for j in range(comps):
        first = j // SUB * SUB
        starts.append((at, first))
        at += comps - first
    return starts, at


def gram_kernel(dosage_ref, present_ref, comps_ref, out_ref, lhs_ref):
    comps, people = comps_ref.shape
    markers = dosage_ref.shape[0]
    starts, total = group_starts(comps)
    chunk = 512 if people % 512 == 0 else people
    acc = None
    for at in range(0, people, chunk):
        span = slice(at, at + chunk)
        obs = present_ref[:, span].astype(F32)
        tgt = 0.5 * dosage_ref[:, span].astype(F32) * obs
        rhs = jnp.concatenate([obs, tgt], axis=0).astype(BF16)
        x = comps_ref[:, span]
        for j, (start, first) in enumerate(starts):
            lhs_ref[start : start + comps - first, :] = x[first:, :] * x[j : j + 1, :]
        lhs_ref[total : total + comps, :] = x
        tail = lhs_ref.shape[0] - total - comps
        lhs_ref[total + comps :, :] = jnp.ones((tail, chunk), F32)
        for part in split3(lhs_ref[...]):
            term = lax.dot_general(part, rhs, (((1,), (1,)), ((), ())), preferred_element_type=F32)
            acc = term if acc is None else acc + term
    half = total // 2
    out_ref[0:half, :] = jnp.concatenate([acc[0:half, 0:markers], acc[half:total, 0:markers]], axis=1)
    out_ref[half:, :] = acc[total : total + comps + SUB, :]


def gram_call(dosage, present, components):
    markers, people = dosage.shape
    comps = components.shape[0]
    total = group_starts(comps)[1]
    chunk = 512 if people % 512 == 0 else people
    return pl.pallas_call(
        gram_kernel,
        out_shape=jax.ShapeDtypeStruct((total // 2 + comps + SUB, 2 * markers), F32),
        scratch_shapes=[pltpu.VMEM((total + comps + 2 * SUB, chunk), F32)],
        compiler_params=pltpu.CompilerParams(vmem_limit_bytes=VMEM_LIMIT),
        name="gram",
    )(dosage, present, components)


def coef_rows(comps):
    return 6 * comps + 2 * SUB


def below(old, first, new):
    return new if first == 0 else jnp.concatenate([old[:first], new], axis=0)


def solve_kernel(comps, markers, *refs):
    out_ref = refs[-1]
    summed = refs[0][...]
    for ref in refs[1:-1]:
        summed = summed + ref[...]
    starts, total = group_starts(comps)
    half = total // 2
    left, right = summed[:, 0:markers], summed[:, markers : 2 * markers]

    def rows_of(start, count):
        if start + count <= half:
            return left[start : start + count]
        if start >= half:
            return right[start - half : start - half + count]
        return jnp.concatenate([left[start:half], right[0 : start + count - half]], axis=0)

    columns = [rows_of(start, comps - first) for start, first in starts]
    firsts = [first for _, first in starts]
    edge = left[half : half + comps]
    count = left[half + comps : half + comps + 1]
    moment = right[half : half + comps]
    moment_one = right[half + comps : half + comps + 1]
    factor, edge_f, moment_f = [], [], []
    for j in range(comps):
        first = firsts[j]
        column = columns[j]
        inv = 1.0 / column[j - first : j - first + 1]
        scaled = column * inv
        edge_j = edge[j : j + 1]
        moment_j = moment[j : j + 1]
        edge_s, moment_s = edge_j * inv, moment_j * inv
        row = lax.broadcasted_iota(jnp.int32, column.shape, 0) + first
        factor.append(jnp.where(row > j, scaled, 0.0))
        edge_f.append(edge_s)
        moment_f.append(moment_s)
        count = count - edge_s * edge_j
        moment_one = moment_one - edge_s * moment_j
        if j + 1 < comps:
            edge = below(edge, first, edge[first:] - column * edge_s)
            moment = below(moment, first, moment[first:] - column * moment_s)
        for k in range(j + 1, comps):
            offset = firsts[k] - first
            columns[k] = columns[k] - scaled[offset:] * column[k - first : k - first + 1]
    last = moment_one / count
    index = lax.broadcasted_iota(jnp.int32, (SUB, markers), 0)
    groups = [jnp.zeros((SUB, markers), F32) for _ in range(comps // SUB)]
    for j in range(comps - 1, -1, -1):
        first = firsts[j]
        value = moment_f[j] - edge_f[j] * last
        total_term = None
        for g in range(first // SUB, comps // SUB):
            term = factor[j][g * SUB - first : (g + 1) * SUB - first] * groups[g]
            total_term = term if total_term is None else total_term + term
        value = value - jnp.sum(total_term, axis=0, keepdims=True)
        g = j // SUB
        groups[g] = jnp.where(index == j - first, value, groups[g])
    coef = jnp.concatenate(groups, axis=0)
    c1, c2, c3 = [part.astype(F32) for part in split3(coef)]
    l1, l2, l3 = [part.astype(F32) for part in split3(last)]
    index = lax.broadcasted_iota(jnp.int32, (2 * SUB, markers), 0)
    ones = jnp.where(index == 0, l1, jnp.where(index == 1, l2, jnp.where(index == 2, l3, 0.0)))
    stacked = jnp.concatenate([c1, c1, c2, c2, c1, c3, ones], axis=0).astype(BF16)
    eye = (
        lax.broadcasted_iota(jnp.int32, (markers, markers), 0)
        == lax.broadcasted_iota(jnp.int32, (markers, markers), 1)
    ).astype(F32).astype(BF16)
    turned = lax.dot_general(eye, stacked, (((1,), (1,)), ((), ())), preferred_element_type=F32)
    out_ref[...] = turned.astype(BF16)


def solve_call(parts, comps, markers):
    return pl.pallas_call(
        functools.partial(solve_kernel, comps, markers),
        out_shape=jax.ShapeDtypeStruct((markers, coef_rows(comps)), BF16),
        compiler_params=pltpu.CompilerParams(vmem_limit_bytes=VMEM_LIMIT),
        name="solve",
    )(*parts)


def design_parts(x):
    d1, d2, d3 = split3(x)
    ones = jnp.ones((2 * SUB, x.shape[1]), BF16)
    return jnp.concatenate([d1, d2, d1, d2, d3, d1, ones], axis=0)


def panel(coef, x, dosage, present):
    fitted = lax.dot_general(
        coef, design_parts(x), (((1,), (0,)), ((), ())), preferred_element_type=F32
    )
    freq = jnp.clip(fitted, 0.01, 0.99)
    observed = present.astype(F32)
    resid = observed * (dosage.astype(F32) - 2.0 * freq)
    sdev = observed * jnp.sqrt(freq * (1.0 - freq))
    return resid.astype(BF16), (2.0 * sdev).astype(BF16)


def kin_kernel(rows, ratio, cols, raw_ref, comps_ref, col_comps_ref, *refs):
    coef_refs = refs[:cols]
    piece_refs = refs[cols : cols + rows * ratio]
    out_ref, coef, raw_cols, col_r, col_s, sems = refs[cols + rows * ratio :]
    here = coef_refs[0].shape[0]
    width = out_ref.shape[1]

    @pl.when(pl.program_id(0) == 0)
    def _():
        r = lax.axis_index("rows")
        q = lax.axis_index("cols")
        copies = []
        for d in range(cols):
            place = pl.multiple_of((q ^ d) * here, here)
            copies.append(
                pltpu.make_async_copy(coef_refs[d], coef.at[pl.ds(place, here), :], sems.at[len(copies)])
            )
        for d in range(rows):
            for k in range(ratio):
                owner = (r ^ d) * ratio + lax.rem(lax.rem(q, ratio) + ratio - k, ratio)
                place = pl.multiple_of(owner * here, here)
                copies.append(
                    pltpu.make_async_copy(
                        piece_refs[d * ratio + k],
                        raw_cols.at[:, pl.ds(place, here), :],
                        sems.at[len(copies)],
                    )
                )
        for copy in copies:
            copy.start()
        for copy in copies:
            copy.wait()
        step = 256 if width % 256 == 0 else width
        for at in range(0, width, step):
            span = slice(at, at + step)
            resid, sdev = panel(
                coef[...], col_comps_ref[:, span], raw_cols[0, :, span], raw_cols[1, :, span]
            )
            col_r[:, span] = resid
            col_s[:, span] = sdev

    resid, sdev = panel(coef[...], comps_ref[...], raw_ref[0], raw_ref[1])
    contract = (((0,), (0,)), ((), ()))
    step = 512 if width % 512 == 0 else width
    for at in range(0, width, step):
        span = slice(at, at + step)
        numer = lax.dot_general(resid, col_r[:, span], contract, preferred_element_type=F32)
        denom = lax.dot_general(sdev, col_s[:, span], contract, preferred_element_type=F32)
        out_ref[:, span] = numer / denom


def kin_call(rows, ratio, cols, raw, components, col_comps, coefs, pieces):
    _, markers, people = raw.shape
    comps, width = col_comps.shape
    tile = 512 if people % 512 == 0 else people
    anywhere = pl.BlockSpec(memory_space=pl.ANY)
    return pl.pallas_call(
        functools.partial(kin_kernel, rows, ratio, cols),
        grid=(people // tile,),
        in_specs=[
            pl.BlockSpec((2, markers, tile), lambda i: (0, 0, i)),
            pl.BlockSpec((comps, tile), lambda i: (0, i)),
            pl.BlockSpec((comps, width), lambda i: (0, 0)),
        ]
        + [anywhere] * (len(coefs) + len(pieces)),
        out_specs=pl.BlockSpec((tile, width), lambda i: (i, 0)),
        out_shape=jax.ShapeDtypeStruct((people, width), F32),
        scratch_shapes=[
            pltpu.VMEM((markers, coef_rows(comps)), BF16),
            pltpu.VMEM((2, markers, width), BF16),
            pltpu.VMEM((markers, width), BF16),
            pltpu.VMEM((markers, width), BF16),
            pltpu.SemaphoreType.DMA((len(coefs) + len(pieces),)),
        ],
        compiler_params=pltpu.CompilerParams(vmem_limit_bytes=VMEM_LIMIT),
        name="kinship",
    )(raw, components, col_comps, *coefs, *pieces)


def per_device(dosage, present, components):
    rows, cols = lax.axis_size("rows"), lax.axis_size("cols")
    ratio = cols // rows
    markers, people = dosage.shape
    comps = components.shape[0]
    width = people // ratio
    col = lax.axis_index("cols")
    raw = jnp.stack([dosage.astype(BF16), present.astype(BF16)])
    raw_rows = lax.all_gather(raw, "cols", axis=1, tiled=True)

    def across(x, axis, size):
        return [x] + [lax.ppermute(x, axis, [(i, i ^ d) for i in range(size)]) for d in range(1, size)]

    both = ("rows", "cols")
    pieces = []
    for k in range(ratio):
        part = (col % ratio + k) % ratio
        mine = lax.dynamic_slice_in_dim(raw, part * width, width, 2)
        moves = [
            (r * cols + z * ratio + c, z * cols + r * ratio + (c + k) % ratio)
            for r in range(rows)
            for z in range(rows)
            for c in range(ratio)
        ]
        pieces.append(lax.ppermute(mine, both, moves) if len(moves) > 1 else mine)
        if k == 0:
            mine = lax.dynamic_slice_in_dim(components, part * width, width, 1)
            col_comps = lax.ppermute(mine, both, moves) if len(moves) > 1 else mine
    spread = [across(piece, "rows", rows) for piece in pieces]
    pieces = [spread[k][d] for d in range(rows) for k in range(ratio)]

    gram = gram_call(dosage, present, components)
    coef = solve_call(across(gram, "rows", rows), comps, markers)
    coefs = across(coef, "cols", cols)
    return kin_call(rows, ratio, cols, raw_rows, components, col_comps, coefs, pieces)


def solution(mesh):
    placed = (P("cols", "rows"), P("cols", "rows"), P(None, "rows"))
    return jax.shard_map(
        per_device, mesh=mesh, in_specs=placed, out_specs=P("rows", "cols"), check_vma=False
    )
```

time: 311 us -> 191 us (0.61)
  waiting for transfers between devices: 181 us -> 33.4 us
  starting transfers between devices: 0.31 us -> 104 us
  matrix products: 41.5 us -> 0 us
  other arithmetic: 37.9 us -> 2.48 us
  Pallas kernels: 0 us -> 34.7 us
  blocking collectives: 18.2 us -> 0 us
  local copies, waits for them, and re-layouts: 15.7 us -> 2.28 us
    psum x2 -> x0, waiting for transfers between devices: 116 us -> none  [the longest x1 86 us: broadcast(): return lax.psum(block, axis)]
    ppermute x0 -> x19, starting transfers between devices: none -> 104 us  [the longest x16 102 us: across(): lax.ppermute(x, axis, [(i, i ^ d) for i in range(size)])]
    all_gather x1, waiting for transfers between devices: 64.7 us -> 0.01 us  [per_device(): raw_rows = lax.all_gather(raw, 'cols', axis=1, tiled=True)]
    dot_general x5 -> x0, matrix products: 41.5 us -> none  [the longest x1 14.1 us: per_device(): lax.dot_general(full_rows[1], full_cols[1], contract, preferred_element_t...]
    pallas_call x0 -> x3, Pallas kernels: none -> 34.7 us  [the longest x1 21.8 us: kin_call(): pl.pallas_call(functools.partial(kin_kernel, rows, ratio, cols), grid=(pe...]
    ppermute x0 -> x19, waiting for transfers between devices: none -> 33.4 us  [the longest x16 33.4 us: across(): lax.ppermute(x, axis, [(i, i ^ d) for i in range(size)])]
    psum x1 -> x0, blocking collectives: 18.2 us -> none  [per_device(): gram_flat, moment = lax.psum((gram_part, moment_part), 'rows')]
    mul x1 -> x0, local copies, waits for them, and re-layouts: 10.6 us -> none  [per_device(): design[:, None, :] * design[None, :, :]]
  transfers between devices with their start and end apart: 3 -> 20, of which waited for: 3 -> 8; matrix products, arithmetic and copies ran while one was open for 1% -> 1% of each run, Pallas kernels for 0% -> 7%
where the time goes in v1:
time: 191 us
  starting transfers between devices  104 us (54%)
  Pallas kernels  34.7 us (18%)
  waiting for transfers between devices  33.4 us (17%)
  between operations  13.6 us (7%)
  other arithmetic  2.48 us (1%)
  local copies, waits for them, and re-layouts  2.28 us (1%)
    ppermute x16, starting transfers between devices, across(): lax.ppermute(x, axis, [(i, i ^ d) for i in range(size)])  102 us
    ppermute x16, waiting for transfers between devices, across(): lax.ppermute(x, axis, [(i, i ^ d) for i in range(size)])  33.4 us
    pallas_call x1, Pallas kernels, kin_call(): pl.pallas_call(functools.partial(kin_kernel, rows, ratio, cols), grid=(pe...  21.8 us
    pallas_call x1, Pallas kernels, solve_call(): pl.pallas_call(functools.partial(solve_kernel, comps, markers), out_shape...  7.32 us
    pallas_call x1, Pallas kernels, gram_call(): pl.pallas_call(gram_kernel, out_shape=jax.ShapeDtypeStruct((total // 2 +...  5.65 us
  transfers between devices with their start and end apart: 20, of which 8 were waited for; matrix products, arithmetic and copies ran while one was open for 1% of the time, Pallas kernels for 7%

profile of v1, /device:TPU:0, one launch (start us, length us, event | category | flops | bytes accessed | tf_op | source)
XLA Modules:
  0.0 190.8 jit_solution(11981555446889298300)
XLA Ops:
  6.5 1.5 convert_bitcast_fusion
  8.0 0.9 pad_maximum_fusion
  9.6 5.6 %gram.1.refs_0_ = f32[360,128]{1,0:T(8,128)} custom-call(s32[64,3072]{1,0:T(8,128)} %dosage_ref.1, s32[64,3072]{1,0:T(8,128)} %present_ref.1, f32[32,3072]{1,0:T(8,128)} %comps_ref.3), custom_call_target="tpu_custom_call" | custom-call | tf_op jit(solution)/shard_map/gram/pallas_call | solution.py:62
  15.3 6.4 %collective-permute-start.3 = (f32[360,128]{1,0:T(8,128)}, f32[360,128]{1,0:T(8,128)S(1)}, u32[]{:S(2)}, u32[]{:S(2)}) collective-permute-start(f32[360,128]{1,0:T(8,128)} %gram.1.refs_0_), channel_id=1, source_target_pairs={{0,24},{8,16},{16,8},{24,0},{1,25},{9,17},{17,9},{25,1},{2,26},{10... | collective-permute-start | bytes 552968 | tf_op jit(solution)/shard_map/ppermute | solution.py:265
  22.9 6.5 %collective-permute-start.18 = (bf16[2,64,1536]{2,1,0:T(8,128)(2,1)S(1)}, bf16[2,64,1536]{2,1,0:T(8,128)(2,1)S(1)}, u32[]{:S(2)}, u32[]{:S(2)}) collective-permute-start(bf16[2,64,1536]{2,1,0:T(8,128)(2,1)S(1)} %collective-permute-done.12.refs_9_), channel_id=1, source_target_pairs={{0,24},{8,16},{16,8},{24,0},{1,25},{9,17},{17,9},{25,1},{2,26},{10... | collective-permute-start | bytes 1179656 | tf_op jit(solution)/shard_map/ppermute | solution.py:265
  29.4 0.9 constant_dynamic-slice_fusion
  30.3 0.8 collective-permute-done.3.refs_3_
  31.9 10.0 %collective-permute-done.1.refs_1_ = f32[360,128]{1,0:T(8,128)S(1)} collective-permute-done((f32[360,128]{1,0:T(8,128)}, f32[360,128]{1,0:T(8,128)S(1)}, u32[]{:S(2)}, u32[]{:S(2)}) %collective-permute-start.1) | collective-permute-done | bytes 184352 | tf_op jit(solution)/shard_map/ppermute | solution.py:265
  42.6 7.3 %solve.1.refs_0_ = bf16[64,208]{1,0:T(8,128)(2,1)} custom-call(f32[360,128]{1,0:T(8,128)} %gram.1.refs_0_, f32[360,128]{1,0:T(8,128)} %copy-done.11, f32[360,128]{1,0:T(8,128)} %copy-done.10, f32[360,128]{1,0:T(8,128)} %copy-done.9), custom_call_target="tpu_custom_call" | custom-call | tf_op jit(solution)/shard_map/solve/pallas_call | solution.py:150
  49.9 3.2 %collective-permute-start.9 = (bf16[64,208]{1,0:T(8,128)(2,1)}, bf16[64,208]{1,0:T(8,128)(2,1)S(1)}, u32[]{:S(2)}, u32[]{:S(2)}) collective-permute-start(bf16[64,208]{1,0:T(8,128)(2,1)} %solve.1.refs_0_), channel_id=1, source_target_pairs={{0,6},{1,7},{2,4},{3,5},{4,2},{5,3},{6,0},{7,1},{8,14},{9,15},{10,... | collective-permute-start | bytes 79880 | tf_op jit(solution)/shard_map/ppermute | solution.py:265
  53.1 49.9 %collective-permute-start.8 = (bf16[64,208]{1,0:T(8,128)(2,1)}, bf16[64,208]{1,0:T(8,128)(2,1)S(1)}, u32[]{:S(2)}, u32[]{:S(2)}) collective-permute-start(bf16[64,208]{1,0:T(8,128)(2,1)} %solve.1.refs_0_), channel_id=1, source_target_pairs={{0,5},{1,4},{2,7},{3,6},{4,1},{5,0},{6,3},{7,2},{8,13},{9,12},{10,... | collective-permute-start | bytes 79880 | tf_op jit(solution)/shard_map/ppermute | solution.py:265
  103.0 1.8 collective-permute-start.7
  104.8 22.9 %collective-permute-start.6 = (bf16[64,208]{1,0:T(8,128)(2,1)}, bf16[64,208]{1,0:T(8,128)(2,1)S(1)}, u32[]{:S(2)}, u32[]{:S(2)}) collective-permute-start(bf16[64,208]{1,0:T(8,128)(2,1)} %solve.1.refs_0_), channel_id=1, source_target_pairs={{0,3},{1,2},{2,1},{3,0},{4,7},{5,6},{6,5},{7,4},{8,11},{9,10},{10,... | collective-permute-start | bytes 79880 | tf_op jit(solution)/shard_map/ppermute | solution.py:265
  127.7 2.2 %collective-permute-start.5 = (bf16[64,208]{1,0:T(8,128)(2,1)}, bf16[64,208]{1,0:T(8,128)(2,1)S(1)}, u32[]{:S(2)}, u32[]{:S(2)}) collective-permute-start(bf16[64,208]{1,0:T(8,128)(2,1)} %solve.1.refs_0_), channel_id=1, source_target_pairs={{0,2},{1,3},{2,0},{3,1},{4,6},{5,7},{6,4},{7,5},{8,10},{9,11},{10,... | collective-permute-start | bytes 79880 | tf_op jit(solution)/shard_map/ppermute | solution.py:265
  130.4 3.0 %collective-permute-start.16 = (bf16[2,64,1536]{2,1,0:T(8,128)(2,1)S(1)}, bf16[2,64,1536]{2,1,0:T(8,128)(2,1)S(1)}, u32[]{:S(2)}, u32[]{:S(2)}) collective-permute-start(bf16[2,64,1536]{2,1,0:T(8,128)(2,1)S(1)} %collective-permute-done.12.refs_9_), channel_id=1, source_target_pairs={{0,16},{8,24},{16,0},{24,8},{1,17},{9,25},{17,1},{25,9},{2,18},{10... | collective-permute-start | bytes 1179656 | tf_op jit(solution)/shard_map/ppermute | solution.py:265
  133.3 2.6 %collective-permute-start.14 = (bf16[2,64,1536]{2,1,0:T(8,128)(2,1)S(1)}, bf16[2,64,1536]{2,1,0:T(8,128)(2,1)S(1)}, u32[]{:S(2)}, u32[]{:S(2)}) collective-permute-start(bf16[2,64,1536]{2,1,0:T(8,128)(2,1)S(1)} %collective-permute-done.12.refs_9_), channel_id=1, source_target_pairs={{0,8},{8,0},{16,24},{24,16},{1,9},{9,1},{17,25},{25,17},{2,10},{10... | collective-permute-start | bytes 1179656 | tf_op jit(solution)/shard_map/ppermute | solution.py:265
  135.9 1.0 collective-permute-start.17
  137.4 1.9 %collective-permute-start.13 = (bf16[2,64,1536]{2,1,0:T(8,128)(2,1)S(1)}, bf16[2,64,1536]{2,1,0:T(8,128)(2,1)S(1)}, u32[]{:S(2)}, u32[]{:S(2)}) collective-permute-start(bf16[2,64,1536]{2,1,0:T(8,128)(2,1)S(1)} %collective-permute-done.11.refs_8_), channel_id=1, source_target_pairs={{0,8},{8,0},{16,24},{24,16},{1,9},{9,1},{17,25},{25,17},{2,10},{10... | collective-permute-start | bytes 1179656 | tf_op jit(solution)/shard_map/ppermute | solution.py:265
  139.4 3.9 %collective-permute-done.16.refs_13_ = bf16[2,64,1536]{2,1,0:T(8,128)(2,1)S(1)} collective-permute-done((bf16[2,64,1536]{2,1,0:T(8,128)(2,1)S(1)}, bf16[2,64,1536]{2,1,0:T(8,128)(2,1)S(1)}, u32[]{:S(2)}, u32[]{:S(2)}) %collective-permute-start.16) | collective-permute-done | bytes 393248 | tf_op jit(solution)/shard_map/ppermute | solution.py:265
  143.3 2.6 %collective-permute-done.14.refs_11_ = bf16[2,64,1536]{2,1,0:T(8,128)(2,1)S(1)} collective-permute-done((bf16[2,64,1536]{2,1,0:T(8,128)(2,1)S(1)}, bf16[2,64,1536]{2,1,0:T(8,128)(2,1)S(1)}, u32[]{:S(2)}, u32[]{:S(2)}) %collective-permute-start.14) | collective-permute-done | bytes 393248 | tf_op jit(solution)/shard_map/ppermute | solution.py:265
  145.9 9.5 %collective-permute-done.17.refs_14_ = bf16[2,64,1536]{2,1,0:T(8,128)(2,1)S(1)} collective-permute-done((bf16[2,64,1536]{2,1,0:T(8,128)(2,1)S(1)}, bf16[2,64,1536]{2,1,0:T(8,128)(2,1)S(1)}, u32[]{:S(2)}, u32[]{:S(2)}) %collective-permute-start.17) | collective-permute-done | bytes 393248 | tf_op jit(solution)/shard_map/ppermute | solution.py:265
  155.4 4.5 %collective-permute-done.15.refs_12_ = bf16[2,64,1536]{2,1,0:T(8,128)(2,1)S(1)} collective-permute-done((bf16[2,64,1536]{2,1,0:T(8,128)(2,1)S(1)}, bf16[2,64,1536]{2,1,0:T(8,128)(2,1)S(1)}, u32[]{:S(2)}, u32[]{:S(2)}) %collective-permute-start.15) | collective-permute-done | bytes 393248 | tf_op jit(solution)/shard_map/ppermute | solution.py:265
  159.9 1.5 collective-permute-done.13.refs_10_
  162.1 21.8 %kinship.1 = f32[3072,1536]{1,0:T(8,128)} custom-call(bf16[2,512,3072]{2,1,0:T(8,128)(2,1)} %all-gather.2.cloned.1.call-done.raw_ref, f32[32,3072]{1,0:T(8,128)} %comps_ref.3, f32[32,1536]{1,0:T(8,128)} %copy-done.8, bf16[64,208]{1,0:T(8,128)(2,1)} %solve.1.refs_0_, bf16[64,208]{1,0:T(8,128)(2,1)} %collective-permute-done.4.refs_1_, ...), custom_call_target="tpu_custom_call" | custom-call | tf_op jit(solution)/shard_map/kinship/pallas_call | solution.py:231
  (60 shorter events, 4.9 us)
Async XLA Ops:
  6.5 154.9 %all-gather.2.cloned.1.call-start = ((), (), s32[]{:S(2)}) async-start(), calls=%async_computation | async-start | bytes 7077888 | tf_op jit(solution)/shard_map/all_gather | solution.py:262
  9.1 13.8 %collective-permute-start.12 = (bf16[2,64,1536]{2,1,0:T(8,128)(2,1)S(1)}, bf16[2,64,1536]{2,1,0:T(8,128)(2,1)S(1)}, u32[]{:S(2)}, u32[]{:S(2)}) collective-permute-start(bf16[2,64,1536]{2,1,0:T(8,128)(2,1)S(1)} %get-tuple-element.5), channel_id=1, source_target_pairs={{0,1},{1,0},{2,9},{3,8},{4,17},{5,16},{6,25},{7,24},{8,3},{9,2},{1... | collective-permute-start | bytes 1179656 | tf_op jit(solution)/shard_map/ppermute | solution.py:278
  15.3 15.9 %collective-permute-start.3 = (f32[360,128]{1,0:T(8,128)}, f32[360,128]{1,0:T(8,128)S(1)}, u32[]{:S(2)}, u32[]{:S(2)}) collective-permute-start(f32[360,128]{1,0:T(8,128)} %gram.1.refs_0_), channel_id=1, source_target_pairs={{0,24},{8,16},{16,8},{24,0},{1,25},{9,17},{17,9},{25,1},{2,26},{10... | collective-permute-start | bytes 552968 | tf_op jit(solution)/shard_map/ppermute | solution.py:265
  21.7 10.2 %collective-permute-start.2 = (f32[360,128]{1,0:T(8,128)}, f32[360,128]{1,0:T(8,128)S(1)}, u32[]{:S(2)}, u32[]{:S(2)}) collective-permute-start(f32[360,128]{1,0:T(8,128)} %gram.1.refs_0_), channel_id=1, source_target_pairs={{0,16},{8,24},{16,0},{24,8},{1,17},{9,25},{17,1},{25,9},{2,18},{10... | collective-permute-start | bytes 552968 | tf_op jit(solution)/shard_map/ppermute | solution.py:265
  21.7 20.2 %collective-permute-start.1 = (f32[360,128]{1,0:T(8,128)}, f32[360,128]{1,0:T(8,128)S(1)}, u32[]{:S(2)}, u32[]{:S(2)}) collective-permute-start(f32[360,128]{1,0:T(8,128)} %gram.1.refs_0_), channel_id=1, source_target_pairs={{0,8},{8,0},{16,24},{24,16},{1,9},{9,1},{17,25},{25,17},{2,10},{10... | collective-permute-start | bytes 552968 | tf_op jit(solution)/shard_map/ppermute | solution.py:265
  22.2 113.7 %collective-permute-start.11 = (bf16[2,64,1536]{2,1,0:T(8,128)(2,1)S(1)}, bf16[2,64,1536]{2,1,0:T(8,128)(2,1)S(1)}, u32[]{:S(2)}, u32[]{:S(2)}) collective-permute-start(bf16[2,64,1536]{2,1,0:T(8,128)(2,1)S(1)} %get-tuple-element.6), channel_id=1, source_target_pairs={{0,0},{1,1},{2,8},{3,9},{4,16},{5,17},{6,24},{7,25},{8,2},{9,3},{1... | collective-permute-start | bytes 1179656 | tf_op jit(solution)/shard_map/ppermute | solution.py:278
  22.9 138.5 %copy-start = (bf16[2,64,1536]{2,1,0:T(8,128)(2,1)}, bf16[2,64,1536]{2,1,0:T(8,128)(2,1)S(1)}, u32[]{:S(2)}) copy-start(bf16[2,64,1536]{2,1,0:T(8,128)(2,1)S(1)} %collective-permute-done.12.refs_9_) | copy-start | bytes 1179652
  22.9 114.5 %collective-permute-start.18 = (bf16[2,64,1536]{2,1,0:T(8,128)(2,1)S(1)}, bf16[2,64,1536]{2,1,0:T(8,128)(2,1)S(1)}, u32[]{:S(2)}, u32[]{:S(2)}) collective-permute-start(bf16[2,64,1536]{2,1,0:T(8,128)(2,1)S(1)} %collective-permute-done.12.refs_9_), channel_id=1, source_target_pairs={{0,24},{8,16},{16,8},{24,0},{1,25},{9,17},{17,9},{25,1},{2,26},{10... | collective-permute-start | bytes 1179656 | tf_op jit(solution)/shard_map/ppermute | solution.py:265
  31.2 21.9 %collective-permute-start = (f32[32,1536]{1,0:T(8,128)S(1)}, f32[32,1536]{1,0:T(8,128)S(1)}, u32[]{:S(2)}, u32[]{:S(2)}) collective-permute-start(f32[32,1536]{1,0:T(8,128)S(1)} %constant_dynamic-slice_fusion), channel_id=1, source_target_pairs={{0,0},{1,1},{2,8},{3,9},{4,16},{5,17},{6,24},{7,25},{8,2},{9,3},{1... | collective-permute-start | bytes 589832 | tf_op jit(solution)/shard_map/ppermute | solution.py:281
  49.9 53.1 %collective-permute-start.10 = (bf16[64,208]{1,0:T(8,128)(2,1)}, bf16[64,208]{1,0:T(8,128)(2,1)S(1)}, u32[]{:S(2)}, u32[]{:S(2)}) collective-permute-start(bf16[64,208]{1,0:T(8,128)(2,1)} %solve.1.refs_0_), channel_id=1, source_target_pairs={{0,7},{1,6},{2,5},{3,4},{4,3},{5,2},{6,1},{7,0},{8,15},{9,14},{10,... | collective-permute-start | bytes 79880 | tf_op jit(solution)/shard_map/ppermute | solution.py:265
  49.9 54.9 %collective-permute-start.9 = (bf16[64,208]{1,0:T(8,128)(2,1)}, bf16[64,208]{1,0:T(8,128)(2,1)S(1)}, u32[]{:S(2)}, u32[]{:S(2)}) collective-permute-start(bf16[64,208]{1,0:T(8,128)(2,1)} %solve.1.refs_0_), channel_id=1, source_target_pairs={{0,6},{1,7},{2,4},{3,5},{4,2},{5,3},{6,0},{7,1},{8,14},{9,15},{10,... | collective-permute-start | bytes 79880 | tf_op jit(solution)/shard_map/ppermute | solution.py:265
  53.1 108.3 %copy-start.8 = (f32[32,1536]{1,0:T(8,128)}, f32[32,1536]{1,0:T(8,128)S(1)}, u32[]{:S(2)}) copy-start(f32[32,1536]{1,0:T(8,128)S(1)} %collective-permute-done.col_comps_ref) | copy-start | bytes 589828
  53.1 74.6 %collective-permute-start.8 = (bf16[64,208]{1,0:T(8,128)(2,1)}, bf16[64,208]{1,0:T(8,128)(2,1)S(1)}, u32[]{:S(2)}, u32[]{:S(2)}) collective-permute-start(bf16[64,208]{1,0:T(8,128)(2,1)} %solve.1.refs_0_), channel_id=1, source_target_pairs={{0,5},{1,4},{2,7},{3,6},{4,1},{5,0},{6,3},{7,2},{8,13},{9,12},{10,... | collective-permute-start | bytes 79880 | tf_op jit(solution)/shard_map/ppermute | solution.py:265
  103.0 58.5 %copy-start.12 = (bf16[64,208]{1,0:T(8,128)(2,1)}, bf16[64,208]{1,0:T(8,128)(2,1)S(1)}, u32[]{:S(2)}) copy-start(bf16[64,208]{1,0:T(8,128)(2,1)S(1)} %collective-permute-done.10.refs_7_) | copy-start | bytes 79876
  103.0 26.9 %collective-permute-start.7 = (bf16[64,208]{1,0:T(8,128)(2,1)}, bf16[64,208]{1,0:T(8,128)(2,1)S(1)}, u32[]{:S(2)}, u32[]{:S(2)}) collective-permute-start(bf16[64,208]{1,0:T(8,128)(2,1)} %solve.1.refs_0_), channel_id=1, source_target_pairs={{0,4},{1,5},{2,6},{3,7},{4,0},{5,1},{6,2},{7,3},{8,12},{9,13},{10,... | collective-permute-start | bytes 79880 | tf_op jit(solution)/shard_map/ppermute | solution.py:265
  104.8 56.6 %copy-start.13 = (bf16[64,208]{1,0:T(8,128)(2,1)}, bf16[64,208]{1,0:T(8,128)(2,1)S(1)}, u32[]{:S(2)}) copy-start(bf16[64,208]{1,0:T(8,128)(2,1)S(1)} %collective-permute-done.9.refs_6_) | copy-start | bytes 79876
  104.8 25.6 %collective-permute-start.6 = (bf16[64,208]{1,0:T(8,128)(2,1)}, bf16[64,208]{1,0:T(8,128)(2,1)S(1)}, u32[]{:S(2)}, u32[]{:S(2)}) collective-permute-start(bf16[64,208]{1,0:T(8,128)(2,1)} %solve.1.refs_0_), channel_id=1, source_target_pairs={{0,3},{1,2},{2,1},{3,0},{4,7},{5,6},{6,5},{7,4},{8,11},{9,10},{10,... | collective-permute-start | bytes 79880 | tf_op jit(solution)/shard_map/ppermute | solution.py:265
  127.7 5.6 %collective-permute-start.5 = (bf16[64,208]{1,0:T(8,128)(2,1)}, bf16[64,208]{1,0:T(8,128)(2,1)S(1)}, u32[]{:S(2)}, u32[]{:S(2)}) collective-permute-start(bf16[64,208]{1,0:T(8,128)(2,1)} %solve.1.refs_0_), channel_id=1, source_target_pairs={{0,2},{1,3},{2,0},{3,1},{4,6},{5,7},{6,4},{7,5},{8,10},{9,11},{10,... | collective-permute-start | bytes 79880 | tf_op jit(solution)/shard_map/ppermute | solution.py:265
  129.9 7.0 %collective-permute-start.4 = (bf16[64,208]{1,0:T(8,128)(2,1)}, bf16[64,208]{1,0:T(8,128)(2,1)}, u32[]{:S(2)}, u32[]{:S(2)}) collective-permute-start(bf16[64,208]{1,0:T(8,128)(2,1)} %solve.1.refs_0_), channel_id=1, source_target_pairs={{0,1},{1,0},{2,3},{3,2},{4,5},{5,4},{6,7},{7,6},{8,9},{9,8},{10,11... | collective-permute-start | bytes 79880 | tf_op jit(solution)/shard_map/ppermute | solution.py:265
  130.4 12.9 %collective-permute-start.16 = (bf16[2,64,1536]{2,1,0:T(8,128)(2,1)S(1)}, bf16[2,64,1536]{2,1,0:T(8,128)(2,1)S(1)}, u32[]{:S(2)}, u32[]{:S(2)}) collective-permute-start(bf16[2,64,1536]{2,1,0:T(8,128)(2,1)S(1)} %collective-permute-done.12.refs_9_), channel_id=1, source_target_pairs={{0,16},{8,24},{16,0},{24,8},{1,17},{9,25},{17,1},{25,9},{2,18},{10... | collective-permute-start | bytes 1179656 | tf_op jit(solution)/shard_map/ppermute | solution.py:265
  133.3 12.6 %collective-permute-start.14 = (bf16[2,64,1536]{2,1,0:T(8,128)(2,1)S(1)}, bf16[2,64,1536]{2,1,0:T(8,128)(2,1)S(1)}, u32[]{:S(2)}, u32[]{:S(2)}) collective-permute-start(bf16[2,64,1536]{2,1,0:T(8,128)(2,1)S(1)} %collective-permute-done.12.refs_9_), channel_id=1, source_target_pairs={{0,8},{8,0},{16,24},{24,16},{1,9},{9,1},{17,25},{25,17},{2,10},{10... | collective-permute-start | bytes 1179656 | tf_op jit(solution)/shard_map/ppermute | solution.py:265
  135.9 19.5 %collective-permute-start.17 = (bf16[2,64,1536]{2,1,0:T(8,128)(2,1)S(1)}, bf16[2,64,1536]{2,1,0:T(8,128)(2,1)S(1)}, u32[]{:S(2)}, u32[]{:S(2)}) collective-permute-start(bf16[2,64,1536]{2,1,0:T(8,128)(2,1)S(1)} %collective-permute-done.11.refs_8_), channel_id=1, source_target_pairs={{0,24},{8,16},{16,8},{24,0},{1,25},{9,17},{17,9},{25,1},{2,26},{10... | collective-permute-start | bytes 1179656 | tf_op jit(solution)/shard_map/ppermute | solution.py:265
  136.9 23.0 %collective-permute-start.15 = (bf16[2,64,1536]{2,1,0:T(8,128)(2,1)S(1)}, bf16[2,64,1536]{2,1,0:T(8,128)(2,1)S(1)}, u32[]{:S(2)}, u32[]{:S(2)}) collective-permute-start(bf16[2,64,1536]{2,1,0:T(8,128)(2,1)S(1)} %collective-permute-done.11.refs_8_), channel_id=1, source_target_pairs={{0,16},{8,24},{16,0},{24,8},{1,17},{9,25},{17,1},{25,9},{2,18},{10... | collective-permute-start | bytes 1179656 | tf_op jit(solution)/shard_map/ppermute | solution.py:265
  137.4 24.0 %collective-permute-start.13 = (bf16[2,64,1536]{2,1,0:T(8,128)(2,1)S(1)}, bf16[2,64,1536]{2,1,0:T(8,128)(2,1)S(1)}, u32[]{:S(2)}, u32[]{:S(2)}) collective-permute-start(bf16[2,64,1536]{2,1,0:T(8,128)(2,1)S(1)} %collective-permute-done.11.refs_8_), channel_id=1, source_target_pairs={{0,8},{8,0},{16,24},{24,16},{1,9},{9,1},{17,25},{25,17},{2,10},{10... | collective-permute-start | bytes 1179656 | tf_op jit(solution)/shard_map/ppermute | solution.py:265
  (14 other events, 238.0 us)
Sparse Core Ops, SparseCore 0:
  9.1 124.8 all-gather.1

commit v2 on v1

--- a/solution.py
+++ b/solution.py
@@ -10,6 +10,7 @@
 F32, BF16 = jnp.float32, jnp.bfloat16
 VMEM_LIMIT = 56 * 1024 * 1024
 SUB = 8
+CHUNKS = 2
 
 
 def split3(x):
@@ -172,48 +173,82 @@
     return resid.astype(BF16), (2.0 * sdev).astype(BF16)
 
 
-def kin_kernel(rows, ratio, cols, raw_ref, comps_ref, col_comps_ref, *refs):
+def reversed_bits(value, size):
+    bits = size.bit_length() - 1
+    return sum(((value >> i) & 1) << (bits - 1 - i) for i in range(bits))
+
+
+def line_of(plane, source, size):
+    return source ^ reversed_bits(plane, size)
+
+
+def columns_kernel(rows, ratio, cols, col_comps_ref, *refs):
     coef_refs = refs[:cols]
     piece_refs = refs[cols : cols + rows * ratio]
-    out_ref, coef, raw_cols, col_r, col_s, sems = refs[cols + rows * ratio :]
+    coef_out, col_r, col_s, coef, raw_cols, sems = refs[cols + rows * ratio :]
     here = coef_refs[0].shape[0]
+    width = col_r.shape[1]
+    r = lax.axis_index("rows")
+    q = lax.axis_index("cols")
+    copies = []
+    for d in range(cols):
+        place = pl.multiple_of((q ^ d) * here, here)
+        copies.append(
+            pltpu.make_async_copy(coef_refs[d], coef.at[pl.ds(place, here), :], sems.at[len(copies)])
+        )
+    for d in range(rows):
+        for k in range(ratio):
+            source = line_of(q // ratio, r ^ d, rows)
+            owner = source * ratio + lax.rem(lax.rem(q, ratio) + ratio - k, ratio)
+            place = pl.multiple_of(owner * here, here)
+            copies.append(
+                pltpu.make_async_copy(
+                    piece_refs[d * ratio + k],
+                    raw_cols.at[:, pl.ds(place, here), :],
+                    sems.at[len(copies)],
+                )
+            )
+    for copy in copies:
+        copy.start()
+    for copy in copies:
+        copy.wait()
+    coef_out[...] = coef[...]
+    step = 256 if width % 256 == 0 else width
+    for at in range(0, width, step):
+        span = slice(at, at + step)
+        resid, sdev = panel(
+            coef[...], col_comps_ref[:, span], raw_cols[0, :, span], raw_cols[1, :, span]
+        )
+        col_r[:, span] = resid
+        col_s[:, span] = sdev
+
+
+def columns_call(rows, ratio, cols, col_comps, coefs, pieces):
+    comps, width = col_comps.shape
+    markers = coefs[0].shape[0] * cols
+    anywhere = pl.BlockSpec(memory_space=pl.ANY)
+    return pl.pallas_call(
+        functools.partial(columns_kernel, rows, ratio, cols),
+        in_specs=[pl.BlockSpec(memory_space=pltpu.VMEM)] + [anywhere] * (len(coefs) + len(pieces)),
+        out_shape=(
+            jax.ShapeDtypeStruct((markers, coef_rows(comps)), BF16),
+            jax.ShapeDtypeStruct((markers, width), BF16),
+            jax.ShapeDtypeStruct((markers, width), BF16),
+        ),
+        scratch_shapes=[
+            pltpu.VMEM((markers, coef_rows(comps)), BF16),
+            pltpu.VMEM((2, markers, width), BF16),
+            pltpu.SemaphoreType.DMA((len(coefs) + len(pieces),)),
+        ],
+        compiler_params=pltpu.CompilerParams(vmem_limit_bytes=VMEM_LIMIT),
+        name="columns",
+    )(col_comps, *coefs, *pieces)
+
+
+def kin_kernel(raw_ref, comps_ref, coef_ref, col_r, col_s, *refs):
+    out_ref = refs[-1]
     width = out_ref.shape[1]
-
-    @pl.when(pl.program_id(0) == 0)
-    def _():
-        r = lax.axis_index("rows")
-        q = lax.axis_index("cols")
-        copies = []
-        for d in range(cols):
-            place = pl.multiple_of((q ^ d) * here, here)
-            copies.append(
-                pltpu.make_async_copy(coef_refs[d], coef.at[pl.ds(place, here), :], sems.at[len(copies)])
-            )
-        for d in range(rows):
-            for k in range(ratio):
-                owner = (r ^ d) * ratio + lax.rem(lax.rem(q, ratio) + ratio - k, ratio)
-                place = pl.multiple_of(owner * here, here)
-                copies.append(
-                    pltpu.make_async_copy(
-                        piece_refs[d * ratio + k],
-                        raw_cols.at[:, pl.ds(place, here), :],
-                        sems.at[len(copies)],
-                    )
-                )
-        for copy in copies:
-            copy.start()
-        for copy in copies:
-            copy.wait()
-        step = 256 if width % 256 == 0 else width
-        for at in range(0, width, step):
-            span = slice(at, at + step)
-            resid, sdev = panel(
-                coef[...], col_comps_ref[:, span], raw_cols[0, :, span], raw_cols[1, :, span]
-            )
-            col_r[:, span] = resid
-            col_s[:, span] = sdev
-
-    resid, sdev = panel(coef[...], comps_ref[...], raw_ref[0], raw_ref[1])
+    resid, sdev = panel(coef_ref[...], comps_ref[...], raw_ref[0], raw_ref[1])
     contract = (((0,), (0,)), ((), ()))
     step = 512 if width % 512 == 0 else width
     for at in range(0, width, step):
@@ -223,32 +258,36 @@
         out_ref[:, span] = numer / denom
 
 
-def kin_call(rows, ratio, cols, raw, components, col_comps, coefs, pieces):
-    _, markers, people = raw.shape
-    comps, width = col_comps.shape
-    tile = 512 if people % 512 == 0 else people
-    anywhere = pl.BlockSpec(memory_space=pl.ANY)
+def kin_call(start, raw, components, coef, col_r, col_s, before):
+    _, markers, count = raw.shape
+    comps, people = components.shape
+    width = col_r.shape[1]
+    tile = 512 if count % 512 == 0 else count
+    first = start // tile
+    whole = lambda i: (0, 0)
+    in_specs = [
+        pl.BlockSpec((2, markers, tile), lambda i: (0, 0, i)),
+        pl.BlockSpec((comps, tile), lambda i: (0, i + first)),
+        pl.BlockSpec(coef.shape, whole),
+        pl.BlockSpec((markers, width), whole),
+        pl.BlockSpec((markers, width), whole),
+    ]
+    operands = [raw, components, coef, col_r, col_s]
+    aliases = {}
+    if before is not None:
+        in_specs.append(pl.BlockSpec(memory_space=pl.ANY))
+        aliases = {len(operands): 0}
+        operands.append(before)
     return pl.pallas_call(
-        functools.partial(kin_kernel, rows, ratio, cols),
-        grid=(people // tile,),
-        in_specs=[
-            pl.BlockSpec((2, markers, tile), lambda i: (0, 0, i)),
-            pl.BlockSpec((comps, tile), lambda i: (0, i)),
-            pl.BlockSpec((comps, width), lambda i: (0, 0)),
-        ]
-        + [anywhere] * (len(coefs) + len(pieces)),
-        out_specs=pl.BlockSpec((tile, width), lambda i: (i, 0)),
+        kin_kernel,
+        grid=(count // tile,),
+        in_specs=in_specs,
+        out_specs=pl.BlockSpec((tile, width), lambda i: (i + first, 0)),
         out_shape=jax.ShapeDtypeStruct((people, width), F32),
-        scratch_shapes=[
-            pltpu.VMEM((markers, coef_rows(comps)), BF16),
-            pltpu.VMEM((2, markers, width), BF16),
-            pltpu.VMEM((markers, width), BF16),
-            pltpu.VMEM((markers, width), BF16),
-            pltpu.SemaphoreType.DMA((len(coefs) + len(pieces),)),
-        ],
+        input_output_aliases=aliases,
         compiler_params=pltpu.CompilerParams(vmem_limit_bytes=VMEM_LIMIT),
         name="kinship",
-    )(raw, components, col_comps, *coefs, *pieces)
+    )(*operands)
 
 
 def per_device(dosage, present, components):
@@ -259,7 +298,6 @@
     width = people // ratio
     col = lax.axis_index("cols")
     raw = jnp.stack([dosage.astype(BF16), present.astype(BF16)])
-    raw_rows = lax.all_gather(raw, "cols", axis=1, tiled=True)
 
     def across(x, axis, size):
         return [x] + [lax.ppermute(x, axis, [(i, i ^ d) for i in range(size)]) for d in range(1, size)]
@@ -270,7 +308,7 @@
         part = (col % ratio + k) % ratio
         mine = lax.dynamic_slice_in_dim(raw, part * width, width, 2)
         moves = [
-            (r * cols + z * ratio + c, z * cols + r * ratio + (c + k) % ratio)
+            (r * cols + z * ratio + c, line_of(r, z, rows) * cols + r * ratio + (c + k) % ratio)
             for r in range(rows)
             for z in range(rows)
             for c in range(ratio)
@@ -279,13 +317,22 @@
         if k == 0:
             mine = lax.dynamic_slice_in_dim(components, part * width, width, 1)
             col_comps = lax.ppermute(mine, both, moves) if len(moves) > 1 else mine
+    raw, *pieces = lax.optimization_barrier((raw, *pieces))
+    starts = [people * i // CHUNKS for i in range(CHUNKS + 1)]
+    raw_rows = [
+        lax.all_gather(raw[:, :, a:b], "cols", axis=1, tiled=True) for a, b in zip(starts, starts[1:])
+    ]
     spread = [across(piece, "rows", rows) for piece in pieces]
     pieces = [spread[k][d] for d in range(rows) for k in range(ratio)]
 
     gram = gram_call(dosage, present, components)
     coef = solve_call(across(gram, "rows", rows), comps, markers)
     coefs = across(coef, "cols", cols)
-    return kin_call(rows, ratio, cols, raw_rows, components, col_comps, coefs, pieces)
+    coef, col_r, col_s = columns_call(rows, ratio, cols, col_comps, coefs, pieces)
+    out = None
+    for start, part in zip(starts, raw_rows):
+        out = kin_call(start, part, components, coef, col_r, col_s, out)
+    return out
 
 
 def solution(mesh):

time: 191 us -> 180 us (0.942)
  starting transfers between devices: 104 us -> 85.9 us
  Pallas kernels: 34.7 us -> 42.6 us
    ppermute x16, starting transfers between devices: 102 us -> 83.8 us  [across(): lax.ppermute(x, axis, [(i, i ^ d) for i in range(size)])]
    pallas_call x1 -> x3, Pallas kernels: 21.8 us -> 29.6 us  [the longest x2 22.6 us: kin_call(): pl.pallas_call(kin_kernel, grid=(count // tile,), in_specs=in_specs, out_...]
    ppermute x16, waiting for transfers between devices: 33.4 us -> 31 us  [across(): lax.ppermute(x, axis, [(i, i ^ d) for i in range(size)])]
  transfers between devices with their start and end apart: 20 -> 21, of which waited for: 8 -> 11; matrix products, arithmetic and copies ran while one was open for 1% -> 0% of each run, Pallas kernels for 7% -> 17%
where the time goes in v2:
time: 180 us; the launch traced here: 179 us
  starting transfers between devices  85.9 us (48%)
  Pallas kernels  42.6 us (24%)
  waiting for transfers between devices  32.4 us (18%)
  between operations  13.6 us (8%)
  local copies, waits for them, and re-layouts  3.12 us (2%)
    ppermute x16, starting transfers between devices, across(): lax.ppermute(x, axis, [(i, i ^ d) for i in range(size)])  83.8 us
    ppermute x16, waiting for transfers between devices, across(): lax.ppermute(x, axis, [(i, i ^ d) for i in range(size)])  31 us
    pallas_call x2, Pallas kernels, kin_call(): pl.pallas_call(kin_kernel, grid=(count // tile,), in_specs=in_specs, out_...  22.6 us
    pallas_call x1, Pallas kernels, solve_call(): pl.pallas_call(functools.partial(solve_kernel, comps, markers), out_shape...  7.35 us
    pallas_call x1, Pallas kernels, columns_call(): pl.pallas_call(functools.partial(columns_kernel, rows, ratio, cols), in_s...  7.02 us
    pallas_call x1, Pallas kernels, gram_call(): pl.pallas_call(gram_kernel, out_shape=jax.ShapeDtypeStruct((total // 2 +...  5.65 us
  transfers between devices with their start and end apart: 21, of which 11 were waited for; matrix products, arithmetic and copies ran while one was open for 0% of the time, Pallas kernels for 17%

profile of v2, /device:TPU:0, one launch (start us, length us, event | category | flops | bytes accessed | tf_op | source)
XLA Modules:
  0.0 179.2 jit_solution(11667577697136514789)
XLA Ops:
  6.5 1.5 convert_bitcast_fusion
  10.0 1.0 fusion.2
  11.8 5.7 %gram.1.refs_0_ = f32[360,128]{1,0:T(8,128)} custom-call(s32[64,3072]{1,0:T(8,128)} %dosage_ref.1, s32[64,3072]{1,0:T(8,128)} %present_ref.1, f32[32,3072]{1,0:T(8,128)} %comps_ref.5), custom_call_target="tpu_custom_call" | custom-call | tf_op jit(solution)/shard_map/gram/pallas_call | solution.py:63
  17.4 25.6 %collective-permute-start.5 = (f32[360,128]{1,0:T(8,128)}, f32[360,128]{1,0:T(8,128)S(1)}, u32[]{:S(2)}, u32[]{:S(2)}) collective-permute-start(f32[360,128]{1,0:T(8,128)} %gram.1.refs_0_), channel_id=1, source_target_pairs={{0,24},{8,16},{16,8},{24,0},{1,25},{9,17},{17,9},{25,1},{2,26},{10... | collective-permute-start | bytes 552968 | tf_op jit(solution)/shard_map/ppermute | solution.py:303
  43.1 31.5 %collective-permute-start.4 = (f32[360,128]{1,0:T(8,128)}, f32[360,128]{1,0:T(8,128)S(1)}, u32[]{:S(2)}, u32[]{:S(2)}) collective-permute-start(f32[360,128]{1,0:T(8,128)} %gram.1.refs_0_), channel_id=1, source_target_pairs={{0,16},{8,24},{16,0},{24,8},{1,17},{9,25},{17,1},{25,9},{2,18},{10... | collective-permute-start | bytes 552968 | tf_op jit(solution)/shard_map/ppermute | solution.py:303
  74.5 1.5 collective-permute-start.17
  76.9 4.9 %collective-permute-done.4.refs_2_ = f32[360,128]{1,0:T(8,128)S(1)} collective-permute-done((f32[360,128]{1,0:T(8,128)}, f32[360,128]{1,0:T(8,128)S(1)}, u32[]{:S(2)}, u32[]{:S(2)}) %collective-permute-start.4) | collective-permute-done | bytes 184352 | tf_op jit(solution)/shard_map/ppermute | solution.py:303
  81.8 0.9 collective-permute-done.3.refs_1_
  83.4 7.3 %solve.1.refs_0_ = bf16[64,208]{1,0:T(8,128)(2,1)} custom-call(f32[360,128]{1,0:T(8,128)} %gram.1.refs_0_, f32[360,128]{1,0:T(8,128)} %copy-done.12, f32[360,128]{1,0:T(8,128)} %copy-done.11, f32[360,128]{1,0:T(8,128)} %copy-done.10), custom_call_target="tpu_custom_call" | custom-call | tf_op jit(solution)/shard_map/solve/pallas_call | solution.py:151
  90.7 2.3 %collective-permute-start.12 = (bf16[64,208]{1,0:T(8,128)(2,1)}, bf16[64,208]{1,0:T(8,128)(2,1)S(1)}, u32[]{:S(2)}, u32[]{:S(2)}) collective-permute-start(bf16[64,208]{1,0:T(8,128)(2,1)} %solve.1.refs_0_), channel_id=1, source_target_pairs={{0,7},{1,6},{2,5},{3,4},{4,3},{5,2},{6,1},{7,0},{8,15},{9,14},{10,... | collective-permute-start | bytes 79880 | tf_op jit(solution)/shard_map/ppermute | solution.py:303
  93.0 1.2 collective-permute-start.11
  94.2 9.5 %collective-permute-start.10 = (bf16[64,208]{1,0:T(8,128)(2,1)}, bf16[64,208]{1,0:T(8,128)(2,1)S(1)}, u32[]{:S(2)}, u32[]{:S(2)}) collective-permute-start(bf16[64,208]{1,0:T(8,128)(2,1)} %solve.1.refs_0_), channel_id=1, source_target_pairs={{0,5},{1,4},{2,7},{3,6},{4,1},{5,0},{6,3},{7,2},{8,13},{9,12},{10,... | collective-permute-start | bytes 79880 | tf_op jit(solution)/shard_map/ppermute | solution.py:303
  103.8 1.6 collective-permute-start.9
  105.4 3.9 %collective-permute-start.8 = (bf16[64,208]{1,0:T(8,128)(2,1)}, bf16[64,208]{1,0:T(8,128)(2,1)S(1)}, u32[]{:S(2)}, u32[]{:S(2)}) collective-permute-start(bf16[64,208]{1,0:T(8,128)(2,1)} %solve.1.refs_0_), channel_id=1, source_target_pairs={{0,3},{1,2},{2,1},{3,0},{4,7},{5,6},{6,5},{7,4},{8,11},{9,10},{10,... | collective-permute-start | bytes 79880 | tf_op jit(solution)/shard_map/ppermute | solution.py:303
  109.3 2.3 %collective-permute-start.7 = (bf16[64,208]{1,0:T(8,128)(2,1)}, bf16[64,208]{1,0:T(8,128)(2,1)S(1)}, u32[]{:S(2)}, u32[]{:S(2)}) collective-permute-start(bf16[64,208]{1,0:T(8,128)(2,1)} %solve.1.refs_0_), channel_id=1, source_target_pairs={{0,2},{1,3},{2,0},{3,1},{4,6},{5,7},{6,4},{7,5},{8,10},{9,11},{10,... | collective-permute-start | bytes 79880 | tf_op jit(solution)/shard_map/ppermute | solution.py:303
  112.7 1.0 collective-permute-done.9.refs_4_
  113.8 3.7 %collective-permute-done.8.refs_3_ = bf16[64,208]{1,0:T(8,128)(2,1)S(1)} collective-permute-done((bf16[64,208]{1,0:T(8,128)(2,1)}, bf16[64,208]{1,0:T(8,128)(2,1)S(1)}, u32[]{:S(2)}, u32[]{:S(2)}) %collective-permute-start.8) | collective-permute-done | bytes 26656 | tf_op jit(solution)/shard_map/ppermute | solution.py:303
  117.6 3.4 %collective-permute-start.16 = (bf16[2,64,1536]{2,1,0:T(8,128)(2,1)S(1)}, bf16[2,64,1536]{2,1,0:T(8,128)(2,1)S(1)}, u32[]{:S(2)}, u32[]{:S(2)}) collective-permute-start(bf16[2,64,1536]{2,1,0:T(8,128)(2,1)S(1)} %collective-permute-done.1.refs_9_), channel_id=1, source_target_pairs={{0,16},{8,24},{16,0},{24,8},{1,17},{9,25},{17,1},{25,9},{2,18},{10... | collective-permute-start | bytes 1179656 | tf_op jit(solution)/shard_map/ppermute | solution.py:303
  121.1 11.6 %collective-permute-done.15.refs_12_ = bf16[2,64,1536]{2,1,0:T(8,128)(2,1)S(1)} collective-permute-done((bf16[2,64,1536]{2,1,0:T(8,128)(2,1)S(1)}, bf16[2,64,1536]{2,1,0:T(8,128)(2,1)S(1)}, u32[]{:S(2)}, u32[]{:S(2)}) %collective-permute-start.15) | collective-permute-done | bytes 393248 | tf_op jit(solution)/shard_map/ppermute | solution.py:303
  132.7 3.1 %collective-permute-done.18.refs_15_ = bf16[2,64,1536]{2,1,0:T(8,128)(2,1)S(1)} collective-permute-done((bf16[2,64,1536]{2,1,0:T(8,128)(2,1)S(1)}, bf16[2,64,1536]{2,1,0:T(8,128)(2,1)S(1)}, u32[]{:S(2)}, u32[]{:S(2)}) %collective-permute-start.18) | collective-permute-done | bytes 393248 | tf_op jit(solution)/shard_map/ppermute | solution.py:303
  135.7 5.5 %collective-permute-done.16.refs_13_ = bf16[2,64,1536]{2,1,0:T(8,128)(2,1)S(1)} collective-permute-done((bf16[2,64,1536]{2,1,0:T(8,128)(2,1)S(1)}, bf16[2,64,1536]{2,1,0:T(8,128)(2,1)S(1)}, u32[]{:S(2)}, u32[]{:S(2)}) %collective-permute-start.16) | collective-permute-done | bytes 393248 | tf_op jit(solution)/shard_map/ppermute | solution.py:303
  142.7 7.0 %columns.1 = (bf16[512,208]{1,0:T(8,128)(2,1)}, bf16[512,1536]{1,0:T(8,128)(2,1)}, bf16[512,1536]{1,0:T(8,128)(2,1)}) custom-call(f32[32,1536]{1,0:T(8,128)} %copy-done.9, bf16[64,208]{1,0:T(8,128)(2,1)} %solve.1.refs_0_, bf16[64,208]{1,0:T(8,128)(2,1)} %copy-done.19, bf16[64,208]{1,0:T(8,128)(2,1)} %copy-done.18, bf16[64,208]{1,0:T(8,128)(2,1)} %copy-done.17, ...), custom_call_target="tpu_custom_call" | custom-call | tf_op jit(solution)/shard_map/columns/pallas_call | solution.py:230
  149.8 11.3 %kinship.2.refs_0_ = f32[3072,1536]{1,0:T(8,128)} custom-call(bf16[2,512,1536]{2,1,0:T(8,128)(2,1)} %all-gather.5.cloned.1.call-done.raw_ref, f32[32,3072]{1,0:T(8,128)} %comps_ref.5, bf16[512,208]{1,0:T(8,128)(2,1)} %get-tuple-element.14.coef_ref, bf16[512,1536]{1,0:T(8,128)(2,1)} %get-tuple-element.15.col_r, bf16[512,1536]{1,0:T(8,128)(2,1)} %get-tuple-element.16.col_s), custom_call_target="tpu_custom_call" | custom-call | tf_op jit(solution)/shard_map/kinship/pallas_call | solution.py:281
  161.1 11.3 %kinship.3 = f32[3072,1536]{1,0:T(8,128)} custom-call(bf16[2,512,1536]{2,1,0:T(8,128)(2,1)} %all-gather.3.cloned.1.call-done.raw_ref, f32[32,3072]{1,0:T(8,128)} %comps_ref.5, bf16[512,208]{1,0:T(8,128)(2,1)} %get-tuple-element.14.coef_ref, bf16[512,1536]{1,0:T(8,128)(2,1)} %get-tuple-element.15.col_r, ...), custom_call_target="tpu_custom_call", output_to_operand_aliasing={{}: (5, {})} | custom-call | tf_op jit(solution)/shard_map/kinship/pallas_call | solution.py:281
  (70 shorter events, 7.0 us)
Async XLA Ops:
  6.5 143.3 %all-gather.5.cloned.1.call-start = ((), (), s32[]{:S(2)}) async-start(), calls=%async_computation.1 | async-start | bytes 3538944 | tf_op jit(solution)/shard_map/all_gather | solution.py:323
  8.1 67.9 %copy-start = (f32[32,3072]{1,0:T(8,128)S(1)}, f32[32,3072]{1,0:T(8,128)}, u32[]{:S(2)}) copy-start(f32[32,3072]{1,0:T(8,128)} %comps_ref.5) | copy-start | bytes 1179652
  8.1 1.9 %collective-permute-start.1 = (bf16[2,64,1536]{2,1,0:T(8,128)(2,1)S(1)}, bf16[2,64,1536]{2,1,0:T(8,128)(2,1)S(1)}, u32[]{:S(2)}, u32[]{:S(2)}) collective-permute-start(bf16[2,64,1536]{2,1,0:T(8,128)(2,1)S(1)} %get-tuple-element.19), channel_id=1, source_target_pairs={{0,1},{1,0},{2,9},{3,8},{4,17},{5,16},{6,25},{7,24},{8,19},{9,18},... | collective-permute-start | bytes 1179656 | tf_op jit(solution)/shard_map/ppermute | solution.py:316
  8.6 1.4 collective-permute-start
  10.0 131.4 %copy-start.1 = (bf16[2,64,1536]{2,1,0:T(8,128)(2,1)}, bf16[2,64,1536]{2,1,0:T(8,128)(2,1)S(1)}, u32[]{:S(2)}) copy-start(bf16[2,64,1536]{2,1,0:T(8,128)(2,1)S(1)} %collective-permute-done.1.refs_9_) | copy-start | bytes 1179652
  10.0 131.4 %copy-start.2 = (bf16[2,64,1536]{2,1,0:T(8,128)(2,1)}, bf16[2,64,1536]{2,1,0:T(8,128)(2,1)S(1)}, u32[]{:S(2)}) copy-start(bf16[2,64,1536]{2,1,0:T(8,128)(2,1)S(1)} %collective-permute-done.refs_8_) | copy-start | bytes 1179652
  11.0 150.1 %all-gather.3.cloned.1.call-start = ((), (), s32[]{:S(2)}) async-start(), calls=%async_computation | async-start | bytes 3538944 | tf_op jit(solution)/shard_map/all_gather | solution.py:323
  17.4 59.4 %collective-permute-start.5 = (f32[360,128]{1,0:T(8,128)}, f32[360,128]{1,0:T(8,128)S(1)}, u32[]{:S(2)}, u32[]{:S(2)}) collective-permute-start(f32[360,128]{1,0:T(8,128)} %gram.1.refs_0_), channel_id=1, source_target_pairs={{0,24},{8,16},{16,8},{24,0},{1,25},{9,17},{17,9},{25,1},{2,26},{10... | collective-permute-start | bytes 552968 | tf_op jit(solution)/shard_map/ppermute | solution.py:303
  43.1 38.7 %collective-permute-start.4 = (f32[360,128]{1,0:T(8,128)}, f32[360,128]{1,0:T(8,128)S(1)}, u32[]{:S(2)}, u32[]{:S(2)}) collective-permute-start(f32[360,128]{1,0:T(8,128)} %gram.1.refs_0_), channel_id=1, source_target_pairs={{0,16},{8,24},{16,0},{24,8},{1,17},{9,25},{17,1},{25,9},{2,18},{10... | collective-permute-start | bytes 552968 | tf_op jit(solution)/shard_map/ppermute | solution.py:303
  74.5 8.2 %collective-permute-start.3 = (f32[360,128]{1,0:T(8,128)}, f32[360,128]{1,0:T(8,128)S(1)}, u32[]{:S(2)}, u32[]{:S(2)}) collective-permute-start(f32[360,128]{1,0:T(8,128)} %gram.1.refs_0_), channel_id=1, source_target_pairs={{0,8},{8,0},{16,24},{24,16},{1,9},{9,1},{17,25},{25,17},{2,10},{10... | collective-permute-start | bytes 552968 | tf_op jit(solution)/shard_map/ppermute | solution.py:303
  74.5 46.4 %collective-permute-start.17 = (bf16[2,64,1536]{2,1,0:T(8,128)(2,1)S(1)}, bf16[2,64,1536]{2,1,0:T(8,128)(2,1)S(1)}, u32[]{:S(2)}, u32[]{:S(2)}) collective-permute-start(bf16[2,64,1536]{2,1,0:T(8,128)(2,1)S(1)} %collective-permute-done.refs_8_), channel_id=1, source_target_pairs={{0,24},{8,16},{16,8},{24,0},{1,25},{9,17},{17,9},{25,1},{2,26},{10... | collective-permute-start | bytes 1179656 | tf_op jit(solution)/shard_map/ppermute | solution.py:303
  76.0 27.8 %collective-permute-start.2 = (f32[32,1536]{1,0:T(8,128)S(1)}, f32[32,1536]{1,0:T(8,128)S(1)}, u32[]{:S(2)}, u32[]{:S(2)}) collective-permute-start(f32[32,1536]{1,0:T(8,128)S(1)} %constant_dynamic-slice_fusion), channel_id=1, source_target_pairs={{0,0},{1,1},{2,8},{3,9},{4,16},{5,17},{6,24},{7,25},{8,18},{9,19},... | collective-permute-start | bytes 589832 | tf_op jit(solution)/shard_map/ppermute | solution.py:319
  90.7 14.7 %collective-permute-start.12 = (bf16[64,208]{1,0:T(8,128)(2,1)}, bf16[64,208]{1,0:T(8,128)(2,1)S(1)}, u32[]{:S(2)}, u32[]{:S(2)}) collective-permute-start(bf16[64,208]{1,0:T(8,128)(2,1)} %solve.1.refs_0_), channel_id=1, source_target_pairs={{0,7},{1,6},{2,5},{3,4},{4,3},{5,2},{6,1},{7,0},{8,15},{9,14},{10,... | collective-permute-start | bytes 79880 | tf_op jit(solution)/shard_map/ppermute | solution.py:303
  93.0 16.3 %collective-permute-start.11 = (bf16[64,208]{1,0:T(8,128)(2,1)}, bf16[64,208]{1,0:T(8,128)(2,1)S(1)}, u32[]{:S(2)}, u32[]{:S(2)}) collective-permute-start(bf16[64,208]{1,0:T(8,128)(2,1)} %solve.1.refs_0_), channel_id=1, source_target_pairs={{0,6},{1,7},{2,4},{3,5},{4,2},{5,3},{6,0},{7,1},{8,14},{9,15},{10,... | collective-permute-start | bytes 79880 | tf_op jit(solution)/shard_map/ppermute | solution.py:303
  94.2 17.5 %collective-permute-start.10 = (bf16[64,208]{1,0:T(8,128)(2,1)}, bf16[64,208]{1,0:T(8,128)(2,1)S(1)}, u32[]{:S(2)}, u32[]{:S(2)}) collective-permute-start(bf16[64,208]{1,0:T(8,128)(2,1)} %solve.1.refs_0_), channel_id=1, source_target_pairs={{0,5},{1,4},{2,7},{3,6},{4,1},{5,0},{6,3},{7,2},{8,13},{9,12},{10,... | collective-permute-start | bytes 79880 | tf_op jit(solution)/shard_map/ppermute | solution.py:303
  103.8 9.9 %collective-permute-start.9 = (bf16[64,208]{1,0:T(8,128)(2,1)}, bf16[64,208]{1,0:T(8,128)(2,1)S(1)}, u32[]{:S(2)}, u32[]{:S(2)}) collective-permute-start(bf16[64,208]{1,0:T(8,128)(2,1)} %solve.1.refs_0_), channel_id=1, source_target_pairs={{0,4},{1,5},{2,6},{3,7},{4,0},{5,1},{6,2},{7,3},{8,12},{9,13},{10,... | collective-permute-start | bytes 79880 | tf_op jit(solution)/shard_map/ppermute | solution.py:303
  105.4 12.0 %collective-permute-start.8 = (bf16[64,208]{1,0:T(8,128)(2,1)}, bf16[64,208]{1,0:T(8,128)(2,1)S(1)}, u32[]{:S(2)}, u32[]{:S(2)}) collective-permute-start(bf16[64,208]{1,0:T(8,128)(2,1)} %solve.1.refs_0_), channel_id=1, source_target_pairs={{0,3},{1,2},{2,1},{3,0},{4,7},{5,6},{6,5},{7,4},{8,11},{9,10},{10,... | collective-permute-start | bytes 79880 | tf_op jit(solution)/shard_map/ppermute | solution.py:303
  109.3 8.3 %collective-permute-start.7 = (bf16[64,208]{1,0:T(8,128)(2,1)}, bf16[64,208]{1,0:T(8,128)(2,1)S(1)}, u32[]{:S(2)}, u32[]{:S(2)}) collective-permute-start(bf16[64,208]{1,0:T(8,128)(2,1)} %solve.1.refs_0_), channel_id=1, source_target_pairs={{0,2},{1,3},{2,0},{3,1},{4,6},{5,7},{6,4},{7,5},{8,10},{9,11},{10,... | collective-permute-start | bytes 79880 | tf_op jit(solution)/shard_map/ppermute | solution.py:303
  111.8 5.8 %collective-permute-start.6 = (bf16[64,208]{1,0:T(8,128)(2,1)}, bf16[64,208]{1,0:T(8,128)(2,1)S(1)}, u32[]{:S(2)}, u32[]{:S(2)}) collective-permute-start(bf16[64,208]{1,0:T(8,128)(2,1)} %solve.1.refs_0_), channel_id=1, source_target_pairs={{0,1},{1,0},{2,3},{3,2},{4,5},{5,4},{6,7},{7,6},{8,9},{9,8},{10,11... | collective-permute-start | bytes 79880 | tf_op jit(solution)/shard_map/ppermute | solution.py:303
  113.7 18.9 %collective-permute-start.15 = (bf16[2,64,1536]{2,1,0:T(8,128)(2,1)S(1)}, bf16[2,64,1536]{2,1,0:T(8,128)(2,1)S(1)}, u32[]{:S(2)}, u32[]{:S(2)}) collective-permute-start(bf16[2,64,1536]{2,1,0:T(8,128)(2,1)S(1)} %collective-permute-done.refs_8_), channel_id=1, source_target_pairs={{0,16},{8,24},{16,0},{24,8},{1,17},{9,25},{17,1},{25,9},{2,18},{10... | collective-permute-start | bytes 1179656 | tf_op jit(solution)/shard_map/ppermute | solution.py:303
  117.5 15.2 %collective-permute-start.13 = (bf16[2,64,1536]{2,1,0:T(8,128)(2,1)S(1)}, bf16[2,64,1536]{2,1,0:T(8,128)(2,1)S(1)}, u32[]{:S(2)}, u32[]{:S(2)}) collective-permute-start(bf16[2,64,1536]{2,1,0:T(8,128)(2,1)S(1)} %collective-permute-done.refs_8_), channel_id=1, source_target_pairs={{0,8},{8,0},{16,24},{24,16},{1,9},{9,1},{17,25},{25,17},{2,10},{10... | collective-permute-start | bytes 1179656 | tf_op jit(solution)/shard_map/ppermute | solution.py:303
  117.6 18.2 %collective-permute-start.18 = (bf16[2,64,1536]{2,1,0:T(8,128)(2,1)S(1)}, bf16[2,64,1536]{2,1,0:T(8,128)(2,1)S(1)}, u32[]{:S(2)}, u32[]{:S(2)}) collective-permute-start(bf16[2,64,1536]{2,1,0:T(8,128)(2,1)S(1)} %collective-permute-done.1.refs_9_), channel_id=1, source_target_pairs={{0,24},{8,16},{16,8},{24,0},{1,25},{9,17},{17,9},{25,1},{2,26},{10... | collective-permute-start | bytes 1179656 | tf_op jit(solution)/shard_map/ppermute | solution.py:303
  117.6 23.6 %collective-permute-start.16 = (bf16[2,64,1536]{2,1,0:T(8,128)(2,1)S(1)}, bf16[2,64,1536]{2,1,0:T(8,128)(2,1)S(1)}, u32[]{:S(2)}, u32[]{:S(2)}) collective-permute-start(bf16[2,64,1536]{2,1,0:T(8,128)(2,1)S(1)} %collective-permute-done.1.refs_9_), channel_id=1, source_target_pairs={{0,16},{8,24},{16,0},{24,8},{1,17},{9,25},{17,1},{25,9},{2,18},{10... | collective-permute-start | bytes 1179656 | tf_op jit(solution)/shard_map/ppermute | solution.py:303
  121.0 20.3 %collective-permute-start.14 = (bf16[2,64,1536]{2,1,0:T(8,128)(2,1)S(1)}, bf16[2,64,1536]{2,1,0:T(8,128)(2,1)S(1)}, u32[]{:S(2)}, u32[]{:S(2)}) collective-permute-start(bf16[2,64,1536]{2,1,0:T(8,128)(2,1)S(1)} %collective-permute-done.1.refs_9_), channel_id=1, source_target_pairs={{0,8},{8,0},{16,24},{24,16},{1,9},{9,1},{17,25},{25,17},{2,10},{10... | collective-permute-start | bytes 1179656 | tf_op jit(solution)/shard_map/ppermute | solution.py:303
  (17 other events, 286.6 us)
Sparse Core Ops, SparseCore 0:
  11.2 108.1 all-gather.4
  121.0 38.4 all-gather.2

commit v3 on v2

--- a/solution.py
+++ b/solution.py
@@ -10,7 +10,7 @@
 F32, BF16 = jnp.float32, jnp.bfloat16
 VMEM_LIMIT = 56 * 1024 * 1024
 SUB = 8
-CHUNKS = 2
+CHUNKS = 1
 
 
 def split3(x):
@@ -173,19 +173,10 @@
     return resid.astype(BF16), (2.0 * sdev).astype(BF16)
 
 
-def reversed_bits(value, size):
-    bits = size.bit_length() - 1
-    return sum(((value >> i) & 1) << (bits - 1 - i) for i in range(bits))
-
-
-def line_of(plane, source, size):
-    return source ^ reversed_bits(plane, size)
-
-
 def columns_kernel(rows, ratio, cols, col_comps_ref, *refs):
     coef_refs = refs[:cols]
-    piece_refs = refs[cols : cols + rows * ratio]
-    coef_out, col_r, col_s, coef, raw_cols, sems = refs[cols + rows * ratio :]
+    piece_refs = refs[cols : cols + rows]
+    coef_out, col_r, col_s, coef, raw_cols, sems = refs[cols + rows :]
     here = coef_refs[0].shape[0]
     width = col_r.shape[1]
     r = lax.axis_index("rows")
@@ -196,16 +187,16 @@
         copies.append(
             pltpu.make_async_copy(coef_refs[d], coef.at[pl.ds(place, here), :], sems.at[len(copies)])
         )
+    height = piece_refs[0].shape[1]
     for d in range(rows):
-        for k in range(ratio):
-            source = line_of(q // ratio, r ^ d, rows)
-            owner = source * ratio + lax.rem(lax.rem(q, ratio) + ratio - k, ratio)
-            place = pl.multiple_of(owner * here, here)
+        begin = (r ^ d) * height
+        k, part, inside = begin // (2 * here), lax.rem(begin // here, 2), lax.rem(begin, here)
+        for e in range(rows):
+            owner = ((q // ratio) ^ e) * ratio + lax.rem(q + ratio - k, ratio)
+            place = pl.multiple_of(owner * here + inside, height)
             copies.append(
                 pltpu.make_async_copy(
-                    piece_refs[d * ratio + k],
-                    raw_cols.at[:, pl.ds(place, here), :],
-                    sems.at[len(copies)],
+                    piece_refs[d].at[e], raw_cols.at[part, pl.ds(place, height), :], sems.at[len(copies)]
                 )
             )
     for copy in copies:
@@ -238,7 +229,7 @@
         scratch_shapes=[
             pltpu.VMEM((markers, coef_rows(comps)), BF16),
             pltpu.VMEM((2, markers, width), BF16),
-            pltpu.SemaphoreType.DMA((len(coefs) + len(pieces),)),
+            pltpu.SemaphoreType.DMA((cols + rows * rows,)),
         ],
         compiler_params=pltpu.CompilerParams(vmem_limit_bytes=VMEM_LIMIT),
         name="columns",
@@ -302,28 +293,41 @@
     def across(x, axis, size):
         return [x] + [lax.ppermute(x, axis, [(i, i ^ d) for i in range(size)]) for d in range(1, size)]
 
-    both = ("rows", "cols")
-    pieces = []
-    for k in range(ratio):
-        part = (col % ratio + k) % ratio
-        mine = lax.dynamic_slice_in_dim(raw, part * width, width, 2)
-        moves = [
-            (r * cols + z * ratio + c, line_of(r, z, rows) * cols + r * ratio + (c + k) % ratio)
-            for r in range(rows)
-            for z in range(rows)
-            for c in range(ratio)
-        ]
-        pieces.append(lax.ppermute(mine, both, moves) if len(moves) > 1 else mine)
-        if k == 0:
-            mine = lax.dynamic_slice_in_dim(components, part * width, width, 1)
-            col_comps = lax.ppermute(mine, both, moves) if len(moves) > 1 else mine
-    raw, *pieces = lax.optimization_barrier((raw, *pieces))
     starts = [people * i // CHUNKS for i in range(CHUNKS + 1)]
     raw_rows = [
         lax.all_gather(raw[:, :, a:b], "cols", axis=1, tiled=True) for a, b in zip(starts, starts[1:])
     ]
-    spread = [across(piece, "rows", rows) for piece in pieces]
-    pieces = [spread[k][d] for d in range(rows) for k in range(ratio)]
+
+    row = lax.axis_index("rows")
+    core, plane = col % ratio, col // ratio
+    halves = []
+    for k in range(ratio):
+        part = (core + k) % ratio
+        mine = lax.dynamic_slice_in_dim(raw, part * width, width, 2).reshape(2 * markers, width)
+        swaps = [(z * ratio + c, z * ratio + (c + k) % ratio) for z in range(rows) for c in range(ratio)]
+        halves.append(lax.ppermute(mine, "cols", swaps) if k else mine)
+    held = jnp.concatenate(halves, axis=0)
+    height = held.shape[0] // rows
+    quarters = []
+    for d in range(rows):
+        mine = lax.dynamic_slice_in_dim(held, (row ^ d) * height, height, 0)
+        quarters.append(lax.ppermute(mine, "rows", [(i, i ^ d) for i in range(rows)]) if d else mine)
+    quarters = jnp.stack(quarters)
+    moved = []
+    for e in range(rows):
+        mine = lax.dynamic_index_in_dim(quarters, row ^ plane ^ e, 0, keepdims=False)
+        hops = [(z * ratio + c, (z ^ e) * ratio + c) for z in range(rows) for c in range(ratio)]
+        moved.append(lax.ppermute(mine, "cols", hops) if e else mine)
+    pieces = across(jnp.stack(moved), "rows", rows)
+
+    mine = lax.dynamic_slice_in_dim(components, core * width, width, 1)
+    moves = [
+        (r * cols + z * ratio + c, z * cols + r * ratio + c)
+        for r in range(rows)
+        for z in range(rows)
+        for c in range(ratio)
+    ]
+    col_comps = lax.ppermute(mine, ("rows", "cols"), moves)
 
     gram = gram_call(dosage, present, components)
     coef = solve_call(across(gram, "rows", rows), comps, markers)

time: 180 us -> 179 us (level); the launches traced: 179 us -> 176 us
  starting transfers between devices: 85.9 us -> 30.6 us
  waiting for transfers between devices: 32.4 us -> 87.2 us
  Pallas kernels: 42.6 us -> 38.5 us
  other arithmetic: 1.61 us -> 3.43 us
    ppermute x16 -> x13, starting transfers between devices: 83.8 us -> 20.3 us  [across(): lax.ppermute(x, axis, [(i, i ^ d) for i in range(size)])]
    ppermute x3 -> x8, waiting for transfers between devices: 0.59 us -> 47.3 us  [the longest x3 36.6 us: per_device(): moved.append(lax.ppermute(mine, 'cols', hops) if e else mine)]
    ppermute x16 -> x13, waiting for transfers between devices: 31 us -> 39.8 us  [across(): lax.ppermute(x, axis, [(i, i ^ d) for i in range(size)])]
    ppermute x3 -> x8, starting transfers between devices: 2.03 us -> 10.3 us  [the longest x3 4.47 us: per_device(): lax.ppermute(mine, 'rows', [(i, i ^ d) for i in range(rows)])]
    pallas_call x2 -> x1, Pallas kernels: 22.6 us -> 18.6 us  [kin_call(): pl.pallas_call(kin_kernel, grid=(count // tile,), in_specs=in_specs, out_...]
  transfers between devices with their start and end apart: 21 -> 22, of which waited for: 11 -> 12; matrix products, arithmetic and copies ran while one was open for 0% -> 1% of each run, Pallas kernels for 17% -> 11%
where the time goes in v3:
time: 179 us; the launch traced here: 176 us
  waiting for transfers between devices  87.2 us (49%)
  Pallas kernels  38.5 us (22%)
  starting transfers between devices  30.6 us (17%)
  between operations  13.6 us (8%)
  other arithmetic  3.43 us (2%)
  local copies, waits for them, and re-layouts  2.84 us (2%)
    ppermute x13, waiting for transfers between devices, across(): lax.ppermute(x, axis, [(i, i ^ d) for i in range(size)])  39.8 us
    ppermute x3, waiting for transfers between devices, per_device(): moved.append(lax.ppermute(mine, 'cols', hops) if e else mine)  36.6 us
    ppermute x13, starting transfers between devices, across(): lax.ppermute(x, axis, [(i, i ^ d) for i in range(size)])  20.3 us
    pallas_call x1, Pallas kernels, kin_call(): pl.pallas_call(kin_kernel, grid=(count // tile,), in_specs=in_specs, out_...  18.6 us
    ppermute x3, waiting for transfers between devices, per_device(): lax.ppermute(mine, 'rows', [(i, i ^ d) for i in range(rows)])  9.34 us
    pallas_call x1, Pallas kernels, solve_call(): pl.pallas_call(functools.partial(solve_kernel, comps, markers), out_shape...  7.31 us
    pallas_call x1, Pallas kernels, columns_call(): pl.pallas_call(functools.partial(columns_kernel, rows, ratio, cols), in_s...  7.04 us
    pallas_call x1, Pallas kernels, gram_call(): pl.pallas_call(gram_kernel, out_shape=jax.ShapeDtypeStruct((total // 2 +...  5.63 us
  transfers between devices with their start and end apart: 22, of which 12 were waited for; matrix products, arithmetic and copies ran while one was open for 1% of the time, Pallas kernels for 11%

profile of v3, /device:TPU:0, one launch (start us, length us, event | category | flops | bytes accessed | tf_op | source)
XLA Modules:
  0.0 176.2 jit_solution(18372372414791310465)
XLA Ops:
  6.5 1.5 convert_bitcast_fusion
  11.7 2.9 %collective-permute-start.12 = (bf16[64,1536]{1,0:T(8,128)(2,1)S(1)}, bf16[64,1536]{1,0:T(8,128)(2,1)S(1)}, u32[]{:S(2)}, u32[]{:S(2)}) collective-permute-start(bf16[64,1536]{1,0:T(8,128)(2,1)S(1)} %get-tuple-element.16), channel_id=1, source_target_pairs={{0,8},{8,0},{16,24},{24,16},{1,9},{9,1},{17,25},{25,17},{2,10},{10... | collective-permute-start | bytes 589832 | tf_op jit(solution)/shard_map/ppermute | solution.py:314
  14.7 1.5 collective-permute-start.13
  16.2 4.1 %collective-permute-done.12 = bf16[64,1536]{1,0:T(8,128)(2,1)S(1)} collective-permute-done((bf16[64,1536]{1,0:T(8,128)(2,1)S(1)}, bf16[64,1536]{1,0:T(8,128)(2,1)S(1)}, u32[]{:S(2)}, u32[]{:S(2)}) %collective-permute-start.12) | collective-permute-done | bytes 196640 | tf_op jit(solution)/shard_map/ppermute | solution.py:314
  20.3 5.2 %collective-permute-done.13 = bf16[64,1536]{1,0:T(8,128)(2,1)S(1)} collective-permute-done((bf16[64,1536]{1,0:T(8,128)(2,1)S(1)}, bf16[64,1536]{1,0:T(8,128)(2,1)S(1)}, u32[]{:S(2)}, u32[]{:S(2)}) %collective-permute-start.13) | collective-permute-done | bytes 196640 | tf_op jit(solution)/shard_map/ppermute | solution.py:314
  25.7 3.7 %collective-permute-start.17 = (bf16[64,1536]{1,0:T(8,128)(2,1)S(1)}, bf16[64,1536]{1,0:T(8,128)(2,1)S(1)}, u32[]{:S(2)}, u32[]{:S(2)}) collective-permute-start(bf16[64,1536]{1,0:T(8,128)(2,1)S(1)} %get-tuple-element.12), channel_id=1, source_target_pairs={{0,6},{1,7},{2,4},{3,5},{4,2},{5,3},{6,0},{7,1},{8,14},{9,15},{10,... | collective-permute-start | bytes 589832 | tf_op jit(solution)/shard_map/ppermute | solution.py:320
  30.2 9.4 %collective-permute-done.17 = bf16[64,1536]{1,0:T(8,128)(2,1)S(1)} collective-permute-done((bf16[64,1536]{1,0:T(8,128)(2,1)S(1)}, bf16[64,1536]{1,0:T(8,128)(2,1)S(1)}, u32[]{:S(2)}, u32[]{:S(2)}) %collective-permute-start.17) | collective-permute-done | bytes 196640 | tf_op jit(solution)/shard_map/ppermute | solution.py:320
  39.5 27.3 %collective-permute-done.16 = bf16[64,1536]{1,0:T(8,128)(2,1)S(1)} collective-permute-done((bf16[64,1536]{1,0:T(8,128)(2,1)S(1)}, bf16[64,1536]{1,0:T(8,128)(2,1)S(1)}, u32[]{:S(2)}, u32[]{:S(2)}) %collective-permute-start.16) | collective-permute-done | bytes 196640 | tf_op jit(solution)/shard_map/ppermute | solution.py:320
  66.9 2.0 %collective-permute-start.20 = (bf16[4,64,1536]{2,1,0:T(8,128)(2,1)S(1)}, bf16[4,64,1536]{2,1,0:T(8,128)(2,1)S(1)}, u32[]{:S(2)}, u32[]{:S(2)}) collective-permute-start(bf16[4,64,1536]{2,1,0:T(8,128)(2,1)S(1)} %pad_maximum_fusion.2.refs_8_), channel_id=1, source_target_pairs={{0,24},{8,16},{16,8},{24,0},{1,25},{9,17},{17,9},{25,1},{2,26},{10... | collective-permute-start | bytes 2359304 | tf_op jit(solution)/shard_map/ppermute | solution.py:294
  70.5 5.6 %gram.1.refs_0_ = f32[360,128]{1,0:T(8,128)} custom-call(s32[64,3072]{1,0:T(8,128)} %dosage_ref.1, s32[64,3072]{1,0:T(8,128)} %present_ref.1, f32[32,3072]{1,0:T(8,128)} %comps_ref.3), custom_call_target="tpu_custom_call" | custom-call | tf_op jit(solution)/shard_map/gram/pallas_call | solution.py:63
  76.1 1.9 %collective-permute-start.3 = (f32[360,128]{1,0:T(8,128)}, f32[360,128]{1,0:T(8,128)}, u32[]{:S(2)}, u32[]{:S(2)}) collective-permute-start(f32[360,128]{1,0:T(8,128)} %gram.1.refs_0_), channel_id=1, source_target_pairs={{0,24},{8,16},{16,8},{24,0},{1,25},{9,17},{17,9},{25,1},{2,26},{10... | collective-permute-start | bytes 552968 | tf_op jit(solution)/shard_map/ppermute | solution.py:294
  79.0 29.2 %collective-permute-done.3.refs_3_ = f32[360,128]{1,0:T(8,128)} collective-permute-done((f32[360,128]{1,0:T(8,128)}, f32[360,128]{1,0:T(8,128)}, u32[]{:S(2)}, u32[]{:S(2)}) %collective-permute-start.3) | collective-permute-done | bytes 184352 | tf_op jit(solution)/shard_map/ppermute | solution.py:294
  108.2 1.5 collective-permute-start.1
  109.7 2.3 %collective-permute-done.2.refs_2_ = f32[360,128]{1,0:T(8,128)} collective-permute-done((f32[360,128]{1,0:T(8,128)}, f32[360,128]{1,0:T(8,128)}, u32[]{:S(2)}, u32[]{:S(2)}) %collective-permute-start.2) | collective-permute-done | bytes 184352 | tf_op jit(solution)/shard_map/ppermute | solution.py:294
  114.7 7.3 %solve.1.refs_0_ = bf16[64,208]{1,0:T(8,128)(2,1)} custom-call(f32[360,128]{1,0:T(8,128)} %gram.1.refs_0_, f32[360,128]{1,0:T(8,128)} %copy-done.6, f32[360,128]{1,0:T(8,128)} %collective-permute-done.2.refs_2_, f32[360,128]{1,0:T(8,128)} %collective-permute-done.3.refs_3_), custom_call_target="tpu_custom_call" | custom-call | tf_op jit(solution)/shard_map/solve/pallas_call | solution.py:151
  122.0 3.9 %collective-permute-start.10 = (bf16[64,208]{1,0:T(8,128)(2,1)}, bf16[64,208]{1,0:T(8,128)(2,1)S(1)}, u32[]{:S(2)}, u32[]{:S(2)}) collective-permute-start(bf16[64,208]{1,0:T(8,128)(2,1)} %solve.1.refs_0_), channel_id=1, source_target_pairs={{0,7},{1,6},{2,5},{3,4},{4,3},{5,2},{6,1},{7,0},{8,15},{9,14},{10,... | collective-permute-start | bytes 79880 | tf_op jit(solution)/shard_map/ppermute | solution.py:294
  127.9 2.4 %collective-permute-start.8 = (bf16[64,208]{1,0:T(8,128)(2,1)}, bf16[64,208]{1,0:T(8,128)(2,1)S(1)}, u32[]{:S(2)}, u32[]{:S(2)}) collective-permute-start(bf16[64,208]{1,0:T(8,128)(2,1)} %solve.1.refs_0_), channel_id=1, source_target_pairs={{0,5},{1,4},{2,7},{3,6},{4,1},{5,0},{6,3},{7,2},{8,13},{9,12},{10,... | collective-permute-start | bytes 79880 | tf_op jit(solution)/shard_map/ppermute | solution.py:294
  130.3 1.7 collective-permute-done.9.refs_6_
  132.0 1.9 %collective-permute-start.7 = (bf16[64,208]{1,0:T(8,128)(2,1)}, bf16[64,208]{1,0:T(8,128)(2,1)S(1)}, u32[]{:S(2)}, u32[]{:S(2)}) collective-permute-start(bf16[64,208]{1,0:T(8,128)(2,1)} %solve.1.refs_0_), channel_id=1, source_target_pairs={{0,4},{1,5},{2,6},{3,7},{4,0},{5,1},{6,2},{7,3},{8,12},{9,13},{10,... | collective-permute-start | bytes 79880 | tf_op jit(solution)/shard_map/ppermute | solution.py:294
  134.8 2.1 %collective-permute-done.7.refs_4_ = bf16[64,208]{1,0:T(8,128)(2,1)S(1)} collective-permute-done((bf16[64,208]{1,0:T(8,128)(2,1)}, bf16[64,208]{1,0:T(8,128)(2,1)S(1)}, u32[]{:S(2)}, u32[]{:S(2)}) %collective-permute-start.7) | collective-permute-done | bytes 26656 | tf_op jit(solution)/shard_map/ppermute | solution.py:294
  137.0 2.5 %collective-permute-start.5 = (bf16[64,208]{1,0:T(8,128)(2,1)}, bf16[64,208]{1,0:T(8,128)(2,1)S(1)}, u32[]{:S(2)}, u32[]{:S(2)}) collective-permute-start(bf16[64,208]{1,0:T(8,128)(2,1)} %solve.1.refs_0_), channel_id=1, source_target_pairs={{0,2},{1,3},{2,0},{3,1},{4,6},{5,7},{6,4},{7,5},{8,10},{9,11},{10,... | collective-permute-start | bytes 79880 | tf_op jit(solution)/shard_map/ppermute | solution.py:294
  139.5 2.1 %collective-permute-done.5.refs_2_ = bf16[64,208]{1,0:T(8,128)(2,1)S(1)} collective-permute-done((bf16[64,208]{1,0:T(8,128)(2,1)}, bf16[64,208]{1,0:T(8,128)(2,1)S(1)}, u32[]{:S(2)}, u32[]{:S(2)}) %collective-permute-start.5) | collective-permute-done | bytes 26656 | tf_op jit(solution)/shard_map/ppermute | solution.py:294
  143.7 7.0 %columns.1 = (bf16[512,208]{1,0:T(8,128)(2,1)}, bf16[512,1536]{1,0:T(8,128)(2,1)}, bf16[512,1536]{1,0:T(8,128)(2,1)}) custom-call(f32[32,1536]{1,0:T(8,128)} %copy-done.5, bf16[64,208]{1,0:T(8,128)(2,1)} %solve.1.refs_0_, bf16[64,208]{1,0:T(8,128)(2,1)} %copy-done.13, bf16[64,208]{1,0:T(8,128)(2,1)} %copy-done.12, bf16[64,208]{1,0:T(8,128)(2,1)} %copy-done.11, ...), custom_call_target="tpu_custom_call" | custom-call | tf_op jit(solution)/shard_map/columns/pallas_call | solution.py:221
  150.8 18.6 %kinship.1 = f32[3072,1536]{1,0:T(8,128)} custom-call(bf16[2,512,3072]{2,1,0:T(8,128)(2,1)} %all-gather.2.cloned.1.call-done.raw_ref, f32[32,3072]{1,0:T(8,128)} %comps_ref.3, bf16[512,208]{1,0:T(8,128)(2,1)} %get-tuple-element.8.coef_ref, bf16[512,1536]{1,0:T(8,128)(2,1)} %get-tuple-element.9.col_r, bf16[512,1536]{1,0:T(8,128)(2,1)} %get-tuple-element.10.col_s), custom_call_target="tpu_custom_call" | custom-call | tf_op jit(solution)/shard_map/kinship/pallas_call | solution.py:272
  (61 shorter events, 15.0 us)
Async XLA Ops:
  6.5 144.2 %all-gather.2.cloned.1.call-start = ((), (), s32[]{:S(2)}) async-start(), calls=%async_computation | async-start | bytes 7077888 | tf_op jit(solution)/shard_map/all_gather | solution.py:298
  8.0 101.7 %copy-start.1 = (f32[32,3072]{1,0:T(8,128)S(1)}, f32[32,3072]{1,0:T(8,128)}, u32[]{:S(2)}) copy-start(f32[32,3072]{1,0:T(8,128)} %comps_ref.3) | copy-start | bytes 1179652
  9.1 1.9 %collective-permute-start.11 = (bf16[128,1536]{1,0:T(8,128)(2,1)S(1)}, bf16[128,1536]{1,0:T(8,128)(2,1)S(1)}, u32[]{:S(2)}, u32[]{:S(2)}) collective-permute-start(bf16[128,1536]{1,0:T(8,128)(2,1)S(1)} %bitcast.21), channel_id=1, source_target_pairs={{0,1},{1,0},{2,3},{3,2},{4,5},{5,4},{6,7},{7,6},{8,9},{9,8},{10,11... | collective-permute-start | bytes 1179656 | tf_op jit(solution)/shard_map/ppermute | solution.py:308
  11.7 8.6 %collective-permute-start.12 = (bf16[64,1536]{1,0:T(8,128)(2,1)S(1)}, bf16[64,1536]{1,0:T(8,128)(2,1)S(1)}, u32[]{:S(2)}, u32[]{:S(2)}) collective-permute-start(bf16[64,1536]{1,0:T(8,128)(2,1)S(1)} %get-tuple-element.16), channel_id=1, source_target_pairs={{0,8},{8,0},{16,24},{24,16},{1,9},{9,1},{17,25},{25,17},{2,10},{10... | collective-permute-start | bytes 589832 | tf_op jit(solution)/shard_map/ppermute | solution.py:314
  14.7 10.9 %collective-permute-start.13 = (bf16[64,1536]{1,0:T(8,128)(2,1)S(1)}, bf16[64,1536]{1,0:T(8,128)(2,1)S(1)}, u32[]{:S(2)}, u32[]{:S(2)}) collective-permute-start(bf16[64,1536]{1,0:T(8,128)(2,1)S(1)} %get-tuple-element.17), channel_id=1, source_target_pairs={{0,16},{8,24},{16,0},{24,8},{1,17},{9,25},{17,1},{25,9},{2,18},{10... | collective-permute-start | bytes 589832 | tf_op jit(solution)/shard_map/ppermute | solution.py:314
  16.2 9.4 %collective-permute-start.14 = (bf16[64,1536]{1,0:T(8,128)(2,1)S(1)}, bf16[64,1536]{1,0:T(8,128)(2,1)S(1)}, u32[]{:S(2)}, u32[]{:S(2)}) collective-permute-start(bf16[64,1536]{1,0:T(8,128)(2,1)S(1)} %get-tuple-element.18), channel_id=1, source_target_pairs={{0,24},{8,16},{16,8},{24,0},{1,25},{9,17},{17,9},{25,1},{2,26},{10... | collective-permute-start | bytes 589832 | tf_op jit(solution)/shard_map/ppermute | solution.py:314
  25.7 13.8 %collective-permute-start.17 = (bf16[64,1536]{1,0:T(8,128)(2,1)S(1)}, bf16[64,1536]{1,0:T(8,128)(2,1)S(1)}, u32[]{:S(2)}, u32[]{:S(2)}) collective-permute-start(bf16[64,1536]{1,0:T(8,128)(2,1)S(1)} %get-tuple-element.12), channel_id=1, source_target_pairs={{0,6},{1,7},{2,4},{3,5},{4,2},{5,3},{6,0},{7,1},{8,14},{9,15},{10,... | collective-permute-start | bytes 589832 | tf_op jit(solution)/shard_map/ppermute | solution.py:320
  29.4 37.4 %collective-permute-start.16 = (bf16[64,1536]{1,0:T(8,128)(2,1)S(1)}, bf16[64,1536]{1,0:T(8,128)(2,1)S(1)}, u32[]{:S(2)}, u32[]{:S(2)}) collective-permute-start(bf16[64,1536]{1,0:T(8,128)(2,1)S(1)} %get-tuple-element.13), channel_id=1, source_target_pairs={{0,4},{1,5},{2,6},{3,7},{4,0},{5,1},{6,2},{7,3},{8,12},{9,13},{10,... | collective-permute-start | bytes 589832 | tf_op jit(solution)/shard_map/ppermute | solution.py:320
  29.4 37.4 %collective-permute-start.15 = (bf16[64,1536]{1,0:T(8,128)(2,1)S(1)}, bf16[64,1536]{1,0:T(8,128)(2,1)S(1)}, u32[]{:S(2)}, u32[]{:S(2)}) collective-permute-start(bf16[64,1536]{1,0:T(8,128)(2,1)S(1)} %get-tuple-element.14), channel_id=1, source_target_pairs={{0,2},{1,3},{2,0},{3,1},{4,6},{5,7},{6,4},{7,5},{8,10},{9,11},{10,... | collective-permute-start | bytes 589832 | tf_op jit(solution)/shard_map/ppermute | solution.py:320
  66.9 74.7 %copy-start = (bf16[4,64,1536]{2,1,0:T(8,128)(2,1)}, bf16[4,64,1536]{2,1,0:T(8,128)(2,1)S(1)}, u32[]{:S(2)}) copy-start(bf16[4,64,1536]{2,1,0:T(8,128)(2,1)S(1)} %pad_maximum_fusion.2.refs_8_) | copy-start | bytes 2359300
  66.9 74.6 %collective-permute-start.20 = (bf16[4,64,1536]{2,1,0:T(8,128)(2,1)S(1)}, bf16[4,64,1536]{2,1,0:T(8,128)(2,1)S(1)}, u32[]{:S(2)}, u32[]{:S(2)}) collective-permute-start(bf16[4,64,1536]{2,1,0:T(8,128)(2,1)S(1)} %pad_maximum_fusion.2.refs_8_), channel_id=1, source_target_pairs={{0,24},{8,16},{16,8},{24,0},{1,25},{9,17},{17,9},{25,1},{2,26},{10... | collective-permute-start | bytes 2359304 | tf_op jit(solution)/shard_map/ppermute | solution.py:294
  68.9 72.7 %collective-permute-start.19 = (bf16[4,64,1536]{2,1,0:T(8,128)(2,1)S(1)}, bf16[4,64,1536]{2,1,0:T(8,128)(2,1)S(1)}, u32[]{:S(2)}, u32[]{:S(2)}) collective-permute-start(bf16[4,64,1536]{2,1,0:T(8,128)(2,1)S(1)} %pad_maximum_fusion.2.refs_8_), channel_id=1, source_target_pairs={{0,16},{8,24},{16,0},{24,8},{1,17},{9,25},{17,1},{25,9},{2,18},{10... | collective-permute-start | bytes 2359304 | tf_op jit(solution)/shard_map/ppermute | solution.py:294
  69.9 71.7 %collective-permute-start.18 = (bf16[4,64,1536]{2,1,0:T(8,128)(2,1)S(1)}, bf16[4,64,1536]{2,1,0:T(8,128)(2,1)S(1)}, u32[]{:S(2)}, u32[]{:S(2)}) collective-permute-start(bf16[4,64,1536]{2,1,0:T(8,128)(2,1)S(1)} %pad_maximum_fusion.2.refs_8_), channel_id=1, source_target_pairs={{0,8},{8,0},{16,24},{24,16},{1,9},{9,1},{17,25},{25,17},{2,10},{10... | collective-permute-start | bytes 2359304 | tf_op jit(solution)/shard_map/ppermute | solution.py:294
  76.1 32.1 %collective-permute-start.3 = (f32[360,128]{1,0:T(8,128)}, f32[360,128]{1,0:T(8,128)}, u32[]{:S(2)}, u32[]{:S(2)}) collective-permute-start(f32[360,128]{1,0:T(8,128)} %gram.1.refs_0_), channel_id=1, source_target_pairs={{0,24},{8,16},{16,8},{24,0},{1,25},{9,17},{17,9},{25,1},{2,26},{10... | collective-permute-start | bytes 552968 | tf_op jit(solution)/shard_map/ppermute | solution.py:294
  78.0 34.0 %collective-permute-start.2 = (f32[360,128]{1,0:T(8,128)}, f32[360,128]{1,0:T(8,128)}, u32[]{:S(2)}, u32[]{:S(2)}) collective-permute-start(f32[360,128]{1,0:T(8,128)} %gram.1.refs_0_), channel_id=1, source_target_pairs={{0,16},{8,24},{16,0},{24,8},{1,17},{9,25},{17,1},{25,9},{2,18},{10... | collective-permute-start | bytes 552968 | tf_op jit(solution)/shard_map/ppermute | solution.py:294
  108.2 5.7 %collective-permute-start.1 = (f32[360,128]{1,0:T(8,128)}, f32[360,128]{1,0:T(8,128)S(1)}, u32[]{:S(2)}, u32[]{:S(2)}) collective-permute-start(f32[360,128]{1,0:T(8,128)} %gram.1.refs_0_), channel_id=1, source_target_pairs={{0,8},{8,0},{16,24},{24,16},{1,9},{9,1},{17,25},{25,17},{2,10},{10... | collective-permute-start | bytes 552968 | tf_op jit(solution)/shard_map/ppermute | solution.py:294
  112.0 13.8 %collective-permute-start = (f32[32,1536]{1,0:T(8,128)S(1)}, f32[32,1536]{1,0:T(8,128)S(1)}, u32[]{:S(2)}, u32[]{:S(2)}) collective-permute-start(f32[32,1536]{1,0:T(8,128)S(1)} %constant_dynamic-slice_fusion.1), channel_id=1, source_target_pairs={{0,0},{1,1},{2,8},{3,9},{4,16},{5,17},{6,24},{7,25},{8,2},{9,3},{1... | collective-permute-start | bytes 589832 | tf_op jit(solution)/shard_map/ppermute | solution.py:330
  122.0 5.9 %collective-permute-start.10 = (bf16[64,208]{1,0:T(8,128)(2,1)}, bf16[64,208]{1,0:T(8,128)(2,1)S(1)}, u32[]{:S(2)}, u32[]{:S(2)}) collective-permute-start(bf16[64,208]{1,0:T(8,128)(2,1)} %solve.1.refs_0_), channel_id=1, source_target_pairs={{0,7},{1,6},{2,5},{3,4},{4,3},{5,2},{6,1},{7,0},{8,15},{9,14},{10,... | collective-permute-start | bytes 79880 | tf_op jit(solution)/shard_map/ppermute | solution.py:294
  125.9 6.1 %collective-permute-start.9 = (bf16[64,208]{1,0:T(8,128)(2,1)}, bf16[64,208]{1,0:T(8,128)(2,1)S(1)}, u32[]{:S(2)}, u32[]{:S(2)}) collective-permute-start(bf16[64,208]{1,0:T(8,128)(2,1)} %solve.1.refs_0_), channel_id=1, source_target_pairs={{0,6},{1,7},{2,4},{3,5},{4,2},{5,3},{6,0},{7,1},{8,14},{9,15},{10,... | collective-permute-start | bytes 79880 | tf_op jit(solution)/shard_map/ppermute | solution.py:294
  127.9 6.0 %collective-permute-start.8 = (bf16[64,208]{1,0:T(8,128)(2,1)}, bf16[64,208]{1,0:T(8,128)(2,1)S(1)}, u32[]{:S(2)}, u32[]{:S(2)}) collective-permute-start(bf16[64,208]{1,0:T(8,128)(2,1)} %solve.1.refs_0_), channel_id=1, source_target_pairs={{0,5},{1,4},{2,7},{3,6},{4,1},{5,0},{6,3},{7,2},{8,13},{9,12},{10,... | collective-permute-start | bytes 79880 | tf_op jit(solution)/shard_map/ppermute | solution.py:294
  132.0 5.0 %collective-permute-start.7 = (bf16[64,208]{1,0:T(8,128)(2,1)}, bf16[64,208]{1,0:T(8,128)(2,1)S(1)}, u32[]{:S(2)}, u32[]{:S(2)}) collective-permute-start(bf16[64,208]{1,0:T(8,128)(2,1)} %solve.1.refs_0_), channel_id=1, source_target_pairs={{0,4},{1,5},{2,6},{3,7},{4,0},{5,1},{6,2},{7,3},{8,12},{9,13},{10,... | collective-permute-start | bytes 79880 | tf_op jit(solution)/shard_map/ppermute | solution.py:294
  133.9 5.6 %collective-permute-start.6 = (bf16[64,208]{1,0:T(8,128)(2,1)}, bf16[64,208]{1,0:T(8,128)(2,1)S(1)}, u32[]{:S(2)}, u32[]{:S(2)}) collective-permute-start(bf16[64,208]{1,0:T(8,128)(2,1)} %solve.1.refs_0_), channel_id=1, source_target_pairs={{0,3},{1,2},{2,1},{3,0},{4,7},{5,6},{6,5},{7,4},{8,11},{9,10},{10,... | collective-permute-start | bytes 79880 | tf_op jit(solution)/shard_map/ppermute | solution.py:294
  137.0 4.6 %collective-permute-start.5 = (bf16[64,208]{1,0:T(8,128)(2,1)}, bf16[64,208]{1,0:T(8,128)(2,1)S(1)}, u32[]{:S(2)}, u32[]{:S(2)}) collective-permute-start(bf16[64,208]{1,0:T(8,128)(2,1)} %solve.1.refs_0_), channel_id=1, source_target_pairs={{0,2},{1,3},{2,0},{3,1},{4,6},{5,7},{6,4},{7,5},{8,10},{9,11},{10,... | collective-permute-start | bytes 79880 | tf_op jit(solution)/shard_map/ppermute | solution.py:294
  139.5 2.1 %collective-permute-start.4 = (bf16[64,208]{1,0:T(8,128)(2,1)}, bf16[64,208]{1,0:T(8,128)(2,1)S(1)}, u32[]{:S(2)}, u32[]{:S(2)}) collective-permute-start(bf16[64,208]{1,0:T(8,128)(2,1)} %solve.1.refs_0_), channel_id=1, source_target_pairs={{0,1},{1,0},{2,3},{3,2},{4,5},{5,4},{6,7},{7,6},{8,9},{9,8},{10,11... | collective-permute-start | bytes 79880 | tf_op jit(solution)/shard_map/ppermute | solution.py:294
  (12 other events, 58.9 us)
Sparse Core Ops, SparseCore 0:
  9.1 83.9 all-gather.1

commit v4 on v3

--- a/solution.py
+++ b/solution.py
@@ -174,10 +174,9 @@
 
 
 def columns_kernel(rows, ratio, cols, col_comps_ref, *refs):
-    coef_refs = refs[:cols]
-    piece_refs = refs[cols : cols + rows]
-    coef_out, col_r, col_s, coef, raw_cols, sems = refs[cols + rows :]
-    here = coef_refs[0].shape[0]
+    coef_ref, piece_refs = refs[0], refs[1 : 1 + rows]
+    coef_out, col_r, col_s, coef, raw_cols, sems = refs[1 + rows :]
+    here = coef_ref.shape[1]
     width = col_r.shape[1]
     r = lax.axis_index("rows")
     q = lax.axis_index("cols")
@@ -185,7 +184,7 @@
     for d in range(cols):
         place = pl.multiple_of((q ^ d) * here, here)
         copies.append(
-            pltpu.make_async_copy(coef_refs[d], coef.at[pl.ds(place, here), :], sems.at[len(copies)])
+            pltpu.make_async_copy(coef_ref.at[d], coef.at[pl.ds(place, here), :], sems.at[len(copies)])
         )
     height = piece_refs[0].shape[1]
     for d in range(rows):
@@ -216,11 +215,11 @@
 
 def columns_call(rows, ratio, cols, col_comps, coefs, pieces):
     comps, width = col_comps.shape
-    markers = coefs[0].shape[0] * cols
+    markers = coefs.shape[1] * cols
     anywhere = pl.BlockSpec(memory_space=pl.ANY)
     return pl.pallas_call(
         functools.partial(columns_kernel, rows, ratio, cols),
-        in_specs=[pl.BlockSpec(memory_space=pltpu.VMEM)] + [anywhere] * (len(coefs) + len(pieces)),
+        in_specs=[pl.BlockSpec(memory_space=pltpu.VMEM)] + [anywhere] * (1 + len(pieces)),
         out_shape=(
             jax.ShapeDtypeStruct((markers, coef_rows(comps)), BF16),
             jax.ShapeDtypeStruct((markers, width), BF16),
@@ -233,32 +232,35 @@
         ],
         compiler_params=pltpu.CompilerParams(vmem_limit_bytes=VMEM_LIMIT),
         name="columns",
-    )(col_comps, *coefs, *pieces)
+    )(col_comps, coefs, *pieces)
 
 
 def kin_kernel(raw_ref, comps_ref, coef_ref, col_r, col_s, *refs):
-    out_ref = refs[-1]
+    out_ref, row_r, row_s = refs[-3:]
     width = out_ref.shape[1]
     resid, sdev = panel(coef_ref[...], comps_ref[...], raw_ref[0], raw_ref[1])
-    contract = (((0,), (0,)), ((), ()))
+    resid, sdev = resid.T, sdev.T
     step = 512 if width % 512 == 0 else width
     for at in range(0, width, step):
         span = slice(at, at + step)
-        numer = lax.dot_general(resid, col_r[:, span], contract, preferred_element_type=F32)
-        denom = lax.dot_general(sdev, col_s[:, span], contract, preferred_element_type=F32)
+        numer = jnp.dot(row_r[...], col_r[:, span], preferred_element_type=F32)
+        denom = jnp.dot(row_s[...], col_s[:, span], preferred_element_type=F32)
         out_ref[:, span] = numer / denom
+    row_r[...] = resid
+    row_s[...] = sdev
 
 
 def kin_call(start, raw, components, coef, col_r, col_s, before):
     _, markers, count = raw.shape
     comps, people = components.shape
     width = col_r.shape[1]
-    tile = 512 if count % 512 == 0 else count
+    tile = 256 if count % 256 == 0 else count
     first = start // tile
+    last = count // tile - 1
     whole = lambda i: (0, 0)
     in_specs = [
-        pl.BlockSpec((2, markers, tile), lambda i: (0, 0, i)),
-        pl.BlockSpec((comps, tile), lambda i: (0, i + first)),
+        pl.BlockSpec((2, markers, tile), lambda i: (0, 0, jnp.minimum(i, last))),
+        pl.BlockSpec((comps, tile), lambda i: (0, jnp.minimum(i, last) + first)),
         pl.BlockSpec(coef.shape, whole),
         pl.BlockSpec((markers, width), whole),
         pl.BlockSpec((markers, width), whole),
@@ -271,10 +273,11 @@
         operands.append(before)
     return pl.pallas_call(
         kin_kernel,
-        grid=(count // tile,),
+        grid=(count // tile + 1,),
         in_specs=in_specs,
-        out_specs=pl.BlockSpec((tile, width), lambda i: (i + first, 0)),
+        out_specs=pl.BlockSpec((tile, width), lambda i: (jnp.maximum(i - 1, 0) + first, 0)),
         out_shape=jax.ShapeDtypeStruct((people, width), F32),
+        scratch_shapes=[pltpu.VMEM((tile, markers), BF16), pltpu.VMEM((tile, markers), BF16)],
         input_output_aliases=aliases,
         compiler_params=pltpu.CompilerParams(vmem_limit_bytes=VMEM_LIMIT),
         name="kinship",
@@ -306,19 +309,29 @@
         mine = lax.dynamic_slice_in_dim(raw, part * width, width, 2).reshape(2 * markers, width)
         swaps = [(z * ratio + c, z * ratio + (c + k) % ratio) for z in range(rows) for c in range(ratio)]
         halves.append(lax.ppermute(mine, "cols", swaps) if k else mine)
-    held = jnp.concatenate(halves, axis=0)
+    gram = gram_call(dosage, present, components)
+    held, gram = lax.optimization_barrier((jnp.concatenate(halves, axis=0), gram))
+    grams = across(gram, "rows", rows)
     height = held.shape[0] // rows
     quarters = []
     for d in range(rows):
         mine = lax.dynamic_slice_in_dim(held, (row ^ d) * height, height, 0)
         quarters.append(lax.ppermute(mine, "rows", [(i, i ^ d) for i in range(rows)]) if d else mine)
-    quarters = jnp.stack(quarters)
+    quarters, *grams = lax.optimization_barrier((jnp.stack(quarters), *grams))
+    coef = solve_call(grams, comps, markers)
     moved = []
     for e in range(rows):
         mine = lax.dynamic_index_in_dim(quarters, row ^ plane ^ e, 0, keepdims=False)
         hops = [(z * ratio + c, (z ^ e) * ratio + c) for z in range(rows) for c in range(ratio)]
         moved.append(lax.ppermute(mine, "cols", hops) if e else mine)
-    pieces = across(jnp.stack(moved), "rows", rows)
+    moved, coef = lax.optimization_barrier((jnp.stack(moved), coef))
+    pieces = across(moved, "rows", rows)
+    coefs = coef[None]
+    hop = 1
+    while hop < cols:
+        other = lax.ppermute(coefs, "cols", [(i, i ^ hop) for i in range(cols)])
+        coefs = jnp.concatenate([coefs, other], axis=0)
+        hop *= 2
 
     mine = lax.dynamic_slice_in_dim(components, core * width, width, 1)
     moves = [
@@ -329,9 +342,6 @@
     ]
     col_comps = lax.ppermute(mine, ("rows", "cols"), moves)
 
-    gram = gram_call(dosage, present, components)
-    coef = solve_call(across(gram, "rows", rows), comps, markers)
-    coefs = across(coef, "cols", cols)
     coef, col_r, col_s = columns_call(rows, ratio, cols, col_comps, coefs, pieces)
     out = None
     for start, part in zip(starts, raw_rows):

time: 179 us -> 158 us (0.88)
  starting transfers between devices: 30.6 us -> 18.7 us
  waiting for transfers between devices: 87.2 us -> 76.9 us
  other arithmetic: 3.43 us -> 5.9 us
  Pallas kernels: 38.5 us -> 40.7 us
    ppermute x0 -> x3, waiting for transfers between devices: none -> 21.4 us  [per_device(): other = lax.ppermute(coefs, 'cols', [(i, i ^ hop) for i in range(cols)])]
    ppermute x13 -> x6, waiting for transfers between devices: 39.8 us -> 20.6 us  [across(): lax.ppermute(x, axis, [(i, i ^ d) for i in range(size)])]
    ppermute x13 -> x6, starting transfers between devices: 20.3 us -> 8.81 us  [across(): lax.ppermute(x, axis, [(i, i ^ d) for i in range(size)])]
    ppermute x3, waiting for transfers between devices: 36.6 us -> 30.4 us  [per_device(): moved.append(lax.ppermute(mine, 'cols', hops) if e else mine)]
    ppermute x3, waiting for transfers between devices: 9.34 us -> 4.57 us  [per_device(): lax.ppermute(mine, 'rows', [(i, i ^ d) for i in range(rows)])]
    concatenate x0 -> x4, other arithmetic: none -> 3.22 us  [the longest x3 3.17 us: per_device(): coefs = jnp.concatenate([coefs, other], axis=0)]
    pallas_call x1, Pallas kernels: 18.6 us -> 20.6 us  [kin_call(): pl.pallas_call(kin_kernel, grid=(count // tile + 1,), in_specs=in_specs,...]
    unnamed x28 -> x24, local copies, waits for them, and re-layouts: 2.76 us -> 0.92 us
  transfers between devices with their start and end apart: 22 -> 18, of which waited for: 12 -> 13; matrix products, arithmetic and copies ran while one was open for 1% -> 2% of each run, Pallas kernels for 11% -> 13%
where the time goes in v4:
time: 158 us; the launch traced here: 157 us
  waiting for transfers between devices  76.9 us (49%)
  Pallas kernels  40.7 us (26%)
  starting transfers between devices  18.7 us (12%)
  between operations  13.6 us (9%)
  other arithmetic  5.9 us (4%)
    ppermute x3, waiting for transfers between devices, per_device(): moved.append(lax.ppermute(mine, 'cols', hops) if e else mine)  30.4 us
    ppermute x3, waiting for transfers between devices, per_device(): other = lax.ppermute(coefs, 'cols', [(i, i ^ hop) for i in range(cols)])  21.4 us
    pallas_call x1, Pallas kernels, kin_call(): pl.pallas_call(kin_kernel, grid=(count // tile + 1,), in_specs=in_specs,...  20.6 us
    ppermute x6, waiting for transfers between devices, across(): lax.ppermute(x, axis, [(i, i ^ d) for i in range(size)])  20.6 us
    ppermute x6, starting transfers between devices, across(): lax.ppermute(x, axis, [(i, i ^ d) for i in range(size)])  8.81 us
    pallas_call x1, Pallas kernels, solve_call(): pl.pallas_call(functools.partial(solve_kernel, comps, markers), out_shape...  7.32 us
    pallas_call x1, Pallas kernels, columns_call(): pl.pallas_call(functools.partial(columns_kernel, rows, ratio, cols), in_s...  7.07 us
    pallas_call x1, Pallas kernels, gram_call(): pl.pallas_call(gram_kernel, out_shape=jax.ShapeDtypeStruct((total // 2 +...  5.65 us
  transfers between devices with their start and end apart: 18, of which 13 were waited for; matrix products, arithmetic and copies ran while one was open for 2% of the time, Pallas kernels for 13%

profile of v4, /device:TPU:0, one launch (start us, length us, event | category | flops | bytes accessed | tf_op | source)
XLA Modules:
  0.0 156.9 jit_solution(11702216604548504199)
XLA Ops:
  6.5 1.5 convert_bitcast_fusion
  8.0 0.9 pad_maximum_fusion
  9.6 5.7 %gram.1.refs_0_ = f32[360,128]{1,0:T(8,128)} custom-call(s32[64,3072]{1,0:T(8,128)} %dosage_ref.1, s32[64,3072]{1,0:T(8,128)} %present_ref.1, f32[32,3072]{1,0:T(8,128)} %comps_ref.3), custom_call_target="tpu_custom_call" | custom-call | tf_op jit(solution)/shard_map/gram/pallas_call | solution.py:63
  15.4 3.5 %collective-permute-start.4 = (bf16[64,1536]{1,0:T(8,128)(2,1)S(1)}, bf16[64,1536]{1,0:T(8,128)(2,1)S(1)}, u32[]{:S(2)}, u32[]{:S(2)}) collective-permute-start(bf16[64,1536]{1,0:T(8,128)(2,1)S(1)} %get-tuple-element.34), channel_id=1, source_target_pairs={{0,24},{8,16},{16,8},{24,0},{1,25},{9,17},{17,9},{25,1},{2,26},{10... | collective-permute-start | bytes 589832 | tf_op jit(solution)/shard_map/ppermute | solution.py:319
  19.6 2.8 %collective-permute-start.7 = (f32[360,128]{1,0:T(8,128)S(1)}, f32[360,128]{1,0:T(8,128)S(1)}, u32[]{:S(2)}, u32[]{:S(2)}) collective-permute-start(f32[360,128]{1,0:T(8,128)S(1)} %copy-done.5), channel_id=1, source_target_pairs={{0,24},{8,16},{16,8},{24,0},{1,25},{9,17},{17,9},{25,1},{2,26},{10... | collective-permute-start | bytes 552968 | tf_op jit(solution)/shard_map/ppermute | solution.py:297
  23.0 1.8 %collective-permute-done.4 = bf16[64,1536]{1,0:T(8,128)(2,1)S(1)} collective-permute-done((bf16[64,1536]{1,0:T(8,128)(2,1)S(1)}, bf16[64,1536]{1,0:T(8,128)(2,1)S(1)}, u32[]{:S(2)}, u32[]{:S(2)}) %collective-permute-start.4) | collective-permute-done | bytes 196640 | tf_op jit(solution)/shard_map/ppermute | solution.py:319
  24.8 1.9 %collective-permute-start.5 = (f32[360,128]{1,0:T(8,128)S(1)}, f32[360,128]{1,0:T(8,128)S(1)}, u32[]{:S(2)}, u32[]{:S(2)}) collective-permute-start(f32[360,128]{1,0:T(8,128)S(1)} %copy-done.5), channel_id=1, source_target_pairs={{0,8},{8,0},{16,24},{24,16},{1,9},{9,1},{17,25},{25,17},{2,10},{10... | collective-permute-start | bytes 552968 | tf_op jit(solution)/shard_map/ppermute | solution.py:297
  26.6 2.4 %collective-permute-done.3 = bf16[64,1536]{1,0:T(8,128)(2,1)S(1)} collective-permute-done((bf16[64,1536]{1,0:T(8,128)(2,1)S(1)}, bf16[64,1536]{1,0:T(8,128)(2,1)S(1)}, u32[]{:S(2)}, u32[]{:S(2)}) %collective-permute-start.3) | collective-permute-done | bytes 196640 | tf_op jit(solution)/shard_map/ppermute | solution.py:319
  29.5 3.4 %collective-permute-done.7.refs_3_ = f32[360,128]{1,0:T(8,128)S(1)} collective-permute-done((f32[360,128]{1,0:T(8,128)S(1)}, f32[360,128]{1,0:T(8,128)S(1)}, u32[]{:S(2)}, u32[]{:S(2)}) %collective-permute-start.7) | collective-permute-done | bytes 184352 | tf_op jit(solution)/shard_map/ppermute | solution.py:297
  33.0 3.7 %collective-permute-done.6.refs_2_ = f32[360,128]{1,0:T(8,128)S(1)} collective-permute-done((f32[360,128]{1,0:T(8,128)S(1)}, f32[360,128]{1,0:T(8,128)S(1)}, u32[]{:S(2)}, u32[]{:S(2)}) %collective-permute-start.6) | collective-permute-done | bytes 184352 | tf_op jit(solution)/shard_map/ppermute | solution.py:297
  37.0 3.7 %collective-permute-start.10 = (bf16[64,1536]{1,0:T(8,128)(2,1)S(1)}, bf16[64,1536]{1,0:T(8,128)(2,1)S(1)}, u32[]{:S(2)}, u32[]{:S(2)}) collective-permute-start(bf16[64,1536]{1,0:T(8,128)(2,1)S(1)} %get-tuple-element.30), channel_id=1, source_target_pairs={{0,6},{1,7},{2,4},{3,5},{4,2},{5,3},{6,0},{7,1},{8,14},{9,15},{10,... | collective-permute-start | bytes 589832 | tf_op jit(solution)/shard_map/ppermute | solution.py:326
  41.5 7.3 %solve.1 = bf16[64,208]{1,0:T(8,128)(2,1)} custom-call(f32[360,128]{1,0:T(8,128)} %gram.1.refs_0_, f32[360,128]{1,0:T(8,128)} %copy-done.11, f32[360,128]{1,0:T(8,128)} %copy-done.10, f32[360,128]{1,0:T(8,128)} %copy-done.9), custom_call_target="tpu_custom_call" | custom-call | tf_op jit(solution)/shard_map/solve/pallas_call | solution.py:151
  48.8 2.0 %collective-permute-done.10 = bf16[64,1536]{1,0:T(8,128)(2,1)S(1)} collective-permute-done((bf16[64,1536]{1,0:T(8,128)(2,1)S(1)}, bf16[64,1536]{1,0:T(8,128)(2,1)S(1)}, u32[]{:S(2)}, u32[]{:S(2)}) %collective-permute-start.10) | collective-permute-done | bytes 196640 | tf_op jit(solution)/shard_map/ppermute | solution.py:326
  50.9 28.3 %collective-permute-done.9 = bf16[64,1536]{1,0:T(8,128)(2,1)S(1)} collective-permute-done((bf16[64,1536]{1,0:T(8,128)(2,1)S(1)}, bf16[64,1536]{1,0:T(8,128)(2,1)S(1)}, u32[]{:S(2)}, u32[]{:S(2)}) %collective-permute-start.9) | collective-permute-done | bytes 196640 | tf_op jit(solution)/shard_map/ppermute | solution.py:326
  79.3 1.5 collective-permute-start.16
  80.8 1.5 collective-permute-start.15
  82.9 1.2 collective-permute-done.11
  84.7 8.4 %collective-permute-done.12 = bf16[2,64,208]{2,1,0:T(8,128)(2,1)} collective-permute-done((bf16[2,64,208]{2,1,0:T(8,128)(2,1)}, bf16[2,64,208]{2,1,0:T(8,128)(2,1)}, u32[]{:S(2)}, u32[]{:S(2)}) %collective-permute-start.12) | collective-permute-done | bytes 53280 | tf_op jit(solution)/shard_map/ppermute | solution.py:332
  94.8 11.8 %collective-permute-done.13 = bf16[4,64,208]{2,1,0:T(8,128)(2,1)S(1)} collective-permute-done((bf16[4,64,208]{2,1,0:T(8,128)(2,1)S(1)}, bf16[4,64,208]{2,1,0:T(8,128)(2,1)S(1)}, u32[]{:S(2)}, u32[]{:S(2)}) %collective-permute-start.13) | collective-permute-done | bytes 106528 | tf_op jit(solution)/shard_map/ppermute | solution.py:332
  106.6 1.6 %pad_maximum_fusion.4.refs_0_ = bf16[8,64,208]{2,1,0:T(8,128)(2,1)} fusion(bf16[4,64,208]{2,1,0:T(8,128)(2,1)S(1)} %collective-permute-done.13, bf16[2,64,208]{2,1,0:T(8,128)(2,1)} %collective-permute-done.12, bf16[1,64,208]{2,1,0:T(8,128)(2,1)} %copy-done.7, bf16[1,64,208]{2,1,0:T(8,128)(2,1)} %bitcast.23), kind=kLoop, calls=%fused_computation.12 | loop fusion | flops 319488 | bytes 425984 | tf_op jit(solution)/shard_map/concatenate | solution.py:333
  108.3 11.1 %collective-permute-done.15.refs_3_ = bf16[4,64,1536]{2,1,0:T(8,128)(2,1)S(1)} collective-permute-done((bf16[4,64,1536]{2,1,0:T(8,128)(2,1)S(1)}, bf16[4,64,1536]{2,1,0:T(8,128)(2,1)S(1)}, u32[]{:S(2)}, u32[]{:S(2)}) %collective-permute-start.15) | collective-permute-done | bytes 786464 | tf_op jit(solution)/shard_map/ppermute | solution.py:297
  119.3 2.1 %collective-permute-done.14.refs_2_ = bf16[4,64,1536]{2,1,0:T(8,128)(2,1)S(1)} collective-permute-done((bf16[4,64,1536]{2,1,0:T(8,128)(2,1)S(1)}, bf16[4,64,1536]{2,1,0:T(8,128)(2,1)S(1)}, u32[]{:S(2)}, u32[]{:S(2)}) %collective-permute-start.14) | collective-permute-done | bytes 786464 | tf_op jit(solution)/shard_map/ppermute | solution.py:297
  122.3 7.1 %columns.1 = (bf16[512,208]{1,0:T(8,128)(2,1)}, bf16[512,1536]{1,0:T(8,128)(2,1)}, bf16[512,1536]{1,0:T(8,128)(2,1)}) custom-call(f32[32,1536]{1,0:T(8,128)} %copy-done.8, bf16[8,64,208]{2,1,0:T(8,128)(2,1)} %pad_maximum_fusion.4.refs_0_, bf16[4,64,1536]{2,1,0:T(8,128)(2,1)} %copy-done, bf16[4,64,1536]{2,1,0:T(8,128)(2,1)} %copy-done.4, ...), custom_call_target="tpu_custom_call" | custom-call | tf_op jit(solution)/shard_map/columns/pallas_call | solution.py:220
  129.4 20.6 %kinship.1 = f32[3072,1536]{1,0:T(8,128)} custom-call(bf16[2,512,3072]{2,1,0:T(8,128)(2,1)} %all-gather.2.cloned.1.call-done.raw_ref, f32[32,3072]{1,0:T(8,128)} %comps_ref.3, bf16[512,208]{1,0:T(8,128)(2,1)} %get-tuple-element.26.coef_ref, bf16[512,1536]{1,0:T(8,128)(2,1)} %get-tuple-element.27.col_r, bf16[512,1536]{1,0:T(8,128)(2,1)} %get-tuple-element.28.col_s), custom_call_target="tpu_custom_call" | custom-call | tf_op jit(solution)/shard_map/kinship/pallas_call | solution.py:274
  (53 shorter events, 7.5 us)
Async XLA Ops:
  6.5 122.9 %all-gather.2.cloned.1.call-start = ((), (), s32[]{:S(2)}) async-start(), calls=%async_computation | async-start | bytes 7077888 | tf_op jit(solution)/shard_map/all_gather | solution.py:301
  9.1 6.2 %collective-permute-start.1 = (bf16[128,1536]{1,0:T(8,128)(2,1)S(1)}, bf16[128,1536]{1,0:T(8,128)(2,1)S(1)}, u32[]{:S(2)}, u32[]{:S(2)}) collective-permute-start(bf16[128,1536]{1,0:T(8,128)(2,1)S(1)} %bitcast.26), channel_id=1, source_target_pairs={{0,1},{1,0},{2,3},{3,2},{4,5},{5,4},{6,7},{7,6},{8,9},{9,8},{10,11... | collective-permute-start | bytes 1179656 | tf_op jit(solution)/shard_map/ppermute | solution.py:311
  15.4 9.3 %collective-permute-start.4 = (bf16[64,1536]{1,0:T(8,128)(2,1)S(1)}, bf16[64,1536]{1,0:T(8,128)(2,1)S(1)}, u32[]{:S(2)}, u32[]{:S(2)}) collective-permute-start(bf16[64,1536]{1,0:T(8,128)(2,1)S(1)} %get-tuple-element.34), channel_id=1, source_target_pairs={{0,24},{8,16},{16,8},{24,0},{1,25},{9,17},{17,9},{25,1},{2,26},{10... | collective-permute-start | bytes 589832 | tf_op jit(solution)/shard_map/ppermute | solution.py:319
  19.0 10.0 %collective-permute-start.3 = (bf16[64,1536]{1,0:T(8,128)(2,1)S(1)}, bf16[64,1536]{1,0:T(8,128)(2,1)S(1)}, u32[]{:S(2)}, u32[]{:S(2)}) collective-permute-start(bf16[64,1536]{1,0:T(8,128)(2,1)S(1)} %get-tuple-element.35), channel_id=1, source_target_pairs={{0,16},{8,24},{16,0},{24,8},{1,17},{9,25},{17,1},{25,9},{2,18},{10... | collective-permute-start | bytes 589832 | tf_op jit(solution)/shard_map/ppermute | solution.py:319
  19.5 10.0 %collective-permute-start.2 = (bf16[64,1536]{1,0:T(8,128)(2,1)S(1)}, bf16[64,1536]{1,0:T(8,128)(2,1)S(1)}, u32[]{:S(2)}, u32[]{:S(2)}) collective-permute-start(bf16[64,1536]{1,0:T(8,128)(2,1)S(1)} %get-tuple-element.36), channel_id=1, source_target_pairs={{0,8},{8,0},{16,24},{24,16},{1,9},{9,1},{17,25},{25,17},{2,10},{10... | collective-permute-start | bytes 589832 | tf_op jit(solution)/shard_map/ppermute | solution.py:319
  19.6 13.4 %collective-permute-start.7 = (f32[360,128]{1,0:T(8,128)S(1)}, f32[360,128]{1,0:T(8,128)S(1)}, u32[]{:S(2)}, u32[]{:S(2)}) collective-permute-start(f32[360,128]{1,0:T(8,128)S(1)} %copy-done.5), channel_id=1, source_target_pairs={{0,24},{8,16},{16,8},{24,0},{1,25},{9,17},{17,9},{25,1},{2,26},{10... | collective-permute-start | bytes 552968 | tf_op jit(solution)/shard_map/ppermute | solution.py:297
  22.4 14.2 %collective-permute-start.6 = (f32[360,128]{1,0:T(8,128)S(1)}, f32[360,128]{1,0:T(8,128)S(1)}, u32[]{:S(2)}, u32[]{:S(2)}) collective-permute-start(f32[360,128]{1,0:T(8,128)S(1)} %copy-done.5), channel_id=1, source_target_pairs={{0,16},{8,24},{16,0},{24,8},{1,17},{9,25},{17,1},{25,9},{2,18},{10... | collective-permute-start | bytes 552968 | tf_op jit(solution)/shard_map/ppermute | solution.py:297
  24.8 12.2 %collective-permute-start.5 = (f32[360,128]{1,0:T(8,128)S(1)}, f32[360,128]{1,0:T(8,128)S(1)}, u32[]{:S(2)}, u32[]{:S(2)}) collective-permute-start(f32[360,128]{1,0:T(8,128)S(1)} %copy-done.5), channel_id=1, source_target_pairs={{0,8},{8,0},{16,24},{24,16},{1,9},{9,1},{17,25},{25,17},{2,10},{10... | collective-permute-start | bytes 552968 | tf_op jit(solution)/shard_map/ppermute | solution.py:297
  33.0 8.5 %copy-start.9 = (f32[360,128]{1,0:T(8,128)}, f32[360,128]{1,0:T(8,128)S(1)}, u32[]{:S(2)}) copy-start(f32[360,128]{1,0:T(8,128)S(1)} %collective-permute-done.7.refs_3_) | copy-start | bytes 552964
  37.0 57.1 %copy-start.1 = (f32[32,3072]{1,0:T(8,128)S(1)}, f32[32,3072]{1,0:T(8,128)}, u32[]{:S(2)}) copy-start(f32[32,3072]{1,0:T(8,128)} %comps_ref.3) | copy-start | bytes 1179652
  37.0 13.8 %collective-permute-start.10 = (bf16[64,1536]{1,0:T(8,128)(2,1)S(1)}, bf16[64,1536]{1,0:T(8,128)(2,1)S(1)}, u32[]{:S(2)}, u32[]{:S(2)}) collective-permute-start(bf16[64,1536]{1,0:T(8,128)(2,1)S(1)} %get-tuple-element.30), channel_id=1, source_target_pairs={{0,6},{1,7},{2,4},{3,5},{4,2},{5,3},{6,0},{7,1},{8,14},{9,15},{10,... | collective-permute-start | bytes 589832 | tf_op jit(solution)/shard_map/ppermute | solution.py:326
  40.7 38.5 %collective-permute-start.9 = (bf16[64,1536]{1,0:T(8,128)(2,1)S(1)}, bf16[64,1536]{1,0:T(8,128)(2,1)S(1)}, u32[]{:S(2)}, u32[]{:S(2)}) collective-permute-start(bf16[64,1536]{1,0:T(8,128)(2,1)S(1)} %get-tuple-element.31), channel_id=1, source_target_pairs={{0,4},{1,5},{2,6},{3,7},{4,0},{5,1},{6,2},{7,3},{8,12},{9,13},{10,... | collective-permute-start | bytes 589832 | tf_op jit(solution)/shard_map/ppermute | solution.py:326
  40.7 38.5 %collective-permute-start.8 = (bf16[64,1536]{1,0:T(8,128)(2,1)S(1)}, bf16[64,1536]{1,0:T(8,128)(2,1)S(1)}, u32[]{:S(2)}, u32[]{:S(2)}) collective-permute-start(bf16[64,1536]{1,0:T(8,128)(2,1)S(1)} %get-tuple-element.32), channel_id=1, source_target_pairs={{0,2},{1,3},{2,0},{3,1},{4,6},{5,7},{6,4},{7,5},{8,10},{9,11},{10,... | collective-permute-start | bytes 589832 | tf_op jit(solution)/shard_map/ppermute | solution.py:326
  48.8 34.1 %copy-start.6 = (bf16[64,208]{1,0:T(8,128)(2,1)S(1)}, bf16[64,208]{1,0:T(8,128)(2,1)}, u32[]{:S(2)}) copy-start(bf16[64,208]{1,0:T(8,128)(2,1)} %solve.1) | copy-start | bytes 79876
  79.3 42.1 %copy-start = (bf16[4,64,1536]{2,1,0:T(8,128)(2,1)}, bf16[4,64,1536]{2,1,0:T(8,128)(2,1)S(1)}, u32[]{:S(2)}) copy-start(bf16[4,64,1536]{2,1,0:T(8,128)(2,1)S(1)} %pad_maximum_fusion.3.refs_1_) | copy-start | bytes 2359300
  79.3 28.9 %collective-permute-start.16 = (bf16[4,64,1536]{2,1,0:T(8,128)(2,1)S(1)}, bf16[4,64,1536]{2,1,0:T(8,128)(2,1)S(1)}, u32[]{:S(2)}, u32[]{:S(2)}) collective-permute-start(bf16[4,64,1536]{2,1,0:T(8,128)(2,1)S(1)} %pad_maximum_fusion.3.refs_1_), channel_id=1, source_target_pairs={{0,24},{8,16},{16,8},{24,0},{1,25},{9,17},{17,9},{25,1},{2,26},{10... | collective-permute-start | bytes 2359304 | tf_op jit(solution)/shard_map/ppermute | solution.py:297
  80.8 38.5 %collective-permute-start.15 = (bf16[4,64,1536]{2,1,0:T(8,128)(2,1)S(1)}, bf16[4,64,1536]{2,1,0:T(8,128)(2,1)S(1)}, u32[]{:S(2)}, u32[]{:S(2)}) collective-permute-start(bf16[4,64,1536]{2,1,0:T(8,128)(2,1)S(1)} %pad_maximum_fusion.3.refs_1_), channel_id=1, source_target_pairs={{0,16},{8,24},{16,0},{24,8},{1,17},{9,25},{17,1},{25,9},{2,18},{10... | collective-permute-start | bytes 2359304 | tf_op jit(solution)/shard_map/ppermute | solution.py:297
  82.3 39.1 %collective-permute-start.14 = (bf16[4,64,1536]{2,1,0:T(8,128)(2,1)S(1)}, bf16[4,64,1536]{2,1,0:T(8,128)(2,1)S(1)}, u32[]{:S(2)}, u32[]{:S(2)}) collective-permute-start(bf16[4,64,1536]{2,1,0:T(8,128)(2,1)S(1)} %pad_maximum_fusion.3.refs_1_), channel_id=1, source_target_pairs={{0,8},{8,0},{16,24},{24,16},{1,9},{9,1},{17,25},{25,17},{2,10},{10... | collective-permute-start | bytes 2359304 | tf_op jit(solution)/shard_map/ppermute | solution.py:297
  82.9 1.2 collective-permute-start.11
  84.7 8.4 %collective-permute-start.12 = (bf16[2,64,208]{2,1,0:T(8,128)(2,1)}, bf16[2,64,208]{2,1,0:T(8,128)(2,1)}, u32[]{:S(2)}, u32[]{:S(2)}) collective-permute-start(bf16[2,64,208]{2,1,0:T(8,128)(2,1)} %pad_maximum_fusion.6), channel_id=1, source_target_pairs={{0,2},{1,3},{2,0},{3,1},{4,6},{5,7},{6,4},{7,5},{8,10},{9,11},{10,... | collective-permute-start | bytes 159752 | tf_op jit(solution)/shard_map/ppermute | solution.py:332
  94.0 12.6 %collective-permute-start.13 = (bf16[4,64,208]{2,1,0:T(8,128)(2,1)S(1)}, bf16[4,64,208]{2,1,0:T(8,128)(2,1)S(1)}, u32[]{:S(2)}, u32[]{:S(2)}) collective-permute-start(bf16[4,64,208]{2,1,0:T(8,128)(2,1)S(1)} %pad_maximum_fusion.5), channel_id=1, source_target_pairs={{0,4},{1,5},{2,6},{3,7},{4,0},{5,1},{6,2},{7,3},{8,12},{9,13},{10,... | collective-permute-start | bytes 319496 | tf_op jit(solution)/shard_map/ppermute | solution.py:332
  94.1 14.1 %collective-permute-start = (f32[32,1536]{1,0:T(8,128)S(1)}, f32[32,1536]{1,0:T(8,128)S(1)}, u32[]{:S(2)}, u32[]{:S(2)}) collective-permute-start(f32[32,1536]{1,0:T(8,128)S(1)} %constant_dynamic-slice_fusion.4), channel_id=1, source_target_pairs={{0,0},{1,1},{2,8},{3,9},{4,16},{5,17},{6,24},{7,25},{8,2},{9,3},{1... | collective-permute-start | bytes 589832 | tf_op jit(solution)/shard_map/ppermute | solution.py:343
  108.2 13.2 %copy-start.8 = (f32[32,1536]{1,0:T(8,128)}, f32[32,1536]{1,0:T(8,128)S(1)}, u32[]{:S(2)}) copy-start(f32[32,1536]{1,0:T(8,128)S(1)} %collective-permute-done.col_comps_ref) | copy-start | bytes 589828
  108.2 13.2 %copy-start.2 = (bf16[4,64,1536]{2,1,0:T(8,128)(2,1)}, bf16[4,64,1536]{2,1,0:T(8,128)(2,1)S(1)}, u32[]{:S(2)}) copy-start(bf16[4,64,1536]{2,1,0:T(8,128)(2,1)S(1)} %collective-permute-done.16.refs_4_) | copy-start | bytes 2359300
  (6 other events, 17.3 us)
Sparse Core Ops, SparseCore 0:
  9.1 84.1 all-gather.1

commit v5 on v3

--- a/solution.py
+++ b/solution.py
@@ -10,7 +10,6 @@
 F32, BF16 = jnp.float32, jnp.bfloat16
 VMEM_LIMIT = 56 * 1024 * 1024
 SUB = 8
-CHUNKS = 1
 
 
 def split3(x):
@@ -133,7 +132,8 @@
         value = value - jnp.sum(total_term, axis=0, keepdims=True)
         g = j // SUB
         groups[g] = jnp.where(index == j - first, value, groups[g])
-    coef = jnp.concatenate(groups, axis=0)
+    coef = 2.0 * jnp.concatenate(groups, axis=0)
+    last = 2.0 * last
     c1, c2, c3 = [part.astype(F32) for part in split3(coef)]
     l1, l2, l3 = [part.astype(F32) for part in split3(last)]
     index = lax.broadcasted_iota(jnp.int32, (2 * SUB, markers), 0)
@@ -166,18 +166,18 @@
     fitted = lax.dot_general(
         coef, design_parts(x), (((1,), (0,)), ((), ())), preferred_element_type=F32
     )
-    freq = jnp.clip(fitted, 0.01, 0.99)
+    twice = jnp.clip(fitted, 0.02, 1.98)
     observed = present.astype(F32)
-    resid = observed * (dosage.astype(F32) - 2.0 * freq)
-    sdev = observed * jnp.sqrt(freq * (1.0 - freq))
-    return resid.astype(BF16), (2.0 * sdev).astype(BF16)
-
-
-def columns_kernel(rows, ratio, cols, col_comps_ref, *refs):
-    coef_refs = refs[:cols]
-    piece_refs = refs[cols : cols + rows]
-    coef_out, col_r, col_s, coef, raw_cols, sems = refs[cols + rows :]
-    here = coef_refs[0].shape[0]
+    spread = twice * (2.0 - twice)
+    resid = observed * (dosage.astype(F32) - twice)
+    sdev = observed * (spread * lax.rsqrt(spread))
+    return resid.astype(BF16), sdev.astype(BF16)
+
+
+def columns_kernel(rows, ratio, cols, groups, col_comps_ref, *refs):
+    coef_ref, piece_refs = refs[0], refs[1 : 1 + groups * rows]
+    coef_out, col_r, col_s, coef, raw_cols, sems = refs[1 + groups * rows :]
+    here = coef_ref.shape[1]
     width = col_r.shape[1]
     r = lax.axis_index("rows")
     q = lax.axis_index("cols")
@@ -185,18 +185,19 @@
     for d in range(cols):
         place = pl.multiple_of((q ^ d) * here, here)
         copies.append(
-            pltpu.make_async_copy(coef_refs[d], coef.at[pl.ds(place, here), :], sems.at[len(copies)])
+            pltpu.make_async_copy(coef_ref.at[d], coef.at[pl.ds(place, here), :], sems.at[len(copies)])
         )
     height = piece_refs[0].shape[1]
     for d in range(rows):
         begin = (r ^ d) * height
         k, part, inside = begin // (2 * here), lax.rem(begin // here, 2), lax.rem(begin, here)
-        for e in range(rows):
+        found = [ref.at[i] for ref in piece_refs[d::rows] for i in range(ref.shape[0])]
+        for e, piece in enumerate(found):
             owner = ((q // ratio) ^ e) * ratio + lax.rem(q + ratio - k, ratio)
             place = pl.multiple_of(owner * here + inside, height)
             copies.append(
                 pltpu.make_async_copy(
-                    piece_refs[d].at[e], raw_cols.at[part, pl.ds(place, height), :], sems.at[len(copies)]
+                    piece, raw_cols.at[part, pl.ds(place, height), :], sems.at[len(copies)]
                 )
             )
     for copy in copies:
@@ -216,11 +217,11 @@
 
 def columns_call(rows, ratio, cols, col_comps, coefs, pieces):
     comps, width = col_comps.shape
-    markers = coefs[0].shape[0] * cols
+    markers = coefs.shape[1] * cols
     anywhere = pl.BlockSpec(memory_space=pl.ANY)
     return pl.pallas_call(
-        functools.partial(columns_kernel, rows, ratio, cols),
-        in_specs=[pl.BlockSpec(memory_space=pltpu.VMEM)] + [anywhere] * (len(coefs) + len(pieces)),
+        functools.partial(columns_kernel, rows, ratio, cols, len(pieces) // rows),
+        in_specs=[pl.BlockSpec(memory_space=pltpu.VMEM)] + [anywhere] * (1 + len(pieces)),
         out_shape=(
             jax.ShapeDtypeStruct((markers, coef_rows(comps)), BF16),
             jax.ShapeDtypeStruct((markers, width), BF16),
@@ -233,52 +234,103 @@
         ],
         compiler_params=pltpu.CompilerParams(vmem_limit_bytes=VMEM_LIMIT),
         name="columns",
-    )(col_comps, *coefs, *pieces)
-
-
-def kin_kernel(raw_ref, comps_ref, coef_ref, col_r, col_s, *refs):
-    out_ref = refs[-1]
-    width = out_ref.shape[1]
-    resid, sdev = panel(coef_ref[...], comps_ref[...], raw_ref[0], raw_ref[1])
+    )(col_comps, coefs, *pieces)
+
+
+def quotient(numer, denom):
+    inverse = pl.reciprocal(denom, approx=True)
+    return numer * (inverse * (2.0 - denom * inverse))
+
+
+def kin_kernel(rows, ratio, turn, start_ref, comps_ref, coef_ref, col_r, col_s, *refs):
+    own_ref = refs[0]
+    from_left, from_right = refs[1:rows], refs[rows : 2 * rows - 1]
+    out_ref, raw, sems = refs[-3:]
+    tile, width = out_ref.shape
+    here = own_ref.shape[0] // (2 * ratio)
+    plane = lax.axis_index("cols") // ratio
+    core = lax.rem(lax.axis_index("cols"), ratio)
+    step = pl.program_id(0)
+
+    def copies(block_ref, slot):
+        source = lax.rem(plane - slot + rows, rows)
+        for k in range(ratio):
+            owner = source * ratio + lax.rem(core + 2 * ratio - turn - k, ratio)
+            place = pl.multiple_of(owner * here, here)
+            for part in range(2):
+                begin = (2 * k + part) * here
+                yield pltpu.make_async_copy(
+                    block_ref.at[begin : begin + here, :],
+                    raw.at[part, pl.ds(place, here), :],
+                    sems.at[(slot * ratio + k) * 2 + part],
+                )
+
+    @pl.when(step == 0)
+    def _():
+        for copy in copies(own_ref, 0):
+            copy.start()
+        for slot in range(1, rows):
+
+            @pl.when(plane >= slot)
+            def _():
+                for copy in copies(from_left[slot - 1], slot):
+                    copy.start()
+
+            @pl.when(plane < slot)
+            def _():
+                for copy in copies(from_right[rows - slot - 1], slot):
+                    copy.start()
+
+        for slot in range(rows):
+            for copy in copies(own_ref, slot):
+                copy.wait()
+
+    here_span = pl.ds(pl.multiple_of(step * tile, tile), tile)
+    resid, sdev = panel(coef_ref[...], comps_ref[...], raw[0, :, here_span], raw[1, :, here_span])
     contract = (((0,), (0,)), ((), ()))
-    step = 512 if width % 512 == 0 else width
-    for at in range(0, width, step):
-        span = slice(at, at + step)
+    wide = 512 if width % 512 == 0 else width
+    for at in range(0, width, wide):
+        span = slice(at, at + wide)
         numer = lax.dot_general(resid, col_r[:, span], contract, preferred_element_type=F32)
         denom = lax.dot_general(sdev, col_s[:, span], contract, preferred_element_type=F32)
-        out_ref[:, span] = numer / denom
-
-
-def kin_call(start, raw, components, coef, col_r, col_s, before):
-    _, markers, count = raw.shape
+        out_ref[:, span] = quotient(numer, denom)
+
+
+def kin_call(rows, ratio, turn, start, components, coef, col_r, col_s, blocks, before):
+    height, count = blocks[0].shape
     comps, people = components.shape
-    width = col_r.shape[1]
-    tile = 512 if count % 512 == 0 else count
-    first = start // tile
-    whole = lambda i: (0, 0)
+    markers, width = col_r.shape
+    tile = 256 if count % 256 == 0 else count
+    whole = lambda i, at: (0, 0)
     in_specs = [
-        pl.BlockSpec((2, markers, tile), lambda i: (0, 0, i)),
-        pl.BlockSpec((comps, tile), lambda i: (0, i + first)),
+        pl.BlockSpec((comps, tile), lambda i, at: (0, i + at[0])),
         pl.BlockSpec(coef.shape, whole),
         pl.BlockSpec((markers, width), whole),
         pl.BlockSpec((markers, width), whole),
-    ]
-    operands = [raw, components, coef, col_r, col_s]
+    ] + [pl.BlockSpec(memory_space=pl.ANY)] * len(blocks)
+    operands = [components, coef, col_r, col_s, *blocks]
     aliases = {}
     if before is not None:
         in_specs.append(pl.BlockSpec(memory_space=pl.ANY))
+        operands.append(before)
         aliases = {len(operands): 0}
-        operands.append(before)
     return pl.pallas_call(
-        kin_kernel,
-        grid=(count // tile,),
-        in_specs=in_specs,
-        out_specs=pl.BlockSpec((tile, width), lambda i: (i + first, 0)),
+        functools.partial(kin_kernel, rows, ratio, turn),
+        grid_spec=pltpu.PrefetchScalarGridSpec(
+            num_scalar_prefetch=1,
+            grid=(count // tile,),
+            in_specs=in_specs,
+            out_specs=pl.BlockSpec((tile, width), lambda i, at: (i + at[0], 0)),
+            scratch_shapes=[
+                pltpu.VMEM((2, markers, count), BF16),
+                pltpu.SemaphoreType.DMA((rows * ratio * 2,)),
+            ],
+        ),
         out_shape=jax.ShapeDtypeStruct((people, width), F32),
         input_output_aliases=aliases,
         compiler_params=pltpu.CompilerParams(vmem_limit_bytes=VMEM_LIMIT),
         name="kinship",
-    )(*operands)
+    )((start // tile)[None].astype(jnp.int32), *operands)
 
 
 def per_device(dosage, present, components):
@@ -287,55 +339,81 @@
     markers, people = dosage.shape
     comps = components.shape[0]
     width = people // ratio
+    row = lax.axis_index("rows")
     col = lax.axis_index("cols")
-    raw = jnp.stack([dosage.astype(BF16), present.astype(BF16)])
+    core, plane = col % ratio, col // ratio
+
+    def pairs(hop):
+        moves = [(z, c, *hop(z, c)) for z in range(rows) for c in range(ratio)]
+        return [(z * ratio + c, y * ratio + b) for z, c, y, b in moves if 0 <= y < rows]
 
     def across(x, axis, size):
         return [x] + [lax.ppermute(x, axis, [(i, i ^ d) for i in range(size)]) for d in range(1, size)]
 
-    starts = [people * i // CHUNKS for i in range(CHUNKS + 1)]
-    raw_rows = [
-        lax.all_gather(raw[:, :, a:b], "cols", axis=1, tiled=True) for a, b in zip(starts, starts[1:])
-    ]
-
-    row = lax.axis_index("rows")
-    core, plane = col % ratio, col // ratio
+    def swap(x, k):
+        return lax.ppermute(x, "cols", pairs(lambda z, c: (z, (c + k) % ratio))) if k else x
+
+    def along(x, way):
+        return lax.ppermute(x, "cols", pairs(lambda z, c: (z + way, c)))
+
     halves = []
     for k in range(ratio):
-        part = (core + k) % ratio
-        mine = lax.dynamic_slice_in_dim(raw, part * width, width, 2).reshape(2 * markers, width)
-        swaps = [(z * ratio + c, z * ratio + (c + k) % ratio) for z in range(rows) for c in range(ratio)]
-        halves.append(lax.ppermute(mine, "cols", swaps) if k else mine)
+        begin = (core + k) % ratio * width
+        both = [lax.dynamic_slice_in_dim(x, begin, width, 1).astype(BF16) for x in (dosage, present)]
+        halves.append(swap(jnp.concatenate(both, axis=0), k))
     held = jnp.concatenate(halves, axis=0)
+    held, dosage, present = lax.optimization_barrier((held, dosage, present))
+    from_left, from_right = [along(held, 1)], [along(held, -1)]
+
     height = held.shape[0] // rows
     quarters = []
     for d in range(rows):
         mine = lax.dynamic_slice_in_dim(held, (row ^ d) * height, height, 0)
         quarters.append(lax.ppermute(mine, "rows", [(i, i ^ d) for i in range(rows)]) if d else mine)
-    quarters = jnp.stack(quarters)
+    gram = gram_call(dosage, present, components)
+    col_comps = lax.dynamic_slice_in_dim(components, core * width, width, 1)
+    grams = across(gram, "rows", rows)
+    quarters, grams, col_comps, from_left[0], from_right[0] = lax.optimization_barrier(
+        (jnp.stack(quarters), grams, col_comps, from_left[0], from_right[0])
+    )
     moved = []
     for e in range(rows):
         mine = lax.dynamic_index_in_dim(quarters, row ^ plane ^ e, 0, keepdims=False)
-        hops = [(z * ratio + c, (z ^ e) * ratio + c) for z in range(rows) for c in range(ratio)]
-        moved.append(lax.ppermute(mine, "cols", hops) if e else mine)
-    pieces = across(jnp.stack(moved), "rows", rows)
-
-    mine = lax.dynamic_slice_in_dim(components, core * width, width, 1)
-    moves = [
-        (r * cols + z * ratio + c, z * cols + r * ratio + c)
-        for r in range(rows)
-        for z in range(rows)
-        for c in range(ratio)
+        moved.append(lax.ppermute(mine, "cols", pairs(lambda z, c: (z ^ e, c))) if e else mine)
+    coefs = solve_call(grams, comps, markers)[None]
+    sent = [
+        lax.ppermute(
+            col_comps,
+            ("rows", "cols"),
+            [(z * cols + z * ratio + c, (z ^ d) * cols + z * ratio + c) for z in range(rows) for c in range(ratio)],
+        )
+        for d in range(1, rows)
     ]
-    col_comps = lax.ppermute(mine, ("rows", "cols"), moves)
-
-    gram = gram_call(dosage, present, components)
-    coef = solve_call(across(gram, "rows", rows), comps, markers)
-    coefs = across(coef, "cols", cols)
-    coef, col_r, col_s = columns_call(rows, ratio, cols, col_comps, coefs, pieces)
+    moved, coefs, sent, held, from_left, from_right = lax.optimization_barrier(
+        (moved, coefs, sent, held, from_left, from_right)
+    )
+    pieces = []
+    for step in range(rows - 2):
+        begin, end = rows * step // (rows - 2), rows * (step + 1) // (rows - 2)
+        pieces.append(across(jnp.stack(moved[begin:end]), "rows", rows))
+        from_left.append(along(from_left[-1], 1))
+        from_right.append(along(from_right[-1], -1))
+        hop = 1
+        while step == 0 and hop < cols:
+            other = lax.ppermute(coefs, "cols", [(i, i ^ hop) for i in range(cols)])
+            coefs = jnp.concatenate([coefs, other], axis=0)
+            hop *= 2
+        if step < rows - 3:
+            pieces, coefs, held, from_left, from_right = lax.optimization_barrier(
+                (pieces, coefs, held, from_left, from_right)
+            )
+    col_comps = sum(sent, jnp.where(row == plane, col_comps, 0.0))
+    coef, col_r, col_s = columns_call(rows, ratio, cols, col_comps, coefs, sum(pieces, []))
     out = None
-    for start, part in zip(starts, raw_rows):
-        out = kin_call(start, part, components, coef, col_r, col_s, out)
+    for turn in range(ratio):
+        start = (core + ratio - turn) % ratio * width
+        came = [swap(block, turn) for block in [held, *from_left, *from_right]]
+        out = kin_call(rows, ratio, turn, start, components, coef, col_r, col_s, came, out)
     return out
 
 

time: 179 us -> 167 us (0.933); the launches traced: 176 us -> 166 us
  waiting for transfers between devices: 87.2 us -> 57.4 us
  starting transfers between devices: 30.6 us -> 54.7 us
  between operations: 13.6 us -> 0.71 us
  Pallas kernels: 38.5 us -> 45.6 us
  other arithmetic: 3.43 us -> 5.78 us
    ppermute x5 -> x23, starting transfers between devices: 5.81 us -> 38.2 us  [the longest x6 14.8 us: along(): return lax.ppermute(x, 'cols', pairs(lambda z, c: (z + way, c)))]
    ppermute x13 -> x9, waiting for transfers between devices: 39.8 us -> 25.9 us  [across(): lax.ppermute(x, axis, [(i, i ^ d) for i in range(size)])]
    ppermute x3, waiting for transfers between devices: 9.34 us -> 0.01 us  [per_device(): lax.ppermute(mine, 'rows', [(i, i ^ d) for i in range(rows)])]
    ppermute x13 -> x9, starting transfers between devices: 20.3 us -> 12.9 us  [across(): lax.ppermute(x, axis, [(i, i ^ d) for i in range(size)])]
    pallas_call x2 -> x3, Pallas kernels: 25.6 us -> 32.6 us  [the longest x2 26.3 us: kin_call(): pl.pallas_call(functools.partial(kin_kernel, rows, ratio, turn), grid_spe...]
    ppermute x5 -> x23, waiting for transfers between devices: 38 us -> 31.5 us  [the longest x3 22 us: per_device(): other = lax.ppermute(coefs, 'cols', [(i, i ^ hop) for i in range(cols)])]
    another operation x6 -> x3, other arithmetic: 3.43 us -> 0.18 us  [the longest x1 0.1 us: per_device(): jnp.stack(quarters)]
    concatenate x0 -> x5, other arithmetic: none -> 2.41 us  [the longest x3 2.33 us: per_device(): coefs = jnp.concatenate([coefs, other], axis=0)]
  transfers between devices with their start and end apart: 22 -> 35, of which waited for: 12 -> 12; matrix products, arithmetic and copies ran while one was open for 1% -> 2% of each run, Pallas kernels for 11% -> 19%
where the time goes in v5:
time: 167 us; the launch traced here: 166 us
  waiting for transfers between devices  57.4 us (34%)
  starting transfers between devices  54.7 us (33%)
  Pallas kernels  45.6 us (27%)
  other arithmetic  5.78 us (3%)
  local copies, waits for them, and re-layouts  2.23 us (1%)
    pallas_call x2, Pallas kernels, kin_call(): pl.pallas_call(functools.partial(kin_kernel, rows, ratio, turn), grid_spe...  26.3 us
    ppermute x9, waiting for transfers between devices, across(): lax.ppermute(x, axis, [(i, i ^ d) for i in range(size)])  25.9 us
    ppermute x3, waiting for transfers between devices, per_device(): other = lax.ppermute(coefs, 'cols', [(i, i ^ hop) for i in range(cols)])  22 us
    ppermute x6, starting transfers between devices, along(): return lax.ppermute(x, 'cols', pairs(lambda z, c: (z + way, c)))  14.8 us
    ppermute x9, starting transfers between devices, across(): lax.ppermute(x, axis, [(i, i ^ d) for i in range(size)])  12.9 us
    ppermute x3, starting transfers between devices, per_device(): lax.ppermute(col_comps, ('rows', 'cols'), [(z * cols + z * ratio + c, (z...  8.67 us
    ppermute x3, starting transfers between devices, per_device(): other = lax.ppermute(coefs, 'cols', [(i, i ^ hop) for i in range(cols)])  8.5 us
    ppermute x6, waiting for transfers between devices, along(): return lax.ppermute(x, 'cols', pairs(lambda z, c: (z + way, c)))  8.15 us
  transfers between devices with their start and end apart: 35, of which 12 were waited for; matrix products, arithmetic and copies ran while one was open for 2% of the time, Pallas kernels for 19%

profile of v5, /device:TPU:0, one launch (start us, length us, event | category | flops | bytes accessed | tf_op | source)
XLA Modules:
  0.0 166.4 jit_solution(7856717347069532747)
XLA Ops:
  4.9 5.5 %collective-permute-start.7 = (bf16[256,1536]{1,0:T(8,128)(2,1)S(1)}, bf16[256,1536]{1,0:T(8,128)(2,1)S(1)}, u32[]{:S(2)}, u32[]{:S(2)}) collective-permute-start(bf16[256,1536]{1,0:T(8,128)(2,1)S(1)} %pad_maximum_fusion.refs_0_), channel_id=1, source_target_pairs={{0,2},{1,3},{2,4},{3,5},{4,6},{5,7},{8,10},{9,11},{10,12},{11,13},... | collective-permute-start | bytes 2359304 | tf_op jit(solution)/shard_map/ppermute | solution.py:357
  10.5 2.9 %collective-permute-start.3 = (bf16[64,1536]{1,0:T(8,128)(2,1)S(1)}, bf16[64,1536]{1,0:T(8,128)(2,1)S(1)}, u32[]{:S(2)}, u32[]{:S(2)}) collective-permute-start(bf16[64,1536]{1,0:T(8,128)(2,1)S(1)} %get-tuple-element.80), channel_id=1, source_target_pairs={{0,24},{8,16},{16,8},{24,0},{1,25},{9,17},{17,9},{25,1},{2,26},{10... | collective-permute-start | bytes 589832 | tf_op jit(solution)/shard_map/ppermute | solution.py:372
  14.1 5.6 %gram.1.refs_0_ = f32[360,128]{1,0:T(8,128)} custom-call(s32[64,3072]{1,0:T(8,128)} %dosage_ref, s32[64,3072]{1,0:T(8,128)} %present_ref, f32[32,3072]{1,0:T(8,128)} %comps_ref.5), custom_call_target="tpu_custom_call" | custom-call | tf_op jit(solution)/shard_map/gram/pallas_call | solution.py:62
  19.8 2.9 %collective-permute-start.6 = (f32[360,128]{1,0:T(8,128)}, f32[360,128]{1,0:T(8,128)S(1)}, u32[]{:S(2)}, u32[]{:S(2)}) collective-permute-start(f32[360,128]{1,0:T(8,128)} %gram.1.refs_0_), channel_id=1, source_target_pairs={{0,24},{8,16},{16,8},{24,0},{1,25},{9,17},{17,9},{25,1},{2,26},{10... | collective-permute-start | bytes 552968 | tf_op jit(solution)/shard_map/ppermute | solution.py:351
  24.8 2.7 %collective-permute-done.6.refs_3_ = f32[360,128]{1,0:T(8,128)S(1)} collective-permute-done((f32[360,128]{1,0:T(8,128)}, f32[360,128]{1,0:T(8,128)S(1)}, u32[]{:S(2)}, u32[]{:S(2)}) %collective-permute-start.6) | collective-permute-done | bytes 184352 | tf_op jit(solution)/shard_map/ppermute | solution.py:351
  27.6 2.8 %collective-permute-done.5.refs_2_ = f32[360,128]{1,0:T(8,128)S(1)} collective-permute-done((f32[360,128]{1,0:T(8,128)}, f32[360,128]{1,0:T(8,128)S(1)}, u32[]{:S(2)}, u32[]{:S(2)}) %collective-permute-start.5) | collective-permute-done | bytes 184352 | tf_op jit(solution)/shard_map/ppermute | solution.py:351
  35.4 4.0 %collective-permute-start.14 = (f32[32,1536]{1,0:T(8,128)S(1)}, f32[32,1536]{1,0:T(8,128)S(1)}, u32[]{:S(2)}, u32[]{:S(2)}) collective-permute-start(f32[32,1536]{1,0:T(8,128)S(1)} %constant_dynamic-slice_fusion), channel_id=1, source_target_pairs={{0,24},{1,25},{10,18},{11,19},{20,12},{21,13},{30,6},{31,7}} | collective-permute-start | bytes 589832 | tf_op jit(solution)/shard_map/ppermute | solution.py:385
  40.8 3.3 %collective-permute-start.12 = (f32[32,1536]{1,0:T(8,128)S(1)}, f32[32,1536]{1,0:T(8,128)S(1)}, u32[]{:S(2)}, u32[]{:S(2)}) collective-permute-start(f32[32,1536]{1,0:T(8,128)S(1)} %constant_dynamic-slice_fusion), channel_id=1, source_target_pairs={{0,8},{1,9},{10,2},{11,3},{20,28},{21,29},{30,22},{31,23}} | collective-permute-start | bytes 589832 | tf_op jit(solution)/shard_map/ppermute | solution.py:385
  44.1 7.3 %solve.1 = bf16[64,208]{1,0:T(8,128)(2,1)} custom-call(f32[360,128]{1,0:T(8,128)} %gram.1.refs_0_, f32[360,128]{1,0:T(8,128)} %copy-done.21, f32[360,128]{1,0:T(8,128)} %copy-done.20, f32[360,128]{1,0:T(8,128)} %copy-done.19), custom_call_target="tpu_custom_call" | custom-call | tf_op jit(solution)/shard_map/solve/pallas_call | solution.py:151
  54.4 5.5 %collective-permute-start.19 = (bf16[2,64,208]{2,1,0:T(8,128)(2,1)S(1)}, bf16[2,64,208]{2,1,0:T(8,128)(2,1)S(1)}, u32[]{:S(2)}, u32[]{:S(2)}) collective-permute-start(bf16[2,64,208]{2,1,0:T(8,128)(2,1)S(1)} %pad_maximum_fusion.7), channel_id=1, source_target_pairs={{0,2},{1,3},{2,0},{3,1},{4,6},{5,7},{6,4},{7,5},{8,10},{9,11},{10,... | collective-permute-start | bytes 159752 | tf_op jit(solution)/shard_map/ppermute | solution.py:403
  60.0 1.7 %collective-permute-start.17 = (bf16[2,64,1536]{2,1,0:T(8,128)(2,1)S(1)}, bf16[2,64,1536]{2,1,0:T(8,128)(2,1)S(1)}, u32[]{:S(2)}, u32[]{:S(2)}) collective-permute-start(bf16[2,64,1536]{2,1,0:T(8,128)(2,1)S(1)} %pad_maximum_fusion.3.refs_1_), channel_id=1, source_target_pairs={{0,24},{8,16},{16,8},{24,0},{1,25},{9,17},{17,9},{25,1},{2,26},{10... | collective-permute-start | bytes 1179656 | tf_op jit(solution)/shard_map/ppermute | solution.py:351
  61.7 2.8 %collective-permute-start.21 = (bf16[256,1536]{1,0:T(8,128)(2,1)S(1)}, bf16[256,1536]{1,0:T(8,128)(2,1)}, u32[]{:S(2)}, u32[]{:S(2)}) collective-permute-start(bf16[256,1536]{1,0:T(8,128)(2,1)S(1)} %collective-permute-done.7.refs_1_), channel_id=1, source_target_pairs={{0,2},{1,3},{2,4},{3,5},{4,6},{5,7},{8,10},{9,11},{10,12},{11,13},... | collective-permute-start | bytes 2359304 | tf_op jit(solution)/shard_map/ppermute | solution.py:357
  66.6 3.0 %collective-permute-start.20 = (bf16[4,64,208]{2,1,0:T(8,128)(2,1)S(1)}, bf16[4,64,208]{2,1,0:T(8,128)(2,1)S(1)}, u32[]{:S(2)}, u32[]{:S(2)}) collective-permute-start(bf16[4,64,208]{2,1,0:T(8,128)(2,1)S(1)} %pad_maximum_fusion.6), channel_id=1, source_target_pairs={{0,4},{1,5},{2,6},{3,7},{4,0},{5,1},{6,2},{7,3},{8,12},{9,13},{10,... | collective-permute-start | bytes 319496 | tf_op jit(solution)/shard_map/ppermute | solution.py:403
  70.8 20.5 %collective-permute-done.20 = bf16[4,64,208]{2,1,0:T(8,128)(2,1)S(1)} collective-permute-done((bf16[4,64,208]{2,1,0:T(8,128)(2,1)S(1)}, bf16[4,64,208]{2,1,0:T(8,128)(2,1)S(1)}, u32[]{:S(2)}, u32[]{:S(2)}) %collective-permute-start.20) | collective-permute-done | bytes 106528 | tf_op jit(solution)/shard_map/ppermute | solution.py:403
  91.3 2.6 %collective-permute-start.15 = (bf16[2,64,1536]{2,1,0:T(8,128)(2,1)S(1)}, bf16[2,64,1536]{2,1,0:T(8,128)(2,1)S(1)}, u32[]{:S(2)}, u32[]{:S(2)}) collective-permute-start(bf16[2,64,1536]{2,1,0:T(8,128)(2,1)S(1)} %pad_maximum_fusion.3.refs_1_), channel_id=1, source_target_pairs={{0,8},{8,0},{16,24},{24,16},{1,9},{9,1},{17,25},{25,17},{2,10},{10... | collective-permute-start | bytes 1179656 | tf_op jit(solution)/shard_map/ppermute | solution.py:351
  96.3 7.6 %collective-permute-done.15.refs_2_ = bf16[2,64,1536]{2,1,0:T(8,128)(2,1)S(1)} collective-permute-done((bf16[2,64,1536]{2,1,0:T(8,128)(2,1)S(1)}, bf16[2,64,1536]{2,1,0:T(8,128)(2,1)S(1)}, u32[]{:S(2)}, u32[]{:S(2)}) %collective-permute-start.15) | collective-permute-done | bytes 393248 | tf_op jit(solution)/shard_map/ppermute | solution.py:351
  104.6 2.3 %collective-permute-start.29 = (bf16[256,1536]{1,0:T(8,128)(2,1)}, bf16[256,1536]{1,0:T(8,128)(2,1)}, u32[]{:S(2)}, u32[]{:S(2)}) collective-permute-start(bf16[256,1536]{1,0:T(8,128)(2,1)} %collective-permute-done.21.refs_2_), channel_id=1, source_target_pairs={{0,2},{1,3},{2,4},{3,5},{4,6},{5,7},{8,10},{9,11},{10,12},{11,13},... | collective-permute-start | bytes 2359304 | tf_op jit(solution)/shard_map/ppermute | solution.py:357
  106.9 3.9 %collective-permute-done.25.refs_8_ = bf16[2,64,1536]{2,1,0:T(8,128)(2,1)S(1)} collective-permute-done((bf16[2,64,1536]{2,1,0:T(8,128)(2,1)S(1)}, bf16[2,64,1536]{2,1,0:T(8,128)(2,1)S(1)}, u32[]{:S(2)}, u32[]{:S(2)}) %collective-permute-start.25) | collective-permute-done | bytes 393248 | tf_op jit(solution)/shard_map/ppermute | solution.py:351
  113.9 7.5 %collective-permute-done.23.refs_6_ = bf16[2,64,1536]{2,1,0:T(8,128)(2,1)S(1)} collective-permute-done((bf16[2,64,1536]{2,1,0:T(8,128)(2,1)S(1)}, bf16[2,64,1536]{2,1,0:T(8,128)(2,1)S(1)}, u32[]{:S(2)}, u32[]{:S(2)}) %collective-permute-start.23) | collective-permute-done | bytes 393248 | tf_op jit(solution)/shard_map/ppermute | solution.py:351
  123.5 7.0 %collective-permute-done.33.refs_6_ = bf16[256,1536]{1,0:T(8,128)(2,1)} collective-permute-done((bf16[256,1536]{1,0:T(8,128)(2,1)}, bf16[256,1536]{1,0:T(8,128)(2,1)}, u32[]{:S(2)}, u32[]{:S(2)}) %collective-permute-start.33) | collective-permute-done | bytes 786464 | tf_op jit(solution)/shard_map/ppermute | solution.py:357
  130.7 1.7 %add_add_fusion.col_comps_ref = f32[32,1536]{1,0:T(8,128)} fusion(f32[32,1536]{1,0:T(8,128)S(1)} %collective-permute-done.14, f32[32,1536]{1,0:T(8,128)} %copy-done.17, f32[32,1536]{1,0:T(8,128)} %copy-done.18, f32[32,1536]{1,0:T(8,128)S(1)} %constant_dynamic-slice_fusion, pred[]{:T(512)S(6)} %eq.9), kind=kLoop, calls=%fused_computation.10 | loop fusion | flops 196608 | bytes 983041 | tf_op jit(solution)/shard_map/add | solution.py:410
  132.4 6.3 %columns.1 = (bf16[512,208]{1,0:T(8,128)(2,1)}, bf16[512,1536]{1,0:T(8,128)(2,1)}, bf16[512,1536]{1,0:T(8,128)(2,1)}) custom-call(f32[32,1536]{1,0:T(8,128)} %add_add_fusion.col_comps_ref, bf16[8,64,208]{2,1,0:T(8,128)(2,1)} %pad_maximum_fusion.5.refs_0_, bf16[2,64,1536]{2,1,0:T(8,128)(2,1)} %copy-done.2, bf16[2,64,1536]{2,1,0:T(8,128)(2,1)} %copy-done.13, ...), custom_call_target="tpu_custom_call" | custom-call | tf_op jit(solution)/shard_map/columns/pallas_call | solution.py:222
  138.7 13.2 %kinship.2.refs_7_ = f32[3072,1536]{1,0:T(8,128)} custom-call(s32[1]{0:T(128)} %bitcast.14.start_ref, f32[32,3072]{1,0:T(8,128)} %comps_ref.5, bf16[512,208]{1,0:T(8,128)(2,1)} %get-tuple-element.67.coef_ref, bf16[512,1536]{1,0:T(8,128)(2,1)} %get-tuple-element.68.col_r, bf16[512,1536]{1,0:T(8,128)(2,1)} %get-tuple-element.69.col_s, ...), custom_call_target="tpu_custom_call" | custom-call | tf_op jit(solution)/shard_map/kinship/pallas_call | solution.py:317
  153.1 13.1 %kinship.3 = f32[3072,1536]{1,0:T(8,128)} custom-call(s32[1]{0:T(128)} %bitcast.start_ref, f32[32,3072]{1,0:T(8,128)} %comps_ref.5, bf16[512,208]{1,0:T(8,128)(2,1)} %get-tuple-element.67.coef_ref, bf16[512,1536]{1,0:T(8,128)(2,1)} %get-tuple-element.68.col_r, bf16[512,1536]{1,0:T(8,128)(2,1)} %get-tuple-element.69.col_s, ...), custom_call_target="tpu_custom_call", output_to_operand_aliasing={{}: (12, {})} | custom-call | tf_op jit(solution)/shard_map/kinship/pallas_call | solution.py:317
  (108 shorter events, 29.5 us)
Async XLA Ops:
  3.4 27.4 %collective-permute-start.8 = (bf16[256,1536]{1,0:T(8,128)(2,1)S(1)}, bf16[256,1536]{1,0:T(8,128)(2,1)S(1)}, u32[]{:S(2)}, u32[]{:S(2)}) collective-permute-start(bf16[256,1536]{1,0:T(8,128)(2,1)S(1)} %pad_maximum_fusion.refs_0_), channel_id=1, source_target_pairs={{2,0},{3,1},{4,2},{5,3},{6,4},{7,5},{10,8},{11,9},{12,10},{13,11},... | collective-permute-start | bytes 2359304 | tf_op jit(solution)/shard_map/ppermute | solution.py:357
  4.9 26.0 %collective-permute-start.7 = (bf16[256,1536]{1,0:T(8,128)(2,1)S(1)}, bf16[256,1536]{1,0:T(8,128)(2,1)S(1)}, u32[]{:S(2)}, u32[]{:S(2)}) collective-permute-start(bf16[256,1536]{1,0:T(8,128)(2,1)S(1)} %pad_maximum_fusion.refs_0_), channel_id=1, source_target_pairs={{0,2},{1,3},{2,4},{3,5},{4,6},{5,7},{8,10},{9,11},{10,12},{11,13},... | collective-permute-start | bytes 2359304 | tf_op jit(solution)/shard_map/ppermute | solution.py:357
  32.4 19.0 %collective-permute-start.10 = (bf16[64,1536]{1,0:T(8,128)(2,1)S(1)}, bf16[64,1536]{1,0:T(8,128)(2,1)S(1)}, u32[]{:S(2)}, u32[]{:S(2)}) collective-permute-start(bf16[64,1536]{1,0:T(8,128)(2,1)S(1)} %get-tuple-element.76), channel_id=1, source_target_pairs={{0,4},{1,5},{2,6},{3,7},{4,0},{5,1},{6,2},{7,3},{8,12},{9,13},{10,... | collective-permute-start | bytes 589832 | tf_op jit(solution)/shard_map/ppermute | solution.py:382
  34.0 17.5 %collective-permute-start.9 = (bf16[64,1536]{1,0:T(8,128)(2,1)S(1)}, bf16[64,1536]{1,0:T(8,128)(2,1)S(1)}, u32[]{:S(2)}, u32[]{:S(2)}) collective-permute-start(bf16[64,1536]{1,0:T(8,128)(2,1)S(1)} %get-tuple-element.77), channel_id=1, source_target_pairs={{0,2},{1,3},{2,0},{3,1},{4,6},{5,7},{6,4},{7,5},{8,10},{9,11},{10,... | collective-permute-start | bytes 589832 | tf_op jit(solution)/shard_map/ppermute | solution.py:382
  35.4 16.1 %collective-permute-start.14 = (f32[32,1536]{1,0:T(8,128)S(1)}, f32[32,1536]{1,0:T(8,128)S(1)}, u32[]{:S(2)}, u32[]{:S(2)}) collective-permute-start(f32[32,1536]{1,0:T(8,128)S(1)} %constant_dynamic-slice_fusion), channel_id=1, source_target_pairs={{0,24},{1,25},{10,18},{11,19},{20,12},{21,13},{30,6},{31,7}} | collective-permute-start | bytes 589832 | tf_op jit(solution)/shard_map/ppermute | solution.py:385
  39.5 12.0 %collective-permute-start.13 = (f32[32,1536]{1,0:T(8,128)S(1)}, f32[32,1536]{1,0:T(8,128)S(1)}, u32[]{:S(2)}, u32[]{:S(2)}) collective-permute-start(f32[32,1536]{1,0:T(8,128)S(1)} %constant_dynamic-slice_fusion), channel_id=1, source_target_pairs={{0,16},{1,17},{10,26},{11,27},{20,4},{21,5},{30,14},{31,15}} | collective-permute-start | bytes 589832 | tf_op jit(solution)/shard_map/ppermute | solution.py:385
  54.4 11.5 %collective-permute-start.19 = (bf16[2,64,208]{2,1,0:T(8,128)(2,1)S(1)}, bf16[2,64,208]{2,1,0:T(8,128)(2,1)S(1)}, u32[]{:S(2)}, u32[]{:S(2)}) collective-permute-start(bf16[2,64,208]{2,1,0:T(8,128)(2,1)S(1)} %pad_maximum_fusion.7), channel_id=1, source_target_pairs={{0,2},{1,3},{2,0},{3,1},{4,6},{5,7},{6,4},{7,5},{8,10},{9,11},{10,... | collective-permute-start | bytes 159752 | tf_op jit(solution)/shard_map/ppermute | solution.py:403
  60.0 34.1 %collective-permute-start.17 = (bf16[2,64,1536]{2,1,0:T(8,128)(2,1)S(1)}, bf16[2,64,1536]{2,1,0:T(8,128)(2,1)S(1)}, u32[]{:S(2)}, u32[]{:S(2)}) collective-permute-start(bf16[2,64,1536]{2,1,0:T(8,128)(2,1)S(1)} %pad_maximum_fusion.3.refs_1_), channel_id=1, source_target_pairs={{0,24},{8,16},{16,8},{24,0},{1,25},{9,17},{17,9},{25,1},{2,26},{10... | collective-permute-start | bytes 1179656 | tf_op jit(solution)/shard_map/ppermute | solution.py:351
  61.7 42.3 %collective-permute-start.21 = (bf16[256,1536]{1,0:T(8,128)(2,1)S(1)}, bf16[256,1536]{1,0:T(8,128)(2,1)}, u32[]{:S(2)}, u32[]{:S(2)}) collective-permute-start(bf16[256,1536]{1,0:T(8,128)(2,1)S(1)} %collective-permute-done.7.refs_1_), channel_id=1, source_target_pairs={{0,2},{1,3},{2,4},{3,5},{4,6},{5,7},{8,10},{9,11},{10,12},{11,13},... | collective-permute-start | bytes 2359304 | tf_op jit(solution)/shard_map/ppermute | solution.py:357
  64.5 39.5 %collective-permute-start.22 = (bf16[256,1536]{1,0:T(8,128)(2,1)S(1)}, bf16[256,1536]{1,0:T(8,128)(2,1)}, u32[]{:S(2)}, u32[]{:S(2)}) collective-permute-start(bf16[256,1536]{1,0:T(8,128)(2,1)S(1)} %collective-permute-done.8.refs_4_), channel_id=1, source_target_pairs={{2,0},{3,1},{4,2},{5,3},{6,4},{7,5},{10,8},{11,9},{12,10},{13,11},... | collective-permute-start | bytes 2359304 | tf_op jit(solution)/shard_map/ppermute | solution.py:357
  66.6 24.7 %collective-permute-start.20 = (bf16[4,64,208]{2,1,0:T(8,128)(2,1)S(1)}, bf16[4,64,208]{2,1,0:T(8,128)(2,1)S(1)}, u32[]{:S(2)}, u32[]{:S(2)}) collective-permute-start(bf16[4,64,208]{2,1,0:T(8,128)(2,1)S(1)} %pad_maximum_fusion.6), channel_id=1, source_target_pairs={{0,4},{1,5},{2,6},{3,7},{4,0},{5,1},{6,2},{7,3},{8,12},{9,13},{10,... | collective-permute-start | bytes 319496 | tf_op jit(solution)/shard_map/ppermute | solution.py:403
  69.6 25.6 %collective-permute-start.16 = (bf16[2,64,1536]{2,1,0:T(8,128)(2,1)S(1)}, bf16[2,64,1536]{2,1,0:T(8,128)(2,1)S(1)}, u32[]{:S(2)}, u32[]{:S(2)}) collective-permute-start(bf16[2,64,1536]{2,1,0:T(8,128)(2,1)S(1)} %pad_maximum_fusion.3.refs_1_), channel_id=1, source_target_pairs={{0,16},{8,24},{16,0},{24,8},{1,17},{9,25},{17,1},{25,9},{2,18},{10... | collective-permute-start | bytes 1179656 | tf_op jit(solution)/shard_map/ppermute | solution.py:351
  91.3 12.7 %collective-permute-start.15 = (bf16[2,64,1536]{2,1,0:T(8,128)(2,1)S(1)}, bf16[2,64,1536]{2,1,0:T(8,128)(2,1)S(1)}, u32[]{:S(2)}, u32[]{:S(2)}) collective-permute-start(bf16[2,64,1536]{2,1,0:T(8,128)(2,1)S(1)} %pad_maximum_fusion.3.refs_1_), channel_id=1, source_target_pairs={{0,8},{8,0},{16,24},{24,16},{1,9},{9,1},{17,25},{25,17},{2,10},{10... | collective-permute-start | bytes 1179656 | tf_op jit(solution)/shard_map/ppermute | solution.py:351
  94.0 16.8 %collective-permute-start.25 = (bf16[2,64,1536]{2,1,0:T(8,128)(2,1)S(1)}, bf16[2,64,1536]{2,1,0:T(8,128)(2,1)S(1)}, u32[]{:S(2)}, u32[]{:S(2)}) collective-permute-start(bf16[2,64,1536]{2,1,0:T(8,128)(2,1)S(1)} %pad_maximum_fusion.4.refs_5_), channel_id=1, source_target_pairs={{0,24},{8,16},{16,8},{24,0},{1,25},{9,17},{17,9},{25,1},{2,26},{10... | collective-permute-start | bytes 1179656 | tf_op jit(solution)/shard_map/ppermute | solution.py:351
  95.2 17.9 %collective-permute-start.24 = (bf16[2,64,1536]{2,1,0:T(8,128)(2,1)S(1)}, bf16[2,64,1536]{2,1,0:T(8,128)(2,1)S(1)}, u32[]{:S(2)}, u32[]{:S(2)}) collective-permute-start(bf16[2,64,1536]{2,1,0:T(8,128)(2,1)S(1)} %pad_maximum_fusion.4.refs_5_), channel_id=1, source_target_pairs={{0,16},{8,24},{16,0},{24,8},{1,17},{9,25},{17,1},{25,9},{2,18},{10... | collective-permute-start | bytes 1179656 | tf_op jit(solution)/shard_map/ppermute | solution.py:351
  104.0 17.4 %collective-permute-start.26 = (bf16[256,1536]{1,0:T(8,128)(2,1)S(1)}, bf16[256,1536]{1,0:T(8,128)(2,1)S(1)}, u32[]{:S(2)}, u32[]{:S(2)}) collective-permute-start(bf16[256,1536]{1,0:T(8,128)(2,1)S(1)} %pad_maximum_fusion.refs_0_), channel_id=1, source_target_pairs={{0,1},{1,0},{2,3},{3,2},{4,5},{5,4},{6,7},{7,6},{8,9},{9,8},{10,11... | collective-permute-start | bytes 2359304 | tf_op jit(solution)/shard_map/ppermute | solution.py:354
  104.1 17.8 %collective-permute-start.27 = (bf16[256,1536]{1,0:T(8,128)(2,1)S(1)}, bf16[256,1536]{1,0:T(8,128)(2,1)S(1)}, u32[]{:S(2)}, u32[]{:S(2)}) collective-permute-start(bf16[256,1536]{1,0:T(8,128)(2,1)S(1)} %collective-permute-done.7.refs_1_), channel_id=1, source_target_pairs={{0,1},{1,0},{2,3},{3,2},{4,5},{5,4},{6,7},{7,6},{8,9},{9,8},{10,11... | collective-permute-start | bytes 2359304 | tf_op jit(solution)/shard_map/ppermute | solution.py:354
  104.6 18.9 %collective-permute-start.29 = (bf16[256,1536]{1,0:T(8,128)(2,1)}, bf16[256,1536]{1,0:T(8,128)(2,1)}, u32[]{:S(2)}, u32[]{:S(2)}) collective-permute-start(bf16[256,1536]{1,0:T(8,128)(2,1)} %collective-permute-done.21.refs_2_), channel_id=1, source_target_pairs={{0,2},{1,3},{2,4},{3,5},{4,6},{5,7},{8,10},{9,11},{10,12},{11,13},... | collective-permute-start | bytes 2359304 | tf_op jit(solution)/shard_map/ppermute | solution.py:357
  110.8 19.7 %collective-permute-start.33 = (bf16[256,1536]{1,0:T(8,128)(2,1)}, bf16[256,1536]{1,0:T(8,128)(2,1)}, u32[]{:S(2)}, u32[]{:S(2)}) collective-permute-start(bf16[256,1536]{1,0:T(8,128)(2,1)} %collective-permute-done.22.refs_5_), channel_id=1, source_target_pairs={{2,0},{3,1},{4,2},{5,3},{6,4},{7,5},{10,8},{11,9},{12,10},{13,11},... | collective-permute-start | bytes 2359304 | tf_op jit(solution)/shard_map/ppermute | solution.py:357
  121.4 30.5 %collective-permute-start.28 = (bf16[256,1536]{1,0:T(8,128)(2,1)}, bf16[256,1536]{1,0:T(8,128)(2,1)}, u32[]{:S(2)}, u32[]{:S(2)}) collective-permute-start(bf16[256,1536]{1,0:T(8,128)(2,1)} %collective-permute-done.21.refs_2_), channel_id=1, source_target_pairs={{0,1},{1,0},{2,3},{3,2},{4,5},{5,4},{6,7},{7,6},{8,9},{9,8},{10,11... | collective-permute-start | bytes 2359304 | tf_op jit(solution)/shard_map/ppermute | solution.py:354
  121.4 30.5 %collective-permute-start.32 = (bf16[256,1536]{1,0:T(8,128)(2,1)}, bf16[256,1536]{1,0:T(8,128)(2,1)S(1)}, u32[]{:S(2)}, u32[]{:S(2)}) collective-permute-start(bf16[256,1536]{1,0:T(8,128)(2,1)} %collective-permute-done.22.refs_5_), channel_id=1, source_target_pairs={{0,1},{1,0},{2,3},{3,2},{4,5},{5,4},{6,7},{7,6},{8,9},{9,8},{10,11... | collective-permute-start | bytes 2359304 | tf_op jit(solution)/shard_map/ppermute | solution.py:354
  121.9 29.9 %collective-permute-start.31 = (bf16[256,1536]{1,0:T(8,128)(2,1)S(1)}, bf16[256,1536]{1,0:T(8,128)(2,1)S(1)}, u32[]{:S(2)}, u32[]{:S(2)}) collective-permute-start(bf16[256,1536]{1,0:T(8,128)(2,1)S(1)} %collective-permute-done.8.refs_4_), channel_id=1, source_target_pairs={{0,1},{1,0},{2,3},{3,2},{4,5},{5,4},{6,7},{7,6},{8,9},{9,8},{10,11... | collective-permute-start | bytes 2359304 | tf_op jit(solution)/shard_map/ppermute | solution.py:354
  123.5 28.4 %collective-permute-start.30 = (bf16[256,1536]{1,0:T(8,128)(2,1)}, bf16[256,1536]{1,0:T(8,128)(2,1)}, u32[]{:S(2)}, u32[]{:S(2)}) collective-permute-start(bf16[256,1536]{1,0:T(8,128)(2,1)} %collective-permute-done.29.refs_3_), channel_id=1, source_target_pairs={{0,1},{1,0},{2,3},{3,2},{4,5},{5,4},{6,7},{7,6},{8,9},{9,8},{10,11... | collective-permute-start | bytes 2359304 | tf_op jit(solution)/shard_map/ppermute | solution.py:354
  130.5 21.4 %collective-permute-start.34 = (bf16[256,1536]{1,0:T(8,128)(2,1)}, bf16[256,1536]{1,0:T(8,128)(2,1)}, u32[]{:S(2)}, u32[]{:S(2)}) collective-permute-start(bf16[256,1536]{1,0:T(8,128)(2,1)} %collective-permute-done.33.refs_6_), channel_id=1, source_target_pairs={{0,1},{1,0},{2,3},{3,2},{4,5},{5,4},{6,7},{7,6},{8,9},{9,8},{10,11... | collective-permute-start | bytes 2359304 | tf_op jit(solution)/shard_map/ppermute | solution.py:354
  (33 other events, 777.7 us)

commit v6 on v5

--- a/solution.py
+++ b/solution.py
@@ -174,30 +174,35 @@
     return resid.astype(BF16), sdev.astype(BF16)
 
 
-def columns_kernel(rows, ratio, cols, groups, col_comps_ref, *refs):
-    coef_ref, piece_refs = refs[0], refs[1 : 1 + groups * rows]
-    coef_out, col_r, col_s, coef, raw_cols, sems = refs[1 + groups * rows :]
-    here = coef_ref.shape[1]
+def columns_kernel(rows, ratio, cols, col_comps_ref, *refs):
+    coef_refs, piece_refs = refs[:rows], refs[rows : 2 * rows]
+    coef_out, col_r, col_s, coef, raw_cols, sems = refs[2 * rows :]
+    here = coef_refs[0].shape[0] // ratio
     width = col_r.shape[1]
     r = lax.axis_index("rows")
     q = lax.axis_index("cols")
     copies = []
-    for d in range(cols):
-        place = pl.multiple_of((q ^ d) * here, here)
-        copies.append(
-            pltpu.make_async_copy(coef_ref.at[d], coef.at[pl.ds(place, here), :], sems.at[len(copies)])
-        )
+    for e in range(rows):
+        for k in range(ratio):
+            owner = ((q // ratio) ^ e) * ratio + lax.rem(q + ratio - k, ratio)
+            place = pl.multiple_of(owner * here, here)
+            copies.append(
+                pltpu.make_async_copy(
+                    coef_refs[e].at[k * here : (k + 1) * here, :],
+                    coef.at[pl.ds(place, here), :],
+                    sems.at[len(copies)],
+                )
+            )
     height = piece_refs[0].shape[1]
     for d in range(rows):
         begin = (r ^ d) * height
         k, part, inside = begin // (2 * here), lax.rem(begin // here, 2), lax.rem(begin, here)
-        found = [ref.at[i] for ref in piece_refs[d::rows] for i in range(ref.shape[0])]
-        for e, piece in enumerate(found):
+        for e in range(rows):
             owner = ((q // ratio) ^ e) * ratio + lax.rem(q + ratio - k, ratio)
             place = pl.multiple_of(owner * here + inside, height)
             copies.append(
                 pltpu.make_async_copy(
-                    piece, raw_cols.at[part, pl.ds(place, height), :], sems.at[len(copies)]
+                    piece_refs[d].at[e], raw_cols.at[part, pl.ds(place, height), :], sems.at[len(copies)]
                 )
             )
     for copy in copies:
@@ -217,11 +222,11 @@
 
 def columns_call(rows, ratio, cols, col_comps, coefs, pieces):
     comps, width = col_comps.shape
-    markers = coefs.shape[1] * cols
+    markers = coefs[0].shape[0] * rows
     anywhere = pl.BlockSpec(memory_space=pl.ANY)
     return pl.pallas_call(
-        functools.partial(columns_kernel, rows, ratio, cols, len(pieces) // rows),
-        in_specs=[pl.BlockSpec(memory_space=pltpu.VMEM)] + [anywhere] * (1 + len(pieces)),
+        functools.partial(columns_kernel, rows, ratio, cols),
+        in_specs=[pl.BlockSpec(memory_space=pltpu.VMEM)] + [anywhere] * (len(coefs) + len(pieces)),
         out_shape=(
             jax.ShapeDtypeStruct((markers, coef_rows(comps)), BF16),
             jax.ShapeDtypeStruct((markers, width), BF16),
@@ -234,7 +239,7 @@
         ],
         compiler_params=pltpu.CompilerParams(vmem_limit_bytes=VMEM_LIMIT),
         name="columns",
-    )(col_comps, coefs, *pieces)
+    )(col_comps, *coefs, *pieces)
 
 
 def quotient(numer, denom):
@@ -243,70 +248,56 @@
 
 
 def kin_kernel(rows, ratio, turn, start_ref, comps_ref, coef_ref, col_r, col_s, *refs):
-    own_ref = refs[0]
-    from_left, from_right = refs[1:rows], refs[rows : 2 * rows - 1]
-    out_ref, raw, sems = refs[-3:]
-    tile, width = out_ref.shape
-    here = own_ref.shape[0] // (2 * ratio)
-    plane = lax.axis_index("cols") // ratio
-    core = lax.rem(lax.axis_index("cols"), ratio)
-    step = pl.program_id(0)
-
-    def copies(block_ref, slot):
-        source = lax.rem(plane - slot + rows, rows)
-        for k in range(ratio):
-            owner = source * ratio + lax.rem(core + 2 * ratio - turn - k, ratio)
-            place = pl.multiple_of(owner * here, here)
-            for part in range(2):
-                begin = (2 * k + part) * here
-                yield pltpu.make_async_copy(
-                    block_ref.at[begin : begin + here, :],
-                    raw.at[part, pl.ds(place, here), :],
-                    sems.at[(slot * ratio + k) * 2 + part],
-                )
-
-    @pl.when(step == 0)
+    block_refs = refs[:rows]
+    out_ref, raw, row_r, row_s, sems = refs[-5:]
+    count = out_ref.shape[0]
+    here = block_refs[0].shape[0] // (2 * ratio)
+
+    @pl.when(pl.program_id(0) == 0)
     def _():
-        for copy in copies(own_ref, 0):
+        plane = lax.axis_index("cols") // ratio
+        core = lax.rem(lax.axis_index("cols"), ratio)
+        copies = []
+        for slot in range(rows):
+            source = lax.rem(plane - slot + rows, rows)
+            for k in range(ratio):
+                owner = source * ratio + lax.rem(core + 2 * ratio - turn - k, ratio)
+                place = pl.multiple_of(owner * here, here)
+                for part in range(2):
+                    begin = (2 * k + part) * here
+                    copies.append(
+                        pltpu.make_async_copy(
+                            block_refs[slot].at[begin : begin + here, :],
+                            raw.at[part, pl.ds(place, here), :],
+                            sems.at[len(copies)],
+                        )
+                    )
+        for copy in copies:
             copy.start()
-        for slot in range(1, rows):
-
-            @pl.when(plane >= slot)
-            def _():
-                for copy in copies(from_left[slot - 1], slot):
-                    copy.start()
-
-            @pl.when(plane < slot)
-            def _():
-                for copy in copies(from_right[rows - slot - 1], slot):
-                    copy.start()
-
-        for slot in range(rows):
-            for copy in copies(own_ref, slot):
-                copy.wait()
-
-    here_span = pl.ds(pl.multiple_of(step * tile, tile), tile)
-    resid, sdev = panel(coef_ref[...], comps_ref[...], raw[0, :, here_span], raw[1, :, here_span])
-    contract = (((0,), (0,)), ((), ()))
-    wide = 512 if width % 512 == 0 else width
-    for at in range(0, width, wide):
-        span = slice(at, at + wide)
-        numer = lax.dot_general(resid, col_r[:, span], contract, preferred_element_type=F32)
-        denom = lax.dot_general(sdev, col_s[:, span], contract, preferred_element_type=F32)
-        out_ref[:, span] = quotient(numer, denom)
-
-
-def kin_call(rows, ratio, turn, start, components, coef, col_r, col_s, blocks, before):
-    height, count = blocks[0].shape
+        for copy in copies:
+            copy.wait()
+        step = 256 if count % 256 == 0 else count
+        for at in range(0, count, step):
+            span = slice(at, at + step)
+            resid, sdev = panel(coef_ref[...], comps_ref[:, span], raw[0, :, span], raw[1, :, span])
+            row_r[span, :] = resid.T
+            row_s[span, :] = sdev.T
+
+    numer = jnp.dot(row_r[...], col_r[...], preferred_element_type=F32)
+    denom = jnp.dot(row_s[...], col_s[...], preferred_element_type=F32)
+    out_ref[...] = quotient(numer, denom)
+
+
+def kin_call(rows, ratio, turn, part, components, coef, col_r, col_s, blocks, before):
+    count = blocks[0].shape[1]
     comps, people = components.shape
     markers, width = col_r.shape
-    tile = 256 if count % 256 == 0 else count
-    whole = lambda i, at: (0, 0)
+    wide = 256 if width % 256 == 0 else width
     in_specs = [
-        pl.BlockSpec((comps, tile), lambda i, at: (0, i + at[0])),
-        pl.BlockSpec(coef.shape, whole),
-        pl.BlockSpec((markers, width), whole),
-        pl.BlockSpec((markers, width), whole),
+        pl.BlockSpec((comps, count), lambda i, at: (0, at[0])),
+        pl.BlockSpec(coef.shape, lambda i, at: (0, 0)),
+        pl.BlockSpec((markers, wide), lambda i, at: (0, i)),
+        pl.BlockSpec((markers, wide), lambda i, at: (0, i)),
     ] + [pl.BlockSpec(memory_space=pl.ANY)] * len(blocks)
     operands = [components, coef, col_r, col_s, *blocks]
     aliases = {}
@@ -318,11 +309,13 @@
         functools.partial(kin_kernel, rows, ratio, turn),
         grid_spec=pltpu.PrefetchScalarGridSpec(
             num_scalar_prefetch=1,
-            grid=(count // tile,),
+            grid=(width // wide,),
             in_specs=in_specs,
-            out_specs=pl.BlockSpec((tile, width), lambda i, at: (i + at[0], 0)),
+            out_specs=pl.BlockSpec((count, wide), lambda i, at: (at[0], i)),
             scratch_shapes=[
                 pltpu.VMEM((2, markers, count), BF16),
+                pltpu.VMEM((count, markers), BF16),
+                pltpu.VMEM((count, markers), BF16),
                 pltpu.SemaphoreType.DMA((rows * ratio * 2,)),
             ],
         ),
@@ -330,7 +323,7 @@
         input_output_aliases=aliases,
         compiler_params=pltpu.CompilerParams(vmem_limit_bytes=VMEM_LIMIT),
         name="kinship",
-    )((start // tile)[None].astype(jnp.int32), *operands)
+    )(part[None].astype(jnp.int32), *operands)
 
 
 def per_device(dosage, present, components):
@@ -372,48 +365,60 @@
         quarters.append(lax.ppermute(mine, "rows", [(i, i ^ d) for i in range(rows)]) if d else mine)
     gram = gram_call(dosage, present, components)
     col_comps = lax.dynamic_slice_in_dim(components, core * width, width, 1)
-    grams = across(gram, "rows", rows)
-    quarters, grams, col_comps, from_left[0], from_right[0] = lax.optimization_barrier(
-        (jnp.stack(quarters), grams, col_comps, from_left[0], from_right[0])
+    hops = [1 << i for i in range(rows.bit_length() - 1)]
+    first, later = hops[0], hops[1:]
+
+    def doubled(x, hop):
+        moves = [
+            (r * cols + z * ratio + c, (r ^ hop) * cols + z * ratio + c)
+            for z in range(rows)
+            for r in range(rows)
+            if (r ^ z) < hop
+            for c in range(ratio)
+        ]
+        return jnp.where((row ^ plane) < hop, x, lax.ppermute(x, ("rows", "cols"), moves))
+
+    quarters, gram, col_comps, from_left, from_right = lax.optimization_barrier(
+        (jnp.stack(quarters), gram, col_comps, from_left, from_right)
     )
     moved = []
     for e in range(rows):
         mine = lax.dynamic_index_in_dim(quarters, row ^ plane ^ e, 0, keepdims=False)
         moved.append(lax.ppermute(mine, "cols", pairs(lambda z, c: (z ^ e, c))) if e else mine)
-    coefs = solve_call(grams, comps, markers)[None]
-    sent = [
-        lax.ppermute(
-            col_comps,
-            ("rows", "cols"),
-            [(z * cols + z * ratio + c, (z ^ d) * cols + z * ratio + c) for z in range(rows) for c in range(ratio)],
-        )
-        for d in range(1, rows)
-    ]
-    moved, coefs, sent, held, from_left, from_right = lax.optimization_barrier(
-        (moved, coefs, sent, held, from_left, from_right)
+    for hop in hops[:-1]:
+        gram = gram + lax.ppermute(gram, "rows", [(i, i ^ hop) for i in range(rows)])
+    grams = [gram, lax.ppermute(gram, "rows", [(i, i ^ hops[-1]) for i in range(rows)])]
+    coef = solve_call(grams, comps, markers)
+    coef = jnp.concatenate([swap(coef, k) for k in range(ratio)], axis=0)
+    col_comps = doubled(col_comps, first)
+    moved, coef, col_comps, held, from_left, from_right = lax.optimization_barrier(
+        (jnp.stack(moved), coef, col_comps, held, from_left, from_right)
     )
-    pieces = []
+    coefs = [lax.ppermute(coef, "cols", pairs(lambda z, c: (z ^ e, c))) if e else coef for e in range(rows)]
+    coefs, from_left, from_right = lax.optimization_barrier((coefs, from_left, from_right))
+    for hop in later:
+        col_comps = doubled(col_comps, hop)
+    pieces = [moved]
     for step in range(rows - 2):
-        begin, end = rows * step // (rows - 2), rows * (step + 1) // (rows - 2)
-        pieces.append(across(jnp.stack(moved[begin:end]), "rows", rows))
         from_left.append(along(from_left[-1], 1))
         from_right.append(along(from_right[-1], -1))
-        hop = 1
-        while step == 0 and hop < cols:
-            other = lax.ppermute(coefs, "cols", [(i, i ^ hop) for i in range(cols)])
-            coefs = jnp.concatenate([coefs, other], axis=0)
-            hop *= 2
+        begin, end = (rows * step + rows - 3) // (rows - 2), (rows * (step + 1) + rows - 3) // (rows - 2)
+        for d in range(max(begin, 1), min(end, rows - 1) + 1 if step < rows - 3 else rows):
+            if d == len(pieces):
+                pieces.append(lax.ppermute(moved, "rows", [(i, i ^ d) for i in range(rows)]))
         if step < rows - 3:
-            pieces, coefs, held, from_left, from_right = lax.optimization_barrier(
-                (pieces, coefs, held, from_left, from_right)
+            pieces, col_comps, held, from_left, from_right = lax.optimization_barrier(
+                (pieces, col_comps, held, from_left, from_right)
             )
-    col_comps = sum(sent, jnp.where(row == plane, col_comps, 0.0))
-    coef, col_r, col_s = columns_call(rows, ratio, cols, col_comps, coefs, sum(pieces, []))
+    slots = [held]
+    for slot in range(1, rows):
+        slots.append(jnp.where(plane >= slot, from_left[slot - 1], from_right[rows - slot - 1]))
+    coef, col_r, col_s = columns_call(rows, ratio, cols, col_comps, coefs, pieces)
     out = None
     for turn in range(ratio):
-        start = (core + ratio - turn) % ratio * width
-        came = [swap(block, turn) for block in [held, *from_left, *from_right]]
-        out = kin_call(rows, ratio, turn, start, components, coef, col_r, col_s, came, out)
+        part = (core + ratio - turn) % ratio
+        came = [swap(block, turn) for block in slots]
+        out = kin_call(rows, ratio, turn, part, components, coef, col_r, col_s, came, out)
     return out
 
 

time: 167 us -> 143 us (0.86)
  waiting for transfers between devices: 57.4 us -> 40.9 us
  starting transfers between devices: 54.7 us -> 48.7 us
    ppermute x15 -> x10, waiting for transfers between devices: 47.9 us -> 14.7 us  [the longest x2 9.73 us: doubled(): lax.ppermute(x, ('rows', 'cols'), moves)]
    ppermute x6, waiting for transfers between devices: 8.15 us -> 20.8 us  [along(): return lax.ppermute(x, 'cols', pairs(lambda z, c: (z + way, c)))]
    ppermute x15 -> x10, starting transfers between devices: 30.1 us -> 21.4 us  [the longest x3 7.76 us: per_device(): lax.ppermute(moved, 'rows', [(i, i ^ d) for i in range(rows)])]
    select_n x0 -> x5, other arithmetic: none -> 3.25 us  [the longest x3 2.53 us: per_device(): jnp.where(plane >= slot, from_left[slot - 1], from_right[rows - slot - 1])]
    ppermute x6, starting transfers between devices: 14.8 us -> 18 us  [along(): return lax.ppermute(x, 'cols', pairs(lambda z, c: (z + way, c)))]
    ppermute x3, waiting for transfers between devices: 0.01 us -> 2.83 us  [per_device(): lax.ppermute(mine, 'rows', [(i, i ^ d) for i in range(rows)])]
    concatenate x3 -> x1, other arithmetic: 2.33 us -> 0.01 us  [per_device(): coef = jnp.concatenate([swap(coef, k) for k in range(ratio)], axis=0)]
    add x1, other arithmetic: 1.75 us -> 0.03 us  [per_device(): gram + lax.ppermute(gram, 'rows', [(i, i ^ hop) for i in range(rows)])]
  transfers between devices with their start and end apart: 35 -> 28, of which waited for: 12 -> 12; matrix products, arithmetic and copies ran while one was open for 2% -> 3% of each run, Pallas kernels for 19% -> 23%
where the time goes in v6:
time: 143 us
  starting transfers between devices  48.7 us (34%)
  Pallas kernels  45.7 us (32%)
  waiting for transfers between devices  40.9 us (29%)
  other arithmetic  5.89 us (4%)
    pallas_call x2, Pallas kernels, kin_call(): pl.pallas_call(functools.partial(kin_kernel, rows, ratio, turn), grid_spe...  26.4 us
    ppermute x6, waiting for transfers between devices, along(): return lax.ppermute(x, 'cols', pairs(lambda z, c: (z + way, c)))  20.8 us
    ppermute x6, starting transfers between devices, along(): return lax.ppermute(x, 'cols', pairs(lambda z, c: (z + way, c)))  18 us
    ppermute x2, waiting for transfers between devices, doubled(): lax.ppermute(x, ('rows', 'cols'), moves)  9.73 us
    ppermute x3, starting transfers between devices, per_device(): lax.ppermute(moved, 'rows', [(i, i ^ d) for i in range(rows)])  7.76 us
    pallas_call x1, Pallas kernels, solve_call(): pl.pallas_call(functools.partial(solve_kernel, comps, markers), out_shape...  7.13 us
    pallas_call x1, Pallas kernels, columns_call(): pl.pallas_call(functools.partial(columns_kernel, rows, ratio, cols), in_s...  6.47 us
    ppermute x2, starting transfers between devices, doubled(): lax.ppermute(x, ('rows', 'cols'), moves)  6.17 us
  transfers between devices with their start and end apart: 28, of which 12 were waited for; matrix products, arithmetic and copies ran while one was open for 3% of the time, Pallas kernels for 23%

profile of v6, /device:TPU:0, one launch (start us, length us, event | category | flops | bytes accessed | tf_op | source)
XLA Modules:
  0.0 142.6 jit_solution(6751572640898870130)
XLA Ops:
  4.9 5.5 %collective-permute-start.4 = (bf16[256,1536]{1,0:T(8,128)(2,1)S(1)}, bf16[256,1536]{1,0:T(8,128)(2,1)S(1)}, u32[]{:S(2)}, u32[]{:S(2)}) collective-permute-start(bf16[256,1536]{1,0:T(8,128)(2,1)S(1)} %pad_maximum_fusion.refs_0_), channel_id=1, source_target_pairs={{0,2},{1,3},{2,4},{3,5},{4,6},{5,7},{8,10},{9,11},{10,12},{11,13},... | collective-permute-start | bytes 2359304 | tf_op jit(solution)/shard_map/ppermute | solution.py:350
  10.5 2.9 %collective-permute-start.3 = (bf16[64,1536]{1,0:T(8,128)(2,1)S(1)}, bf16[64,1536]{1,0:T(8,128)(2,1)S(1)}, u32[]{:S(2)}, u32[]{:S(2)}) collective-permute-start(bf16[64,1536]{1,0:T(8,128)(2,1)S(1)} %get-tuple-element.74), channel_id=1, source_target_pairs={{0,24},{8,16},{16,8},{24,0},{1,25},{9,17},{17,9},{25,1},{2,26},{10... | collective-permute-start | bytes 589832 | tf_op jit(solution)/shard_map/ppermute | solution.py:365
  14.1 5.6 %gram.1 = f32[360,128]{1,0:T(8,128)} custom-call(s32[64,3072]{1,0:T(8,128)} %dosage_ref, s32[64,3072]{1,0:T(8,128)} %present_ref, f32[32,3072]{1,0:T(8,128)} %comps_ref.5), custom_call_target="tpu_custom_call" | custom-call | tf_op jit(solution)/shard_map/gram/pallas_call | solution.py:62
  19.8 2.6 %collective-permute-done.2 = bf16[64,1536]{1,0:T(8,128)(2,1)S(1)} collective-permute-done((bf16[64,1536]{1,0:T(8,128)(2,1)S(1)}, bf16[64,1536]{1,0:T(8,128)(2,1)S(1)}, u32[]{:S(2)}, u32[]{:S(2)}) %collective-permute-start.2) | collective-permute-done | bytes 196640 | tf_op jit(solution)/shard_map/ppermute | solution.py:365
  22.7 3.5 %collective-permute-done.5 = bf16[256,1536]{1,0:T(8,128)(2,1)S(1)} collective-permute-done((bf16[256,1536]{1,0:T(8,128)(2,1)S(1)}, bf16[256,1536]{1,0:T(8,128)(2,1)S(1)}, u32[]{:S(2)}, u32[]{:S(2)}) %collective-permute-start.5) | collective-permute-done | bytes 786464 | tf_op jit(solution)/shard_map/ppermute | solution.py:350
  27.4 1.6 %collective-permute-start.9 = (f32[360,128]{1,0:T(8,128)S(1)}, f32[360,128]{1,0:T(8,128)S(1)}, u32[]{:S(2)}, u32[]{:S(2)}) collective-permute-start(f32[360,128]{1,0:T(8,128)S(1)} %copy-done.8), channel_id=1, source_target_pairs={{0,8},{8,0},{16,24},{24,16},{1,9},{9,1},{17,25},{25,17},{2,10},{10... | collective-permute-start | bytes 552968 | tf_op jit(solution)/shard_map/ppermute | solution.py:389
  29.1 2.3 %collective-permute-start.12 = (f32[32,1536]{1,0:T(8,128)S(1)}, f32[32,1536]{1,0:T(8,128)S(1)}, u32[]{:S(2)}, u32[]{:S(2)}) collective-permute-start(f32[32,1536]{1,0:T(8,128)S(1)} %constant_dynamic-slice_fusion.1), channel_id=1, source_target_pairs={{0,8},{1,9},{10,2},{11,3},{20,28},{21,29},{30,22},{31,23}} | collective-permute-start | bytes 589832 | tf_op jit(solution)/shard_map/ppermute | solution.py:379
  31.4 3.0 %collective-permute-start.8 = (bf16[64,1536]{1,0:T(8,128)(2,1)S(1)}, bf16[64,1536]{1,0:T(8,128)(2,1)S(1)}, u32[]{:S(2)}, u32[]{:S(2)}) collective-permute-start(bf16[64,1536]{1,0:T(8,128)(2,1)S(1)} %get-tuple-element.70), channel_id=1, source_target_pairs={{0,6},{1,7},{2,4},{3,5},{4,2},{5,3},{6,0},{7,1},{8,14},{9,15},{10,... | collective-permute-start | bytes 589832 | tf_op jit(solution)/shard_map/ppermute | solution.py:387
  37.4 4.2 %collective-permute-done.10.refs_1_ = f32[360,128]{1,0:T(8,128)S(1)} collective-permute-done((f32[360,128]{1,0:T(8,128)S(1)}, f32[360,128]{1,0:T(8,128)S(1)}, u32[]{:S(2)}, u32[]{:S(2)}) %collective-permute-start.10) | collective-permute-done | bytes 184352 | tf_op jit(solution)/shard_map/ppermute | solution.py:390
  42.2 7.1 %solve.1 = bf16[64,208]{1,0:T(8,128)(2,1)} custom-call(f32[360,128]{1,0:T(8,128)} %copy-done.7, f32[360,128]{1,0:T(8,128)} %copy-done.10), custom_call_target="tpu_custom_call" | custom-call | tf_op jit(solution)/shard_map/solve/pallas_call | solution.py:151
  51.6 2.3 %collective-permute-start.18 = (bf16[128,208]{1,0:T(8,128)(2,1)S(1)}, bf16[128,208]{1,0:T(8,128)(2,1)S(1)}, u32[]{:S(2)}, u32[]{:S(2)}) collective-permute-start(bf16[128,208]{1,0:T(8,128)(2,1)S(1)} %pad_maximum_fusion.4.refs_0_), channel_id=1, source_target_pairs={{0,6},{1,7},{2,4},{3,5},{4,2},{5,3},{6,0},{7,1},{8,14},{9,15},{10,... | collective-permute-start | bytes 159752 | tf_op jit(solution)/shard_map/ppermute | solution.py:397
  53.9 2.1 %collective-permute-start.16 = (bf16[128,208]{1,0:T(8,128)(2,1)S(1)}, bf16[128,208]{1,0:T(8,128)(2,1)S(1)}, u32[]{:S(2)}, u32[]{:S(2)}) collective-permute-start(bf16[128,208]{1,0:T(8,128)(2,1)S(1)} %pad_maximum_fusion.4.refs_0_), channel_id=1, source_target_pairs={{0,2},{1,3},{2,0},{3,1},{4,6},{5,7},{6,4},{7,5},{8,10},{9,11},{10,... | collective-permute-start | bytes 159752 | tf_op jit(solution)/shard_map/ppermute | solution.py:397
  56.0 2.2 %collective-permute-start.14 = (bf16[4,64,1536]{2,1,0:T(8,128)(2,1)}, bf16[4,64,1536]{2,1,0:T(8,128)(2,1)}, u32[]{:S(2)}, u32[]{:S(2)}) collective-permute-start(bf16[4,64,1536]{2,1,0:T(8,128)(2,1)} %pad_maximum_fusion.2.refs_4_), channel_id=1, source_target_pairs={{0,16},{8,24},{16,0},{24,8},{1,17},{9,25},{17,1},{25,9},{2,18},{10... | collective-permute-start | bytes 2359304 | tf_op jit(solution)/shard_map/ppermute | solution.py:408
  60.0 3.7 %collective-permute-start.19 = (bf16[256,1536]{1,0:T(8,128)(2,1)S(1)}, bf16[256,1536]{1,0:T(8,128)(2,1)}, u32[]{:S(2)}, u32[]{:S(2)}) collective-permute-start(bf16[256,1536]{1,0:T(8,128)(2,1)S(1)} %collective-permute-done.4), channel_id=1, source_target_pairs={{0,2},{1,3},{2,4},{3,5},{4,6},{5,7},{8,10},{9,11},{10,12},{11,13},... | collective-permute-start | bytes 2359304 | tf_op jit(solution)/shard_map/ppermute | solution.py:350
  65.0 3.9 %collective-permute-start.15 = (f32[32,1536]{1,0:T(8,128)S(1)}, f32[32,1536]{1,0:T(8,128)S(1)}, u32[]{:S(2)}, u32[]{:S(2)}) collective-permute-start(f32[32,1536]{1,0:T(8,128)S(1)} %broadcast_select_fusion.4), channel_id=1, source_target_pairs={{0,16},{1,17},{8,24},{9,25},{2,18},{3,19},{10,26},{11,27},{20,4},{... | collective-permute-start | bytes 589832 | tf_op jit(solution)/shard_map/ppermute | solution.py:379
  68.9 9.7 %collective-permute-done.15 = f32[32,1536]{1,0:T(8,128)S(1)} collective-permute-done((f32[32,1536]{1,0:T(8,128)S(1)}, f32[32,1536]{1,0:T(8,128)S(1)}, u32[]{:S(2)}, u32[]{:S(2)}) %collective-permute-start.15) | collective-permute-done | bytes 196640 | tf_op jit(solution)/shard_map/ppermute | solution.py:379
  79.4 4.6 %collective-permute-done.20 = bf16[256,1536]{1,0:T(8,128)(2,1)} collective-permute-done((bf16[256,1536]{1,0:T(8,128)(2,1)S(1)}, bf16[256,1536]{1,0:T(8,128)(2,1)}, u32[]{:S(2)}, u32[]{:S(2)}) %collective-permute-start.20) | collective-permute-done | bytes 786464 | tf_op jit(solution)/shard_map/ppermute | solution.py:350
  85.2 4.6 %collective-permute-start.21 = (bf16[4,64,1536]{2,1,0:T(8,128)(2,1)}, bf16[4,64,1536]{2,1,0:T(8,128)(2,1)}, u32[]{:S(2)}, u32[]{:S(2)}) collective-permute-start(bf16[4,64,1536]{2,1,0:T(8,128)(2,1)} %pad_maximum_fusion.2.refs_4_), channel_id=1, source_target_pairs={{0,24},{8,16},{16,8},{24,0},{1,25},{9,17},{17,9},{25,1},{2,26},{10... | collective-permute-start | bytes 2359304 | tf_op jit(solution)/shard_map/ppermute | solution.py:408
  89.8 4.8 %collective-permute-start.26 = (bf16[256,1536]{1,0:T(8,128)(2,1)}, bf16[256,1536]{1,0:T(8,128)(2,1)S(1)}, u32[]{:S(2)}, u32[]{:S(2)}) collective-permute-start(bf16[256,1536]{1,0:T(8,128)(2,1)} %collective-permute-done.19), channel_id=1, source_target_pairs={{0,2},{1,3},{2,4},{3,5},{4,6},{5,7},{8,10},{9,11},{10,12},{11,13},... | collective-permute-start | bytes 2359304 | tf_op jit(solution)/shard_map/ppermute | solution.py:350
  96.4 7.0 %collective-permute-done.23 = bf16[256,1536]{1,0:T(8,128)(2,1)} collective-permute-done((bf16[256,1536]{1,0:T(8,128)(2,1)}, bf16[256,1536]{1,0:T(8,128)(2,1)}, u32[]{:S(2)}, u32[]{:S(2)}) %collective-permute-start.23) | collective-permute-done | bytes 786464 | tf_op jit(solution)/shard_map/ppermute | solution.py:350
  104.8 4.5 %collective-permute-done.26 = bf16[256,1536]{1,0:T(8,128)(2,1)S(1)} collective-permute-done((bf16[256,1536]{1,0:T(8,128)(2,1)}, bf16[256,1536]{1,0:T(8,128)(2,1)S(1)}, u32[]{:S(2)}, u32[]{:S(2)}) %collective-permute-start.26) | collective-permute-done | bytes 786464 | tf_op jit(solution)/shard_map/ppermute | solution.py:350
  109.5 6.5 %columns.1 = (bf16[512,208]{1,0:T(8,128)(2,1)}, bf16[512,1536]{1,0:T(8,128)(2,1)}, bf16[512,1536]{1,0:T(8,128)(2,1)}) custom-call(f32[32,1536]{1,0:T(8,128)} %broadcast_select_fusion.3.col_comps_ref, bf16[128,208]{1,0:T(8,128)(2,1)} %copy-done.9, bf16[128,208]{1,0:T(8,128)(2,1)} %copy-done.14, bf16[128,208]{1,0:T(8,128)(2,1)} %copy-done.13, ...), custom_call_target="tpu_custom_call" | custom-call | tf_op jit(solution)/shard_map/columns/pallas_call | solution.py:227
  116.0 13.2 %kinship.2.refs_4_ = f32[3072,1536]{1,0:T(8,128)} custom-call(s32[1]{0:T(128)} %bitcast.11.start_ref, f32[32,3072]{1,0:T(8,128)} %comps_ref.5, bf16[512,208]{1,0:T(8,128)(2,1)} %get-tuple-element.61.coef_ref, bf16[512,1536]{1,0:T(8,128)(2,1)} %get-tuple-element.62.col_r, bf16[512,1536]{1,0:T(8,128)(2,1)} %get-tuple-element.63.col_s, ...), custom_call_target="tpu_custom_call" | custom-call | tf_op jit(solution)/shard_map/kinship/pallas_call | solution.py:308
  129.3 13.2 %kinship.3 = f32[3072,1536]{1,0:T(8,128)} custom-call(s32[1]{0:T(128)} %bitcast.start_ref, f32[32,3072]{1,0:T(8,128)} %comps_ref.5, bf16[512,208]{1,0:T(8,128)(2,1)} %get-tuple-element.61.coef_ref, bf16[512,1536]{1,0:T(8,128)(2,1)} %get-tuple-element.62.col_r, bf16[512,1536]{1,0:T(8,128)(2,1)} %get-tuple-element.63.col_s, ...), custom_call_target="tpu_custom_call", output_to_operand_aliasing={{}: (9, {})} | custom-call | tf_op jit(solution)/shard_map/kinship/pallas_call | solution.py:308
  (82 shorter events, 21.2 us)
Async XLA Ops:
  3.4 22.8 %collective-permute-start.5 = (bf16[256,1536]{1,0:T(8,128)(2,1)S(1)}, bf16[256,1536]{1,0:T(8,128)(2,1)S(1)}, u32[]{:S(2)}, u32[]{:S(2)}) collective-permute-start(bf16[256,1536]{1,0:T(8,128)(2,1)S(1)} %pad_maximum_fusion.refs_0_), channel_id=1, source_target_pairs={{2,0},{3,1},{4,2},{5,3},{6,4},{7,5},{10,8},{11,9},{12,10},{13,11},... | collective-permute-start | bytes 2359304 | tf_op jit(solution)/shard_map/ppermute | solution.py:350
  4.9 22.6 %collective-permute-start.4 = (bf16[256,1536]{1,0:T(8,128)(2,1)S(1)}, bf16[256,1536]{1,0:T(8,128)(2,1)S(1)}, u32[]{:S(2)}, u32[]{:S(2)}) collective-permute-start(bf16[256,1536]{1,0:T(8,128)(2,1)S(1)} %pad_maximum_fusion.refs_0_), channel_id=1, source_target_pairs={{0,2},{1,3},{2,4},{3,5},{4,6},{5,7},{8,10},{9,11},{10,12},{11,13},... | collective-permute-start | bytes 2359304 | tf_op jit(solution)/shard_map/ppermute | solution.py:350
  10.5 9.3 %collective-permute-start.3 = (bf16[64,1536]{1,0:T(8,128)(2,1)S(1)}, bf16[64,1536]{1,0:T(8,128)(2,1)S(1)}, u32[]{:S(2)}, u32[]{:S(2)}) collective-permute-start(bf16[64,1536]{1,0:T(8,128)(2,1)S(1)} %get-tuple-element.74), channel_id=1, source_target_pairs={{0,24},{8,16},{16,8},{24,0},{1,25},{9,17},{17,9},{25,1},{2,26},{10... | collective-permute-start | bytes 589832 | tf_op jit(solution)/shard_map/ppermute | solution.py:365
  13.5 8.9 %collective-permute-start.2 = (bf16[64,1536]{1,0:T(8,128)(2,1)S(1)}, bf16[64,1536]{1,0:T(8,128)(2,1)S(1)}, u32[]{:S(2)}, u32[]{:S(2)}) collective-permute-start(bf16[64,1536]{1,0:T(8,128)(2,1)S(1)} %get-tuple-element.75), channel_id=1, source_target_pairs={{0,16},{8,24},{16,0},{24,8},{1,17},{9,25},{17,1},{25,9},{2,18},{10... | collective-permute-start | bytes 589832 | tf_op jit(solution)/shard_map/ppermute | solution.py:365
  14.0 8.6 %collective-permute-start.1 = (bf16[64,1536]{1,0:T(8,128)(2,1)S(1)}, bf16[64,1536]{1,0:T(8,128)(2,1)S(1)}, u32[]{:S(2)}, u32[]{:S(2)}) collective-permute-start(bf16[64,1536]{1,0:T(8,128)(2,1)S(1)} %get-tuple-element.76), channel_id=1, source_target_pairs={{0,8},{8,0},{16,24},{24,16},{1,9},{9,1},{17,25},{25,17},{2,10},{10... | collective-permute-start | bytes 589832 | tf_op jit(solution)/shard_map/ppermute | solution.py:365
  27.4 8.5 %collective-permute-start.9 = (f32[360,128]{1,0:T(8,128)S(1)}, f32[360,128]{1,0:T(8,128)S(1)}, u32[]{:S(2)}, u32[]{:S(2)}) collective-permute-start(f32[360,128]{1,0:T(8,128)S(1)} %copy-done.8), channel_id=1, source_target_pairs={{0,8},{8,0},{16,24},{24,16},{1,9},{9,1},{17,25},{25,17},{2,10},{10... | collective-permute-start | bytes 552968 | tf_op jit(solution)/shard_map/ppermute | solution.py:389
  29.1 8.3 %collective-permute-start.12 = (f32[32,1536]{1,0:T(8,128)S(1)}, f32[32,1536]{1,0:T(8,128)S(1)}, u32[]{:S(2)}, u32[]{:S(2)}) collective-permute-start(f32[32,1536]{1,0:T(8,128)S(1)} %constant_dynamic-slice_fusion.1), channel_id=1, source_target_pairs={{0,8},{1,9},{10,2},{11,3},{20,28},{21,29},{30,22},{31,23}} | collective-permute-start | bytes 589832 | tf_op jit(solution)/shard_map/ppermute | solution.py:379
  31.4 17.9 %collective-permute-start.8 = (bf16[64,1536]{1,0:T(8,128)(2,1)S(1)}, bf16[64,1536]{1,0:T(8,128)(2,1)S(1)}, u32[]{:S(2)}, u32[]{:S(2)}) collective-permute-start(bf16[64,1536]{1,0:T(8,128)(2,1)S(1)} %get-tuple-element.70), channel_id=1, source_target_pairs={{0,6},{1,7},{2,4},{3,5},{4,2},{5,3},{6,0},{7,1},{8,14},{9,15},{10,... | collective-permute-start | bytes 589832 | tf_op jit(solution)/shard_map/ppermute | solution.py:387
  34.4 16.1 %collective-permute-start.7 = (bf16[64,1536]{1,0:T(8,128)(2,1)S(1)}, bf16[64,1536]{1,0:T(8,128)(2,1)S(1)}, u32[]{:S(2)}, u32[]{:S(2)}) collective-permute-start(bf16[64,1536]{1,0:T(8,128)(2,1)S(1)} %get-tuple-element.71), channel_id=1, source_target_pairs={{0,4},{1,5},{2,6},{3,7},{4,0},{5,1},{6,2},{7,3},{8,12},{9,13},{10,... | collective-permute-start | bytes 589832 | tf_op jit(solution)/shard_map/ppermute | solution.py:387
  34.4 16.1 %collective-permute-start.6 = (bf16[64,1536]{1,0:T(8,128)(2,1)S(1)}, bf16[64,1536]{1,0:T(8,128)(2,1)S(1)}, u32[]{:S(2)}, u32[]{:S(2)}) collective-permute-start(bf16[64,1536]{1,0:T(8,128)(2,1)S(1)} %get-tuple-element.72), channel_id=1, source_target_pairs={{0,2},{1,3},{2,0},{3,1},{4,6},{5,7},{6,4},{7,5},{8,10},{9,11},{10,... | collective-permute-start | bytes 589832 | tf_op jit(solution)/shard_map/ppermute | solution.py:387
  51.6 7.6 %collective-permute-start.18 = (bf16[128,208]{1,0:T(8,128)(2,1)S(1)}, bf16[128,208]{1,0:T(8,128)(2,1)S(1)}, u32[]{:S(2)}, u32[]{:S(2)}) collective-permute-start(bf16[128,208]{1,0:T(8,128)(2,1)S(1)} %pad_maximum_fusion.4.refs_0_), channel_id=1, source_target_pairs={{0,6},{1,7},{2,4},{3,5},{4,2},{5,3},{6,0},{7,1},{8,14},{9,15},{10,... | collective-permute-start | bytes 159752 | tf_op jit(solution)/shard_map/ppermute | solution.py:397
  53.9 6.1 %collective-permute-start.16 = (bf16[128,208]{1,0:T(8,128)(2,1)S(1)}, bf16[128,208]{1,0:T(8,128)(2,1)S(1)}, u32[]{:S(2)}, u32[]{:S(2)}) collective-permute-start(bf16[128,208]{1,0:T(8,128)(2,1)S(1)} %pad_maximum_fusion.4.refs_0_), channel_id=1, source_target_pairs={{0,2},{1,3},{2,0},{3,1},{4,6},{5,7},{6,4},{7,5},{8,10},{9,11},{10,... | collective-permute-start | bytes 159752 | tf_op jit(solution)/shard_map/ppermute | solution.py:397
  56.0 23.3 %collective-permute-start.14 = (bf16[4,64,1536]{2,1,0:T(8,128)(2,1)}, bf16[4,64,1536]{2,1,0:T(8,128)(2,1)}, u32[]{:S(2)}, u32[]{:S(2)}) collective-permute-start(bf16[4,64,1536]{2,1,0:T(8,128)(2,1)} %pad_maximum_fusion.2.refs_4_), channel_id=1, source_target_pairs={{0,16},{8,24},{16,0},{24,8},{1,17},{9,25},{17,1},{25,9},{2,18},{10... | collective-permute-start | bytes 2359304 | tf_op jit(solution)/shard_map/ppermute | solution.py:408
  58.3 21.1 %collective-permute-start.13 = (bf16[4,64,1536]{2,1,0:T(8,128)(2,1)}, bf16[4,64,1536]{2,1,0:T(8,128)(2,1)}, u32[]{:S(2)}, u32[]{:S(2)}) collective-permute-start(bf16[4,64,1536]{2,1,0:T(8,128)(2,1)} %pad_maximum_fusion.2.refs_4_), channel_id=1, source_target_pairs={{0,8},{8,0},{16,24},{24,16},{1,9},{9,1},{17,25},{25,17},{2,10},{10... | collective-permute-start | bytes 2359304 | tf_op jit(solution)/shard_map/ppermute | solution.py:408
  60.0 19.4 %collective-permute-start.19 = (bf16[256,1536]{1,0:T(8,128)(2,1)S(1)}, bf16[256,1536]{1,0:T(8,128)(2,1)}, u32[]{:S(2)}, u32[]{:S(2)}) collective-permute-start(bf16[256,1536]{1,0:T(8,128)(2,1)S(1)} %collective-permute-done.4), channel_id=1, source_target_pairs={{0,2},{1,3},{2,4},{3,5},{4,6},{5,7},{8,10},{9,11},{10,12},{11,13},... | collective-permute-start | bytes 2359304 | tf_op jit(solution)/shard_map/ppermute | solution.py:350
  63.7 20.2 %collective-permute-start.20 = (bf16[256,1536]{1,0:T(8,128)(2,1)S(1)}, bf16[256,1536]{1,0:T(8,128)(2,1)}, u32[]{:S(2)}, u32[]{:S(2)}) collective-permute-start(bf16[256,1536]{1,0:T(8,128)(2,1)S(1)} %collective-permute-done.5), channel_id=1, source_target_pairs={{2,0},{3,1},{4,2},{5,3},{6,4},{7,5},{10,8},{11,9},{12,10},{13,11},... | collective-permute-start | bytes 2359304 | tf_op jit(solution)/shard_map/ppermute | solution.py:350
  65.0 13.6 %collective-permute-start.15 = (f32[32,1536]{1,0:T(8,128)S(1)}, f32[32,1536]{1,0:T(8,128)S(1)}, u32[]{:S(2)}, u32[]{:S(2)}) collective-permute-start(f32[32,1536]{1,0:T(8,128)S(1)} %broadcast_select_fusion.4), channel_id=1, source_target_pairs={{0,16},{1,17},{8,24},{9,25},{2,18},{3,19},{10,26},{11,27},{20,4},{... | collective-permute-start | bytes 589832 | tf_op jit(solution)/shard_map/ppermute | solution.py:379
  83.9 19.5 %collective-permute-start.23 = (bf16[256,1536]{1,0:T(8,128)(2,1)}, bf16[256,1536]{1,0:T(8,128)(2,1)}, u32[]{:S(2)}, u32[]{:S(2)}) collective-permute-start(bf16[256,1536]{1,0:T(8,128)(2,1)} %collective-permute-done.20), channel_id=1, source_target_pairs={{2,0},{3,1},{4,2},{5,3},{6,4},{7,5},{10,8},{11,9},{12,10},{13,11},... | collective-permute-start | bytes 2359304 | tf_op jit(solution)/shard_map/ppermute | solution.py:350
  85.2 24.3 %collective-permute-start.21 = (bf16[4,64,1536]{2,1,0:T(8,128)(2,1)}, bf16[4,64,1536]{2,1,0:T(8,128)(2,1)}, u32[]{:S(2)}, u32[]{:S(2)}) collective-permute-start(bf16[4,64,1536]{2,1,0:T(8,128)(2,1)} %pad_maximum_fusion.2.refs_4_), channel_id=1, source_target_pairs={{0,24},{8,16},{16,8},{24,0},{1,25},{9,17},{17,9},{25,1},{2,26},{10... | collective-permute-start | bytes 2359304 | tf_op jit(solution)/shard_map/ppermute | solution.py:408
  89.8 19.5 %collective-permute-start.26 = (bf16[256,1536]{1,0:T(8,128)(2,1)}, bf16[256,1536]{1,0:T(8,128)(2,1)S(1)}, u32[]{:S(2)}, u32[]{:S(2)}) collective-permute-start(bf16[256,1536]{1,0:T(8,128)(2,1)} %collective-permute-done.19), channel_id=1, source_target_pairs={{0,2},{1,3},{2,4},{3,5},{4,6},{5,7},{8,10},{9,11},{10,12},{11,13},... | collective-permute-start | bytes 2359304 | tf_op jit(solution)/shard_map/ppermute | solution.py:350
  95.8 33.4 %collective-permute-start.25 = (bf16[256,1536]{1,0:T(8,128)(2,1)S(1)}, bf16[256,1536]{1,0:T(8,128)(2,1)}, u32[]{:S(2)}, u32[]{:S(2)}) collective-permute-start(bf16[256,1536]{1,0:T(8,128)(2,1)S(1)} %broadcast_select_fusion.1.refs_2_), channel_id=1, source_target_pairs={{0,1},{1,0},{2,3},{3,2},{4,5},{5,4},{6,7},{7,6},{8,9},{9,8},{10,11... | collective-permute-start | bytes 2359304 | tf_op jit(solution)/shard_map/ppermute | solution.py:347
  95.9 33.3 %collective-permute-start.22 = (bf16[256,1536]{1,0:T(8,128)(2,1)S(1)}, bf16[256,1536]{1,0:T(8,128)(2,1)}, u32[]{:S(2)}, u32[]{:S(2)}) collective-permute-start(bf16[256,1536]{1,0:T(8,128)(2,1)S(1)} %pad_maximum_fusion.refs_0_), channel_id=1, source_target_pairs={{0,1},{1,0},{2,3},{3,2},{4,5},{5,4},{6,7},{7,6},{8,9},{9,8},{10,11... | collective-permute-start | bytes 2359304 | tf_op jit(solution)/shard_map/ppermute | solution.py:347
  104.7 24.5 %collective-permute-start.24 = (bf16[256,1536]{1,0:T(8,128)(2,1)S(1)}, bf16[256,1536]{1,0:T(8,128)(2,1)}, u32[]{:S(2)}, u32[]{:S(2)}) collective-permute-start(bf16[256,1536]{1,0:T(8,128)(2,1)S(1)} %broadcast_select_fusion.2.refs_1_), channel_id=1, source_target_pairs={{0,1},{1,0},{2,3},{3,2},{4,5},{5,4},{6,7},{7,6},{8,9},{9,8},{10,11... | collective-permute-start | bytes 2359304 | tf_op jit(solution)/shard_map/ppermute | solution.py:347
  109.4 19.9 %collective-permute-start.27 = (bf16[256,1536]{1,0:T(8,128)(2,1)S(1)}, bf16[256,1536]{1,0:T(8,128)(2,1)}, u32[]{:S(2)}, u32[]{:S(2)}) collective-permute-start(bf16[256,1536]{1,0:T(8,128)(2,1)S(1)} %broadcast_select_fusion.refs_3_), channel_id=1, source_target_pairs={{0,1},{1,0},{2,3},{3,2},{4,5},{5,4},{6,7},{7,6},{8,9},{9,8},{10,11... | collective-permute-start | bytes 2359304 | tf_op jit(solution)/shard_map/ppermute | solution.py:347
  (19 other events, 405.4 us)

commit v7 on v1

--- a/solution.py
+++ b/solution.py
@@ -132,7 +132,8 @@
         value = value - jnp.sum(total_term, axis=0, keepdims=True)
         g = j // SUB
         groups[g] = jnp.where(index == j - first, value, groups[g])
-    coef = jnp.concatenate(groups, axis=0)
+    coef = 2.0 * jnp.concatenate(groups, axis=0)
+    last = 2.0 * last
     c1, c2, c3 = [part.astype(F32) for part in split3(coef)]
     l1, l2, l3 = [part.astype(F32) for part in split3(last)]
     index = lax.broadcasted_iota(jnp.int32, (2 * SUB, markers), 0)
@@ -161,94 +162,239 @@
     return jnp.concatenate([d1, d2, d1, d2, d3, d1, ones], axis=0)
 
 
-def panel(coef, x, dosage, present):
-    fitted = lax.dot_general(
-        coef, design_parts(x), (((1,), (0,)), ((), ())), preferred_element_type=F32
-    )
-    freq = jnp.clip(fitted, 0.01, 0.99)
-    observed = present.astype(F32)
-    resid = observed * (dosage.astype(F32) - 2.0 * freq)
-    sdev = observed * jnp.sqrt(freq * (1.0 - freq))
-    return resid.astype(BF16), (2.0 * sdev).astype(BF16)
-
-
-def kin_kernel(rows, ratio, cols, raw_ref, comps_ref, col_comps_ref, *refs):
-    coef_refs = refs[:cols]
-    piece_refs = refs[cols : cols + rows * ratio]
-    out_ref, coef, raw_cols, col_r, col_s, sems = refs[cols + rows * ratio :]
-    here = coef_refs[0].shape[0]
-    width = out_ref.shape[1]
+def factors(twice):
+    twice = jnp.clip(twice, 0.02, 1.98)
+    spread = twice * (2.0 - twice)
+    return twice, spread * lax.rsqrt(spread)
+
+
+def weigh(fitted, dosage, observed):
+    twice, spread = factors(fitted)
+    return (observed * (dosage - twice)).astype(BF16), (observed * spread).astype(BF16)
+
+
+def parted(block, groups):
+    block = block.astype(F32)
+    height = block.shape[0] // (2 * groups)
+    dosage = [block[2 * g * height : (2 * g + 1) * height] for g in range(groups)]
+    present = [block[(2 * g + 1) * height : (2 * g + 2) * height] for g in range(groups)]
+    if groups == 1:
+        return dosage[0], present[0]
+    return jnp.concatenate(dosage, axis=0), jnp.concatenate(present, axis=0)
+
+
+def early_source(plane, rows):
+    return jnp.where(plane == 0, 1, plane - 1)
+
+
+def late_source(plane, rows):
+    return jnp.where(plane == 0, rows - 1, jnp.where(plane == rows - 1, 0, plane + 1))
+
+
+def slot_of(source, plane, rows):
+    slot = lax.rem(plane - source + rows, rows) - 1
+    slot = jnp.where(source == early_source(plane, rows), rows - 2, slot)
+    slot = jnp.where(source == late_source(plane, rows), rows - 1, slot)
+    return jnp.where(source == plane, 0, slot)
+
+
+def early_kernel(rows, near, row_x_ref, col_x_ref, *refs):
+    coef_refs, refs = refs[: rows.bit_length()], refs[rows.bit_length() :]
+    held_ref, refs = refs[0], refs[1:]
+    from_left, from_right = refs[: rows - 2], refs[rows - 2 : 2 * rows - 4]
+    piece_refs, refs = refs[2 * rows - 4 : 2 * rows - 4 + near], refs[2 * rows - 4 + near :]
+    row_out, col_out, row_fit, col_fit, coef, fit = refs
+    chip = coef_refs[0].shape[0]
+    height = chip // rows
+    space = coef.shape[0] // rows
+    row = lax.axis_index("rows")
+    plane = lax.axis_index("cols") // (lax.axis_size("cols") // rows)
+    slots = [slot_of(plane ^ e, plane, rows) for e in range(rows)]
 
     @pl.when(pl.program_id(0) == 0)
     def _():
-        r = lax.axis_index("rows")
-        q = lax.axis_index("cols")
-        copies = []
-        for d in range(cols):
-            place = pl.multiple_of((q ^ d) * here, here)
-            copies.append(
-                pltpu.make_async_copy(coef_refs[d], coef.at[pl.ds(place, here), :], sems.at[len(copies)])
-            )
-        for d in range(rows):
-            for k in range(ratio):
-                owner = (r ^ d) * ratio + lax.rem(lax.rem(q, ratio) + ratio - k, ratio)
-                place = pl.multiple_of(owner * here, here)
-                copies.append(
-                    pltpu.make_async_copy(
-                        piece_refs[d * ratio + k],
-                        raw_cols.at[:, pl.ds(place, here), :],
-                        sems.at[len(copies)],
-                    )
-                )
-        for copy in copies:
-            copy.start()
-        for copy in copies:
-            copy.wait()
-        step = 256 if width % 256 == 0 else width
-        for at in range(0, width, step):
-            span = slice(at, at + step)
-            resid, sdev = panel(
-                coef[...], col_comps_ref[:, span], raw_cols[0, :, span], raw_cols[1, :, span]
-            )
-            col_r[:, span] = resid
-            col_s[:, span] = sdev
-
-    resid, sdev = panel(coef[...], comps_ref[...], raw_ref[0], raw_ref[1])
-    contract = (((0,), (0,)), ((), ()))
-    step = 512 if width % 512 == 0 else width
-    for at in range(0, width, step):
-        span = slice(at, at + step)
-        numer = lax.dot_general(resid, col_r[:, span], contract, preferred_element_type=F32)
-        denom = lax.dot_general(sdev, col_s[:, span], contract, preferred_element_type=F32)
-        out_ref[:, span] = numer / denom
-
-
-def kin_call(rows, ratio, cols, raw, components, col_comps, coefs, pieces):
-    _, markers, people = raw.shape
+        if space != chip:
+            coef[...] = jnp.zeros(coef.shape, BF16)
+        found = [ref[at : at + chip, :] for ref in coef_refs for at in range(0, ref.shape[0], chip)]
+        for e in range(rows):
+            coef[pl.ds(pl.multiple_of(slots[e] * space, space), chip), :] = found[e]
+
+    def fitted(x):
+        return lax.dot_general(
+            coef[...], design_parts(x), (((1,), (0,)), ((), ())), preferred_element_type=F32
+        )
+
+    if space != chip:
+        row_out[...] = jnp.zeros(row_out.shape, BF16)
+        col_out[...] = jnp.zeros(col_out.shape, BF16)
+    fit_rows = fitted(row_x_ref[...])
+    for slot in range(rows - 1):
+        if slot == 0:
+            block = held_ref[...]
+        elif slot == rows - 2:
+            block = jnp.where(plane == 0, from_right[0][...], from_left[0][...])
+        else:
+            away = slot + 1
+            block = jnp.where(plane >= away, from_left[away - 1][...], from_right[rows - away - 1][...])
+        resid, sdev = weigh(fit_rows[slot * space : slot * space + chip], *parted(block, rows))
+        row_out[0, :, slot * space : slot * space + chip] = resid.T
+        row_out[1, :, slot * space : slot * space + chip] = sdev.T
+    row_fit[...] = fit_rows[(rows - 1) * space : (rows - 1) * space + chip]
+    fit[...] = fitted(col_x_ref[...])
+    for d in range(rows):
+        for e in range(rows):
+            place = pl.multiple_of(slots[e] * space + (row ^ d) * height, height)
+            here = fit[pl.ds(place, height), :]
+            if d < near:
+                resid, sdev = weigh(here, *parted(piece_refs[d][e], 1))
+                group = slots[e] * (space // height) + (row ^ d)
+                col_out[0, group] = resid
+                col_out[1, group] = sdev
+            else:
+                col_fit[e] = here
+
+
+def early_call(rows, part, components, col_comps, coefs, held, from_left, from_right, pieces):
     comps, width = col_comps.shape
-    tile = 512 if people % 512 == 0 else people
+    chip = coefs[0].shape[0]
+    space = -(-chip // 128) * 128
+    height = chip // rows
+    wide = 256 if width % 256 == 0 else width
+    whole = lambda i, at: (0, 0)
+    block = pl.BlockSpec((2 * chip, wide), lambda i, at: (0, i))
+    piece = pl.BlockSpec((rows, 2 * height, wide), lambda i, at: (0, 0, i))
+    return pl.pallas_call(
+        functools.partial(early_kernel_at, rows, len(pieces)),
+        grid_spec=pltpu.PrefetchScalarGridSpec(
+            num_scalar_prefetch=1,
+            grid=(width // wide,),
+            in_specs=[
+                pl.BlockSpec((comps, wide), lambda i, at: (0, at[0] * (width // wide) + i)),
+                pl.BlockSpec((comps, wide), lambda i, at: (0, i)),
+            ]
+            + [pl.BlockSpec(x.shape, whole) for x in coefs]
+            + [block] * (1 + len(from_left) + len(from_right))
+            + [piece] * len(pieces),
+            out_specs=(
+                pl.BlockSpec((2, wide, rows * space), lambda i, at: (0, i, 0)),
+                pl.BlockSpec((2, rows * space // height, height, wide), lambda i, at: (0, 0, 0, i)),
+                pl.BlockSpec((chip, wide), lambda i, at: (0, i)),
+                pl.BlockSpec((rows, height, wide), lambda i, at: (0, 0, i)),
+            ),
+            scratch_shapes=[
+                pltpu.VMEM((rows * space, coefs[0].shape[1]), BF16),
+                pltpu.VMEM((rows * space, wide), F32),
+            ],
+        ),
+        out_shape=(
+            jax.ShapeDtypeStruct((2, width, rows * space), BF16),
+            jax.ShapeDtypeStruct((2, rows * space // height, height, width), BF16),
+            jax.ShapeDtypeStruct((chip, width), F32),
+            jax.ShapeDtypeStruct((rows, height, width), F32),
+        ),
+        compiler_params=pltpu.CompilerParams(vmem_limit_bytes=VMEM_LIMIT),
+        name="early",
+    )(part[None].astype(jnp.int32), components, col_comps, *coefs, held, *from_left, *from_right, *pieces)
+
+
+def early_kernel_at(rows, near, part_ref, *refs):
+    early_kernel(rows, near, *refs)
+
+
+def late_kernel(rows, group_ref, row_fit, col_fit, left_ref, right_ref, next_ref, piece_ref, *refs):
+    row_out, col_out = refs[2:]
+    plane = lax.axis_index("cols") // (lax.axis_size("cols") // rows)
+    resid, sdev = weigh(col_fit[0], *parted(piece_ref[0], 1))
+    col_out[0, 0] = resid
+    col_out[1, 0] = sdev
+
+    @pl.when(pl.program_id(0) == 0)
+    def _():
+        block = jnp.where(plane == rows - 1, left_ref[...], next_ref[...])
+        block = jnp.where(plane == 0, right_ref[...], block)
+        resid, sdev = weigh(row_fit[...], *parted(block, rows))
+        chip = row_fit.shape[0]
+        if row_out.shape[2] != chip:
+            row_out[...] = jnp.zeros(row_out.shape, BF16)
+        row_out[0, :, 0:chip] = resid.T
+        row_out[1, :, 0:chip] = sdev.T
+
+
+def late_call(rows, groups, row_fit, col_fit, left, right, following, piece, row_panel, col_panel):
+    chip, width = row_fit.shape
+    height = chip // rows
+    space = row_panel.shape[2] // rows
+    whole = pl.BlockSpec((2 * chip, width), lambda e, at: (0, 0))
     anywhere = pl.BlockSpec(memory_space=pl.ANY)
     return pl.pallas_call(
-        functools.partial(kin_kernel, rows, ratio, cols),
-        grid=(people // tile,),
-        in_specs=[
-            pl.BlockSpec((2, markers, tile), lambda i: (0, 0, i)),
-            pl.BlockSpec((comps, tile), lambda i: (0, i)),
-            pl.BlockSpec((comps, width), lambda i: (0, 0)),
-        ]
-        + [anywhere] * (len(coefs) + len(pieces)),
-        out_specs=pl.BlockSpec((tile, width), lambda i: (i, 0)),
+        functools.partial(late_kernel, rows),
+        grid_spec=pltpu.PrefetchScalarGridSpec(
+            num_scalar_prefetch=1,
+            grid=(rows,),
+            in_specs=[
+                pl.BlockSpec((chip, width), lambda e, at: (0, 0)),
+                pl.BlockSpec((1, height, width), lambda e, at: (e, 0, 0)),
+                whole,
+                whole,
+                whole,
+                pl.BlockSpec((1, 2 * height, width), lambda e, at: (e, 0, 0)),
+                anywhere,
+                anywhere,
+            ],
+            out_specs=(
+                pl.BlockSpec((2, width, space), lambda e, at: (0, 0, rows - 1)),
+                pl.BlockSpec((2, 1, height, width), lambda e, at: (0, at[e], 0, 0)),
+            ),
+        ),
+        out_shape=(
+            jax.ShapeDtypeStruct(row_panel.shape, BF16),
+            jax.ShapeDtypeStruct(col_panel.shape, BF16),
+        ),
+        input_output_aliases={7: 0, 8: 1},
+        compiler_params=pltpu.CompilerParams(vmem_limit_bytes=VMEM_LIMIT),
+        name="late",
+    )(groups, row_fit, col_fit, left, right, following, piece, row_panel, col_panel)
+
+
+def quotient(numer, denom):
+    inverse = pl.reciprocal(denom, approx=True)
+    return numer * (inverse * (2.0 - denom * inverse))
+
+
+def kin_kernel(part_ref, row_ref, col_ref, *refs):
+    out_ref = refs[-1]
+    numer = jnp.dot(row_ref[0], col_ref[0], preferred_element_type=F32)
+    denom = jnp.dot(row_ref[1], col_ref[1], preferred_element_type=F32)
+    out_ref[...] = quotient(numer, denom)
+
+
+def kin_call(part, people, row_panel, col_panel, before):
+    _, count, depth = row_panel.shape
+    width = col_panel.shape[2]
+    wide = 256 if width % 256 == 0 else width
+    in_specs = [
+        pl.BlockSpec((2, count, depth), lambda i, at: (0, 0, 0)),
+        pl.BlockSpec((2, depth, wide), lambda i, at: (0, 0, i)),
+    ]
+    operands = [row_panel, col_panel]
+    aliases = {}
+    if before is not None:
+        in_specs.append(pl.BlockSpec(memory_space=pl.ANY))
+        operands.append(before)
+        aliases = {len(operands): 0}
+    return pl.pallas_call(
+        kin_kernel,
+        grid_spec=pltpu.PrefetchScalarGridSpec(
+            num_scalar_prefetch=1,
+            grid=(width // wide,),
+            in_specs=in_specs,
+            out_specs=pl.BlockSpec((count, wide), lambda i, at: (at[0], i)),
+        ),
         out_shape=jax.ShapeDtypeStruct((people, width), F32),
-        scratch_shapes=[
-            pltpu.VMEM((markers, coef_rows(comps)), BF16),
-            pltpu.VMEM((2, markers, width), BF16),
-            pltpu.VMEM((markers, width), BF16),
-            pltpu.VMEM((markers, width), BF16),
-            pltpu.SemaphoreType.DMA((len(coefs) + len(pieces),)),
-        ],
+        input_output_aliases=aliases,
         compiler_params=pltpu.CompilerParams(vmem_limit_bytes=VMEM_LIMIT),
         name="kinship",
-    )(raw, components, col_comps, *coefs, *pieces)
+    )(part[None].astype(jnp.int32), *operands)
 
 
 def per_device(dosage, present, components):
@@ -257,35 +403,111 @@
     markers, people = dosage.shape
     comps = components.shape[0]
     width = people // ratio
+    row = lax.axis_index("rows")
     col = lax.axis_index("cols")
-    raw = jnp.stack([dosage.astype(BF16), present.astype(BF16)])
-    raw_rows = lax.all_gather(raw, "cols", axis=1, tiled=True)
-
-    def across(x, axis, size):
-        return [x] + [lax.ppermute(x, axis, [(i, i ^ d) for i in range(size)]) for d in range(1, size)]
-
-    both = ("rows", "cols")
-    pieces = []
+    core, plane = col % ratio, col // ratio
+
+    def pairs(hop):
+        moves = [(z, c, *hop(z, c)) for z in range(rows) for c in range(ratio)]
+        return [(z * ratio + c, y * ratio + b) for z, c, y, b in moves if 0 <= y < rows]
+
+    def swap(x, k):
+        return lax.ppermute(x, "cols", pairs(lambda z, c: (z, (c + k) % ratio))) if k else x
+
+    def along(x, way):
+        return lax.ppermute(x, "cols", pairs(lambda z, c: (z + way, c)))
+
+    def beside(x, d):
+        return lax.ppermute(x, "rows", [(i, i ^ d) for i in range(rows)]) if d else x
+
+    def across(x, e):
+        return lax.ppermute(x, "cols", pairs(lambda z, c: (z ^ e, c))) if e else x
+
+    def by_core(parts):
+        placed = []
+        for p in range(ratio):
+            chosen = parts[0]
+            for k in range(1, ratio):
+                chosen = jnp.where((core - p) % ratio == k, parts[k], chosen)
+            placed.append(chosen)
+        return jnp.concatenate(placed, axis=0)
+
+    subs = rows // ratio
+    fine = markers // subs
+    halves = []
     for k in range(ratio):
-        part = (col % ratio + k) % ratio
-        mine = lax.dynamic_slice_in_dim(raw, part * width, width, 2)
+        begin = (core + k) % ratio * width
+        both = [
+            lax.dynamic_slice_in_dim(x, begin, width, 1).astype(BF16).reshape(subs, 1, fine, width)
+            for x in (dosage, present)
+        ]
+        halves.append(swap(jnp.concatenate(both, axis=1).reshape(2 * markers, width), k))
+    held = by_core(halves)
+    held, dosage, present = lax.optimization_barrier((held, dosage, present))
+    from_left, from_right = [along(held, 1)], [along(held, -1)]
+
+    height = held.shape[0] // rows
+    quarters = [beside(lax.dynamic_slice_in_dim(held, (row ^ d) * height, height, 0), d) for d in range(rows)]
+    hops = [1 << i for i in range(rows.bit_length() - 1)]
+    gram = gram_call(dosage, present, components)
+    for hop in hops[:-1]:
+        gram = gram + beside(gram, hop)
+    grams = [gram, beside(gram, hops[-1])]
+    col_comps = lax.dynamic_slice_in_dim(components, core * width, width, 1)
+    quarters, grams, col_comps, from_left, from_right = lax.optimization_barrier(
+        (jnp.stack(quarters), grams, col_comps, from_left, from_right)
+    )
+    moved = [
+        across(lax.dynamic_index_in_dim(quarters, row ^ plane ^ e, 0, keepdims=False), e) for e in range(rows)
+    ]
+    def doubled(x, hop):
         moves = [
-            (r * cols + z * ratio + c, z * cols + r * ratio + (c + k) % ratio)
+            (r * cols + z * ratio + c, (r ^ hop) * cols + z * ratio + c)
+            for z in range(rows)
             for r in range(rows)
-            for z in range(rows)
+            if (r ^ z) < hop
             for c in range(ratio)
         ]
-        pieces.append(lax.ppermute(mine, both, moves) if len(moves) > 1 else mine)
-        if k == 0:
-            mine = lax.dynamic_slice_in_dim(components, part * width, width, 1)
-            col_comps = lax.ppermute(mine, both, moves) if len(moves) > 1 else mine
-    spread = [across(piece, "rows", rows) for piece in pieces]
-    pieces = [spread[k][d] for d in range(rows) for k in range(ratio)]
-
-    gram = gram_call(dosage, present, components)
-    coef = solve_call(across(gram, "rows", rows), comps, markers)
-    coefs = across(coef, "cols", cols)
-    return kin_call(rows, ratio, cols, raw_rows, components, col_comps, coefs, pieces)
+        return jnp.where((row ^ plane) < hop, x, lax.ppermute(x, ("rows", "cols"), moves))
+
+    for hop in hops:
+        col_comps = doubled(col_comps, hop)
+    coef = solve_call(grams, comps, markers)
+    moved, coef, col_comps, held, from_left, from_right = lax.optimization_barrier(
+        (jnp.stack(moved), coef, col_comps, held, from_left, from_right)
+    )
+    coefs = [by_core([swap(coef, k) for k in range(ratio)])]
+    for hop in hops:
+        coefs.append(across(coefs[0] if len(coefs) == 1 else jnp.concatenate(coefs, axis=0), hop))
+    near = [moved]
+    for step in range(rows - 3):
+        from_left.append(along(from_left[-1], 1))
+        from_right.append(along(from_right[-1], -1))
+        upto = rows - 1 if step == rows - 4 else min(rows - 1, 2 * step + 3)
+        near += [beside(moved, d) for d in range(len(near), upto)]
+        near, coefs, col_comps, held, from_left, from_right = lax.optimization_barrier(
+            (near, coefs, col_comps, held, from_left, from_right)
+        )
+    last_left, last_right = along(from_left[-1], 1), along(from_right[-1], -1)
+    far = beside(near[0], rows - 1)
+    row_panel, col_panel, row_fit, col_fit = early_call(
+        rows, core, components, col_comps, coefs, held, from_left, from_right, near
+    )
+    space = row_panel.shape[2] // rows
+    groups = jnp.stack(
+        [
+            slot_of(plane ^ e, plane, rows) * (2 * space // height) + (row ^ (rows - 1))
+            for e in range(rows)
+        ]
+    ).astype(jnp.int32)
+    row_panel, col_panel = late_call(
+        rows, groups, row_fit, col_fit, last_left, last_right, from_right[0], far, row_panel, col_panel
+    )
+    col_panel = col_panel.reshape(2, rows * space, width)
+    out = None
+    for turn in range(ratio):
+        out = kin_call((core + ratio - turn) % ratio, people, swap(row_panel, turn), col_panel, out)
+    return out
 
 
 def solution(mesh):

time: 191 us -> 135 us (0.71)
  starting transfers between devices: 104 us -> 42.3 us
  Pallas kernels: 34.7 us -> 49.4 us
  between operations: 13.6 us -> 0.38 us
  other arithmetic: 2.48 us -> 4.97 us
    ppermute x19 -> x24, starting transfers between devices: 104 us -> 42.3 us  [the longest x6 15 us: along(): return lax.ppermute(x, 'cols', pairs(lambda z, c: (z + way, c)))]
    pallas_call x1 -> x4, Pallas kernels: 21.8 us -> 36.6 us  [the longest x2 20.7 us: kin_call(): pl.pallas_call(kin_kernel, grid_spec=pltpu.PrefetchScalarGridSpec(num_sca...]
    ppermute x19 -> x24, waiting for transfers between devices: 33.4 us -> 35 us  [the longest x5 15 us: across(): return lax.ppermute(x, 'cols', pairs(lambda z, c: (z ^ e, c))) if e else x]
  transfers between devices with their start and end apart: 20 -> 24, of which waited for: 8 -> 13; matrix products, arithmetic and copies ran while one was open for 1% -> 2% of each run, Pallas kernels for 7% -> 25%
where the time goes in v7:
time: 135 us; the launch traced here: 134 us
  Pallas kernels  49.4 us (37%)
  starting transfers between devices  42.3 us (31%)
  waiting for transfers between devices  35 us (26%)
  other arithmetic  4.97 us (4%)
  local copies, waits for them, and re-layouts  1.83 us (1%)
    pallas_call x2, Pallas kernels, kin_call(): pl.pallas_call(kin_kernel, grid_spec=pltpu.PrefetchScalarGridSpec(num_sca...  20.7 us
    ppermute x5, waiting for transfers between devices, across(): return lax.ppermute(x, 'cols', pairs(lambda z, c: (z ^ e, c))) if e else x  15 us
    ppermute x6, starting transfers between devices, along(): return lax.ppermute(x, 'cols', pairs(lambda z, c: (z + way, c)))  15 us
    ppermute x8, waiting for transfers between devices, beside(): lax.ppermute(x, 'rows', [(i, i ^ d) for i in range(rows)])  14 us
    ppermute x5, starting transfers between devices, across(): return lax.ppermute(x, 'cols', pairs(lambda z, c: (z ^ e, c))) if e else x  11.9 us
    ppermute x8, starting transfers between devices, beside(): lax.ppermute(x, 'rows', [(i, i ^ d) for i in range(rows)])  10.2 us
    pallas_call x1, Pallas kernels, early_call(): pl.pallas_call(functools.partial(early_kernel_at, rows, len(pieces)), gri...  9.72 us
    pallas_call x1, Pallas kernels, solve_call(): pl.pallas_call(functools.partial(solve_kernel, comps, markers), out_shape...  7.14 us
  transfers between devices with their start and end apart: 24, of which 13 were waited for; matrix products, arithmetic and copies ran while one was open for 2% of the time, Pallas kernels for 25%

profile of v7, /device:TPU:0, one launch (start us, length us, event | category | flops | bytes accessed | tf_op | source)
XLA Modules:
  0.0 133.8 jit_solution(12638454411827606138)
XLA Ops:
  4.8 5.5 %collective-permute-start.6 = (bf16[256,1536]{1,0:T(8,128)(2,1)S(1)}, bf16[256,1536]{1,0:T(8,128)(2,1)S(1)}, u32[]{:S(2)}, u32[]{:S(2)}) collective-permute-start(bf16[256,1536]{1,0:T(8,128)(2,1)S(1)} %pad_maximum_fusion.refs_5_), channel_id=1, source_target_pairs={{0,2},{1,3},{2,4},{3,5},{4,6},{5,7},{8,10},{9,11},{10,12},{11,13},... | collective-permute-start | bytes 2359304 | tf_op jit(solution)/shard_map/ppermute | solution.py:418
  10.4 5.6 %gram.1 = f32[360,128]{1,0:T(8,128)} custom-call(s32[64,3072]{1,0:T(8,128)} %dosage_ref, s32[64,3072]{1,0:T(8,128)} %present_ref, f32[32,3072]{1,0:T(8,128)} %refs_0_.1), custom_call_target="tpu_custom_call" | custom-call | tf_op jit(solution)/shard_map/gram/pallas_call | solution.py:62
  16.1 1.9 %collective-permute-start.4 = (f32[360,128]{1,0:T(8,128)}, f32[360,128]{1,0:T(8,128)S(1)}, u32[]{:S(2)}, u32[]{:S(2)}) collective-permute-start(f32[360,128]{1,0:T(8,128)} %gram.1), channel_id=1, source_target_pairs={{0,8},{8,0},{16,24},{24,16},{1,9},{9,1},{17,25},{25,17},{2,10},{10... | collective-permute-start | bytes 552968 | tf_op jit(solution)/shard_map/ppermute | solution.py:421
  19.7 4.1 %collective-permute-done.4 = f32[360,128]{1,0:T(8,128)S(1)} collective-permute-done((f32[360,128]{1,0:T(8,128)}, f32[360,128]{1,0:T(8,128)S(1)}, u32[]{:S(2)}, u32[]{:S(2)}) %collective-permute-start.4) | collective-permute-done | bytes 184352 | tf_op jit(solution)/shard_map/ppermute | solution.py:421
  23.8 2.0 %collective-permute-start.1 = (bf16[64,1536]{1,0:T(8,128)(2,1)S(1)}, bf16[64,1536]{1,0:T(8,128)(2,1)S(1)}, u32[]{:S(2)}, u32[]{:S(2)}) collective-permute-start(bf16[64,1536]{1,0:T(8,128)(2,1)S(1)} %get-tuple-element.78), channel_id=1, source_target_pairs={{0,8},{8,0},{16,24},{24,16},{1,9},{9,1},{17,25},{25,17},{2,10},{10... | collective-permute-start | bytes 589832 | tf_op jit(solution)/shard_map/ppermute | solution.py:421
  26.8 2.7 %collective-permute-done.3 = bf16[64,1536]{1,0:T(8,128)(2,1)S(1)} collective-permute-done((bf16[64,1536]{1,0:T(8,128)(2,1)S(1)}, bf16[64,1536]{1,0:T(8,128)(2,1)S(1)}, u32[]{:S(2)}, u32[]{:S(2)}) %collective-permute-start.3) | collective-permute-done | bytes 196640 | tf_op jit(solution)/shard_map/ppermute | solution.py:421
  31.3 3.8 %collective-permute-done.5.refs_1_ = f32[360,128]{1,0:T(8,128)S(1)} collective-permute-done((f32[360,128]{1,0:T(8,128)S(1)}, f32[360,128]{1,0:T(8,128)S(1)}, u32[]{:S(2)}, u32[]{:S(2)}) %collective-permute-start.5) | collective-permute-done | bytes 184352 | tf_op jit(solution)/shard_map/ppermute | solution.py:421
  35.1 3.4 %collective-permute-start.11 = (f32[32,1536]{1,0:T(8,128)S(1)}, f32[32,1536]{1,0:T(8,128)S(1)}, u32[]{:S(2)}, u32[]{:S(2)}) collective-permute-start(f32[32,1536]{1,0:T(8,128)S(1)} %constant_dynamic-slice_fusion.1), channel_id=1, source_target_pairs={{0,8},{1,9},{10,2},{11,3},{20,28},{21,29},{30,22},{31,23}} | collective-permute-start | bytes 589832 | tf_op jit(solution)/shard_map/ppermute | solution.py:471
  39.5 3.5 %collective-permute-start.8 = (bf16[64,1536]{1,0:T(8,128)(2,1)S(1)}, bf16[64,1536]{1,0:T(8,128)(2,1)S(1)}, u32[]{:S(2)}, u32[]{:S(2)}) collective-permute-start(bf16[64,1536]{1,0:T(8,128)(2,1)S(1)} %get-tuple-element.74), channel_id=1, source_target_pairs={{0,2},{1,3},{2,0},{3,1},{4,6},{5,7},{6,4},{7,5},{8,10},{9,11},{10,... | collective-permute-start | bytes 589832 | tf_op jit(solution)/shard_map/ppermute | solution.py:424
  43.0 7.1 %solve.1 = bf16[64,208]{1,0:T(8,128)(2,1)} custom-call(f32[360,128]{1,0:T(8,128)} %copy-done.9, f32[360,128]{1,0:T(8,128)} %copy-done.12), custom_call_target="tpu_custom_call" | custom-call | tf_op jit(solution)/shard_map/solve/pallas_call | solution.py:151
  51.5 1.9 %collective-permute-done.9 = bf16[64,1536]{1,0:T(8,128)(2,1)S(1)} collective-permute-done((bf16[64,1536]{1,0:T(8,128)(2,1)S(1)}, bf16[64,1536]{1,0:T(8,128)(2,1)S(1)}, u32[]{:S(2)}, u32[]{:S(2)}) %collective-permute-start.9) | collective-permute-done | bytes 196640 | tf_op jit(solution)/shard_map/ppermute | solution.py:424
  55.4 3.4 %collective-permute-start.18 = (bf16[256,1536]{1,0:T(8,128)(2,1)S(1)}, bf16[256,1536]{1,0:T(8,128)(2,1)S(1)}, u32[]{:S(2)}, u32[]{:S(2)}) collective-permute-start(bf16[256,1536]{1,0:T(8,128)(2,1)S(1)} %collective-permute-done.6.refs_6_), channel_id=1, source_target_pairs={{0,2},{1,3},{2,4},{3,5},{4,6},{5,7},{8,10},{9,11},{10,12},{11,13},... | collective-permute-start | bytes 2359304 | tf_op jit(solution)/shard_map/ppermute | solution.py:418
  60.0 2.5 %collective-permute-start.14 = (bf16[4,64,1536]{2,1,0:T(8,128)(2,1)S(1)}, bf16[4,64,1536]{2,1,0:T(8,128)(2,1)S(1)}, u32[]{:S(2)}, u32[]{:S(2)}) collective-permute-start(bf16[4,64,1536]{2,1,0:T(8,128)(2,1)S(1)} %pad_maximum_fusion.2.refs_10_), channel_id=1, source_target_pairs={{0,16},{8,24},{16,0},{24,8},{1,17},{9,25},{17,1},{25,9},{2,18},{10... | collective-permute-start | bytes 2359304 | tf_op jit(solution)/shard_map/ppermute | solution.py:421
  64.8 2.7 %collective-permute-start.16 = (bf16[128,208]{1,0:T(8,128)(2,1)S(1)}, bf16[128,208]{1,0:T(8,128)(2,1)S(1)}, u32[]{:S(2)}, u32[]{:S(2)}) collective-permute-start(bf16[128,208]{1,0:T(8,128)(2,1)S(1)} %pad_maximum_fusion.6.refs_2_), channel_id=1, source_target_pairs={{0,2},{1,3},{2,0},{3,1},{4,6},{5,7},{6,4},{7,5},{8,10},{9,11},{10,... | collective-permute-start | bytes 159752 | tf_op jit(solution)/shard_map/ppermute | solution.py:424
  67.5 9.2 %collective-permute-done.16.refs_3_ = bf16[128,208]{1,0:T(8,128)(2,1)S(1)} collective-permute-done((bf16[128,208]{1,0:T(8,128)(2,1)S(1)}, bf16[128,208]{1,0:T(8,128)(2,1)S(1)}, u32[]{:S(2)}, u32[]{:S(2)}) %collective-permute-start.16) | collective-permute-done | bytes 53280 | tf_op jit(solution)/shard_map/ppermute | solution.py:424
  76.7 4.7 %collective-permute-start.17 = (bf16[256,208]{1,0:T(8,128)(2,1)S(1)}, bf16[256,208]{1,0:T(8,128)(2,1)S(1)}, u32[]{:S(2)}, u32[]{:S(2)}) collective-permute-start(bf16[256,208]{1,0:T(8,128)(2,1)S(1)} %pad_maximum_fusion.5), channel_id=1, source_target_pairs={{0,4},{1,5},{2,6},{3,7},{4,0},{5,1},{6,2},{7,3},{8,12},{9,13},{10,... | collective-permute-start | bytes 319496 | tf_op jit(solution)/shard_map/ppermute | solution.py:424
  81.5 3.9 %collective-permute-done.17.refs_4_ = bf16[256,208]{1,0:T(8,128)(2,1)S(1)} collective-permute-done((bf16[256,208]{1,0:T(8,128)(2,1)S(1)}, bf16[256,208]{1,0:T(8,128)(2,1)S(1)}, u32[]{:S(2)}, u32[]{:S(2)}) %collective-permute-start.17) | collective-permute-done | bytes 106528 | tf_op jit(solution)/shard_map/ppermute | solution.py:424
  85.5 2.2 %collective-permute-start.20 = (bf16[256,1536]{1,0:T(8,128)(2,1)S(1)}, bf16[256,1536]{1,0:T(8,128)(2,1)}, u32[]{:S(2)}, u32[]{:S(2)}) collective-permute-start(bf16[256,1536]{1,0:T(8,128)(2,1)S(1)} %collective-permute-done.18.refs_7_), channel_id=1, source_target_pairs={{0,2},{1,3},{2,4},{3,5},{4,6},{5,7},{8,10},{9,11},{10,12},{11,13},... | collective-permute-start | bytes 2359304 | tf_op jit(solution)/shard_map/ppermute | solution.py:418
  89.0 2.1 %collective-permute-start.22 = (bf16[4,64,1536]{2,1,0:T(8,128)(2,1)S(1)}, bf16[4,64,1536]{2,1,0:T(8,128)(2,1)}, u32[]{:S(2)}, u32[]{:S(2)}) collective-permute-start(bf16[4,64,1536]{2,1,0:T(8,128)(2,1)S(1)} %pad_maximum_fusion.2.refs_10_), channel_id=1, source_target_pairs={{0,24},{8,16},{16,8},{24,0},{1,25},{9,17},{17,9},{25,1},{2,26},{10... | collective-permute-start | bytes 2359304 | tf_op jit(solution)/shard_map/ppermute | solution.py:421
  91.7 9.7 %early.1 = (bf16[2,1536,512]{2,1,0:T(8,128)(2,1)}, bf16[2,16,32,1536]{3,2,1,0:T(8,128)(2,1)}, f32[128,1536]{1,0:T(8,128)}, f32[4,32,1536]{2,1,0:T(8,128)}) custom-call(s32[1]{0:T(128)} %bitcast.5.part_ref, f32[32,3072]{1,0:T(8,128)} %refs_0_.1, f32[32,1536]{1,0:T(8,128)} %broadcast_select_fusion.1.refs_1_, bf16[128,208]{1,0:T(8,128)(2,1)} %copy-done.10, ...), custom_call_target="tpu_custom_call" | custom-call | tf_op jit(solution)/shard_map/early/pallas_call | solution.py:266
  101.4 2.1 %collective-permute-done.21.right_ref = bf16[256,1536]{1,0:T(8,128)(2,1)} collective-permute-done((bf16[256,1536]{1,0:T(8,128)(2,1)}, bf16[256,1536]{1,0:T(8,128)(2,1)}, u32[]{:S(2)}, u32[]{:S(2)}) %collective-permute-start.21) | collective-permute-done | bytes 786464 | tf_op jit(solution)/shard_map/ppermute | solution.py:418
  105.3 6.2 %late.1 = (bf16[2,1536,512]{2,1,0:T(8,128)(2,1)}, bf16[2,16,32,1536]{3,2,1,0:T(8,128)(2,1)}) custom-call(s32[4]{0:T(128)} %pad_add_fusion.group_ref, f32[128,1536]{1,0:T(8,128)} %get-tuple-element.65.row_fit, f32[4,32,1536]{2,1,0:T(8,128)} %get-tuple-element.66.col_fit, ...), custom_call_target="tpu_custom_call", output_to_operand_aliasing={{0}: (7, {}), {1}: (8, {})} | custom-call | tf_op jit(solution)/shard_map/late/pallas_call | solution.py:329
  111.5 10.4 %kinship.2.refs_0_ = f32[3072,1536]{1,0:T(8,128)} custom-call(s32[1]{0:T(128)} %bitcast.27.part_ref, bf16[2,1536,512]{2,1,0:T(8,128)(2,1)} %get-tuple-element.69.row_ref, bf16[2,512,1536]{2,1,0:T(8,128)(2,1)} %bitcast.38), custom_call_target="tpu_custom_call" | custom-call | tf_op jit(solution)/shard_map/kinship/pallas_call | solution.py:385
  123.5 10.3 %kinship.3 = f32[3072,1536]{1,0:T(8,128)} custom-call(s32[1]{0:T(128)} %bitcast.part_ref, bf16[2,1536,512]{2,1,0:T(8,128)(2,1)} %copy-done.1, bf16[2,512,1536]{2,1,0:T(8,128)(2,1)} %bitcast.39, f32[3072,1536]{1,0:T(8,128)} %kinship.2.refs_0_), custom_call_target="tpu_custom_call", output_to_operand_aliasing={{}: (3, {})} | custom-call | tf_op jit(solution)/shard_map/kinship/pallas_call | solution.py:385
  (75 shorter events, 22.4 us)
Async XLA Ops:
  1.5 1.9 %collective-permute-start = (bf16[128,1536]{1,0:T(8,128)(2,1)S(1)}, bf16[128,1536]{1,0:T(8,128)(2,1)S(1)}, u32[]{:S(2)}, u32[]{:S(2)}) collective-permute-start(bf16[128,1536]{1,0:T(8,128)(2,1)S(1)} %bitcast.44), channel_id=1, source_target_pairs={{0,1},{1,0},{2,3},{3,2},{4,5},{5,4},{6,7},{7,6},{8,9},{9,8},{10,11... | collective-permute-start | bytes 1179656 | tf_op jit(solution)/shard_map/ppermute | solution.py:415
  3.5 31.5 %collective-permute-start.7 = (bf16[256,1536]{1,0:T(8,128)(2,1)S(1)}, bf16[256,1536]{1,0:T(8,128)(2,1)S(1)}, u32[]{:S(2)}, u32[]{:S(2)}) collective-permute-start(bf16[256,1536]{1,0:T(8,128)(2,1)S(1)} %pad_maximum_fusion.refs_5_), channel_id=1, source_target_pairs={{2,0},{3,1},{4,2},{5,3},{6,4},{7,5},{10,8},{11,9},{12,10},{13,11},... | collective-permute-start | bytes 2359304 | tf_op jit(solution)/shard_map/ppermute | solution.py:418
  4.8 30.2 %collective-permute-start.6 = (bf16[256,1536]{1,0:T(8,128)(2,1)S(1)}, bf16[256,1536]{1,0:T(8,128)(2,1)S(1)}, u32[]{:S(2)}, u32[]{:S(2)}) collective-permute-start(bf16[256,1536]{1,0:T(8,128)(2,1)S(1)} %pad_maximum_fusion.refs_5_), channel_id=1, source_target_pairs={{0,2},{1,3},{2,4},{3,5},{4,6},{5,7},{8,10},{9,11},{10,12},{11,13},... | collective-permute-start | bytes 2359304 | tf_op jit(solution)/shard_map/ppermute | solution.py:418
  16.1 7.7 %collective-permute-start.4 = (f32[360,128]{1,0:T(8,128)}, f32[360,128]{1,0:T(8,128)S(1)}, u32[]{:S(2)}, u32[]{:S(2)}) collective-permute-start(f32[360,128]{1,0:T(8,128)} %gram.1), channel_id=1, source_target_pairs={{0,8},{8,0},{16,24},{24,16},{1,9},{9,1},{17,25},{25,17},{2,10},{10... | collective-permute-start | bytes 552968 | tf_op jit(solution)/shard_map/ppermute | solution.py:421
  18.1 11.4 %collective-permute-start.3 = (bf16[64,1536]{1,0:T(8,128)(2,1)S(1)}, bf16[64,1536]{1,0:T(8,128)(2,1)S(1)}, u32[]{:S(2)}, u32[]{:S(2)}) collective-permute-start(bf16[64,1536]{1,0:T(8,128)(2,1)S(1)} %get-tuple-element.76), channel_id=1, source_target_pairs={{0,24},{8,16},{16,8},{24,0},{1,25},{9,17},{17,9},{25,1},{2,26},{10... | collective-permute-start | bytes 589832 | tf_op jit(solution)/shard_map/ppermute | solution.py:421
  19.6 10.2 %collective-permute-start.2 = (bf16[64,1536]{1,0:T(8,128)(2,1)S(1)}, bf16[64,1536]{1,0:T(8,128)(2,1)S(1)}, u32[]{:S(2)}, u32[]{:S(2)}) collective-permute-start(bf16[64,1536]{1,0:T(8,128)(2,1)S(1)} %get-tuple-element.77), channel_id=1, source_target_pairs={{0,16},{8,24},{16,0},{24,8},{1,17},{9,25},{17,1},{25,9},{2,18},{10... | collective-permute-start | bytes 589832 | tf_op jit(solution)/shard_map/ppermute | solution.py:421
  23.8 7.3 %collective-permute-start.1 = (bf16[64,1536]{1,0:T(8,128)(2,1)S(1)}, bf16[64,1536]{1,0:T(8,128)(2,1)S(1)}, u32[]{:S(2)}, u32[]{:S(2)}) collective-permute-start(bf16[64,1536]{1,0:T(8,128)(2,1)S(1)} %get-tuple-element.78), channel_id=1, source_target_pairs={{0,8},{8,0},{16,24},{24,16},{1,9},{9,1},{17,25},{25,17},{2,10},{10... | collective-permute-start | bytes 589832 | tf_op jit(solution)/shard_map/ppermute | solution.py:421
  29.5 5.5 %collective-permute-start.5 = (f32[360,128]{1,0:T(8,128)S(1)}, f32[360,128]{1,0:T(8,128)S(1)}, u32[]{:S(2)}, u32[]{:S(2)}) collective-permute-start(f32[360,128]{1,0:T(8,128)S(1)} %add.115.refs_0_), channel_id=1, source_target_pairs={{0,16},{8,24},{16,0},{24,8},{1,17},{9,25},{17,1},{25,9},{2,18},{10... | collective-permute-start | bytes 552968 | tf_op jit(solution)/shard_map/ppermute | solution.py:421
  35.1 15.1 %collective-permute-start.11 = (f32[32,1536]{1,0:T(8,128)S(1)}, f32[32,1536]{1,0:T(8,128)S(1)}, u32[]{:S(2)}, u32[]{:S(2)}) collective-permute-start(f32[32,1536]{1,0:T(8,128)S(1)} %constant_dynamic-slice_fusion.1), channel_id=1, source_target_pairs={{0,8},{1,9},{10,2},{11,3},{20,28},{21,29},{30,22},{31,23}} | collective-permute-start | bytes 589832 | tf_op jit(solution)/shard_map/ppermute | solution.py:471
  38.6 12.9 %collective-permute-start.10 = (bf16[64,1536]{1,0:T(8,128)(2,1)S(1)}, bf16[64,1536]{1,0:T(8,128)(2,1)S(1)}, u32[]{:S(2)}, u32[]{:S(2)}) collective-permute-start(bf16[64,1536]{1,0:T(8,128)(2,1)S(1)} %get-tuple-element.72), channel_id=1, source_target_pairs={{0,6},{1,7},{2,4},{3,5},{4,2},{5,3},{6,0},{7,1},{8,14},{9,15},{10,... | collective-permute-start | bytes 589832 | tf_op jit(solution)/shard_map/ppermute | solution.py:424
  38.6 14.7 %collective-permute-start.9 = (bf16[64,1536]{1,0:T(8,128)(2,1)S(1)}, bf16[64,1536]{1,0:T(8,128)(2,1)S(1)}, u32[]{:S(2)}, u32[]{:S(2)}) collective-permute-start(bf16[64,1536]{1,0:T(8,128)(2,1)S(1)} %get-tuple-element.73), channel_id=1, source_target_pairs={{0,4},{1,5},{2,6},{3,7},{4,0},{5,1},{6,2},{7,3},{8,12},{9,13},{10,... | collective-permute-start | bytes 589832 | tf_op jit(solution)/shard_map/ppermute | solution.py:424
  39.5 13.9 %collective-permute-start.8 = (bf16[64,1536]{1,0:T(8,128)(2,1)S(1)}, bf16[64,1536]{1,0:T(8,128)(2,1)S(1)}, u32[]{:S(2)}, u32[]{:S(2)}) collective-permute-start(bf16[64,1536]{1,0:T(8,128)(2,1)S(1)} %get-tuple-element.74), channel_id=1, source_target_pairs={{0,2},{1,3},{2,0},{3,1},{4,6},{5,7},{6,4},{7,5},{8,10},{9,11},{10,... | collective-permute-start | bytes 589832 | tf_op jit(solution)/shard_map/ppermute | solution.py:424
  50.2 4.5 %collective-permute-start.12 = (f32[32,1536]{1,0:T(8,128)S(1)}, f32[32,1536]{1,0:T(8,128)S(1)}, u32[]{:S(2)}, u32[]{:S(2)}) collective-permute-start(f32[32,1536]{1,0:T(8,128)S(1)} %broadcast_select_fusion), channel_id=1, source_target_pairs={{0,16},{1,17},{8,24},{9,25},{2,18},{3,19},{10,26},{11,27},{20,4},{... | collective-permute-start | bytes 589832 | tf_op jit(solution)/shard_map/ppermute | solution.py:471
  55.4 30.1 %collective-permute-start.18 = (bf16[256,1536]{1,0:T(8,128)(2,1)S(1)}, bf16[256,1536]{1,0:T(8,128)(2,1)S(1)}, u32[]{:S(2)}, u32[]{:S(2)}) collective-permute-start(bf16[256,1536]{1,0:T(8,128)(2,1)S(1)} %collective-permute-done.6.refs_6_), channel_id=1, source_target_pairs={{0,2},{1,3},{2,4},{3,5},{4,6},{5,7},{8,10},{9,11},{10,12},{11,13},... | collective-permute-start | bytes 2359304 | tf_op jit(solution)/shard_map/ppermute | solution.py:418
  58.7 26.7 %collective-permute-start.19 = (bf16[256,1536]{1,0:T(8,128)(2,1)S(1)}, bf16[256,1536]{1,0:T(8,128)(2,1)}, u32[]{:S(2)}, u32[]{:S(2)}) collective-permute-start(bf16[256,1536]{1,0:T(8,128)(2,1)S(1)} %collective-permute-done.7.refs_8_.next_ref), channel_id=1, source_target_pairs={{2,0},{3,1},{4,2},{5,3},{6,4},{7,5},{10,8},{11,9},{12,10},{13,11},... | collective-permute-start | bytes 2359304 | tf_op jit(solution)/shard_map/ppermute | solution.py:418
  60.0 25.4 %collective-permute-start.14 = (bf16[4,64,1536]{2,1,0:T(8,128)(2,1)S(1)}, bf16[4,64,1536]{2,1,0:T(8,128)(2,1)S(1)}, u32[]{:S(2)}, u32[]{:S(2)}) collective-permute-start(bf16[4,64,1536]{2,1,0:T(8,128)(2,1)S(1)} %pad_maximum_fusion.2.refs_10_), channel_id=1, source_target_pairs={{0,16},{8,24},{16,0},{24,8},{1,17},{9,25},{17,1},{25,9},{2,18},{10... | collective-permute-start | bytes 2359304 | tf_op jit(solution)/shard_map/ppermute | solution.py:421
  62.6 22.9 %collective-permute-start.13 = (bf16[4,64,1536]{2,1,0:T(8,128)(2,1)S(1)}, bf16[4,64,1536]{2,1,0:T(8,128)(2,1)S(1)}, u32[]{:S(2)}, u32[]{:S(2)}) collective-permute-start(bf16[4,64,1536]{2,1,0:T(8,128)(2,1)S(1)} %pad_maximum_fusion.2.refs_10_), channel_id=1, source_target_pairs={{0,8},{8,0},{16,24},{24,16},{1,9},{9,1},{17,25},{25,17},{2,10},{10... | collective-permute-start | bytes 2359304 | tf_op jit(solution)/shard_map/ppermute | solution.py:421
  62.6 1.4 %collective-permute-start.15 = (bf16[64,208]{1,0:T(8,128)(2,1)}, bf16[64,208]{1,0:T(8,128)(2,1)S(1)}, u32[]{:S(2)}, u32[]{:S(2)}) collective-permute-start(bf16[64,208]{1,0:T(8,128)(2,1)} %solve.1), channel_id=1, source_target_pairs={{0,1},{1,0},{2,3},{3,2},{4,5},{5,4},{6,7},{7,6},{8,9},{9,8},{10,11... | collective-permute-start | bytes 79880 | tf_op jit(solution)/shard_map/ppermute | solution.py:415
  64.8 11.9 %collective-permute-start.16 = (bf16[128,208]{1,0:T(8,128)(2,1)S(1)}, bf16[128,208]{1,0:T(8,128)(2,1)S(1)}, u32[]{:S(2)}, u32[]{:S(2)}) collective-permute-start(bf16[128,208]{1,0:T(8,128)(2,1)S(1)} %pad_maximum_fusion.6.refs_2_), channel_id=1, source_target_pairs={{0,2},{1,3},{2,0},{3,1},{4,6},{5,7},{6,4},{7,5},{8,10},{9,11},{10,... | collective-permute-start | bytes 159752 | tf_op jit(solution)/shard_map/ppermute | solution.py:424
  76.7 8.7 %collective-permute-start.17 = (bf16[256,208]{1,0:T(8,128)(2,1)S(1)}, bf16[256,208]{1,0:T(8,128)(2,1)S(1)}, u32[]{:S(2)}, u32[]{:S(2)}) collective-permute-start(bf16[256,208]{1,0:T(8,128)(2,1)S(1)} %pad_maximum_fusion.5), channel_id=1, source_target_pairs={{0,4},{1,5},{2,6},{3,7},{4,0},{5,1},{6,2},{7,3},{8,12},{9,13},{10,... | collective-permute-start | bytes 319496 | tf_op jit(solution)/shard_map/ppermute | solution.py:424
  85.5 16.0 %collective-permute-start.20 = (bf16[256,1536]{1,0:T(8,128)(2,1)S(1)}, bf16[256,1536]{1,0:T(8,128)(2,1)}, u32[]{:S(2)}, u32[]{:S(2)}) collective-permute-start(bf16[256,1536]{1,0:T(8,128)(2,1)S(1)} %collective-permute-done.18.refs_7_), channel_id=1, source_target_pairs={{0,2},{1,3},{2,4},{3,5},{4,6},{5,7},{8,10},{9,11},{10,12},{11,13},... | collective-permute-start | bytes 2359304 | tf_op jit(solution)/shard_map/ppermute | solution.py:418
  87.7 15.9 %collective-permute-start.21 = (bf16[256,1536]{1,0:T(8,128)(2,1)}, bf16[256,1536]{1,0:T(8,128)(2,1)}, u32[]{:S(2)}, u32[]{:S(2)}) collective-permute-start(bf16[256,1536]{1,0:T(8,128)(2,1)} %collective-permute-done.19.refs_9_), channel_id=1, source_target_pairs={{2,0},{3,1},{4,2},{5,3},{6,4},{7,5},{10,8},{11,9},{12,10},{13,11},... | collective-permute-start | bytes 2359304 | tf_op jit(solution)/shard_map/ppermute | solution.py:418
  89.0 16.3 %collective-permute-start.22 = (bf16[4,64,1536]{2,1,0:T(8,128)(2,1)S(1)}, bf16[4,64,1536]{2,1,0:T(8,128)(2,1)}, u32[]{:S(2)}, u32[]{:S(2)}) collective-permute-start(bf16[4,64,1536]{2,1,0:T(8,128)(2,1)S(1)} %pad_maximum_fusion.2.refs_10_), channel_id=1, source_target_pairs={{0,24},{8,16},{16,8},{24,0},{1,25},{9,17},{17,9},{25,1},{2,26},{10... | collective-permute-start | bytes 2359304 | tf_op jit(solution)/shard_map/ppermute | solution.py:421
  111.5 10.4 %collective-permute-start.23 = (bf16[2,1536,512]{2,1,0:T(8,128)(2,1)}, bf16[2,1536,512]{2,1,0:T(8,128)(2,1)S(1)}, u32[]{:S(2)}, u32[]{:S(2)}) collective-permute-start(bf16[2,1536,512]{2,1,0:T(8,128)(2,1)} %get-tuple-element.69.row_ref), channel_id=1, source_target_pairs={{0,1},{1,0},{2,3},{3,2},{4,5},{5,4},{6,7},{7,6},{8,9},{9,8},{10,11... | collective-permute-start | bytes 9437192 | tf_op jit(solution)/shard_map/ppermute | solution.py:415
  (14 other events, 289.1 us)

commit v8 on v7

--- a/solution.py
+++ b/solution.py
@@ -302,17 +302,30 @@
 
 
 def late_kernel(rows, group_ref, row_fit, col_fit, left_ref, right_ref, next_ref, piece_ref, *refs):
-    row_out, col_out = refs[2:]
+    row_out, col_out, block, sem = refs[2:]
     plane = lax.axis_index("cols") // (lax.axis_size("cols") // rows)
+    step = pl.program_id(0)
+
+    @pl.when((step == 0) & (plane == 0))
+    def _():
+        pltpu.make_async_copy(right_ref, block, sem).start()
+
+    @pl.when((step == 0) & (plane == rows - 1))
+    def _():
+        pltpu.make_async_copy(left_ref, block, sem).start()
+
+    @pl.when((step == 0) & (plane > 0) & (plane < rows - 1))
+    def _():
+        pltpu.make_async_copy(next_ref, block, sem).start()
+
     resid, sdev = weigh(col_fit[0], *parted(piece_ref[0], 1))
     col_out[0, 0] = resid
     col_out[1, 0] = sdev
 
-    @pl.when(pl.program_id(0) == 0)
+    @pl.when(step == rows - 1)
     def _():
-        block = jnp.where(plane == rows - 1, left_ref[...], next_ref[...])
-        block = jnp.where(plane == 0, right_ref[...], block)
-        resid, sdev = weigh(row_fit[...], *parted(block, rows))
+        pltpu.make_async_copy(next_ref, block, sem).wait()
+        resid, sdev = weigh(row_fit[...], *parted(block[...], rows))
         chip = row_fit.shape[0]
         if row_out.shape[2] != chip:
             row_out[...] = jnp.zeros(row_out.shape, BF16)
@@ -324,7 +337,6 @@
     chip, width = row_fit.shape
     height = chip // rows
     space = row_panel.shape[2] // rows
-    whole = pl.BlockSpec((2 * chip, width), lambda e, at: (0, 0))
     anywhere = pl.BlockSpec(memory_space=pl.ANY)
     return pl.pallas_call(
         functools.partial(late_kernel, rows),
@@ -334,9 +346,9 @@
             in_specs=[
                 pl.BlockSpec((chip, width), lambda e, at: (0, 0)),
                 pl.BlockSpec((1, height, width), lambda e, at: (e, 0, 0)),
-                whole,
-                whole,
-                whole,
+                anywhere,
+                anywhere,
+                anywhere,
                 pl.BlockSpec((1, 2 * height, width), lambda e, at: (e, 0, 0)),
                 anywhere,
                 anywhere,
@@ -345,6 +357,7 @@
                 pl.BlockSpec((2, width, space), lambda e, at: (0, 0, rows - 1)),
                 pl.BlockSpec((2, 1, height, width), lambda e, at: (0, at[e], 0, 0)),
             ),
+            scratch_shapes=[pltpu.VMEM((2 * chip, width), BF16), pltpu.SemaphoreType.DMA],
         ),
         out_shape=(
             jax.ShapeDtypeStruct(row_panel.shape, BF16),
@@ -363,9 +376,13 @@
 
 def kin_kernel(part_ref, row_ref, col_ref, *refs):
     out_ref = refs[-1]
-    numer = jnp.dot(row_ref[0], col_ref[0], preferred_element_type=F32)
-    denom = jnp.dot(row_ref[1], col_ref[1], preferred_element_type=F32)
-    out_ref[...] = quotient(numer, denom)
+    count = out_ref.shape[0]
+    step = 512 if count % 512 == 0 else count
+    for at in range(0, count, step):
+        span = slice(at, at + step)
+        numer = jnp.dot(row_ref[0, span, :], col_ref[0], preferred_element_type=F32)
+        denom = jnp.dot(row_ref[1, span, :], col_ref[1], preferred_element_type=F32)
+        out_ref[span, :] = quotient(numer, denom)
 
 
 def kin_call(part, people, row_panel, col_panel, before):
@@ -449,17 +466,7 @@
     height = held.shape[0] // rows
     quarters = [beside(lax.dynamic_slice_in_dim(held, (row ^ d) * height, height, 0), d) for d in range(rows)]
     hops = [1 << i for i in range(rows.bit_length() - 1)]
-    gram = gram_call(dosage, present, components)
-    for hop in hops[:-1]:
-        gram = gram + beside(gram, hop)
-    grams = [gram, beside(gram, hops[-1])]
-    col_comps = lax.dynamic_slice_in_dim(components, core * width, width, 1)
-    quarters, grams, col_comps, from_left, from_right = lax.optimization_barrier(
-        (jnp.stack(quarters), grams, col_comps, from_left, from_right)
-    )
-    moved = [
-        across(lax.dynamic_index_in_dim(quarters, row ^ plane ^ e, 0, keepdims=False), e) for e in range(rows)
-    ]
+
     def doubled(x, hop):
         moves = [
             (r * cols + z * ratio + c, (r ^ hop) * cols + z * ratio + c)
@@ -470,15 +477,29 @@
         ]
         return jnp.where((row ^ plane) < hop, x, lax.ppermute(x, ("rows", "cols"), moves))
 
+    quarters[1], dosage, present = lax.optimization_barrier((quarters[1], dosage, present))
+    gram = gram_call(dosage, present, components)
+    gram = gram + beside(gram, hops[0])
+    col_comps = lax.dynamic_slice_in_dim(components, core * width, width, 1)
+    quarters, gram, col_comps, from_left, from_right = lax.optimization_barrier(
+        (jnp.stack(quarters), gram, col_comps, from_left, from_right)
+    )
+    moved = [
+        across(lax.dynamic_index_in_dim(quarters, row ^ plane ^ e, 0, keepdims=False), e) for e in range(rows)
+    ]
+    for hop in hops[1:-1]:
+        gram = gram + beside(gram, hop)
+    grams = [gram, beside(gram, hops[-1])]
     for hop in hops:
         col_comps = doubled(col_comps, hop)
     coef = solve_call(grams, comps, markers)
-    moved, coef, col_comps, held, from_left, from_right = lax.optimization_barrier(
-        (jnp.stack(moved), coef, col_comps, held, from_left, from_right)
+    coefs = [by_core([swap(coef, k) for k in range(ratio)])]
+    for hop in hops[:-1]:
+        coefs.append(across(coefs[0] if len(coefs) == 1 else jnp.concatenate(coefs, axis=0), hop))
+    moved, coefs, col_comps, held, from_left, from_right = lax.optimization_barrier(
+        (jnp.stack(moved), coefs, col_comps, held, from_left, from_right)
     )
-    coefs = [by_core([swap(coef, k) for k in range(ratio)])]
-    for hop in hops:
-        coefs.append(across(coefs[0] if len(coefs) == 1 else jnp.concatenate(coefs, axis=0), hop))
+    coefs.append(across(jnp.concatenate(coefs, axis=0), hops[-1]))
     near = [moved]
     for step in range(rows - 3):
         from_left.append(along(from_left[-1], 1))

time: 135 us -> 142 us (1.052)
  waiting for transfers between devices: 35 us -> 47.4 us
  starting transfers between devices: 42.3 us -> 37.3 us
    ppermute x5, waiting for transfers between devices: 15 us -> 22.5 us  [across(): return lax.ppermute(x, 'cols', pairs(lambda z, c: (z ^ e, c))) if e else x]
    ppermute x6, waiting for transfers between devices: 2.08 us -> 8.54 us  [along(): return lax.ppermute(x, 'cols', pairs(lambda z, c: (z + way, c)))]
    ppermute x5, starting transfers between devices: 11.9 us -> 8.65 us  [across(): return lax.ppermute(x, 'cols', pairs(lambda z, c: (z ^ e, c))) if e else x]
    ppermute x8, starting transfers between devices: 10.2 us -> 8.11 us  [beside(): lax.ppermute(x, 'rows', [(i, i ^ d) for i in range(rows)])]
  transfers between devices with their start and end apart: 24 -> 24, of which waited for: 13 -> 10; matrix products, arithmetic and copies ran while one was open for 2% -> 3% of each run, Pallas kernels for 25% -> 23%
where the time goes in v8:
time: 142 us; the launch traced here: 141 us
  Pallas kernels  48.6 us (34%)
  waiting for transfers between devices  47.4 us (33%)
  starting transfers between devices  37.3 us (26%)
  other arithmetic  5.01 us (4%)
  local copies, waits for them, and re-layouts  2.51 us (2%)
    ppermute x5, waiting for transfers between devices, across(): return lax.ppermute(x, 'cols', pairs(lambda z, c: (z ^ e, c))) if e else x  22.5 us
    pallas_call x2, Pallas kernels, kin_call(): pl.pallas_call(kin_kernel, grid_spec=pltpu.PrefetchScalarGridSpec(num_sca...  20.7 us
    ppermute x6, starting transfers between devices, along(): return lax.ppermute(x, 'cols', pairs(lambda z, c: (z + way, c)))  14.2 us
    ppermute x8, waiting for transfers between devices, beside(): lax.ppermute(x, 'rows', [(i, i ^ d) for i in range(rows)])  12.8 us
    pallas_call x1, Pallas kernels, early_call(): pl.pallas_call(functools.partial(early_kernel_at, rows, len(pieces)), gri...  9.72 us
    ppermute x5, starting transfers between devices, across(): return lax.ppermute(x, 'cols', pairs(lambda z, c: (z ^ e, c))) if e else x  8.65 us
    ppermute x6, waiting for transfers between devices, along(): return lax.ppermute(x, 'cols', pairs(lambda z, c: (z + way, c)))  8.54 us
    ppermute x8, starting transfers between devices, beside(): lax.ppermute(x, 'rows', [(i, i ^ d) for i in range(rows)])  8.11 us
  transfers between devices with their start and end apart: 24, of which 10 were waited for; matrix products, arithmetic and copies ran while one was open for 3% of the time, Pallas kernels for 23%

profile of v8, /device:TPU:0, one launch (start us, length us, event | category | flops | bytes accessed | tf_op | source)
XLA Modules:
  0.0 141.3 jit_solution(15362617817795117257)
XLA Ops:
  0.0 1.4 %dynamic-slice_convert_fusion = (bf16[64,1536]{1,0:T(8,128)(2,1)S(1)}, bf16[64,1536]{1,0:T(8,128)(2,1)S(1)}, bf16[64,1536]{1,0:T(8,128)(2,1)S(1)}, bf16[64,1536]{1,0:T(8,128)(2,1)S(1)}) fusion(s32[64,3072]{1,0:T(8,128)} %present_ref, s32[]{:T(128)S(6)} %select_n.180, s32[]{:T(128)S(6)} %select_n.179, s32[64,3072]{1,0:T(8,128)} %dosage_ref), kind=kLoop, calls=%fused_computation.7 | loop fusion | flops 393216 | bytes 2359304 | tf_op jit(solution)/shard_map/convert_element_type | solution.py:458
  4.8 5.5 %collective-permute-start.5 = (bf16[256,1536]{1,0:T(8,128)(2,1)S(1)}, bf16[256,1536]{1,0:T(8,128)(2,1)S(1)}, u32[]{:S(2)}, u32[]{:S(2)}) collective-permute-start(bf16[256,1536]{1,0:T(8,128)(2,1)S(1)} %pad_maximum_fusion.refs_5_), channel_id=1, source_target_pairs={{0,2},{1,3},{2,4},{3,5},{4,6},{5,7},{8,10},{9,11},{10,12},{11,13},... | collective-permute-start | bytes 2359304 | tf_op jit(solution)/shard_map/ppermute | solution.py:435
  10.5 2.9 %collective-permute-start.3 = (bf16[64,1536]{1,0:T(8,128)(2,1)S(1)}, bf16[64,1536]{1,0:T(8,128)(2,1)S(1)}, u32[]{:S(2)}, u32[]{:S(2)}) collective-permute-start(bf16[64,1536]{1,0:T(8,128)(2,1)S(1)} %get-tuple-element.82), channel_id=1, source_target_pairs={{0,24},{8,16},{16,8},{24,0},{1,25},{9,17},{17,9},{25,1},{2,26},{10... | collective-permute-start | bytes 589832 | tf_op jit(solution)/shard_map/ppermute | solution.py:438
  14.1 8.5 %collective-permute-done.1 = bf16[64,1536]{1,0:T(8,128)(2,1)S(1)} collective-permute-done((bf16[64,1536]{1,0:T(8,128)(2,1)S(1)}, bf16[64,1536]{1,0:T(8,128)(2,1)S(1)}, u32[]{:S(2)}, u32[]{:S(2)}) %collective-permute-start.1) | collective-permute-done | bytes 196640 | tf_op jit(solution)/shard_map/ppermute | solution.py:438
  22.6 5.6 %gram.1 = f32[360,128]{1,0:T(8,128)} custom-call(s32[64,3072]{1,0:T(8,128)} %dosage_ref, s32[64,3072]{1,0:T(8,128)} %present_ref, f32[32,3072]{1,0:T(8,128)} %refs_0_.1), custom_call_target="tpu_custom_call" | custom-call | tf_op jit(solution)/shard_map/gram/pallas_call | solution.py:62
  28.2 1.5 %collective-permute-start.4 = (f32[360,128]{1,0:T(8,128)}, f32[360,128]{1,0:T(8,128)S(1)}, u32[]{:S(2)}, u32[]{:S(2)}) collective-permute-start(f32[360,128]{1,0:T(8,128)} %gram.1), channel_id=1, source_target_pairs={{0,8},{8,0},{16,24},{24,16},{1,9},{9,1},{17,25},{25,17},{2,10},{10... | collective-permute-start | bytes 552968 | tf_op jit(solution)/shard_map/ppermute | solution.py:438
  29.9 4.1 %collective-permute-done.4 = f32[360,128]{1,0:T(8,128)S(1)} collective-permute-done((f32[360,128]{1,0:T(8,128)}, f32[360,128]{1,0:T(8,128)S(1)}, u32[]{:S(2)}, u32[]{:S(2)}) %collective-permute-start.4) | collective-permute-done | bytes 184352 | tf_op jit(solution)/shard_map/ppermute | solution.py:438
  35.4 3.6 %collective-permute-start.13 = (f32[32,1536]{1,0:T(8,128)S(1)}, f32[32,1536]{1,0:T(8,128)S(1)}, u32[]{:S(2)}, u32[]{:S(2)}) collective-permute-start(f32[32,1536]{1,0:T(8,128)S(1)} %constant_dynamic-slice_fusion.1), channel_id=1, source_target_pairs={{0,8},{1,9},{10,2},{11,3},{20,28},{21,29},{30,22},{31,23}} | collective-permute-start | bytes 589832 | tf_op jit(solution)/shard_map/ppermute | solution.py:478
  39.9 3.6 %collective-permute-start.7 = (bf16[64,1536]{1,0:T(8,128)(2,1)S(1)}, bf16[64,1536]{1,0:T(8,128)(2,1)S(1)}, u32[]{:S(2)}, u32[]{:S(2)}) collective-permute-start(bf16[64,1536]{1,0:T(8,128)(2,1)S(1)} %get-tuple-element.80), channel_id=1, source_target_pairs={{0,2},{1,3},{2,0},{3,1},{4,6},{5,7},{6,4},{7,5},{8,10},{9,11},{10,... | collective-permute-start | bytes 589832 | tf_op jit(solution)/shard_map/ppermute | solution.py:441
  44.2 7.1 %solve.1 = bf16[64,208]{1,0:T(8,128)(2,1)} custom-call(f32[360,128]{1,0:T(8,128)} %copy-done.9, f32[360,128]{1,0:T(8,128)} %copy-done.12), custom_call_target="tpu_custom_call" | custom-call | tf_op jit(solution)/shard_map/solve/pallas_call | solution.py:151
  51.4 2.2 %collective-permute-start.14 = (f32[32,1536]{1,0:T(8,128)S(1)}, f32[32,1536]{1,0:T(8,128)S(1)}, u32[]{:S(2)}, u32[]{:S(2)}) collective-permute-start(f32[32,1536]{1,0:T(8,128)S(1)} %broadcast_select_fusion), channel_id=1, source_target_pairs={{0,16},{1,17},{8,24},{9,25},{2,18},{3,19},{10,26},{11,27},{20,4},{... | collective-permute-start | bytes 589832 | tf_op jit(solution)/shard_map/ppermute | solution.py:478
  56.2 2.2 %collective-permute-done.14 = f32[32,1536]{1,0:T(8,128)S(1)} collective-permute-done((f32[32,1536]{1,0:T(8,128)S(1)}, f32[32,1536]{1,0:T(8,128)S(1)}, u32[]{:S(2)}, u32[]{:S(2)}) %collective-permute-start.14) | collective-permute-done | bytes 196640 | tf_op jit(solution)/shard_map/ppermute | solution.py:478
  60.0 2.6 %collective-permute-start.18 = (bf16[256,1536]{1,0:T(8,128)(2,1)S(1)}, bf16[256,1536]{1,0:T(8,128)(2,1)S(1)}, u32[]{:S(2)}, u32[]{:S(2)}) collective-permute-start(bf16[256,1536]{1,0:T(8,128)(2,1)S(1)} %collective-permute-done.5.refs_6_), channel_id=1, source_target_pairs={{0,2},{1,3},{2,4},{3,5},{4,6},{5,7},{8,10},{9,11},{10,12},{11,13},... | collective-permute-start | bytes 2359304 | tf_op jit(solution)/shard_map/ppermute | solution.py:435
  63.9 2.5 %collective-permute-start.16 = (bf16[4,64,1536]{2,1,0:T(8,128)(2,1)S(1)}, bf16[4,64,1536]{2,1,0:T(8,128)(2,1)S(1)}, u32[]{:S(2)}, u32[]{:S(2)}) collective-permute-start(bf16[4,64,1536]{2,1,0:T(8,128)(2,1)S(1)} %pad_maximum_fusion.2.refs_10_), channel_id=1, source_target_pairs={{0,16},{8,24},{16,0},{24,8},{1,17},{9,25},{17,1},{25,9},{2,18},{10... | collective-permute-start | bytes 2359304 | tf_op jit(solution)/shard_map/ppermute | solution.py:438
  66.4 3.7 %collective-permute-start.17 = (bf16[256,208]{1,0:T(8,128)(2,1)S(1)}, bf16[256,208]{1,0:T(8,128)(2,1)S(1)}, u32[]{:S(2)}, u32[]{:S(2)}) collective-permute-start(bf16[256,208]{1,0:T(8,128)(2,1)S(1)} %pad_maximum_fusion.5), channel_id=1, source_target_pairs={{0,4},{1,5},{2,6},{3,7},{4,0},{5,1},{6,2},{7,3},{8,12},{9,13},{10,... | collective-permute-start | bytes 319496 | tf_op jit(solution)/shard_map/ppermute | solution.py:441
  70.1 20.5 %collective-permute-done.17.refs_4_ = bf16[256,208]{1,0:T(8,128)(2,1)S(1)} collective-permute-done((bf16[256,208]{1,0:T(8,128)(2,1)S(1)}, bf16[256,208]{1,0:T(8,128)(2,1)S(1)}, u32[]{:S(2)}, u32[]{:S(2)}) %collective-permute-start.17) | collective-permute-done | bytes 106528 | tf_op jit(solution)/shard_map/ppermute | solution.py:441
  90.7 2.2 %collective-permute-start.20 = (bf16[256,1536]{1,0:T(8,128)(2,1)S(1)}, bf16[256,1536]{1,0:T(8,128)(2,1)}, u32[]{:S(2)}, u32[]{:S(2)}) collective-permute-start(bf16[256,1536]{1,0:T(8,128)(2,1)S(1)} %collective-permute-done.18.refs_7_), channel_id=1, source_target_pairs={{0,2},{1,3},{2,4},{3,5},{4,6},{5,7},{8,10},{9,11},{10,12},{11,13},... | collective-permute-start | bytes 2359304 | tf_op jit(solution)/shard_map/ppermute | solution.py:435
  95.0 9.7 %early.1 = (bf16[2,1536,512]{2,1,0:T(8,128)(2,1)}, bf16[2,16,32,1536]{3,2,1,0:T(8,128)(2,1)}, f32[128,1536]{1,0:T(8,128)}, f32[4,32,1536]{2,1,0:T(8,128)}) custom-call(s32[1]{0:T(128)} %bitcast.5.part_ref, f32[32,3072]{1,0:T(8,128)} %refs_0_.1, f32[32,1536]{1,0:T(8,128)} %broadcast_select_fusion.1.refs_1_, bf16[128,208]{1,0:T(8,128)(2,1)} %copy-done.10, ...), custom_call_target="tpu_custom_call" | custom-call | tf_op jit(solution)/shard_map/early/pallas_call | solution.py:266
  104.8 3.2 %collective-permute-done.20.left_ref = bf16[256,1536]{1,0:T(8,128)(2,1)} collective-permute-done((bf16[256,1536]{1,0:T(8,128)(2,1)S(1)}, bf16[256,1536]{1,0:T(8,128)(2,1)}, u32[]{:S(2)}, u32[]{:S(2)}) %collective-permute-start.20) | collective-permute-done | bytes 786464 | tf_op jit(solution)/shard_map/ppermute | solution.py:435
  108.0 5.3 %collective-permute-done.21.right_ref = bf16[256,1536]{1,0:T(8,128)(2,1)} collective-permute-done((bf16[256,1536]{1,0:T(8,128)(2,1)}, bf16[256,1536]{1,0:T(8,128)(2,1)}, u32[]{:S(2)}, u32[]{:S(2)}) %collective-permute-start.21) | collective-permute-done | bytes 786464 | tf_op jit(solution)/shard_map/ppermute | solution.py:435
  113.5 5.4 %late.1 = (bf16[2,1536,512]{2,1,0:T(8,128)(2,1)}, bf16[2,16,32,1536]{3,2,1,0:T(8,128)(2,1)}) custom-call(s32[4]{0:T(128)} %pad_add_fusion.group_ref, f32[128,1536]{1,0:T(8,128)} %get-tuple-element.71.row_fit, f32[4,32,1536]{2,1,0:T(8,128)} %get-tuple-element.72.col_fit, ...), custom_call_target="tpu_custom_call", output_to_operand_aliasing={{0}: (7, {}), {1}: (8, {})} | custom-call | tf_op jit(solution)/shard_map/late/pallas_call | solution.py:341
  119.0 10.4 %kinship.2.refs_0_ = f32[3072,1536]{1,0:T(8,128)} custom-call(s32[1]{0:T(128)} %bitcast.27.part_ref, bf16[2,1536,512]{2,1,0:T(8,128)(2,1)} %get-tuple-element.75.row_ref, bf16[2,512,1536]{2,1,0:T(8,128)(2,1)} %bitcast.38), custom_call_target="tpu_custom_call" | custom-call | tf_op jit(solution)/shard_map/kinship/pallas_call | solution.py:402
  129.3 1.6 %copy-done.1 = bf16[2,1536,512]{2,1,0:T(8,128)(2,1)} copy-done((bf16[2,1536,512]{2,1,0:T(8,128)(2,1)}, bf16[2,1536,512]{2,1,0:T(8,128)(2,1)S(1)}, u32[]{:S(2)}) %copy-start.1) | copy-done | bytes 3145752
  131.0 10.3 %kinship.3 = f32[3072,1536]{1,0:T(8,128)} custom-call(s32[1]{0:T(128)} %bitcast.part_ref, bf16[2,1536,512]{2,1,0:T(8,128)(2,1)} %copy-done.1, bf16[2,512,1536]{2,1,0:T(8,128)(2,1)} %bitcast.39, f32[3072,1536]{1,0:T(8,128)} %kinship.2.refs_0_), custom_call_target="tpu_custom_call", output_to_operand_aliasing={{}: (3, {})} | custom-call | tf_op jit(solution)/shard_map/kinship/pallas_call | solution.py:402
  (75 shorter events, 14.9 us)
Async XLA Ops:
  1.5 1.9 %collective-permute-start = (bf16[128,1536]{1,0:T(8,128)(2,1)S(1)}, bf16[128,1536]{1,0:T(8,128)(2,1)S(1)}, u32[]{:S(2)}, u32[]{:S(2)}) collective-permute-start(bf16[128,1536]{1,0:T(8,128)(2,1)S(1)} %bitcast.44), channel_id=1, source_target_pairs={{0,1},{1,0},{2,3},{3,2},{4,5},{5,4},{6,7},{7,6},{8,9},{9,8},{10,11... | collective-permute-start | bytes 1179656 | tf_op jit(solution)/shard_map/ppermute | solution.py:432
  3.5 31.4 %collective-permute-start.6 = (bf16[256,1536]{1,0:T(8,128)(2,1)S(1)}, bf16[256,1536]{1,0:T(8,128)(2,1)S(1)}, u32[]{:S(2)}, u32[]{:S(2)}) collective-permute-start(bf16[256,1536]{1,0:T(8,128)(2,1)S(1)} %pad_maximum_fusion.refs_5_), channel_id=1, source_target_pairs={{2,0},{3,1},{4,2},{5,3},{6,4},{7,5},{10,8},{11,9},{12,10},{13,11},... | collective-permute-start | bytes 2359304 | tf_op jit(solution)/shard_map/ppermute | solution.py:435
  4.8 30.2 %collective-permute-start.5 = (bf16[256,1536]{1,0:T(8,128)(2,1)S(1)}, bf16[256,1536]{1,0:T(8,128)(2,1)S(1)}, u32[]{:S(2)}, u32[]{:S(2)}) collective-permute-start(bf16[256,1536]{1,0:T(8,128)(2,1)S(1)} %pad_maximum_fusion.refs_5_), channel_id=1, source_target_pairs={{0,2},{1,3},{2,4},{3,5},{4,6},{5,7},{8,10},{9,11},{10,12},{11,13},... | collective-permute-start | bytes 2359304 | tf_op jit(solution)/shard_map/ppermute | solution.py:435
  10.5 19.2 %collective-permute-start.3 = (bf16[64,1536]{1,0:T(8,128)(2,1)S(1)}, bf16[64,1536]{1,0:T(8,128)(2,1)S(1)}, u32[]{:S(2)}, u32[]{:S(2)}) collective-permute-start(bf16[64,1536]{1,0:T(8,128)(2,1)S(1)} %get-tuple-element.82), channel_id=1, source_target_pairs={{0,24},{8,16},{16,8},{24,0},{1,25},{9,17},{17,9},{25,1},{2,26},{10... | collective-permute-start | bytes 589832 | tf_op jit(solution)/shard_map/ppermute | solution.py:438
  13.5 16.3 %collective-permute-start.2 = (bf16[64,1536]{1,0:T(8,128)(2,1)S(1)}, bf16[64,1536]{1,0:T(8,128)(2,1)S(1)}, u32[]{:S(2)}, u32[]{:S(2)}) collective-permute-start(bf16[64,1536]{1,0:T(8,128)(2,1)S(1)} %get-tuple-element.83), channel_id=1, source_target_pairs={{0,16},{8,24},{16,0},{24,8},{1,17},{9,25},{17,1},{25,9},{2,18},{10... | collective-permute-start | bytes 589832 | tf_op jit(solution)/shard_map/ppermute | solution.py:438
  14.0 8.6 %collective-permute-start.1 = (bf16[64,1536]{1,0:T(8,128)(2,1)S(1)}, bf16[64,1536]{1,0:T(8,128)(2,1)S(1)}, u32[]{:S(2)}, u32[]{:S(2)}) collective-permute-start(bf16[64,1536]{1,0:T(8,128)(2,1)S(1)} %get-tuple-element.84), channel_id=1, source_target_pairs={{0,8},{8,0},{16,24},{24,16},{1,9},{9,1},{17,25},{25,17},{2,10},{10... | collective-permute-start | bytes 589832 | tf_op jit(solution)/shard_map/ppermute | solution.py:438
  28.2 5.7 %collective-permute-start.4 = (f32[360,128]{1,0:T(8,128)}, f32[360,128]{1,0:T(8,128)S(1)}, u32[]{:S(2)}, u32[]{:S(2)}) collective-permute-start(f32[360,128]{1,0:T(8,128)} %gram.1), channel_id=1, source_target_pairs={{0,8},{8,0},{16,24},{24,16},{1,9},{9,1},{17,25},{25,17},{2,10},{10... | collective-permute-start | bytes 552968 | tf_op jit(solution)/shard_map/ppermute | solution.py:438
  35.0 8.5 %collective-permute-start.10 = (f32[360,128]{1,0:T(8,128)S(1)}, f32[360,128]{1,0:T(8,128)S(1)}, u32[]{:S(2)}, u32[]{:S(2)}) collective-permute-start(f32[360,128]{1,0:T(8,128)S(1)} %add.115.refs_0_), channel_id=1, source_target_pairs={{0,16},{8,24},{16,0},{24,8},{1,17},{9,25},{17,1},{25,9},{2,18},{10... | collective-permute-start | bytes 552968 | tf_op jit(solution)/shard_map/ppermute | solution.py:438
  35.4 15.9 %collective-permute-start.13 = (f32[32,1536]{1,0:T(8,128)S(1)}, f32[32,1536]{1,0:T(8,128)S(1)}, u32[]{:S(2)}, u32[]{:S(2)}) collective-permute-start(f32[32,1536]{1,0:T(8,128)S(1)} %constant_dynamic-slice_fusion.1), channel_id=1, source_target_pairs={{0,8},{1,9},{10,2},{11,3},{20,28},{21,29},{30,22},{31,23}} | collective-permute-start | bytes 589832 | tf_op jit(solution)/shard_map/ppermute | solution.py:478
  39.1 14.5 %collective-permute-start.9 = (bf16[64,1536]{1,0:T(8,128)(2,1)S(1)}, bf16[64,1536]{1,0:T(8,128)(2,1)S(1)}, u32[]{:S(2)}, u32[]{:S(2)}) collective-permute-start(bf16[64,1536]{1,0:T(8,128)(2,1)S(1)} %get-tuple-element.78), channel_id=1, source_target_pairs={{0,6},{1,7},{2,4},{3,5},{4,2},{5,3},{6,0},{7,1},{8,14},{9,15},{10,... | collective-permute-start | bytes 589832 | tf_op jit(solution)/shard_map/ppermute | solution.py:441
  39.1 15.5 %collective-permute-start.8 = (bf16[64,1536]{1,0:T(8,128)(2,1)S(1)}, bf16[64,1536]{1,0:T(8,128)(2,1)S(1)}, u32[]{:S(2)}, u32[]{:S(2)}) collective-permute-start(bf16[64,1536]{1,0:T(8,128)(2,1)S(1)} %get-tuple-element.79), channel_id=1, source_target_pairs={{0,4},{1,5},{2,6},{3,7},{4,0},{5,1},{6,2},{7,3},{8,12},{9,13},{10,... | collective-permute-start | bytes 589832 | tf_op jit(solution)/shard_map/ppermute | solution.py:441
  39.9 14.7 %collective-permute-start.7 = (bf16[64,1536]{1,0:T(8,128)(2,1)S(1)}, bf16[64,1536]{1,0:T(8,128)(2,1)S(1)}, u32[]{:S(2)}, u32[]{:S(2)}) collective-permute-start(bf16[64,1536]{1,0:T(8,128)(2,1)S(1)} %get-tuple-element.80), channel_id=1, source_target_pairs={{0,2},{1,3},{2,0},{3,1},{4,6},{5,7},{6,4},{7,5},{8,10},{9,11},{10,... | collective-permute-start | bytes 589832 | tf_op jit(solution)/shard_map/ppermute | solution.py:441
  51.3 3.5 %collective-permute-start.11 = (bf16[64,208]{1,0:T(8,128)(2,1)}, bf16[64,208]{1,0:T(8,128)(2,1)S(1)}, u32[]{:S(2)}, u32[]{:S(2)}) collective-permute-start(bf16[64,208]{1,0:T(8,128)(2,1)} %solve.1), channel_id=1, source_target_pairs={{0,1},{1,0},{2,3},{3,2},{4,5},{5,4},{6,7},{7,6},{8,9},{9,8},{10,11... | collective-permute-start | bytes 79880 | tf_op jit(solution)/shard_map/ppermute | solution.py:432
  51.4 7.0 %collective-permute-start.14 = (f32[32,1536]{1,0:T(8,128)S(1)}, f32[32,1536]{1,0:T(8,128)S(1)}, u32[]{:S(2)}, u32[]{:S(2)}) collective-permute-start(f32[32,1536]{1,0:T(8,128)S(1)} %broadcast_select_fusion), channel_id=1, source_target_pairs={{0,16},{1,17},{8,24},{9,25},{2,18},{3,19},{10,26},{11,27},{20,4},{... | collective-permute-start | bytes 589832 | tf_op jit(solution)/shard_map/ppermute | solution.py:478
  55.6 4.3 %collective-permute-start.12 = (bf16[128,208]{1,0:T(8,128)(2,1)S(1)}, bf16[128,208]{1,0:T(8,128)(2,1)S(1)}, u32[]{:S(2)}, u32[]{:S(2)}) collective-permute-start(bf16[128,208]{1,0:T(8,128)(2,1)S(1)} %pad_maximum_fusion.6.refs_2_), channel_id=1, source_target_pairs={{0,2},{1,3},{2,0},{3,1},{4,6},{5,7},{6,4},{7,5},{8,10},{9,11},{10,... | collective-permute-start | bytes 159752 | tf_op jit(solution)/shard_map/ppermute | solution.py:441
  60.0 30.7 %collective-permute-start.18 = (bf16[256,1536]{1,0:T(8,128)(2,1)S(1)}, bf16[256,1536]{1,0:T(8,128)(2,1)S(1)}, u32[]{:S(2)}, u32[]{:S(2)}) collective-permute-start(bf16[256,1536]{1,0:T(8,128)(2,1)S(1)} %collective-permute-done.5.refs_6_), channel_id=1, source_target_pairs={{0,2},{1,3},{2,4},{3,5},{4,6},{5,7},{8,10},{9,11},{10,12},{11,13},... | collective-permute-start | bytes 2359304 | tf_op jit(solution)/shard_map/ppermute | solution.py:435
  62.6 28.1 %collective-permute-start.19 = (bf16[256,1536]{1,0:T(8,128)(2,1)S(1)}, bf16[256,1536]{1,0:T(8,128)(2,1)}, u32[]{:S(2)}, u32[]{:S(2)}) collective-permute-start(bf16[256,1536]{1,0:T(8,128)(2,1)S(1)} %collective-permute-done.6.refs_8_.next_ref), channel_id=1, source_target_pairs={{2,0},{3,1},{4,2},{5,3},{6,4},{7,5},{10,8},{11,9},{12,10},{13,11},... | collective-permute-start | bytes 2359304 | tf_op jit(solution)/shard_map/ppermute | solution.py:435
  63.9 26.8 %collective-permute-start.16 = (bf16[4,64,1536]{2,1,0:T(8,128)(2,1)S(1)}, bf16[4,64,1536]{2,1,0:T(8,128)(2,1)S(1)}, u32[]{:S(2)}, u32[]{:S(2)}) collective-permute-start(bf16[4,64,1536]{2,1,0:T(8,128)(2,1)S(1)} %pad_maximum_fusion.2.refs_10_), channel_id=1, source_target_pairs={{0,16},{8,24},{16,0},{24,8},{1,17},{9,25},{17,1},{25,9},{2,18},{10... | collective-permute-start | bytes 2359304 | tf_op jit(solution)/shard_map/ppermute | solution.py:438
  66.4 24.3 %collective-permute-start.15 = (bf16[4,64,1536]{2,1,0:T(8,128)(2,1)S(1)}, bf16[4,64,1536]{2,1,0:T(8,128)(2,1)S(1)}, u32[]{:S(2)}, u32[]{:S(2)}) collective-permute-start(bf16[4,64,1536]{2,1,0:T(8,128)(2,1)S(1)} %pad_maximum_fusion.2.refs_10_), channel_id=1, source_target_pairs={{0,8},{8,0},{16,24},{24,16},{1,9},{9,1},{17,25},{25,17},{2,10},{10... | collective-permute-start | bytes 2359304 | tf_op jit(solution)/shard_map/ppermute | solution.py:438
  66.4 24.2 %collective-permute-start.17 = (bf16[256,208]{1,0:T(8,128)(2,1)S(1)}, bf16[256,208]{1,0:T(8,128)(2,1)S(1)}, u32[]{:S(2)}, u32[]{:S(2)}) collective-permute-start(bf16[256,208]{1,0:T(8,128)(2,1)S(1)} %pad_maximum_fusion.5), channel_id=1, source_target_pairs={{0,4},{1,5},{2,6},{3,7},{4,0},{5,1},{6,2},{7,3},{8,12},{9,13},{10,... | collective-permute-start | bytes 319496 | tf_op jit(solution)/shard_map/ppermute | solution.py:441
  90.7 17.3 %collective-permute-start.20 = (bf16[256,1536]{1,0:T(8,128)(2,1)S(1)}, bf16[256,1536]{1,0:T(8,128)(2,1)}, u32[]{:S(2)}, u32[]{:S(2)}) collective-permute-start(bf16[256,1536]{1,0:T(8,128)(2,1)S(1)} %collective-permute-done.18.refs_7_), channel_id=1, source_target_pairs={{0,2},{1,3},{2,4},{3,5},{4,6},{5,7},{8,10},{9,11},{10,12},{11,13},... | collective-permute-start | bytes 2359304 | tf_op jit(solution)/shard_map/ppermute | solution.py:435
  92.9 20.4 %collective-permute-start.21 = (bf16[256,1536]{1,0:T(8,128)(2,1)}, bf16[256,1536]{1,0:T(8,128)(2,1)}, u32[]{:S(2)}, u32[]{:S(2)}) collective-permute-start(bf16[256,1536]{1,0:T(8,128)(2,1)} %collective-permute-done.19.refs_9_), channel_id=1, source_target_pairs={{2,0},{3,1},{4,2},{5,3},{6,4},{7,5},{10,8},{11,9},{12,10},{13,11},... | collective-permute-start | bytes 2359304 | tf_op jit(solution)/shard_map/ppermute | solution.py:435
  94.2 19.3 %collective-permute-start.22 = (bf16[4,64,1536]{2,1,0:T(8,128)(2,1)S(1)}, bf16[4,64,1536]{2,1,0:T(8,128)(2,1)}, u32[]{:S(2)}, u32[]{:S(2)}) collective-permute-start(bf16[4,64,1536]{2,1,0:T(8,128)(2,1)S(1)} %pad_maximum_fusion.2.refs_10_), channel_id=1, source_target_pairs={{0,24},{8,16},{16,8},{24,0},{1,25},{9,17},{17,9},{25,1},{2,26},{10... | collective-permute-start | bytes 2359304 | tf_op jit(solution)/shard_map/ppermute | solution.py:438
  118.9 10.5 %collective-permute-start.23 = (bf16[2,1536,512]{2,1,0:T(8,128)(2,1)}, bf16[2,1536,512]{2,1,0:T(8,128)(2,1)S(1)}, u32[]{:S(2)}, u32[]{:S(2)}) collective-permute-start(bf16[2,1536,512]{2,1,0:T(8,128)(2,1)} %get-tuple-element.75.row_ref), channel_id=1, source_target_pairs={{0,1},{1,0},{2,3},{3,2},{4,5},{5,4},{6,7},{7,6},{8,9},{9,8},{10,11... | collective-permute-start | bytes 9437192 | tf_op jit(solution)/shard_map/ppermute | solution.py:432
  (14 other events, 304.2 us)

commit v9 on v8

--- a/solution.py
+++ b/solution.py
@@ -69,7 +69,7 @@
 
 
 def coef_rows(comps):
-    return 6 * comps + 2 * SUB
+    return 4 * comps
 
 
 def below(old, first, new):
@@ -136,9 +136,9 @@
     last = 2.0 * last
     c1, c2, c3 = [part.astype(F32) for part in split3(coef)]
     l1, l2, l3 = [part.astype(F32) for part in split3(last)]
-    index = lax.broadcasted_iota(jnp.int32, (2 * SUB, markers), 0)
+    index = lax.broadcasted_iota(jnp.int32, (comps, markers), 0)
     ones = jnp.where(index == 0, l1, jnp.where(index == 1, l2, jnp.where(index == 2, l3, 0.0)))
-    stacked = jnp.concatenate([c1, c1, c2, c2, c1, c3, ones], axis=0).astype(BF16)
+    stacked = jnp.concatenate([c1, c2, c3, ones], axis=0).astype(BF16)
     eye = (
         lax.broadcasted_iota(jnp.int32, (markers, markers), 0)
         == lax.broadcasted_iota(jnp.int32, (markers, markers), 1)
@@ -156,10 +156,19 @@
     )(*parts)
 
 
+def doubled_coef(coef):
+    lanes = coef.shape[1]
+    wide = coef.astype(F32)
+    again = jnp.concatenate([wide[:, lanes // 2 :], wide[:, : lanes // 2]], axis=1)
+    index = lax.broadcasted_iota(jnp.int32, wide.shape, 1)
+    again = jnp.where(index < lanes // 2, wide, jnp.where(index < lanes // 4 * 3, again, 0.0))
+    return jnp.concatenate([coef, again.astype(BF16)], axis=1)
+
+
 def design_parts(x):
     d1, d2, d3 = split3(x)
-    ones = jnp.ones((2 * SUB, x.shape[1]), BF16)
-    return jnp.concatenate([d1, d2, d1, d2, d3, d1, ones], axis=0)
+    ones = jnp.ones(x.shape, BF16)
+    return jnp.concatenate([d1, d1, d1, ones, d2, d2, d3, jnp.zeros(x.shape, BF16)], axis=0)
 
 
 def factors(twice):
@@ -183,25 +192,19 @@
     return jnp.concatenate(dosage, axis=0), jnp.concatenate(present, axis=0)
 
 
-def early_source(plane, rows):
-    return jnp.where(plane == 0, 1, plane - 1)
-
-
-def late_source(plane, rows):
-    return jnp.where(plane == 0, rows - 1, jnp.where(plane == rows - 1, 0, plane + 1))
-
-
 def slot_of(source, plane, rows):
-    slot = lax.rem(plane - source + rows, rows) - 1
-    slot = jnp.where(source == early_source(plane, rows), rows - 2, slot)
-    slot = jnp.where(source == late_source(plane, rows), rows - 1, slot)
-    return jnp.where(source == plane, 0, slot)
+    ahead = lax.rem(source - plane + rows, rows)
+    return jnp.where(lax.rem(plane, 2) == 0, ahead, lax.rem(rows - ahead, rows))
+
+
+def by_even(slot, plane, rows):
+    return jnp.where(lax.rem(plane, 2) == 0, plane < rows - slot, plane >= slot)
 
 
 def early_kernel(rows, near, row_x_ref, col_x_ref, *refs):
-    coef_refs, refs = refs[: rows.bit_length()], refs[rows.bit_length() :]
+    coef_refs, refs = refs[:rows], refs[rows:]
     held_ref, refs = refs[0], refs[1:]
-    from_left, from_right = refs[: rows - 2], refs[rows - 2 : 2 * rows - 4]
+    even, odd = refs[: rows - 2], refs[rows - 2 : 2 * rows - 4]
     piece_refs, refs = refs[2 * rows - 4 : 2 * rows - 4 + near], refs[2 * rows - 4 + near :]
     row_out, col_out, row_fit, col_fit, coef, fit = refs
     chip = coef_refs[0].shape[0]
@@ -215,9 +218,9 @@
     def _():
         if space != chip:
             coef[...] = jnp.zeros(coef.shape, BF16)
-        found = [ref[at : at + chip, :] for ref in coef_refs for at in range(0, ref.shape[0], chip)]
         for e in range(rows):
-            coef[pl.ds(pl.multiple_of(slots[e] * space, space), chip), :] = found[e]
+            place = pl.multiple_of(slots[e] * space, space)
+            coef[pl.ds(place, chip), :] = doubled_coef(coef_refs[e][...])
 
     def fitted(x):
         return lax.dot_general(
@@ -231,11 +234,10 @@
     for slot in range(rows - 1):
         if slot == 0:
             block = held_ref[...]
-        elif slot == rows - 2:
-            block = jnp.where(plane == 0, from_right[0][...], from_left[0][...])
+        elif slot == 1:
+            block = even[0][...]
         else:
-            away = slot + 1
-            block = jnp.where(plane >= away, from_left[away - 1][...], from_right[rows - away - 1][...])
+            block = jnp.where(by_even(slot, plane, rows), even[slot - 1][...], odd[rows - slot - 1][...])
         resid, sdev = weigh(fit_rows[slot * space : slot * space + chip], *parted(block, rows))
         row_out[0, :, slot * space : slot * space + chip] = resid.T
         row_out[1, :, slot * space : slot * space + chip] = sdev.T
@@ -254,7 +256,7 @@
                 col_fit[e] = here
 
 
-def early_call(rows, part, components, col_comps, coefs, held, from_left, from_right, pieces):
+def early_call(rows, part, components, col_comps, coefs, held, even, odd, pieces):
     comps, width = col_comps.shape
     chip = coefs[0].shape[0]
     space = -(-chip // 128) * 128
@@ -273,7 +275,7 @@
                 pl.BlockSpec((comps, wide), lambda i, at: (0, i)),
             ]
             + [pl.BlockSpec(x.shape, whole) for x in coefs]
-            + [block] * (1 + len(from_left) + len(from_right))
+            + [block] * (1 + len(even) + len(odd))
             + [piece] * len(pieces),
             out_specs=(
                 pl.BlockSpec((2, wide, rows * space), lambda i, at: (0, i, 0)),
@@ -282,7 +284,7 @@
                 pl.BlockSpec((rows, height, wide), lambda i, at: (0, 0, i)),
             ),
             scratch_shapes=[
-                pltpu.VMEM((rows * space, coefs[0].shape[1]), BF16),
+                pltpu.VMEM((rows * space, 2 * coefs[0].shape[1]), BF16),
                 pltpu.VMEM((rows * space, wide), F32),
             ],
         ),
@@ -294,29 +296,26 @@
         ),
         compiler_params=pltpu.CompilerParams(vmem_limit_bytes=VMEM_LIMIT),
         name="early",
-    )(part[None].astype(jnp.int32), components, col_comps, *coefs, held, *from_left, *from_right, *pieces)
+    )(part[None].astype(jnp.int32), components, col_comps, *coefs, held, *even, *odd, *pieces)
 
 
 def early_kernel_at(rows, near, part_ref, *refs):
     early_kernel(rows, near, *refs)
 
 
-def late_kernel(rows, group_ref, row_fit, col_fit, left_ref, right_ref, next_ref, piece_ref, *refs):
+def late_kernel(rows, group_ref, row_fit, col_fit, even_ref, odd_ref, piece_ref, *refs):
     row_out, col_out, block, sem = refs[2:]
     plane = lax.axis_index("cols") // (lax.axis_size("cols") // rows)
     step = pl.program_id(0)
-
-    @pl.when((step == 0) & (plane == 0))
+    last = by_even(rows - 1, plane, rows)
+
+    @pl.when((step == 0) & last)
     def _():
-        pltpu.make_async_copy(right_ref, block, sem).start()
-
-    @pl.when((step == 0) & (plane == rows - 1))
+        pltpu.make_async_copy(even_ref, block, sem).start()
+
+    @pl.when((step == 0) & jnp.logical_not(last))
     def _():
-        pltpu.make_async_copy(left_ref, block, sem).start()
-
-    @pl.when((step == 0) & (plane > 0) & (plane < rows - 1))
-    def _():
-        pltpu.make_async_copy(next_ref, block, sem).start()
+        pltpu.make_async_copy(odd_ref, block, sem).start()
 
     resid, sdev = weigh(col_fit[0], *parted(piece_ref[0], 1))
     col_out[0, 0] = resid
@@ -324,7 +323,7 @@
 
     @pl.when(step == rows - 1)
     def _():
-        pltpu.make_async_copy(next_ref, block, sem).wait()
+        pltpu.make_async_copy(odd_ref, block, sem).wait()
         resid, sdev = weigh(row_fit[...], *parted(block[...], rows))
         chip = row_fit.shape[0]
         if row_out.shape[2] != chip:
@@ -333,7 +332,7 @@
         row_out[1, :, 0:chip] = sdev.T
 
 
-def late_call(rows, groups, row_fit, col_fit, left, right, following, piece, row_panel, col_panel):
+def late_call(rows, groups, row_fit, col_fit, even, odd, piece, row_panel, col_panel):
     chip, width = row_fit.shape
     height = chip // rows
     space = row_panel.shape[2] // rows
@@ -346,7 +345,6 @@
             in_specs=[
                 pl.BlockSpec((chip, width), lambda e, at: (0, 0)),
                 pl.BlockSpec((1, height, width), lambda e, at: (e, 0, 0)),
-                anywhere,
                 anywhere,
                 anywhere,
                 pl.BlockSpec((1, 2 * height, width), lambda e, at: (e, 0, 0)),
@@ -363,10 +361,10 @@
             jax.ShapeDtypeStruct(row_panel.shape, BF16),
             jax.ShapeDtypeStruct(col_panel.shape, BF16),
         ),
-        input_output_aliases={7: 0, 8: 1},
+        input_output_aliases={6: 0, 7: 1},
         compiler_params=pltpu.CompilerParams(vmem_limit_bytes=VMEM_LIMIT),
         name="late",
-    )(groups, row_fit, col_fit, left, right, following, piece, row_panel, col_panel)
+    )(groups, row_fit, col_fit, even, odd, piece, row_panel, col_panel)
 
 
 def quotient(numer, denom):
@@ -374,15 +372,18 @@
     return numer * (inverse * (2.0 - denom * inverse))
 
 
-def kin_kernel(part_ref, row_ref, col_ref, *refs):
-    out_ref = refs[-1]
-    count = out_ref.shape[0]
-    step = 512 if count % 512 == 0 else count
-    for at in range(0, count, step):
-        span = slice(at, at + step)
-        numer = jnp.dot(row_ref[0, span, :], col_ref[0], preferred_element_type=F32)
-        denom = jnp.dot(row_ref[1, span, :], col_ref[1], preferred_element_type=F32)
-        out_ref[span, :] = quotient(numer, denom)
+def kin_kernel(part_ref, panel_ref, col_ref, *refs):
+    out_ref, row_ref, sem = refs[-3:]
+
+    @pl.when(pl.program_id(0) == 0)
+    def _():
+        copy = pltpu.make_async_copy(panel_ref, row_ref, sem)
+        copy.start()
+        copy.wait()
+
+    numer = jnp.dot(row_ref[0], col_ref[0], preferred_element_type=F32)
+    denom = jnp.dot(row_ref[1], col_ref[1], preferred_element_type=F32)
+    out_ref[...] = quotient(numer, denom)
 
 
 def kin_call(part, people, row_panel, col_panel, before):
@@ -390,7 +391,7 @@
     width = col_panel.shape[2]
     wide = 256 if width % 256 == 0 else width
     in_specs = [
-        pl.BlockSpec((2, count, depth), lambda i, at: (0, 0, 0)),
+        pl.BlockSpec(memory_space=pl.ANY),
         pl.BlockSpec((2, depth, wide), lambda i, at: (0, 0, i)),
     ]
     operands = [row_panel, col_panel]
@@ -406,6 +407,7 @@
             grid=(width // wide,),
             in_specs=in_specs,
             out_specs=pl.BlockSpec((count, wide), lambda i, at: (at[0], i)),
+            scratch_shapes=[pltpu.VMEM(row_panel.shape, BF16), pltpu.SemaphoreType.DMA],
         ),
         out_shape=jax.ShapeDtypeStruct((people, width), F32),
         input_output_aliases=aliases,
@@ -431,8 +433,10 @@
     def swap(x, k):
         return lax.ppermute(x, "cols", pairs(lambda z, c: (z, (c + k) % ratio))) if k else x
 
-    def along(x, way):
-        return lax.ppermute(x, "cols", pairs(lambda z, c: (z + way, c)))
+    def exchange(x, first):
+        other = [z + 1 if (z - first) % 2 == 0 else z - 1 for z in range(rows)]
+        other = [y if 0 <= y < rows else z for z, y in enumerate(other)]
+        return lax.ppermute(x, "cols", pairs(lambda z, c: (other[z], c)))
 
     def beside(x, d):
         return lax.ppermute(x, "rows", [(i, i ^ d) for i in range(rows)]) if d else x
@@ -461,7 +465,7 @@
         halves.append(swap(jnp.concatenate(both, axis=1).reshape(2 * markers, width), k))
     held = by_core(halves)
     held, dosage, present = lax.optimization_barrier((held, dosage, present))
-    from_left, from_right = [along(held, 1)], [along(held, -1)]
+    even, odd = [exchange(held, 0)], [exchange(held, 1)]
 
     height = held.shape[0] // rows
     quarters = [beside(lax.dynamic_slice_in_dim(held, (row ^ d) * height, height, 0), d) for d in range(rows)]
@@ -477,42 +481,38 @@
         ]
         return jnp.where((row ^ plane) < hop, x, lax.ppermute(x, ("rows", "cols"), moves))
 
-    quarters[1], dosage, present = lax.optimization_barrier((quarters[1], dosage, present))
     gram = gram_call(dosage, present, components)
-    gram = gram + beside(gram, hops[0])
     col_comps = lax.dynamic_slice_in_dim(components, core * width, width, 1)
-    quarters, gram, col_comps, from_left, from_right = lax.optimization_barrier(
-        (jnp.stack(quarters), gram, col_comps, from_left, from_right)
+    quarters, gram, col_comps, held, even, odd = lax.optimization_barrier(
+        (jnp.stack(quarters), gram, col_comps, held, even, odd)
     )
     moved = [
         across(lax.dynamic_index_in_dim(quarters, row ^ plane ^ e, 0, keepdims=False), e) for e in range(rows)
     ]
-    for hop in hops[1:-1]:
+    for hop in hops[:-1]:
         gram = gram + beside(gram, hop)
-    grams = [gram, beside(gram, hops[-1])]
-    for hop in hops:
+    coef = solve_call([gram, beside(gram, hops[-1])], comps, markers)
+    coef = by_core([swap(coef, k) for k in range(ratio)])
+    col_comps = doubled(col_comps, hops[0])
+    moved, coef, col_comps, held, even, odd = lax.optimization_barrier(
+        (jnp.stack(moved), coef, col_comps, held, even, odd)
+    )
+    coefs = [across(coef, e) for e in range(rows)]
+    coefs, even, odd = lax.optimization_barrier((coefs, even, odd))
+    for hop in hops[1:]:
         col_comps = doubled(col_comps, hop)
-    coef = solve_call(grams, comps, markers)
-    coefs = [by_core([swap(coef, k) for k in range(ratio)])]
-    for hop in hops[:-1]:
-        coefs.append(across(coefs[0] if len(coefs) == 1 else jnp.concatenate(coefs, axis=0), hop))
-    moved, coefs, col_comps, held, from_left, from_right = lax.optimization_barrier(
-        (jnp.stack(moved), coefs, col_comps, held, from_left, from_right)
-    )
-    coefs.append(across(jnp.concatenate(coefs, axis=0), hops[-1]))
     near = [moved]
     for step in range(rows - 3):
-        from_left.append(along(from_left[-1], 1))
-        from_right.append(along(from_right[-1], -1))
+        even, odd = even + [exchange(odd[-1], 0)], odd + [exchange(even[-1], 1)]
         upto = rows - 1 if step == rows - 4 else min(rows - 1, 2 * step + 3)
         near += [beside(moved, d) for d in range(len(near), upto)]
-        near, coefs, col_comps, held, from_left, from_right = lax.optimization_barrier(
-            (near, coefs, col_comps, held, from_left, from_right)
+        near, coefs, col_comps, held, even, odd = lax.optimization_barrier(
+            (near, coefs, col_comps, held, even, odd)
         )
-    last_left, last_right = along(from_left[-1], 1), along(from_right[-1], -1)
+    last = exchange(odd[-1], 0)
     far = beside(near[0], rows - 1)
     row_panel, col_panel, row_fit, col_fit = early_call(
-        rows, core, components, col_comps, coefs, held, from_left, from_right, near
+        rows, core, components, col_comps, coefs, held, even, odd, near
     )
     space = row_panel.shape[2] // rows
     groups = jnp.stack(
@@ -522,7 +522,7 @@
         ]
     ).astype(jnp.int32)
     row_panel, col_panel = late_call(
-        rows, groups, row_fit, col_fit, last_left, last_right, from_right[0], far, row_panel, col_panel
+        rows, groups, row_fit, col_fit, last, odd[0], far, row_panel, col_panel
     )
     col_panel = col_panel.reshape(2, rows * space, width)
     out = None

time: 142 us -> 130 us (0.915)
  waiting for transfers between devices: 47.4 us -> 34.7 us
  Pallas kernels: 48.6 us -> 50.1 us
    ppermute x5 -> x6, waiting for transfers between devices: 22.5 us -> 1.44 us  [across(): return lax.ppermute(x, 'cols', pairs(lambda z, c: (z ^ e, c))) if e else x]
    ppermute x2, waiting for transfers between devices: 2.2 us -> 11.6 us  [doubled(): lax.ppermute(x, ('rows', 'cols'), moves)]
    ppermute x8, waiting for transfers between devices: 12.8 us -> 9.43 us  [beside(): lax.ppermute(x, 'rows', [(i, i ^ d) for i in range(rows)])]
    ppermute x6 -> x5, starting transfers between devices: 14.2 us -> 12.2 us  [exchange(): return lax.ppermute(x, 'cols', pairs(lambda z, c: (other[z], c)))]
    pallas_call x2, Pallas kernels: 20.7 us -> 22.4 us  [kin_call(): pl.pallas_call(kin_kernel, grid_spec=pltpu.PrefetchScalarGridSpec(num_sca...]
    ppermute x6 -> x5, waiting for transfers between devices: 8.54 us -> 10 us  [exchange(): return lax.ppermute(x, 'cols', pairs(lambda z, c: (other[z], c)))]
    unnamed x28 -> x32, local copies, waits for them, and re-layouts: 2.37 us -> 3.3 us
    ppermute x5 -> x6, starting transfers between devices: 8.65 us -> 8.9 us  [across(): return lax.ppermute(x, 'cols', pairs(lambda z, c: (z ^ e, c))) if e else x]
  transfers between devices with their start and end apart: 24 -> 24, of which waited for: 10 -> 14; matrix products, arithmetic and copies ran while one was open for 3% -> 1% of each run, Pallas kernels for 23% -> 26%
where the time goes in v9:
time: 130 us; the launch traced here: 129 us
  Pallas kernels  50.1 us (39%)
  starting transfers between devices  36.7 us (28%)
  waiting for transfers between devices  34.7 us (27%)
  other arithmetic  4 us (3%)
  local copies, waits for them, and re-layouts  3.44 us (3%)
    pallas_call x2, Pallas kernels, kin_call(): pl.pallas_call(kin_kernel, grid_spec=pltpu.PrefetchScalarGridSpec(num_sca...  22.4 us
    ppermute x5, starting transfers between devices, exchange(): return lax.ppermute(x, 'cols', pairs(lambda z, c: (other[z], c)))  12.2 us
    ppermute x2, waiting for transfers between devices, doubled(): lax.ppermute(x, ('rows', 'cols'), moves)  11.6 us
    ppermute x5, waiting for transfers between devices, exchange(): return lax.ppermute(x, 'cols', pairs(lambda z, c: (other[z], c)))  10 us
    pallas_call x1, Pallas kernels, early_call(): pl.pallas_call(functools.partial(early_kernel_at, rows, len(pieces)), gri...  9.53 us
    ppermute x8, waiting for transfers between devices, beside(): lax.ppermute(x, 'rows', [(i, i ^ d) for i in range(rows)])  9.43 us
    ppermute x6, starting transfers between devices, across(): return lax.ppermute(x, 'cols', pairs(lambda z, c: (z ^ e, c))) if e else x  8.9 us
    ppermute x8, starting transfers between devices, beside(): lax.ppermute(x, 'rows', [(i, i ^ d) for i in range(rows)])  8.55 us
  transfers between devices with their start and end apart: 24, of which 14 were waited for; matrix products, arithmetic and copies ran while one was open for 1% of the time, Pallas kernels for 26%

profile of v9, /device:TPU:0, one launch (start us, length us, event | category | flops | bytes accessed | tf_op | source)
XLA Modules:
  0.0 129.1 jit_solution(1919006426802518523)
XLA Ops:
  4.3 5.8 %collective-permute-start.4 = (bf16[256,1536]{1,0:T(8,128)(2,1)S(1)}, bf16[256,1536]{1,0:T(8,128)(2,1)S(1)}, u32[]{:S(2)}, u32[]{:S(2)}) collective-permute-start(bf16[256,1536]{1,0:T(8,128)(2,1)S(1)} %pad_maximum_fusion.refs_6_), channel_id=1, source_target_pairs={{0,2},{1,3},{2,0},{3,1},{4,6},{5,7},{6,4},{7,5},{8,10},{9,11},{10,... | collective-permute-start | bytes 2359304 | tf_op jit(solution)/shard_map/ppermute | solution.py:439
  10.1 2.5 %collective-permute-start.3 = (bf16[64,1536]{1,0:T(8,128)(2,1)S(1)}, bf16[64,1536]{1,0:T(8,128)(2,1)S(1)}, u32[]{:S(2)}, u32[]{:S(2)}) collective-permute-start(bf16[64,1536]{1,0:T(8,128)(2,1)S(1)} %get-tuple-element.90), channel_id=1, source_target_pairs={{0,24},{8,16},{16,8},{24,0},{1,25},{9,17},{17,9},{25,1},{2,26},{10... | collective-permute-start | bytes 589832 | tf_op jit(solution)/shard_map/ppermute | solution.py:442
  13.7 5.6 %gram.1 = f32[360,128]{1,0:T(8,128)} custom-call(s32[64,3072]{1,0:T(8,128)} %dosage_ref, s32[64,3072]{1,0:T(8,128)} %present_ref, f32[32,3072]{1,0:T(8,128)} %refs_0_.1), custom_call_target="tpu_custom_call" | custom-call | tf_op jit(solution)/shard_map/gram/pallas_call | solution.py:62
  19.3 2.3 %collective-permute-done.2 = bf16[64,1536]{1,0:T(8,128)(2,1)S(1)} collective-permute-done((bf16[64,1536]{1,0:T(8,128)(2,1)S(1)}, bf16[64,1536]{1,0:T(8,128)(2,1)S(1)}, u32[]{:S(2)}, u32[]{:S(2)}) %collective-permute-start.2) | collective-permute-done | bytes 196640 | tf_op jit(solution)/shard_map/ppermute | solution.py:442
  21.9 5.7 %collective-permute-done.4.refs_7_ = bf16[256,1536]{1,0:T(8,128)(2,1)S(1)} collective-permute-done((bf16[256,1536]{1,0:T(8,128)(2,1)S(1)}, bf16[256,1536]{1,0:T(8,128)(2,1)S(1)}, u32[]{:S(2)}, u32[]{:S(2)}) %collective-permute-start.4) | collective-permute-done | bytes 786464 | tf_op jit(solution)/shard_map/ppermute | solution.py:439
  29.1 2.4 %collective-permute-start.12 = (f32[32,1536]{1,0:T(8,128)S(1)}, f32[32,1536]{1,0:T(8,128)S(1)}, u32[]{:S(2)}, u32[]{:S(2)}) collective-permute-start(f32[32,1536]{1,0:T(8,128)S(1)} %constant_dynamic-slice_fusion.1), channel_id=1, source_target_pairs={{0,8},{1,9},{10,2},{11,3},{20,28},{21,29},{30,22},{31,23}} | collective-permute-start | bytes 589832 | tf_op jit(solution)/shard_map/ppermute | solution.py:482
  31.7 2.0 %collective-permute-start.7 = (bf16[64,1536]{1,0:T(8,128)(2,1)S(1)}, bf16[64,1536]{1,0:T(8,128)(2,1)S(1)}, u32[]{:S(2)}, u32[]{:S(2)}) collective-permute-start(bf16[64,1536]{1,0:T(8,128)(2,1)S(1)} %get-tuple-element.87), channel_id=1, source_target_pairs={{0,4},{1,5},{2,6},{3,7},{4,0},{5,1},{6,2},{7,3},{8,12},{9,13},{10,... | collective-permute-start | bytes 589832 | tf_op jit(solution)/shard_map/ppermute | solution.py:445
  33.7 2.3 %collective-permute-start.6 = (bf16[64,1536]{1,0:T(8,128)(2,1)S(1)}, bf16[64,1536]{1,0:T(8,128)(2,1)S(1)}, u32[]{:S(2)}, u32[]{:S(2)}) collective-permute-start(bf16[64,1536]{1,0:T(8,128)(2,1)S(1)} %get-tuple-element.88), channel_id=1, source_target_pairs={{0,2},{1,3},{2,0},{3,1},{4,6},{5,7},{6,4},{7,5},{8,10},{9,11},{10,... | collective-permute-start | bytes 589832 | tf_op jit(solution)/shard_map/ppermute | solution.py:445
  36.9 4.8 %collective-permute-done.10.refs_1_ = f32[360,128]{1,0:T(8,128)S(1)} collective-permute-done((f32[360,128]{1,0:T(8,128)S(1)}, f32[360,128]{1,0:T(8,128)S(1)}, u32[]{:S(2)}, u32[]{:S(2)}) %collective-permute-start.10) | collective-permute-done | bytes 184352 | tf_op jit(solution)/shard_map/ppermute | solution.py:442
  42.4 7.1 %solve.1 = bf16[64,128]{1,0:T(8,128)(2,1)} custom-call(f32[360,128]{1,0:T(8,128)} %copy-done.10, f32[360,128]{1,0:T(8,128)} %copy-done.11), custom_call_target="tpu_custom_call" | custom-call | tf_op jit(solution)/shard_map/solve/pallas_call | solution.py:151
  53.3 2.8 %collective-permute-start.15 = (bf16[128,128]{1,0:T(8,128)(2,1)S(1)}, bf16[128,128]{1,0:T(8,128)(2,1)S(1)}, u32[]{:S(2)}, u32[]{:S(2)}) collective-permute-start(bf16[128,128]{1,0:T(8,128)(2,1)S(1)} %pad_maximum_fusion.5.refs_2_), channel_id=1, source_target_pairs={{0,2},{1,3},{2,0},{3,1},{4,6},{5,7},{6,4},{7,5},{8,10},{9,11},{10,... | collective-permute-start | bytes 98312 | tf_op jit(solution)/shard_map/ppermute | solution.py:445
  58.0 1.6 %collective-permute-start.20 = (bf16[256,1536]{1,0:T(8,128)(2,1)S(1)}, bf16[256,1536]{1,0:T(8,128)(2,1)}, u32[]{:S(2)}, u32[]{:S(2)}) collective-permute-start(bf16[256,1536]{1,0:T(8,128)(2,1)S(1)} %collective-permute-done.4.refs_7_), channel_id=1, source_target_pairs={{0,0},{1,1},{2,4},{3,5},{4,2},{5,3},{6,6},{7,7},{8,8},{9,9},{10,12... | collective-permute-start | bytes 2359304 | tf_op jit(solution)/shard_map/ppermute | solution.py:439
  59.7 2.4 %collective-permute-start.19 = (bf16[256,1536]{1,0:T(8,128)(2,1)S(1)}, bf16[256,1536]{1,0:T(8,128)(2,1)}, u32[]{:S(2)}, u32[]{:S(2)}) collective-permute-start(bf16[256,1536]{1,0:T(8,128)(2,1)S(1)} %collective-permute-done.5.refs_9_.odd_ref), channel_id=1, source_target_pairs={{0,2},{1,3},{2,0},{3,1},{4,6},{5,7},{6,4},{7,5},{8,10},{9,11},{10,... | collective-permute-start | bytes 2359304 | tf_op jit(solution)/shard_map/ppermute | solution.py:439
  62.0 3.9 %collective-permute-start.18 = (f32[32,1536]{1,0:T(8,128)S(1)}, f32[32,1536]{1,0:T(8,128)S(1)}, u32[]{:S(2)}, u32[]{:S(2)}) collective-permute-start(f32[32,1536]{1,0:T(8,128)S(1)} %broadcast_select_fusion.1), channel_id=1, source_target_pairs={{0,16},{1,17},{8,24},{9,25},{2,18},{3,19},{10,26},{11,27},{20,4},{... | collective-permute-start | bytes 589832 | tf_op jit(solution)/shard_map/ppermute | solution.py:482
  66.0 10.9 %collective-permute-done.18 = f32[32,1536]{1,0:T(8,128)S(1)} collective-permute-done((f32[32,1536]{1,0:T(8,128)S(1)}, f32[32,1536]{1,0:T(8,128)S(1)}, u32[]{:S(2)}, u32[]{:S(2)}) %collective-permute-start.18) | collective-permute-done | bytes 196640 | tf_op jit(solution)/shard_map/ppermute | solution.py:482
  78.5 1.7 %collective-permute-start.21 = (bf16[256,1536]{1,0:T(8,128)(2,1)}, bf16[256,1536]{1,0:T(8,128)(2,1)S(1)}, u32[]{:S(2)}, u32[]{:S(2)}) collective-permute-start(bf16[256,1536]{1,0:T(8,128)(2,1)} %collective-permute-done.20.refs_10_), channel_id=1, source_target_pairs={{0,2},{1,3},{2,0},{3,1},{4,6},{5,7},{6,4},{7,5},{8,10},{9,11},{10,... | collective-permute-start | bytes 2359304 | tf_op jit(solution)/shard_map/ppermute | solution.py:439
  80.3 2.6 %collective-permute-start.22 = (bf16[4,64,1536]{2,1,0:T(8,128)(2,1)S(1)}, bf16[4,64,1536]{2,1,0:T(8,128)(2,1)S(1)}, u32[]{:S(2)}, u32[]{:S(2)}) collective-permute-start(bf16[4,64,1536]{2,1,0:T(8,128)(2,1)S(1)} %pad_maximum_fusion.2.refs_11_), channel_id=1, source_target_pairs={{0,24},{8,16},{16,8},{24,0},{1,25},{9,17},{17,9},{25,1},{2,26},{10... | collective-permute-start | bytes 2359304 | tf_op jit(solution)/shard_map/ppermute | solution.py:442
  83.6 9.5 %early.1 = (bf16[2,1536,512]{2,1,0:T(8,128)(2,1)}, bf16[2,16,32,1536]{3,2,1,0:T(8,128)(2,1)}, f32[128,1536]{1,0:T(8,128)}, f32[4,32,1536]{2,1,0:T(8,128)}) custom-call(s32[1]{0:T(128)} %bitcast.5.part_ref, f32[32,3072]{1,0:T(8,128)} %refs_0_.1, f32[32,1536]{1,0:T(8,128)} %broadcast_select_fusion.refs_1_, bf16[128,128]{1,0:T(8,128)(2,1)} %copy-done.12, ...), custom_call_target="tpu_custom_call" | custom-call | tf_op jit(solution)/shard_map/early/pallas_call | solution.py:268
  93.1 3.4 %collective-permute-done.21.even_ref = bf16[256,1536]{1,0:T(8,128)(2,1)S(1)} collective-permute-done((bf16[256,1536]{1,0:T(8,128)(2,1)}, bf16[256,1536]{1,0:T(8,128)(2,1)S(1)}, u32[]{:S(2)}, u32[]{:S(2)}) %collective-permute-start.21) | collective-permute-done | bytes 786464 | tf_op jit(solution)/shard_map/ppermute | solution.py:439
  96.5 2.2 %collective-permute-done.22.piece_ref = bf16[4,64,1536]{2,1,0:T(8,128)(2,1)S(1)} collective-permute-done((bf16[4,64,1536]{2,1,0:T(8,128)(2,1)S(1)}, bf16[4,64,1536]{2,1,0:T(8,128)(2,1)S(1)}, u32[]{:S(2)}, u32[]{:S(2)}) %collective-permute-start.22) | collective-permute-done | bytes 786464 | tf_op jit(solution)/shard_map/ppermute | solution.py:442
  99.6 5.4 %late.1 = (bf16[2,1536,512]{2,1,0:T(8,128)(2,1)}, bf16[2,16,32,1536]{3,2,1,0:T(8,128)(2,1)}) custom-call(s32[4]{0:T(128)} %pad_add_fusion.group_ref, f32[128,1536]{1,0:T(8,128)} %get-tuple-element.79.row_fit, f32[4,32,1536]{2,1,0:T(8,128)} %get-tuple-element.80.col_fit, bf16[256,1536]{1,0:T(8,128)(2,1)} %copy-done.5, ...), custom_call_target="tpu_custom_call", output_to_operand_aliasing={{0}: (6, {}), {1}: (7, {})} | custom-call | tf_op jit(solution)/shard_map/late/pallas_call | solution.py:340
  105.0 11.2 %kinship.2.refs_0_ = f32[3072,1536]{1,0:T(8,128)} custom-call(s32[1]{0:T(128)} %bitcast.27.part_ref, bf16[2,1536,512]{2,1,0:T(8,128)(2,1)} %get-tuple-element.83.panel_ref, bf16[2,512,1536]{2,1,0:T(8,128)(2,1)} %bitcast.38), custom_call_target="tpu_custom_call" | custom-call | tf_op jit(solution)/shard_map/kinship/pallas_call | solution.py:403
  116.3 1.6 %copy-done.1 = bf16[2,1536,512]{2,1,0:T(8,128)(2,1)} copy-done((bf16[2,1536,512]{2,1,0:T(8,128)(2,1)}, bf16[2,1536,512]{2,1,0:T(8,128)(2,1)S(1)}, u32[]{:S(2)}) %copy-start.1) | copy-done | bytes 3145752
  117.9 11.2 %kinship.3 = f32[3072,1536]{1,0:T(8,128)} custom-call(s32[1]{0:T(128)} %bitcast.part_ref, bf16[2,1536,512]{2,1,0:T(8,128)(2,1)} %copy-done.1, bf16[2,512,1536]{2,1,0:T(8,128)(2,1)} %bitcast.39, f32[3072,1536]{1,0:T(8,128)} %kinship.2.refs_0_), custom_call_target="tpu_custom_call", output_to_operand_aliasing={{}: (3, {})} | custom-call | tf_op jit(solution)/shard_map/kinship/pallas_call | solution.py:403
  (78 shorter events, 17.6 us)
Async XLA Ops:
  1.5 1.9 %collective-permute-start = (bf16[128,1536]{1,0:T(8,128)(2,1)S(1)}, bf16[128,1536]{1,0:T(8,128)(2,1)S(1)}, u32[]{:S(2)}, u32[]{:S(2)}) collective-permute-start(bf16[128,1536]{1,0:T(8,128)(2,1)S(1)} %bitcast.44), channel_id=1, source_target_pairs={{0,1},{1,0},{2,3},{3,2},{4,5},{5,4},{6,7},{7,6},{8,9},{9,8},{10,11... | collective-permute-start | bytes 1179656 | tf_op jit(solution)/shard_map/ppermute | solution.py:434
  3.5 18.3 %collective-permute-start.5 = (bf16[256,1536]{1,0:T(8,128)(2,1)S(1)}, bf16[256,1536]{1,0:T(8,128)(2,1)S(1)}, u32[]{:S(2)}, u32[]{:S(2)}) collective-permute-start(bf16[256,1536]{1,0:T(8,128)(2,1)S(1)} %pad_maximum_fusion.refs_6_), channel_id=1, source_target_pairs={{0,0},{1,1},{2,4},{3,5},{4,2},{5,3},{6,6},{7,7},{8,8},{9,9},{10,12... | collective-permute-start | bytes 2359304 | tf_op jit(solution)/shard_map/ppermute | solution.py:439
  4.3 23.3 %collective-permute-start.4 = (bf16[256,1536]{1,0:T(8,128)(2,1)S(1)}, bf16[256,1536]{1,0:T(8,128)(2,1)S(1)}, u32[]{:S(2)}, u32[]{:S(2)}) collective-permute-start(bf16[256,1536]{1,0:T(8,128)(2,1)S(1)} %pad_maximum_fusion.refs_6_), channel_id=1, source_target_pairs={{0,2},{1,3},{2,0},{3,1},{4,6},{5,7},{6,4},{7,5},{8,10},{9,11},{10,... | collective-permute-start | bytes 2359304 | tf_op jit(solution)/shard_map/ppermute | solution.py:439
  10.1 9.2 %collective-permute-start.3 = (bf16[64,1536]{1,0:T(8,128)(2,1)S(1)}, bf16[64,1536]{1,0:T(8,128)(2,1)S(1)}, u32[]{:S(2)}, u32[]{:S(2)}) collective-permute-start(bf16[64,1536]{1,0:T(8,128)(2,1)S(1)} %get-tuple-element.90), channel_id=1, source_target_pairs={{0,24},{8,16},{16,8},{24,0},{1,25},{9,17},{17,9},{25,1},{2,26},{10... | collective-permute-start | bytes 589832 | tf_op jit(solution)/shard_map/ppermute | solution.py:442
  12.6 9.0 %collective-permute-start.2 = (bf16[64,1536]{1,0:T(8,128)(2,1)S(1)}, bf16[64,1536]{1,0:T(8,128)(2,1)S(1)}, u32[]{:S(2)}, u32[]{:S(2)}) collective-permute-start(bf16[64,1536]{1,0:T(8,128)(2,1)S(1)} %get-tuple-element.91), channel_id=1, source_target_pairs={{0,16},{8,24},{16,0},{24,8},{1,17},{9,25},{17,1},{25,9},{2,18},{10... | collective-permute-start | bytes 589832 | tf_op jit(solution)/shard_map/ppermute | solution.py:442
  13.1 8.6 %collective-permute-start.1 = (bf16[64,1536]{1,0:T(8,128)(2,1)S(1)}, bf16[64,1536]{1,0:T(8,128)(2,1)S(1)}, u32[]{:S(2)}, u32[]{:S(2)}) collective-permute-start(bf16[64,1536]{1,0:T(8,128)(2,1)S(1)} %get-tuple-element.92), channel_id=1, source_target_pairs={{0,8},{8,0},{16,24},{24,16},{1,9},{9,1},{17,25},{25,17},{2,10},{10... | collective-permute-start | bytes 589832 | tf_op jit(solution)/shard_map/ppermute | solution.py:442
  27.6 8.5 %collective-permute-start.9 = (f32[360,128]{1,0:T(8,128)}, f32[360,128]{1,0:T(8,128)S(1)}, u32[]{:S(2)}, u32[]{:S(2)}) collective-permute-start(f32[360,128]{1,0:T(8,128)} %gram.1), channel_id=1, source_target_pairs={{0,8},{8,0},{16,24},{24,16},{1,9},{9,1},{17,25},{25,17},{2,10},{10... | collective-permute-start | bytes 552968 | tf_op jit(solution)/shard_map/ppermute | solution.py:442
  29.1 7.8 %collective-permute-start.12 = (f32[32,1536]{1,0:T(8,128)S(1)}, f32[32,1536]{1,0:T(8,128)S(1)}, u32[]{:S(2)}, u32[]{:S(2)}) collective-permute-start(f32[32,1536]{1,0:T(8,128)S(1)} %constant_dynamic-slice_fusion.1), channel_id=1, source_target_pairs={{0,8},{1,9},{10,2},{11,3},{20,28},{21,29},{30,22},{31,23}} | collective-permute-start | bytes 589832 | tf_op jit(solution)/shard_map/ppermute | solution.py:482
  31.6 17.9 %collective-permute-start.8 = (bf16[64,1536]{1,0:T(8,128)(2,1)S(1)}, bf16[64,1536]{1,0:T(8,128)(2,1)S(1)}, u32[]{:S(2)}, u32[]{:S(2)}) collective-permute-start(bf16[64,1536]{1,0:T(8,128)(2,1)S(1)} %get-tuple-element.86), channel_id=1, source_target_pairs={{0,6},{1,7},{2,4},{3,5},{4,2},{5,3},{6,0},{7,1},{8,14},{9,15},{10,... | collective-permute-start | bytes 589832 | tf_op jit(solution)/shard_map/ppermute | solution.py:445
  31.7 18.2 %collective-permute-start.7 = (bf16[64,1536]{1,0:T(8,128)(2,1)S(1)}, bf16[64,1536]{1,0:T(8,128)(2,1)S(1)}, u32[]{:S(2)}, u32[]{:S(2)}) collective-permute-start(bf16[64,1536]{1,0:T(8,128)(2,1)S(1)} %get-tuple-element.87), channel_id=1, source_target_pairs={{0,4},{1,5},{2,6},{3,7},{4,0},{5,1},{6,2},{7,3},{8,12},{9,13},{10,... | collective-permute-start | bytes 589832 | tf_op jit(solution)/shard_map/ppermute | solution.py:445
  33.7 16.1 %collective-permute-start.6 = (bf16[64,1536]{1,0:T(8,128)(2,1)S(1)}, bf16[64,1536]{1,0:T(8,128)(2,1)S(1)}, u32[]{:S(2)}, u32[]{:S(2)}) collective-permute-start(bf16[64,1536]{1,0:T(8,128)(2,1)S(1)} %get-tuple-element.88), channel_id=1, source_target_pairs={{0,2},{1,3},{2,0},{3,1},{4,6},{5,7},{6,4},{7,5},{8,10},{9,11},{10,... | collective-permute-start | bytes 589832 | tf_op jit(solution)/shard_map/ppermute | solution.py:445
  36.1 5.6 %collective-permute-start.10 = (f32[360,128]{1,0:T(8,128)S(1)}, f32[360,128]{1,0:T(8,128)S(1)}, u32[]{:S(2)}, u32[]{:S(2)}) collective-permute-start(f32[360,128]{1,0:T(8,128)S(1)} %add.109.refs_0_), channel_id=1, source_target_pairs={{0,16},{8,24},{16,0},{24,8},{1,17},{9,25},{17,1},{25,9},{2,18},{10... | collective-permute-start | bytes 552968 | tf_op jit(solution)/shard_map/ppermute | solution.py:442
  49.5 1.4 %collective-permute-start.11 = (bf16[64,128]{1,0:T(8,128)(2,1)}, bf16[64,128]{1,0:T(8,128)(2,1)S(1)}, u32[]{:S(2)}, u32[]{:S(2)}) collective-permute-start(bf16[64,128]{1,0:T(8,128)(2,1)} %solve.1), channel_id=1, source_target_pairs={{0,1},{1,0},{2,3},{3,2},{4,5},{5,4},{6,7},{7,6},{8,9},{9,8},{10,11... | collective-permute-start | bytes 49160 | tf_op jit(solution)/shard_map/ppermute | solution.py:434
  51.6 6.0 %collective-permute-start.17 = (bf16[128,128]{1,0:T(8,128)(2,1)S(1)}, bf16[128,128]{1,0:T(8,128)(2,1)S(1)}, u32[]{:S(2)}, u32[]{:S(2)}) collective-permute-start(bf16[128,128]{1,0:T(8,128)(2,1)S(1)} %pad_maximum_fusion.5.refs_2_), channel_id=1, source_target_pairs={{0,6},{1,7},{2,4},{3,5},{4,2},{5,3},{6,0},{7,1},{8,14},{9,15},{10,... | collective-permute-start | bytes 98312 | tf_op jit(solution)/shard_map/ppermute | solution.py:445
  52.0 5.6 %collective-permute-start.16 = (bf16[128,128]{1,0:T(8,128)(2,1)S(1)}, bf16[128,128]{1,0:T(8,128)(2,1)S(1)}, u32[]{:S(2)}, u32[]{:S(2)}) collective-permute-start(bf16[128,128]{1,0:T(8,128)(2,1)S(1)} %pad_maximum_fusion.5.refs_2_), channel_id=1, source_target_pairs={{0,4},{1,5},{2,6},{3,7},{4,0},{5,1},{6,2},{7,3},{8,12},{9,13},{10,... | collective-permute-start | bytes 98312 | tf_op jit(solution)/shard_map/ppermute | solution.py:445
  53.3 4.7 %collective-permute-start.15 = (bf16[128,128]{1,0:T(8,128)(2,1)S(1)}, bf16[128,128]{1,0:T(8,128)(2,1)S(1)}, u32[]{:S(2)}, u32[]{:S(2)}) collective-permute-start(bf16[128,128]{1,0:T(8,128)(2,1)S(1)} %pad_maximum_fusion.5.refs_2_), channel_id=1, source_target_pairs={{0,2},{1,3},{2,0},{3,1},{4,6},{5,7},{6,4},{7,5},{8,10},{9,11},{10,... | collective-permute-start | bytes 98312 | tf_op jit(solution)/shard_map/ppermute | solution.py:445
  56.1 21.5 %collective-permute-start.14 = (bf16[4,64,1536]{2,1,0:T(8,128)(2,1)S(1)}, bf16[4,64,1536]{2,1,0:T(8,128)(2,1)S(1)}, u32[]{:S(2)}, u32[]{:S(2)}) collective-permute-start(bf16[4,64,1536]{2,1,0:T(8,128)(2,1)S(1)} %pad_maximum_fusion.2.refs_11_), channel_id=1, source_target_pairs={{0,16},{8,24},{16,0},{24,8},{1,17},{9,25},{17,1},{25,9},{2,18},{10... | collective-permute-start | bytes 2359304 | tf_op jit(solution)/shard_map/ppermute | solution.py:442
  56.5 21.1 %collective-permute-start.13 = (bf16[4,64,1536]{2,1,0:T(8,128)(2,1)S(1)}, bf16[4,64,1536]{2,1,0:T(8,128)(2,1)}, u32[]{:S(2)}, u32[]{:S(2)}) collective-permute-start(bf16[4,64,1536]{2,1,0:T(8,128)(2,1)S(1)} %pad_maximum_fusion.2.refs_11_), channel_id=1, source_target_pairs={{0,8},{8,0},{16,24},{24,16},{1,9},{9,1},{17,25},{25,17},{2,10},{10... | collective-permute-start | bytes 2359304 | tf_op jit(solution)/shard_map/ppermute | solution.py:442
  58.0 19.6 %collective-permute-start.20 = (bf16[256,1536]{1,0:T(8,128)(2,1)S(1)}, bf16[256,1536]{1,0:T(8,128)(2,1)}, u32[]{:S(2)}, u32[]{:S(2)}) collective-permute-start(bf16[256,1536]{1,0:T(8,128)(2,1)S(1)} %collective-permute-done.4.refs_7_), channel_id=1, source_target_pairs={{0,0},{1,1},{2,4},{3,5},{4,2},{5,3},{6,6},{7,7},{8,8},{9,9},{10,12... | collective-permute-start | bytes 2359304 | tf_op jit(solution)/shard_map/ppermute | solution.py:439
  59.7 18.9 %collective-permute-start.19 = (bf16[256,1536]{1,0:T(8,128)(2,1)S(1)}, bf16[256,1536]{1,0:T(8,128)(2,1)}, u32[]{:S(2)}, u32[]{:S(2)}) collective-permute-start(bf16[256,1536]{1,0:T(8,128)(2,1)S(1)} %collective-permute-done.5.refs_9_.odd_ref), channel_id=1, source_target_pairs={{0,2},{1,3},{2,0},{3,1},{4,6},{5,7},{6,4},{7,5},{8,10},{9,11},{10,... | collective-permute-start | bytes 2359304 | tf_op jit(solution)/shard_map/ppermute | solution.py:439
  62.0 14.8 %collective-permute-start.18 = (f32[32,1536]{1,0:T(8,128)S(1)}, f32[32,1536]{1,0:T(8,128)S(1)}, u32[]{:S(2)}, u32[]{:S(2)}) collective-permute-start(f32[32,1536]{1,0:T(8,128)S(1)} %broadcast_select_fusion.1), channel_id=1, source_target_pairs={{0,16},{1,17},{8,24},{9,25},{2,18},{3,19},{10,26},{11,27},{20,4},{... | collective-permute-start | bytes 589832 | tf_op jit(solution)/shard_map/ppermute | solution.py:482
  78.5 17.9 %collective-permute-start.21 = (bf16[256,1536]{1,0:T(8,128)(2,1)}, bf16[256,1536]{1,0:T(8,128)(2,1)S(1)}, u32[]{:S(2)}, u32[]{:S(2)}) collective-permute-start(bf16[256,1536]{1,0:T(8,128)(2,1)} %collective-permute-done.20.refs_10_), channel_id=1, source_target_pairs={{0,2},{1,3},{2,0},{3,1},{4,6},{5,7},{6,4},{7,5},{8,10},{9,11},{10,... | collective-permute-start | bytes 2359304 | tf_op jit(solution)/shard_map/ppermute | solution.py:439
  80.3 18.4 %collective-permute-start.22 = (bf16[4,64,1536]{2,1,0:T(8,128)(2,1)S(1)}, bf16[4,64,1536]{2,1,0:T(8,128)(2,1)S(1)}, u32[]{:S(2)}, u32[]{:S(2)}) collective-permute-start(bf16[4,64,1536]{2,1,0:T(8,128)(2,1)S(1)} %pad_maximum_fusion.2.refs_11_), channel_id=1, source_target_pairs={{0,24},{8,16},{16,8},{24,0},{1,25},{9,17},{17,9},{25,1},{2,26},{10... | collective-permute-start | bytes 2359304 | tf_op jit(solution)/shard_map/ppermute | solution.py:442
  105.0 11.3 %collective-permute-start.23 = (bf16[2,1536,512]{2,1,0:T(8,128)(2,1)}, bf16[2,1536,512]{2,1,0:T(8,128)(2,1)S(1)}, u32[]{:S(2)}, u32[]{:S(2)}) collective-permute-start(bf16[2,1536,512]{2,1,0:T(8,128)(2,1)} %get-tuple-element.83.panel_ref), channel_id=1, source_target_pairs={{0,1},{1,0},{2,3},{3,2},{4,5},{5,4},{6,7},{7,6},{8,9},{9,8},{10,11... | collective-permute-start | bytes 9437192 | tf_op jit(solution)/shard_map/ppermute | solution.py:434
  (16 other events, 228.0 us)

commit v10 on v9

--- a/solution.py
+++ b/solution.py
@@ -179,7 +179,7 @@
 
 def weigh(fitted, dosage, observed):
     twice, spread = factors(fitted)
-    return (observed * (dosage - twice)).astype(BF16), (observed * spread).astype(BF16)
+    return observed * (dosage - twice), observed * spread
 
 
 def parted(block, groups):
@@ -239,8 +239,8 @@
         else:
             block = jnp.where(by_even(slot, plane, rows), even[slot - 1][...], odd[rows - slot - 1][...])
         resid, sdev = weigh(fit_rows[slot * space : slot * space + chip], *parted(block, rows))
-        row_out[0, :, slot * space : slot * space + chip] = resid.T
-        row_out[1, :, slot * space : slot * space + chip] = sdev.T
+        row_out[0, :, slot * space : slot * space + chip] = resid.astype(BF16).T
+        row_out[1, :, slot * space : slot * space + chip] = sdev.astype(BF16).T
     row_fit[...] = fit_rows[(rows - 1) * space : (rows - 1) * space + chip]
     fit[...] = fitted(col_x_ref[...])
     for d in range(rows):
@@ -250,8 +250,8 @@
             if d < near:
                 resid, sdev = weigh(here, *parted(piece_refs[d][e], 1))
                 group = slots[e] * (space // height) + (row ^ d)
-                col_out[0, group] = resid
-                col_out[1, group] = sdev
+                col_out[0, group] = resid.astype(BF16)
+                col_out[1, group] = sdev.astype(BF16)
             else:
                 col_fit[e] = here
 
@@ -318,8 +318,8 @@
         pltpu.make_async_copy(odd_ref, block, sem).start()
 
     resid, sdev = weigh(col_fit[0], *parted(piece_ref[0], 1))
-    col_out[0, 0] = resid
-    col_out[1, 0] = sdev
+    col_out[0, 0] = resid.astype(BF16)
+    col_out[1, 0] = sdev.astype(BF16)
 
     @pl.when(step == rows - 1)
     def _():
@@ -328,8 +328,8 @@
         chip = row_fit.shape[0]
         if row_out.shape[2] != chip:
             row_out[...] = jnp.zeros(row_out.shape, BF16)
-        row_out[0, :, 0:chip] = resid.T
-        row_out[1, :, 0:chip] = sdev.T
+        row_out[0, :, 0:chip] = resid.T.astype(BF16)
+        row_out[1, :, 0:chip] = sdev.T.astype(BF16)
 
 
 def late_call(rows, groups, row_fit, col_fit, even, odd, piece, row_panel, col_panel):
@@ -372,15 +372,8 @@
     return numer * (inverse * (2.0 - denom * inverse))
 
 
-def kin_kernel(part_ref, panel_ref, col_ref, *refs):
-    out_ref, row_ref, sem = refs[-3:]
-
-    @pl.when(pl.program_id(0) == 0)
-    def _():
-        copy = pltpu.make_async_copy(panel_ref, row_ref, sem)
-        copy.start()
-        copy.wait()
-
+def kin_kernel(part_ref, row_ref, col_ref, *refs):
+    out_ref = refs[-1]
     numer = jnp.dot(row_ref[0], col_ref[0], preferred_element_type=F32)
     denom = jnp.dot(row_ref[1], col_ref[1], preferred_element_type=F32)
     out_ref[...] = quotient(numer, denom)
@@ -389,9 +382,9 @@
 def kin_call(part, people, row_panel, col_panel, before):
     _, count, depth = row_panel.shape
     width = col_panel.shape[2]
-    wide = 256 if width % 256 == 0 else width
+    wide = 512 if width % 512 == 0 else width
     in_specs = [
-        pl.BlockSpec(memory_space=pl.ANY),
+        pl.BlockSpec((2, count, depth), lambda i, at: (0, 0, 0)),
         pl.BlockSpec((2, depth, wide), lambda i, at: (0, 0, i)),
     ]
     operands = [row_panel, col_panel]
@@ -407,7 +400,6 @@
             grid=(width // wide,),
             in_specs=in_specs,
             out_specs=pl.BlockSpec((count, wide), lambda i, at: (at[0], i)),
-            scratch_shapes=[pltpu.VMEM(row_panel.shape, BF16), pltpu.SemaphoreType.DMA],
         ),
         out_shape=jax.ShapeDtypeStruct((people, width), F32),
         input_output_aliases=aliases,
@@ -465,7 +457,8 @@
         halves.append(swap(jnp.concatenate(both, axis=1).reshape(2 * markers, width), k))
     held = by_core(halves)
     held, dosage, present = lax.optimization_barrier((held, dosage, present))
-    even, odd = [exchange(held, 0)], [exchange(held, 1)]
+    odd = [exchange(held, 1)]
+    even = [exchange(held, 0)]
 
     height = held.shape[0] // rows
     quarters = [beside(lax.dynamic_slice_in_dim(held, (row ^ d) * height, height, 0), d) for d in range(rows)]
@@ -482,20 +475,22 @@
         return jnp.where((row ^ plane) < hop, x, lax.ppermute(x, ("rows", "cols"), moves))
 
     gram = gram_call(dosage, present, components)
+    quarters, gram = lax.optimization_barrier((quarters, gram))
+    gram = gram + beside(gram, hops[0])
     col_comps = lax.dynamic_slice_in_dim(components, core * width, width, 1)
-    quarters, gram, col_comps, held, even, odd = lax.optimization_barrier(
-        (jnp.stack(quarters), gram, col_comps, held, even, odd)
+    quarters, gram, col_comps, held, odd, even = lax.optimization_barrier(
+        (jnp.stack(quarters), gram, col_comps, held, odd, even)
     )
     moved = [
         across(lax.dynamic_index_in_dim(quarters, row ^ plane ^ e, 0, keepdims=False), e) for e in range(rows)
     ]
-    for hop in hops[:-1]:
+    for hop in hops[1:-1]:
         gram = gram + beside(gram, hop)
     coef = solve_call([gram, beside(gram, hops[-1])], comps, markers)
     coef = by_core([swap(coef, k) for k in range(ratio)])
     col_comps = doubled(col_comps, hops[0])
-    moved, coef, col_comps, held, even, odd = lax.optimization_barrier(
-        (jnp.stack(moved), coef, col_comps, held, even, odd)
+    moved, coef, col_comps, held, odd, even = lax.optimization_barrier(
+        (jnp.stack(moved), coef, col_comps, held, odd, even)
     )
     coefs = [across(coef, e) for e in range(rows)]
     coefs, even, odd = lax.optimization_barrier((coefs, even, odd))
@@ -503,11 +498,11 @@
         col_comps = doubled(col_comps, hop)
     near = [moved]
     for step in range(rows - 3):
-        even, odd = even + [exchange(odd[-1], 0)], odd + [exchange(even[-1], 1)]
+        odd, even = odd + [exchange(even[-1], 1)], even + [exchange(odd[-1], 0)]
         upto = rows - 1 if step == rows - 4 else min(rows - 1, 2 * step + 3)
         near += [beside(moved, d) for d in range(len(near), upto)]
-        near, coefs, col_comps, held, even, odd = lax.optimization_barrier(
-            (near, coefs, col_comps, held, even, odd)
+        near, coefs, col_comps, held, odd, even = lax.optimization_barrier(
+            (near, coefs, col_comps, held, odd, even)
         )
     last = exchange(odd[-1], 0)
     far = beside(near[0], rows - 1)

time: 130 us -> 128 us (0.985)
  starting transfers between devices: 36.7 us -> 31.8 us
  waiting for transfers between devices: 34.7 us -> 38.3 us
  Pallas kernels: 50.1 us -> 47.9 us
    ppermute x6, waiting for transfers between devices: 1.44 us -> 8.27 us  [across(): return lax.ppermute(x, 'cols', pairs(lambda z, c: (z ^ e, c))) if e else x]
    ppermute x5, waiting for transfers between devices: 10 us -> 5.14 us  [exchange(): return lax.ppermute(x, 'cols', pairs(lambda z, c: (other[z], c)))]
    ppermute x2, starting transfers between devices: 6.38 us -> 3.66 us  [doubled(): lax.ppermute(x, ('rows', 'cols'), moves)]
    ppermute x5, starting transfers between devices: 12.2 us -> 9.68 us  [exchange(): return lax.ppermute(x, 'cols', pairs(lambda z, c: (other[z], c)))]
    pallas_call x2, Pallas kernels: 22.4 us -> 20.3 us  [kin_call(): pl.pallas_call(kin_kernel, grid_spec=pltpu.PrefetchScalarGridSpec(num_sca...]
    ppermute x2, waiting for transfers between devices: 11.6 us -> 13.6 us  [doubled(): lax.ppermute(x, ('rows', 'cols'), moves)]
    unnamed x32 -> x30, local copies, waits for them, and re-layouts: 3.3 us -> 4.17 us
  transfers between devices with their start and end apart: 24 -> 24, of which waited for: 14 -> 11; matrix products, arithmetic and copies ran while one was open for 1% -> 2% of each run, Pallas kernels for 26% -> 25%
where the time goes in v10:
time: 128 us
  Pallas kernels  47.9 us (37%)
  waiting for transfers between devices  38.3 us (30%)
  starting transfers between devices  31.8 us (25%)
  other arithmetic  4.95 us (4%)
  local copies, waits for them, and re-layouts  4.31 us (3%)
    pallas_call x2, Pallas kernels, kin_call(): pl.pallas_call(kin_kernel, grid_spec=pltpu.PrefetchScalarGridSpec(num_sca...  20.3 us
    ppermute x2, waiting for transfers between devices, doubled(): lax.ppermute(x, ('rows', 'cols'), moves)  13.6 us
    ppermute x8, waiting for transfers between devices, beside(): lax.ppermute(x, 'rows', [(i, i ^ d) for i in range(rows)])  9.95 us
    ppermute x5, starting transfers between devices, exchange(): return lax.ppermute(x, 'cols', pairs(lambda z, c: (other[z], c)))  9.68 us
    pallas_call x1, Pallas kernels, early_call(): pl.pallas_call(functools.partial(early_kernel_at, rows, len(pieces)), gri...  9.51 us
    ppermute x6, starting transfers between devices, across(): return lax.ppermute(x, 'cols', pairs(lambda z, c: (z ^ e, c))) if e else x  9.15 us
    ppermute x8, starting transfers between devices, beside(): lax.ppermute(x, 'rows', [(i, i ^ d) for i in range(rows)])  8.71 us
    ppermute x6, waiting for transfers between devices, across(): return lax.ppermute(x, 'cols', pairs(lambda z, c: (z ^ e, c))) if e else x  8.27 us
  transfers between devices with their start and end apart: 24, of which 11 were waited for; matrix products, arithmetic and copies ran while one was open for 2% of the time, Pallas kernels for 25%

profile of v10, /device:TPU:0, one launch (start us, length us, event | category | flops | bytes accessed | tf_op | source)
XLA Modules:
  0.0 127.6 jit_solution(9545765935927151112)
XLA Ops:
  3.5 3.0 %collective-permute-start.6 = (bf16[256,1536]{1,0:T(8,128)(2,1)S(1)}, bf16[256,1536]{1,0:T(8,128)(2,1)S(1)}, u32[]{:S(2)}, u32[]{:S(2)}) collective-permute-start(bf16[256,1536]{1,0:T(8,128)(2,1)S(1)} %pad_maximum_fusion.refs_6_), channel_id=1, source_target_pairs={{0,2},{1,3},{2,0},{3,1},{4,6},{5,7},{6,4},{7,5},{8,10},{9,11},{10,... | collective-permute-start | bytes 2359304 | tf_op jit(solution)/shard_map/ppermute | solution.py:431
  7.4 2.5 %collective-permute-start.3 = (bf16[64,1536]{1,0:T(8,128)(2,1)S(1)}, bf16[64,1536]{1,0:T(8,128)(2,1)S(1)}, u32[]{:S(2)}, u32[]{:S(2)}) collective-permute-start(bf16[64,1536]{1,0:T(8,128)(2,1)S(1)} %get-tuple-element.99), channel_id=1, source_target_pairs={{0,24},{8,16},{16,8},{24,0},{1,25},{9,17},{17,9},{25,1},{2,26},{10... | collective-permute-start | bytes 589832 | tf_op jit(solution)/shard_map/ppermute | solution.py:434
  11.0 5.7 %gram.1 = f32[360,128]{1,0:T(8,128)} custom-call(s32[64,3072]{1,0:T(8,128)} %dosage_ref, s32[64,3072]{1,0:T(8,128)} %present_ref, f32[32,3072]{1,0:T(8,128)} %refs_0_.1), custom_call_target="tpu_custom_call" | custom-call | tf_op jit(solution)/shard_map/gram/pallas_call | solution.py:62
  16.6 2.6 %collective-permute-done.2 = bf16[64,1536]{1,0:T(8,128)(2,1)S(1)} collective-permute-done((bf16[64,1536]{1,0:T(8,128)(2,1)S(1)}, bf16[64,1536]{1,0:T(8,128)(2,1)S(1)}, u32[]{:S(2)}, u32[]{:S(2)}) %collective-permute-start.2) | collective-permute-done | bytes 196640 | tf_op jit(solution)/shard_map/ppermute | solution.py:434
  19.3 1.5 %collective-permute-start.4 = (f32[360,128]{1,0:T(8,128)}, f32[360,128]{1,0:T(8,128)S(1)}, u32[]{:S(2)}, u32[]{:S(2)}) collective-permute-start(f32[360,128]{1,0:T(8,128)} %gram.1), channel_id=1, source_target_pairs={{0,8},{8,0},{16,24},{24,16},{1,9},{9,1},{17,25},{25,17},{2,10},{10... | collective-permute-start | bytes 552968 | tf_op jit(solution)/shard_map/ppermute | solution.py:434
  20.9 5.1 %collective-permute-done.4 = f32[360,128]{1,0:T(8,128)S(1)} collective-permute-done((f32[360,128]{1,0:T(8,128)}, f32[360,128]{1,0:T(8,128)S(1)}, u32[]{:S(2)}, u32[]{:S(2)}) %collective-permute-start.4) | collective-permute-done | bytes 184352 | tf_op jit(solution)/shard_map/ppermute | solution.py:434
  27.0 1.6 %collective-permute-start.10 = (f32[360,128]{1,0:T(8,128)S(1)}, f32[360,128]{1,0:T(8,128)S(1)}, u32[]{:S(2)}, u32[]{:S(2)}) collective-permute-start(f32[360,128]{1,0:T(8,128)S(1)} %add.104.refs_0_), channel_id=1, source_target_pairs={{0,16},{8,24},{16,0},{24,8},{1,17},{9,25},{17,1},{25,9},{2,18},{10... | collective-permute-start | bytes 552968 | tf_op jit(solution)/shard_map/ppermute | solution.py:434
  28.6 2.2 %collective-permute-start.12 = (f32[32,1536]{1,0:T(8,128)S(1)}, f32[32,1536]{1,0:T(8,128)S(1)}, u32[]{:S(2)}, u32[]{:S(2)}) collective-permute-start(f32[32,1536]{1,0:T(8,128)S(1)} %constant_dynamic-slice_fusion.1), channel_id=1, source_target_pairs={{0,8},{1,9},{10,2},{11,3},{20,28},{21,29},{30,22},{31,23}} | collective-permute-start | bytes 589832 | tf_op jit(solution)/shard_map/ppermute | solution.py:475
  31.9 3.7 %collective-permute-start.8 = (bf16[64,1536]{1,0:T(8,128)(2,1)S(1)}, bf16[64,1536]{1,0:T(8,128)(2,1)S(1)}, u32[]{:S(2)}, u32[]{:S(2)}) collective-permute-start(bf16[64,1536]{1,0:T(8,128)(2,1)S(1)} %get-tuple-element.97), channel_id=1, source_target_pairs={{0,4},{1,5},{2,6},{3,7},{4,0},{5,1},{6,2},{7,3},{8,12},{9,13},{10,... | collective-permute-start | bytes 589832 | tf_op jit(solution)/shard_map/ppermute | solution.py:437
  36.3 7.1 %solve.1 = bf16[64,128]{1,0:T(8,128)(2,1)} custom-call(f32[360,128]{1,0:T(8,128)} %copy-done.9, f32[360,128]{1,0:T(8,128)} %copy-done.10), custom_call_target="tpu_custom_call" | custom-call | tf_op jit(solution)/shard_map/solve/pallas_call | solution.py:151
  43.4 7.3 %collective-permute-done.8 = bf16[64,1536]{1,0:T(8,128)(2,1)S(1)} collective-permute-done((bf16[64,1536]{1,0:T(8,128)(2,1)S(1)}, bf16[64,1536]{1,0:T(8,128)(2,1)S(1)}, u32[]{:S(2)}, u32[]{:S(2)}) %collective-permute-start.8) | collective-permute-done | bytes 196640 | tf_op jit(solution)/shard_map/ppermute | solution.py:437
  53.0 3.0 %collective-permute-start.15 = (bf16[128,128]{1,0:T(8,128)(2,1)S(1)}, bf16[128,128]{1,0:T(8,128)(2,1)S(1)}, u32[]{:S(2)}, u32[]{:S(2)}) collective-permute-start(bf16[128,128]{1,0:T(8,128)(2,1)S(1)} %pad_maximum_fusion.5.refs_2_), channel_id=1, source_target_pairs={{0,2},{1,3},{2,0},{3,1},{4,6},{5,7},{6,4},{7,5},{8,10},{9,11},{10,... | collective-permute-start | bytes 98312 | tf_op jit(solution)/shard_map/ppermute | solution.py:437
  58.2 1.7 %collective-permute-start.20 = (bf16[256,1536]{1,0:T(8,128)(2,1)S(1)}, bf16[256,1536]{1,0:T(8,128)(2,1)}, u32[]{:S(2)}, u32[]{:S(2)}) collective-permute-start(bf16[256,1536]{1,0:T(8,128)(2,1)S(1)} %collective-permute-done.5.refs_9_.odd_ref), channel_id=1, source_target_pairs={{0,2},{1,3},{2,0},{3,1},{4,6},{5,7},{6,4},{7,5},{8,10},{9,11},{10,... | collective-permute-start | bytes 2359304 | tf_op jit(solution)/shard_map/ppermute | solution.py:431
  60.0 1.6 %collective-permute-start.19 = (bf16[256,1536]{1,0:T(8,128)(2,1)S(1)}, bf16[256,1536]{1,0:T(8,128)(2,1)}, u32[]{:S(2)}, u32[]{:S(2)}) collective-permute-start(bf16[256,1536]{1,0:T(8,128)(2,1)S(1)} %collective-permute-done.6.refs_7_), channel_id=1, source_target_pairs={{0,0},{1,1},{2,4},{3,5},{4,2},{5,3},{6,6},{7,7},{8,8},{9,9},{10,12... | collective-permute-start | bytes 2359304 | tf_op jit(solution)/shard_map/ppermute | solution.py:431
  61.6 1.5 %collective-permute-start.18 = (f32[32,1536]{1,0:T(8,128)S(1)}, f32[32,1536]{1,0:T(8,128)S(1)}, u32[]{:S(2)}, u32[]{:S(2)}) collective-permute-start(f32[32,1536]{1,0:T(8,128)S(1)} %broadcast_select_fusion.1), channel_id=1, source_target_pairs={{0,16},{1,17},{8,24},{9,25},{2,18},{3,19},{10,26},{11,27},{20,4},{... | collective-permute-start | bytes 589832 | tf_op jit(solution)/shard_map/ppermute | solution.py:475
  63.1 13.6 %collective-permute-done.18 = f32[32,1536]{1,0:T(8,128)S(1)} collective-permute-done((f32[32,1536]{1,0:T(8,128)S(1)}, f32[32,1536]{1,0:T(8,128)S(1)}, u32[]{:S(2)}, u32[]{:S(2)}) %collective-permute-start.18) | collective-permute-done | bytes 196640 | tf_op jit(solution)/shard_map/ppermute | solution.py:475
  78.3 2.6 %collective-permute-start.21 = (bf16[256,1536]{1,0:T(8,128)(2,1)}, bf16[256,1536]{1,0:T(8,128)(2,1)S(1)}, u32[]{:S(2)}, u32[]{:S(2)}) collective-permute-start(bf16[256,1536]{1,0:T(8,128)(2,1)} %collective-permute-done.19.refs_10_), channel_id=1, source_target_pairs={{0,2},{1,3},{2,0},{3,1},{4,6},{5,7},{6,4},{7,5},{8,10},{9,11},{10,... | collective-permute-start | bytes 2359304 | tf_op jit(solution)/shard_map/ppermute | solution.py:431
  82.4 9.5 %early.1 = (bf16[2,1536,512]{2,1,0:T(8,128)(2,1)}, bf16[2,16,32,1536]{3,2,1,0:T(8,128)(2,1)}, f32[128,1536]{1,0:T(8,128)}, f32[4,32,1536]{2,1,0:T(8,128)}) custom-call(s32[1]{0:T(128)} %bitcast.5.part_ref, f32[32,3072]{1,0:T(8,128)} %refs_0_.1, f32[32,1536]{1,0:T(8,128)} %broadcast_select_fusion.refs_1_, bf16[128,128]{1,0:T(8,128)(2,1)} %copy-done.11, ...), custom_call_target="tpu_custom_call" | custom-call | tf_op jit(solution)/shard_map/early/pallas_call | solution.py:268
  91.9 5.1 %collective-permute-done.21.even_ref = bf16[256,1536]{1,0:T(8,128)(2,1)S(1)} collective-permute-done((bf16[256,1536]{1,0:T(8,128)(2,1)}, bf16[256,1536]{1,0:T(8,128)(2,1)S(1)}, u32[]{:S(2)}, u32[]{:S(2)}) %collective-permute-start.21) | collective-permute-done | bytes 786464 | tf_op jit(solution)/shard_map/ppermute | solution.py:431
  97.1 2.1 %collective-permute-done.22.piece_ref = bf16[4,64,1536]{2,1,0:T(8,128)(2,1)S(1)} collective-permute-done((bf16[4,64,1536]{2,1,0:T(8,128)(2,1)S(1)}, bf16[4,64,1536]{2,1,0:T(8,128)(2,1)S(1)}, u32[]{:S(2)}, u32[]{:S(2)}) %collective-permute-start.22) | collective-permute-done | bytes 786464 | tf_op jit(solution)/shard_map/ppermute | solution.py:434
  100.2 5.4 %late.1 = (bf16[2,1536,512]{2,1,0:T(8,128)(2,1)}, bf16[2,16,32,1536]{3,2,1,0:T(8,128)(2,1)}) custom-call(s32[4]{0:T(128)} %pad_add_fusion.group_ref, f32[128,1536]{1,0:T(8,128)} %get-tuple-element.89.row_fit, f32[4,32,1536]{2,1,0:T(8,128)} %get-tuple-element.90.col_fit, bf16[256,1536]{1,0:T(8,128)(2,1)} %copy-done.5, ...), custom_call_target="tpu_custom_call", output_to_operand_aliasing={{0}: (6, {}), {1}: (7, {})} | custom-call | tf_op jit(solution)/shard_map/late/pallas_call | solution.py:340
  105.7 10.1 %kinship.2.refs_0_ = f32[3072,1536]{1,0:T(8,128)} custom-call(s32[1]{0:T(128)} %bitcast.27.part_ref, bf16[2,1536,512]{2,1,0:T(8,128)(2,1)} %get-tuple-element.93.row_ref, bf16[2,512,1536]{2,1,0:T(8,128)(2,1)} %bitcast.37), custom_call_target="tpu_custom_call" | custom-call | tf_op jit(solution)/shard_map/kinship/pallas_call | solution.py:396
  115.8 1.7 %copy-done.1 = bf16[2,1536,512]{2,1,0:T(8,128)(2,1)} copy-done((bf16[2,1536,512]{2,1,0:T(8,128)(2,1)}, bf16[2,1536,512]{2,1,0:T(8,128)(2,1)S(1)}, u32[]{:S(2)}) %copy-start.1) | copy-done | bytes 3145752
  117.5 10.1 %kinship.3 = f32[3072,1536]{1,0:T(8,128)} custom-call(s32[1]{0:T(128)} %bitcast.part_ref, bf16[2,1536,512]{2,1,0:T(8,128)(2,1)} %copy-done.1, bf16[2,512,1536]{2,1,0:T(8,128)(2,1)} %bitcast.38, f32[3072,1536]{1,0:T(8,128)} %kinship.2.refs_0_), custom_call_target="tpu_custom_call", output_to_operand_aliasing={{}: (3, {})} | custom-call | tf_op jit(solution)/shard_map/kinship/pallas_call | solution.py:396
  (76 shorter events, 16.9 us)
Async XLA Ops:
  1.5 1.9 %collective-permute-start = (bf16[128,1536]{1,0:T(8,128)(2,1)S(1)}, bf16[128,1536]{1,0:T(8,128)(2,1)S(1)}, u32[]{:S(2)}, u32[]{:S(2)}) collective-permute-start(bf16[128,1536]{1,0:T(8,128)(2,1)S(1)} %bitcast.44), channel_id=1, source_target_pairs={{0,1},{1,0},{2,3},{3,2},{4,5},{5,4},{6,7},{7,6},{8,9},{9,8},{10,11... | collective-permute-start | bytes 1179656 | tf_op jit(solution)/shard_map/ppermute | solution.py:426
  3.5 23.4 %collective-permute-start.6 = (bf16[256,1536]{1,0:T(8,128)(2,1)S(1)}, bf16[256,1536]{1,0:T(8,128)(2,1)S(1)}, u32[]{:S(2)}, u32[]{:S(2)}) collective-permute-start(bf16[256,1536]{1,0:T(8,128)(2,1)S(1)} %pad_maximum_fusion.refs_6_), channel_id=1, source_target_pairs={{0,2},{1,3},{2,0},{3,1},{4,6},{5,7},{6,4},{7,5},{8,10},{9,11},{10,... | collective-permute-start | bytes 2359304 | tf_op jit(solution)/shard_map/ppermute | solution.py:431
  6.5 20.5 %collective-permute-start.5 = (bf16[256,1536]{1,0:T(8,128)(2,1)S(1)}, bf16[256,1536]{1,0:T(8,128)(2,1)S(1)}, u32[]{:S(2)}, u32[]{:S(2)}) collective-permute-start(bf16[256,1536]{1,0:T(8,128)(2,1)S(1)} %pad_maximum_fusion.refs_6_), channel_id=1, source_target_pairs={{0,0},{1,1},{2,4},{3,5},{4,2},{5,3},{6,6},{7,7},{8,8},{9,9},{10,12... | collective-permute-start | bytes 2359304 | tf_op jit(solution)/shard_map/ppermute | solution.py:431
  7.4 9.2 %collective-permute-start.3 = (bf16[64,1536]{1,0:T(8,128)(2,1)S(1)}, bf16[64,1536]{1,0:T(8,128)(2,1)S(1)}, u32[]{:S(2)}, u32[]{:S(2)}) collective-permute-start(bf16[64,1536]{1,0:T(8,128)(2,1)S(1)} %get-tuple-element.99), channel_id=1, source_target_pairs={{0,24},{8,16},{16,8},{24,0},{1,25},{9,17},{17,9},{25,1},{2,26},{10... | collective-permute-start | bytes 589832 | tf_op jit(solution)/shard_map/ppermute | solution.py:434
  9.9 9.3 %collective-permute-start.2 = (bf16[64,1536]{1,0:T(8,128)(2,1)S(1)}, bf16[64,1536]{1,0:T(8,128)(2,1)S(1)}, u32[]{:S(2)}, u32[]{:S(2)}) collective-permute-start(bf16[64,1536]{1,0:T(8,128)(2,1)S(1)} %get-tuple-element.100), channel_id=1, source_target_pairs={{0,16},{8,24},{16,0},{24,8},{1,17},{9,25},{17,1},{25,9},{2,18},{10... | collective-permute-start | bytes 589832 | tf_op jit(solution)/shard_map/ppermute | solution.py:434
  10.4 8.9 %collective-permute-start.1 = (bf16[64,1536]{1,0:T(8,128)(2,1)S(1)}, bf16[64,1536]{1,0:T(8,128)(2,1)S(1)}, u32[]{:S(2)}, u32[]{:S(2)}) collective-permute-start(bf16[64,1536]{1,0:T(8,128)(2,1)S(1)} %get-tuple-element.101), channel_id=1, source_target_pairs={{0,8},{8,0},{16,24},{24,16},{1,9},{9,1},{17,25},{25,17},{2,10},{10... | collective-permute-start | bytes 589832 | tf_op jit(solution)/shard_map/ppermute | solution.py:434
  19.3 6.7 %collective-permute-start.4 = (f32[360,128]{1,0:T(8,128)}, f32[360,128]{1,0:T(8,128)S(1)}, u32[]{:S(2)}, u32[]{:S(2)}) collective-permute-start(f32[360,128]{1,0:T(8,128)} %gram.1), channel_id=1, source_target_pairs={{0,8},{8,0},{16,24},{24,16},{1,9},{9,1},{17,25},{25,17},{2,10},{10... | collective-permute-start | bytes 552968 | tf_op jit(solution)/shard_map/ppermute | solution.py:434
  27.0 8.6 %collective-permute-start.10 = (f32[360,128]{1,0:T(8,128)S(1)}, f32[360,128]{1,0:T(8,128)S(1)}, u32[]{:S(2)}, u32[]{:S(2)}) collective-permute-start(f32[360,128]{1,0:T(8,128)S(1)} %add.104.refs_0_), channel_id=1, source_target_pairs={{0,16},{8,24},{16,0},{24,8},{1,17},{9,25},{17,1},{25,9},{2,18},{10... | collective-permute-start | bytes 552968 | tf_op jit(solution)/shard_map/ppermute | solution.py:434
  28.6 14.8 %collective-permute-start.12 = (f32[32,1536]{1,0:T(8,128)S(1)}, f32[32,1536]{1,0:T(8,128)S(1)}, u32[]{:S(2)}, u32[]{:S(2)}) collective-permute-start(f32[32,1536]{1,0:T(8,128)S(1)} %constant_dynamic-slice_fusion.1), channel_id=1, source_target_pairs={{0,8},{1,9},{10,2},{11,3},{20,28},{21,29},{30,22},{31,23}} | collective-permute-start | bytes 589832 | tf_op jit(solution)/shard_map/ppermute | solution.py:475
  30.9 12.5 %collective-permute-start.9 = (bf16[64,1536]{1,0:T(8,128)(2,1)S(1)}, bf16[64,1536]{1,0:T(8,128)(2,1)S(1)}, u32[]{:S(2)}, u32[]{:S(2)}) collective-permute-start(bf16[64,1536]{1,0:T(8,128)(2,1)S(1)} %get-tuple-element.96), channel_id=1, source_target_pairs={{0,6},{1,7},{2,4},{3,5},{4,2},{5,3},{6,0},{7,1},{8,14},{9,15},{10,... | collective-permute-start | bytes 589832 | tf_op jit(solution)/shard_map/ppermute | solution.py:437
  31.9 18.8 %collective-permute-start.8 = (bf16[64,1536]{1,0:T(8,128)(2,1)S(1)}, bf16[64,1536]{1,0:T(8,128)(2,1)S(1)}, u32[]{:S(2)}, u32[]{:S(2)}) collective-permute-start(bf16[64,1536]{1,0:T(8,128)(2,1)S(1)} %get-tuple-element.97), channel_id=1, source_target_pairs={{0,4},{1,5},{2,6},{3,7},{4,0},{5,1},{6,2},{7,3},{8,12},{9,13},{10,... | collective-permute-start | bytes 589832 | tf_op jit(solution)/shard_map/ppermute | solution.py:437
  35.6 15.1 %collective-permute-start.7 = (bf16[64,1536]{1,0:T(8,128)(2,1)S(1)}, bf16[64,1536]{1,0:T(8,128)(2,1)S(1)}, u32[]{:S(2)}, u32[]{:S(2)}) collective-permute-start(bf16[64,1536]{1,0:T(8,128)(2,1)S(1)} %get-tuple-element.98), channel_id=1, source_target_pairs={{0,2},{1,3},{2,0},{3,1},{4,6},{5,7},{6,4},{7,5},{8,10},{9,11},{10,... | collective-permute-start | bytes 589832 | tf_op jit(solution)/shard_map/ppermute | solution.py:437
  43.4 7.4 %collective-permute-start.11 = (bf16[64,128]{1,0:T(8,128)(2,1)}, bf16[64,128]{1,0:T(8,128)(2,1)S(1)}, u32[]{:S(2)}, u32[]{:S(2)}) collective-permute-start(bf16[64,128]{1,0:T(8,128)(2,1)} %solve.1), channel_id=1, source_target_pairs={{0,1},{1,0},{2,3},{3,2},{4,5},{5,4},{6,7},{7,6},{8,9},{9,8},{10,11... | collective-permute-start | bytes 49160 | tf_op jit(solution)/shard_map/ppermute | solution.py:426
  51.6 5.8 %collective-permute-start.17 = (bf16[128,128]{1,0:T(8,128)(2,1)S(1)}, bf16[128,128]{1,0:T(8,128)(2,1)S(1)}, u32[]{:S(2)}, u32[]{:S(2)}) collective-permute-start(bf16[128,128]{1,0:T(8,128)(2,1)S(1)} %pad_maximum_fusion.5.refs_2_), channel_id=1, source_target_pairs={{0,6},{1,7},{2,4},{3,5},{4,2},{5,3},{6,0},{7,1},{8,14},{9,15},{10,... | collective-permute-start | bytes 98312 | tf_op jit(solution)/shard_map/ppermute | solution.py:437
  53.0 5.1 %collective-permute-start.16 = (bf16[128,128]{1,0:T(8,128)(2,1)S(1)}, bf16[128,128]{1,0:T(8,128)(2,1)S(1)}, u32[]{:S(2)}, u32[]{:S(2)}) collective-permute-start(bf16[128,128]{1,0:T(8,128)(2,1)S(1)} %pad_maximum_fusion.5.refs_2_), channel_id=1, source_target_pairs={{0,4},{1,5},{2,6},{3,7},{4,0},{5,1},{6,2},{7,3},{8,12},{9,13},{10,... | collective-permute-start | bytes 98312 | tf_op jit(solution)/shard_map/ppermute | solution.py:437
  53.0 5.2 %collective-permute-start.15 = (bf16[128,128]{1,0:T(8,128)(2,1)S(1)}, bf16[128,128]{1,0:T(8,128)(2,1)S(1)}, u32[]{:S(2)}, u32[]{:S(2)}) collective-permute-start(bf16[128,128]{1,0:T(8,128)(2,1)S(1)} %pad_maximum_fusion.5.refs_2_), channel_id=1, source_target_pairs={{0,2},{1,3},{2,0},{3,1},{4,6},{5,7},{6,4},{7,5},{8,10},{9,11},{10,... | collective-permute-start | bytes 98312 | tf_op jit(solution)/shard_map/ppermute | solution.py:437
  56.0 21.3 %collective-permute-start.14 = (bf16[4,64,1536]{2,1,0:T(8,128)(2,1)S(1)}, bf16[4,64,1536]{2,1,0:T(8,128)(2,1)S(1)}, u32[]{:S(2)}, u32[]{:S(2)}) collective-permute-start(bf16[4,64,1536]{2,1,0:T(8,128)(2,1)S(1)} %pad_maximum_fusion.2.refs_11_), channel_id=1, source_target_pairs={{0,16},{8,24},{16,0},{24,8},{1,17},{9,25},{17,1},{25,9},{2,18},{10... | collective-permute-start | bytes 2359304 | tf_op jit(solution)/shard_map/ppermute | solution.py:434
  56.0 21.3 %collective-permute-start.13 = (bf16[4,64,1536]{2,1,0:T(8,128)(2,1)S(1)}, bf16[4,64,1536]{2,1,0:T(8,128)(2,1)}, u32[]{:S(2)}, u32[]{:S(2)}) collective-permute-start(bf16[4,64,1536]{2,1,0:T(8,128)(2,1)S(1)} %pad_maximum_fusion.2.refs_11_), channel_id=1, source_target_pairs={{0,8},{8,0},{16,24},{24,16},{1,9},{9,1},{17,25},{25,17},{2,10},{10... | collective-permute-start | bytes 2359304 | tf_op jit(solution)/shard_map/ppermute | solution.py:434
  58.2 19.1 %collective-permute-start.20 = (bf16[256,1536]{1,0:T(8,128)(2,1)S(1)}, bf16[256,1536]{1,0:T(8,128)(2,1)}, u32[]{:S(2)}, u32[]{:S(2)}) collective-permute-start(bf16[256,1536]{1,0:T(8,128)(2,1)S(1)} %collective-permute-done.5.refs_9_.odd_ref), channel_id=1, source_target_pairs={{0,2},{1,3},{2,0},{3,1},{4,6},{5,7},{6,4},{7,5},{8,10},{9,11},{10,... | collective-permute-start | bytes 2359304 | tf_op jit(solution)/shard_map/ppermute | solution.py:431
  60.0 17.4 %collective-permute-start.19 = (bf16[256,1536]{1,0:T(8,128)(2,1)S(1)}, bf16[256,1536]{1,0:T(8,128)(2,1)}, u32[]{:S(2)}, u32[]{:S(2)}) collective-permute-start(bf16[256,1536]{1,0:T(8,128)(2,1)S(1)} %collective-permute-done.6.refs_7_), channel_id=1, source_target_pairs={{0,0},{1,1},{2,4},{3,5},{4,2},{5,3},{6,6},{7,7},{8,8},{9,9},{10,12... | collective-permute-start | bytes 2359304 | tf_op jit(solution)/shard_map/ppermute | solution.py:431
  61.6 15.1 %collective-permute-start.18 = (f32[32,1536]{1,0:T(8,128)S(1)}, f32[32,1536]{1,0:T(8,128)S(1)}, u32[]{:S(2)}, u32[]{:S(2)}) collective-permute-start(f32[32,1536]{1,0:T(8,128)S(1)} %broadcast_select_fusion.1), channel_id=1, source_target_pairs={{0,16},{1,17},{8,24},{9,25},{2,18},{3,19},{10,26},{11,27},{20,4},{... | collective-permute-start | bytes 589832 | tf_op jit(solution)/shard_map/ppermute | solution.py:475
  78.3 18.8 %collective-permute-start.21 = (bf16[256,1536]{1,0:T(8,128)(2,1)}, bf16[256,1536]{1,0:T(8,128)(2,1)S(1)}, u32[]{:S(2)}, u32[]{:S(2)}) collective-permute-start(bf16[256,1536]{1,0:T(8,128)(2,1)} %collective-permute-done.19.refs_10_), channel_id=1, source_target_pairs={{0,2},{1,3},{2,0},{3,1},{4,6},{5,7},{6,4},{7,5},{8,10},{9,11},{10,... | collective-permute-start | bytes 2359304 | tf_op jit(solution)/shard_map/ppermute | solution.py:431
  80.9 18.3 %collective-permute-start.22 = (bf16[4,64,1536]{2,1,0:T(8,128)(2,1)S(1)}, bf16[4,64,1536]{2,1,0:T(8,128)(2,1)S(1)}, u32[]{:S(2)}, u32[]{:S(2)}) collective-permute-start(bf16[4,64,1536]{2,1,0:T(8,128)(2,1)S(1)} %pad_maximum_fusion.2.refs_11_), channel_id=1, source_target_pairs={{0,24},{8,16},{16,8},{24,0},{1,25},{9,17},{17,9},{25,1},{2,26},{10... | collective-permute-start | bytes 2359304 | tf_op jit(solution)/shard_map/ppermute | solution.py:434
  105.6 10.2 %collective-permute-start.23 = (bf16[2,1536,512]{2,1,0:T(8,128)(2,1)}, bf16[2,1536,512]{2,1,0:T(8,128)(2,1)S(1)}, u32[]{:S(2)}, u32[]{:S(2)}) collective-permute-start(bf16[2,1536,512]{2,1,0:T(8,128)(2,1)} %get-tuple-element.93.row_ref), channel_id=1, source_target_pairs={{0,1},{1,0},{2,3},{3,2},{4,5},{5,4},{6,7},{7,6},{8,9},{9,8},{10,11... | collective-permute-start | bytes 9437192 | tf_op jit(solution)/shard_map/ppermute | solution.py:426
  (15 other events, 204.7 us)

commit v11 on v10

--- a/solution.py
+++ b/solution.py
@@ -9,6 +9,7 @@
 
 F32, BF16 = jnp.float32, jnp.bfloat16
 VMEM_LIMIT = 56 * 1024 * 1024
+VMEM_ALL = 63 * 1024 * 1024
 SUB = 8
 
 
@@ -294,7 +295,7 @@
             jax.ShapeDtypeStruct((chip, width), F32),
             jax.ShapeDtypeStruct((rows, height, width), F32),
         ),
-        compiler_params=pltpu.CompilerParams(vmem_limit_bytes=VMEM_LIMIT),
+        compiler_params=pltpu.CompilerParams(vmem_limit_bytes=VMEM_ALL),
         name="early",
     )(part[None].astype(jnp.int32), components, col_comps, *coefs, held, *even, *odd, *pieces)
 
@@ -362,7 +363,7 @@
             jax.ShapeDtypeStruct(col_panel.shape, BF16),
         ),
         input_output_aliases={6: 0, 7: 1},
-        compiler_params=pltpu.CompilerParams(vmem_limit_bytes=VMEM_LIMIT),
+        compiler_params=pltpu.CompilerParams(vmem_limit_bytes=VMEM_ALL),
         name="late",
     )(groups, row_fit, col_fit, even, odd, piece, row_panel, col_panel)
 
@@ -403,7 +404,7 @@
         ),
         out_shape=jax.ShapeDtypeStruct((people, width), F32),
         input_output_aliases=aliases,
-        compiler_params=pltpu.CompilerParams(vmem_limit_bytes=VMEM_LIMIT),
+        compiler_params=pltpu.CompilerParams(vmem_limit_bytes=VMEM_ALL),
         name="kinship",
     )(part[None].astype(jnp.int32), *operands)
 
@@ -489,11 +490,10 @@
     coef = solve_call([gram, beside(gram, hops[-1])], comps, markers)
     coef = by_core([swap(coef, k) for k in range(ratio)])
     col_comps = doubled(col_comps, hops[0])
-    moved, coef, col_comps, held, odd, even = lax.optimization_barrier(
-        (jnp.stack(moved), coef, col_comps, held, odd, even)
+    coefs = [across(coef, e) for e in range(rows)]
+    moved, coefs, col_comps, held, odd, even = lax.optimization_barrier(
+        (jnp.stack(moved), coefs, col_comps, held, odd, even)
     )
-    coefs = [across(coef, e) for e in range(rows)]
-    coefs, even, odd = lax.optimization_barrier((coefs, even, odd))
     for hop in hops[1:]:
         col_comps = doubled(col_comps, hop)
     near = [moved]

time: 128 us -> 125 us (0.977)
  starting transfers between devices: 31.8 us -> 37.1 us
  waiting for transfers between devices: 38.3 us -> 33.8 us
  local copies, waits for them, and re-layouts: 4.31 us -> 0.85 us
    ppermute x6, waiting for transfers between devices: 8.27 us -> 3.58 us  [across(): return lax.ppermute(x, 'cols', pairs(lambda z, c: (z ^ e, c))) if e else x]
    ppermute x8, starting transfers between devices: 8.71 us -> 12.7 us  [beside(): lax.ppermute(x, 'rows', [(i, i ^ d) for i in range(rows)])]
    unnamed x30 -> x22, local copies, waits for them, and re-layouts: 4.17 us -> 0.71 us
    ppermute x5, waiting for transfers between devices: 5.14 us -> 1.93 us  [exchange(): return lax.ppermute(x, 'cols', pairs(lambda z, c: (other[z], c)))]
    ppermute x2, starting transfers between devices: 3.66 us -> 6.29 us  [doubled(): lax.ppermute(x, ('rows', 'cols'), moves)]
    ppermute x3, waiting for transfers between devices: 1.31 us -> 2.67 us  [swap(): lax.ppermute(x, 'cols', pairs(lambda z, c: (z, (c + k) % ratio)))]
    ppermute x5, starting transfers between devices: 9.68 us -> 8.37 us  [exchange(): return lax.ppermute(x, 'cols', pairs(lambda z, c: (other[z], c)))]
  transfers between devices with their start and end apart: 24 -> 24, of which waited for: 11 -> 11; matrix products, arithmetic and copies ran while one was open for 2% -> 3% of each run, Pallas kernels for 25% -> 26%
where the time goes in v11:
time: 125 us
  Pallas kernels  48 us (38%)
  starting transfers between devices  37.1 us (30%)
  waiting for transfers between devices  33.8 us (27%)
  other arithmetic  4.86 us (4%)
    pallas_call x2, Pallas kernels, kin_call(): pl.pallas_call(kin_kernel, grid_spec=pltpu.PrefetchScalarGridSpec(num_sca...  20.3 us
    ppermute x2, waiting for transfers between devices, doubled(): lax.ppermute(x, ('rows', 'cols'), moves)  14.4 us
    ppermute x8, starting transfers between devices, beside(): lax.ppermute(x, 'rows', [(i, i ^ d) for i in range(rows)])  12.7 us
    ppermute x8, waiting for transfers between devices, beside(): lax.ppermute(x, 'rows', [(i, i ^ d) for i in range(rows)])  11.2 us
    pallas_call x1, Pallas kernels, early_call(): pl.pallas_call(functools.partial(early_kernel_at, rows, len(pieces)), gri...  9.58 us
    ppermute x6, starting transfers between devices, across(): return lax.ppermute(x, 'cols', pairs(lambda z, c: (z ^ e, c))) if e else x  9.15 us
    ppermute x5, starting transfers between devices, exchange(): return lax.ppermute(x, 'cols', pairs(lambda z, c: (other[z], c)))  8.37 us
    pallas_call x1, Pallas kernels, solve_call(): pl.pallas_call(functools.partial(solve_kernel, comps, markers), out_shape...  7.09 us
  transfers between devices with their start and end apart: 24, of which 11 were waited for; matrix products, arithmetic and copies ran while one was open for 3% of the time, Pallas kernels for 26%

profile of v11, /device:TPU:0, one launch (start us, length us, event | category | flops | bytes accessed | tf_op | source)
XLA Modules:
  0.0 124.9 jit_solution(7531304658544620026)
XLA Ops:
  3.5 3.0 %collective-permute-start.6 = (bf16[256,1536]{1,0:T(8,128)(2,1)S(1)}, bf16[256,1536]{1,0:T(8,128)(2,1)S(1)}, u32[]{:S(2)}, u32[]{:S(2)}) collective-permute-start(bf16[256,1536]{1,0:T(8,128)(2,1)S(1)} %pad_maximum_fusion.refs_6_), channel_id=1, source_target_pairs={{0,2},{1,3},{2,0},{3,1},{4,6},{5,7},{6,4},{7,5},{8,10},{9,11},{10,... | collective-permute-start | bytes 2359304 | tf_op jit(solution)/shard_map/ppermute | solution.py:432
  7.4 2.5 %collective-permute-start.3 = (bf16[64,1536]{1,0:T(8,128)(2,1)S(1)}, bf16[64,1536]{1,0:T(8,128)(2,1)S(1)}, u32[]{:S(2)}, u32[]{:S(2)}) collective-permute-start(bf16[64,1536]{1,0:T(8,128)(2,1)S(1)} %get-tuple-element.93), channel_id=1, source_target_pairs={{0,24},{8,16},{16,8},{24,0},{1,25},{9,17},{17,9},{25,1},{2,26},{10... | collective-permute-start | bytes 589832 | tf_op jit(solution)/shard_map/ppermute | solution.py:435
  11.0 5.6 %gram.1 = f32[360,128]{1,0:T(8,128)} custom-call(s32[64,3072]{1,0:T(8,128)} %dosage_ref, s32[64,3072]{1,0:T(8,128)} %present_ref, f32[32,3072]{1,0:T(8,128)} %refs_0_.1), custom_call_target="tpu_custom_call" | custom-call | tf_op jit(solution)/shard_map/gram/pallas_call | solution.py:63
  16.6 2.6 %collective-permute-done.2 = bf16[64,1536]{1,0:T(8,128)(2,1)S(1)} collective-permute-done((bf16[64,1536]{1,0:T(8,128)(2,1)S(1)}, bf16[64,1536]{1,0:T(8,128)(2,1)S(1)}, u32[]{:S(2)}, u32[]{:S(2)}) %collective-permute-start.2) | collective-permute-done | bytes 196640 | tf_op jit(solution)/shard_map/ppermute | solution.py:435
  20.9 5.1 %collective-permute-done.4 = f32[360,128]{1,0:T(8,128)S(1)} collective-permute-done((f32[360,128]{1,0:T(8,128)}, f32[360,128]{1,0:T(8,128)S(1)}, u32[]{:S(2)}, u32[]{:S(2)}) %collective-permute-start.4) | collective-permute-done | bytes 184352 | tf_op jit(solution)/shard_map/ppermute | solution.py:435
  27.0 1.6 %collective-permute-start.10 = (f32[360,128]{1,0:T(8,128)S(1)}, f32[360,128]{1,0:T(8,128)S(1)}, u32[]{:S(2)}, u32[]{:S(2)}) collective-permute-start(f32[360,128]{1,0:T(8,128)S(1)} %add.104.refs_0_), channel_id=1, source_target_pairs={{0,16},{8,24},{16,0},{24,8},{1,17},{9,25},{17,1},{25,9},{2,18},{10... | collective-permute-start | bytes 552968 | tf_op jit(solution)/shard_map/ppermute | solution.py:435
  28.6 2.2 %collective-permute-start.15 = (f32[32,1536]{1,0:T(8,128)S(1)}, f32[32,1536]{1,0:T(8,128)S(1)}, u32[]{:S(2)}, u32[]{:S(2)}) collective-permute-start(f32[32,1536]{1,0:T(8,128)S(1)} %constant_dynamic-slice_fusion.1), channel_id=1, source_target_pairs={{0,8},{1,9},{10,2},{11,3},{20,28},{21,29},{30,22},{31,23}} | collective-permute-start | bytes 589832 | tf_op jit(solution)/shard_map/ppermute | solution.py:476
  31.9 3.7 %collective-permute-start.8 = (bf16[64,1536]{1,0:T(8,128)(2,1)S(1)}, bf16[64,1536]{1,0:T(8,128)(2,1)S(1)}, u32[]{:S(2)}, u32[]{:S(2)}) collective-permute-start(bf16[64,1536]{1,0:T(8,128)(2,1)S(1)} %get-tuple-element.91), channel_id=1, source_target_pairs={{0,4},{1,5},{2,6},{3,7},{4,0},{5,1},{6,2},{7,3},{8,12},{9,13},{10,... | collective-permute-start | bytes 589832 | tf_op jit(solution)/shard_map/ppermute | solution.py:438
  36.2 7.1 %solve.1 = bf16[64,128]{1,0:T(8,128)(2,1)} custom-call(f32[360,128]{1,0:T(8,128)} %copy-done.5, f32[360,128]{1,0:T(8,128)} %copy-done.6), custom_call_target="tpu_custom_call" | custom-call | tf_op jit(solution)/shard_map/solve/pallas_call | solution.py:152
  45.5 1.5 %collective-permute-start.14 = (bf16[128,128]{1,0:T(8,128)(2,1)S(1)}, bf16[128,128]{1,0:T(8,128)(2,1)S(1)}, u32[]{:S(2)}, u32[]{:S(2)}) collective-permute-start(bf16[128,128]{1,0:T(8,128)(2,1)S(1)} %pad_maximum_fusion.5.refs_2_), channel_id=1, source_target_pairs={{0,6},{1,7},{2,4},{3,5},{4,2},{5,3},{6,0},{7,1},{8,14},{9,15},{10,... | collective-permute-start | bytes 98312 | tf_op jit(solution)/shard_map/ppermute | solution.py:438
  47.0 2.0 %collective-permute-start.13 = (bf16[128,128]{1,0:T(8,128)(2,1)S(1)}, bf16[128,128]{1,0:T(8,128)(2,1)S(1)}, u32[]{:S(2)}, u32[]{:S(2)}) collective-permute-start(bf16[128,128]{1,0:T(8,128)(2,1)S(1)} %pad_maximum_fusion.5.refs_2_), channel_id=1, source_target_pairs={{0,4},{1,5},{2,6},{3,7},{4,0},{5,1},{6,2},{7,3},{8,12},{9,13},{10,... | collective-permute-start | bytes 98312 | tf_op jit(solution)/shard_map/ppermute | solution.py:438
  49.9 2.2 %collective-permute-done.8 = bf16[64,1536]{1,0:T(8,128)(2,1)S(1)} collective-permute-done((bf16[64,1536]{1,0:T(8,128)(2,1)S(1)}, bf16[64,1536]{1,0:T(8,128)(2,1)S(1)}, u32[]{:S(2)}, u32[]{:S(2)}) %collective-permute-start.8) | collective-permute-done | bytes 196640 | tf_op jit(solution)/shard_map/ppermute | solution.py:438
  53.9 1.6 %collective-permute-start.19 = (bf16[256,1536]{1,0:T(8,128)(2,1)S(1)}, bf16[256,1536]{1,0:T(8,128)(2,1)}, u32[]{:S(2)}, u32[]{:S(2)}) collective-permute-start(bf16[256,1536]{1,0:T(8,128)(2,1)S(1)} %collective-permute-done.6.refs_7_), channel_id=1, source_target_pairs={{0,0},{1,1},{2,4},{3,5},{4,2},{5,3},{6,6},{7,7},{8,8},{9,9},{10,12... | collective-permute-start | bytes 2359304 | tf_op jit(solution)/shard_map/ppermute | solution.py:432
  55.4 1.5 %collective-permute-start.17 = (bf16[4,64,1536]{2,1,0:T(8,128)(2,1)S(1)}, bf16[4,64,1536]{2,1,0:T(8,128)(2,1)}, u32[]{:S(2)}, u32[]{:S(2)}) collective-permute-start(bf16[4,64,1536]{2,1,0:T(8,128)(2,1)S(1)} %pad_maximum_fusion.2.refs_11_), channel_id=1, source_target_pairs={{0,16},{8,24},{16,0},{24,8},{1,17},{9,25},{17,1},{25,9},{2,18},{10... | collective-permute-start | bytes 2359304 | tf_op jit(solution)/shard_map/ppermute | solution.py:435
  58.1 4.1 %collective-permute-start.18 = (f32[32,1536]{1,0:T(8,128)S(1)}, f32[32,1536]{1,0:T(8,128)S(1)}, u32[]{:S(2)}, u32[]{:S(2)}) collective-permute-start(f32[32,1536]{1,0:T(8,128)S(1)} %broadcast_select_fusion.1), channel_id=1, source_target_pairs={{0,16},{1,17},{8,24},{9,25},{2,18},{3,19},{10,26},{11,27},{20,4},{... | collective-permute-start | bytes 589832 | tf_op jit(solution)/shard_map/ppermute | solution.py:476
  62.2 14.4 %collective-permute-done.18 = f32[32,1536]{1,0:T(8,128)S(1)} collective-permute-done((f32[32,1536]{1,0:T(8,128)S(1)}, f32[32,1536]{1,0:T(8,128)S(1)}, u32[]{:S(2)}, u32[]{:S(2)}) %collective-permute-start.18) | collective-permute-done | bytes 196640 | tf_op jit(solution)/shard_map/ppermute | solution.py:476
  77.4 2.9 %collective-permute-start.21 = (bf16[256,1536]{1,0:T(8,128)(2,1)}, bf16[256,1536]{1,0:T(8,128)(2,1)}, u32[]{:S(2)}, u32[]{:S(2)}) collective-permute-start(bf16[256,1536]{1,0:T(8,128)(2,1)} %collective-permute-done.19.refs_10_), channel_id=1, source_target_pairs={{0,2},{1,3},{2,0},{3,1},{4,6},{5,7},{6,4},{7,5},{8,10},{9,11},{10,... | collective-permute-start | bytes 2359304 | tf_op jit(solution)/shard_map/ppermute | solution.py:432
  80.2 3.4 %collective-permute-start.22 = (bf16[4,64,1536]{2,1,0:T(8,128)(2,1)S(1)}, bf16[4,64,1536]{2,1,0:T(8,128)(2,1)}, u32[]{:S(2)}, u32[]{:S(2)}) collective-permute-start(bf16[4,64,1536]{2,1,0:T(8,128)(2,1)S(1)} %pad_maximum_fusion.2.refs_11_), channel_id=1, source_target_pairs={{0,24},{8,16},{16,8},{24,0},{1,25},{9,17},{17,9},{25,1},{2,26},{10... | collective-permute-start | bytes 2359304 | tf_op jit(solution)/shard_map/ppermute | solution.py:435
  84.2 9.6 %early.1 = (bf16[2,1536,512]{2,1,0:T(8,128)(2,1)}, bf16[2,16,32,1536]{3,2,1,0:T(8,128)(2,1)}, f32[128,1536]{1,0:T(8,128)}, f32[4,32,1536]{2,1,0:T(8,128)}) custom-call(s32[1]{0:T(128)} %bitcast.5.part_ref, f32[32,3072]{1,0:T(8,128)} %refs_0_.1, f32[32,1536]{1,0:T(8,128)} %broadcast_select_fusion.refs_1_, bf16[128,128]{1,0:T(8,128)(2,1)} %copy-done.7, ...), custom_call_target="tpu_custom_call" | custom-call | tf_op jit(solution)/shard_map/early/pallas_call | solution.py:269
  93.8 1.9 %collective-permute-done.21.even_ref = bf16[256,1536]{1,0:T(8,128)(2,1)} collective-permute-done((bf16[256,1536]{1,0:T(8,128)(2,1)}, bf16[256,1536]{1,0:T(8,128)(2,1)}, u32[]{:S(2)}, u32[]{:S(2)}) %collective-permute-start.21) | collective-permute-done | bytes 786464 | tf_op jit(solution)/shard_map/ppermute | solution.py:432
  95.7 3.4 %collective-permute-done.22.piece_ref = bf16[4,64,1536]{2,1,0:T(8,128)(2,1)} collective-permute-done((bf16[4,64,1536]{2,1,0:T(8,128)(2,1)S(1)}, bf16[4,64,1536]{2,1,0:T(8,128)(2,1)}, u32[]{:S(2)}, u32[]{:S(2)}) %collective-permute-start.22) | collective-permute-done | bytes 786464 | tf_op jit(solution)/shard_map/ppermute | solution.py:435
  99.1 5.4 %late.1 = (bf16[2,1536,512]{2,1,0:T(8,128)(2,1)}, bf16[2,16,32,1536]{3,2,1,0:T(8,128)(2,1)}) custom-call(s32[4]{0:T(128)} %pad_add_fusion.group_ref, f32[128,1536]{1,0:T(8,128)} %get-tuple-element.83.row_fit, f32[4,32,1536]{2,1,0:T(8,128)} %get-tuple-element.84.col_fit, ...), custom_call_target="tpu_custom_call", output_to_operand_aliasing={{0}: (6, {}), {1}: (7, {})} | custom-call | tf_op jit(solution)/shard_map/late/pallas_call | solution.py:341
  104.6 10.2 %kinship.2.refs_0_ = f32[3072,1536]{1,0:T(8,128)} custom-call(s32[1]{0:T(128)} %bitcast.27.part_ref, bf16[2,1536,512]{2,1,0:T(8,128)(2,1)} %get-tuple-element.87.row_ref, bf16[2,512,1536]{2,1,0:T(8,128)(2,1)} %bitcast.37), custom_call_target="tpu_custom_call" | custom-call | tf_op jit(solution)/shard_map/kinship/pallas_call | solution.py:397
  114.7 10.1 %kinship.3 = f32[3072,1536]{1,0:T(8,128)} custom-call(s32[1]{0:T(128)} %bitcast.part_ref, bf16[2,1536,512]{2,1,0:T(8,128)(2,1)} %collective-permute-done.23.row_ref, bf16[2,512,1536]{2,1,0:T(8,128)(2,1)} %bitcast.38, f32[3072,1536]{1,0:T(8,128)} %kinship.2.refs_0_), custom_call_target="tpu_custom_call", output_to_operand_aliasing={{}: (3, {})} | custom-call | tf_op jit(solution)/shard_map/kinship/pallas_call | solution.py:397
  (68 shorter events, 16.9 us)
Async XLA Ops:
  1.5 1.9 %collective-permute-start = (bf16[128,1536]{1,0:T(8,128)(2,1)S(1)}, bf16[128,1536]{1,0:T(8,128)(2,1)S(1)}, u32[]{:S(2)}, u32[]{:S(2)}) collective-permute-start(bf16[128,1536]{1,0:T(8,128)(2,1)S(1)} %bitcast.44), channel_id=1, source_target_pairs={{0,1},{1,0},{2,3},{3,2},{4,5},{5,4},{6,7},{7,6},{8,9},{9,8},{10,11... | collective-permute-start | bytes 1179656 | tf_op jit(solution)/shard_map/ppermute | solution.py:427
  3.5 23.4 %collective-permute-start.6 = (bf16[256,1536]{1,0:T(8,128)(2,1)S(1)}, bf16[256,1536]{1,0:T(8,128)(2,1)S(1)}, u32[]{:S(2)}, u32[]{:S(2)}) collective-permute-start(bf16[256,1536]{1,0:T(8,128)(2,1)S(1)} %pad_maximum_fusion.refs_6_), channel_id=1, source_target_pairs={{0,2},{1,3},{2,0},{3,1},{4,6},{5,7},{6,4},{7,5},{8,10},{9,11},{10,... | collective-permute-start | bytes 2359304 | tf_op jit(solution)/shard_map/ppermute | solution.py:432
  6.5 20.5 %collective-permute-start.5 = (bf16[256,1536]{1,0:T(8,128)(2,1)S(1)}, bf16[256,1536]{1,0:T(8,128)(2,1)S(1)}, u32[]{:S(2)}, u32[]{:S(2)}) collective-permute-start(bf16[256,1536]{1,0:T(8,128)(2,1)S(1)} %pad_maximum_fusion.refs_6_), channel_id=1, source_target_pairs={{0,0},{1,1},{2,4},{3,5},{4,2},{5,3},{6,6},{7,7},{8,8},{9,9},{10,12... | collective-permute-start | bytes 2359304 | tf_op jit(solution)/shard_map/ppermute | solution.py:432
  7.4 9.2 %collective-permute-start.3 = (bf16[64,1536]{1,0:T(8,128)(2,1)S(1)}, bf16[64,1536]{1,0:T(8,128)(2,1)S(1)}, u32[]{:S(2)}, u32[]{:S(2)}) collective-permute-start(bf16[64,1536]{1,0:T(8,128)(2,1)S(1)} %get-tuple-element.93), channel_id=1, source_target_pairs={{0,24},{8,16},{16,8},{24,0},{1,25},{9,17},{17,9},{25,1},{2,26},{10... | collective-permute-start | bytes 589832 | tf_op jit(solution)/shard_map/ppermute | solution.py:435
  9.9 9.3 %collective-permute-start.2 = (bf16[64,1536]{1,0:T(8,128)(2,1)S(1)}, bf16[64,1536]{1,0:T(8,128)(2,1)S(1)}, u32[]{:S(2)}, u32[]{:S(2)}) collective-permute-start(bf16[64,1536]{1,0:T(8,128)(2,1)S(1)} %get-tuple-element.94), channel_id=1, source_target_pairs={{0,16},{8,24},{16,0},{24,8},{1,17},{9,25},{17,1},{25,9},{2,18},{10... | collective-permute-start | bytes 589832 | tf_op jit(solution)/shard_map/ppermute | solution.py:435
  10.4 8.9 %collective-permute-start.1 = (bf16[64,1536]{1,0:T(8,128)(2,1)S(1)}, bf16[64,1536]{1,0:T(8,128)(2,1)S(1)}, u32[]{:S(2)}, u32[]{:S(2)}) collective-permute-start(bf16[64,1536]{1,0:T(8,128)(2,1)S(1)} %get-tuple-element.95), channel_id=1, source_target_pairs={{0,8},{8,0},{16,24},{24,16},{1,9},{9,1},{17,25},{25,17},{2,10},{10... | collective-permute-start | bytes 589832 | tf_op jit(solution)/shard_map/ppermute | solution.py:435
  19.3 6.7 %collective-permute-start.4 = (f32[360,128]{1,0:T(8,128)}, f32[360,128]{1,0:T(8,128)S(1)}, u32[]{:S(2)}, u32[]{:S(2)}) collective-permute-start(f32[360,128]{1,0:T(8,128)} %gram.1), channel_id=1, source_target_pairs={{0,8},{8,0},{16,24},{24,16},{1,9},{9,1},{17,25},{25,17},{2,10},{10... | collective-permute-start | bytes 552968 | tf_op jit(solution)/shard_map/ppermute | solution.py:435
  27.0 8.5 %collective-permute-start.10 = (f32[360,128]{1,0:T(8,128)S(1)}, f32[360,128]{1,0:T(8,128)S(1)}, u32[]{:S(2)}, u32[]{:S(2)}) collective-permute-start(f32[360,128]{1,0:T(8,128)S(1)} %add.104.refs_0_), channel_id=1, source_target_pairs={{0,16},{8,24},{16,0},{24,8},{1,17},{9,25},{17,1},{25,9},{2,18},{10... | collective-permute-start | bytes 552968 | tf_op jit(solution)/shard_map/ppermute | solution.py:435
  28.6 14.7 %collective-permute-start.15 = (f32[32,1536]{1,0:T(8,128)S(1)}, f32[32,1536]{1,0:T(8,128)S(1)}, u32[]{:S(2)}, u32[]{:S(2)}) collective-permute-start(f32[32,1536]{1,0:T(8,128)S(1)} %constant_dynamic-slice_fusion.1), channel_id=1, source_target_pairs={{0,8},{1,9},{10,2},{11,3},{20,28},{21,29},{30,22},{31,23}} | collective-permute-start | bytes 589832 | tf_op jit(solution)/shard_map/ppermute | solution.py:476
  30.9 18.2 %collective-permute-start.9 = (bf16[64,1536]{1,0:T(8,128)(2,1)S(1)}, bf16[64,1536]{1,0:T(8,128)(2,1)S(1)}, u32[]{:S(2)}, u32[]{:S(2)}) collective-permute-start(bf16[64,1536]{1,0:T(8,128)(2,1)S(1)} %get-tuple-element.90), channel_id=1, source_target_pairs={{0,6},{1,7},{2,4},{3,5},{4,2},{5,3},{6,0},{7,1},{8,14},{9,15},{10,... | collective-permute-start | bytes 589832 | tf_op jit(solution)/shard_map/ppermute | solution.py:438
  31.9 20.3 %collective-permute-start.8 = (bf16[64,1536]{1,0:T(8,128)(2,1)S(1)}, bf16[64,1536]{1,0:T(8,128)(2,1)S(1)}, u32[]{:S(2)}, u32[]{:S(2)}) collective-permute-start(bf16[64,1536]{1,0:T(8,128)(2,1)S(1)} %get-tuple-element.91), channel_id=1, source_target_pairs={{0,4},{1,5},{2,6},{3,7},{4,0},{5,1},{6,2},{7,3},{8,12},{9,13},{10,... | collective-permute-start | bytes 589832 | tf_op jit(solution)/shard_map/ppermute | solution.py:438
  35.6 16.6 %collective-permute-start.7 = (bf16[64,1536]{1,0:T(8,128)(2,1)S(1)}, bf16[64,1536]{1,0:T(8,128)(2,1)S(1)}, u32[]{:S(2)}, u32[]{:S(2)}) collective-permute-start(bf16[64,1536]{1,0:T(8,128)(2,1)S(1)} %get-tuple-element.92), channel_id=1, source_target_pairs={{0,2},{1,3},{2,0},{3,1},{4,6},{5,7},{6,4},{7,5},{8,10},{9,11},{10,... | collective-permute-start | bytes 589832 | tf_op jit(solution)/shard_map/ppermute | solution.py:438
  43.3 1.4 %collective-permute-start.11 = (bf16[64,128]{1,0:T(8,128)(2,1)}, bf16[64,128]{1,0:T(8,128)(2,1)S(1)}, u32[]{:S(2)}, u32[]{:S(2)}) collective-permute-start(bf16[64,128]{1,0:T(8,128)(2,1)} %solve.1), channel_id=1, source_target_pairs={{0,1},{1,0},{2,3},{3,2},{4,5},{5,4},{6,7},{7,6},{8,9},{9,8},{10,11... | collective-permute-start | bytes 49160 | tf_op jit(solution)/shard_map/ppermute | solution.py:427
  45.5 6.8 %collective-permute-start.14 = (bf16[128,128]{1,0:T(8,128)(2,1)S(1)}, bf16[128,128]{1,0:T(8,128)(2,1)S(1)}, u32[]{:S(2)}, u32[]{:S(2)}) collective-permute-start(bf16[128,128]{1,0:T(8,128)(2,1)S(1)} %pad_maximum_fusion.5.refs_2_), channel_id=1, source_target_pairs={{0,6},{1,7},{2,4},{3,5},{4,2},{5,3},{6,0},{7,1},{8,14},{9,15},{10,... | collective-permute-start | bytes 98312 | tf_op jit(solution)/shard_map/ppermute | solution.py:438
  47.0 6.6 %collective-permute-start.13 = (bf16[128,128]{1,0:T(8,128)(2,1)S(1)}, bf16[128,128]{1,0:T(8,128)(2,1)S(1)}, u32[]{:S(2)}, u32[]{:S(2)}) collective-permute-start(bf16[128,128]{1,0:T(8,128)(2,1)S(1)} %pad_maximum_fusion.5.refs_2_), channel_id=1, source_target_pairs={{0,4},{1,5},{2,6},{3,7},{4,0},{5,1},{6,2},{7,3},{8,12},{9,13},{10,... | collective-permute-start | bytes 98312 | tf_op jit(solution)/shard_map/ppermute | solution.py:438
  49.0 4.6 %collective-permute-start.12 = (bf16[128,128]{1,0:T(8,128)(2,1)S(1)}, bf16[128,128]{1,0:T(8,128)(2,1)S(1)}, u32[]{:S(2)}, u32[]{:S(2)}) collective-permute-start(bf16[128,128]{1,0:T(8,128)(2,1)S(1)} %pad_maximum_fusion.5.refs_2_), channel_id=1, source_target_pairs={{0,2},{1,3},{2,0},{3,1},{4,6},{5,7},{6,4},{7,5},{8,10},{9,11},{10,... | collective-permute-start | bytes 98312 | tf_op jit(solution)/shard_map/ppermute | solution.py:438
  53.6 23.7 %collective-permute-start.20 = (bf16[256,1536]{1,0:T(8,128)(2,1)S(1)}, bf16[256,1536]{1,0:T(8,128)(2,1)}, u32[]{:S(2)}, u32[]{:S(2)}) collective-permute-start(bf16[256,1536]{1,0:T(8,128)(2,1)S(1)} %collective-permute-done.5.refs_9_.odd_ref), channel_id=1, source_target_pairs={{0,2},{1,3},{2,0},{3,1},{4,6},{5,7},{6,4},{7,5},{8,10},{9,11},{10,... | collective-permute-start | bytes 2359304 | tf_op jit(solution)/shard_map/ppermute | solution.py:432
  53.9 23.5 %collective-permute-start.19 = (bf16[256,1536]{1,0:T(8,128)(2,1)S(1)}, bf16[256,1536]{1,0:T(8,128)(2,1)}, u32[]{:S(2)}, u32[]{:S(2)}) collective-permute-start(bf16[256,1536]{1,0:T(8,128)(2,1)S(1)} %collective-permute-done.6.refs_7_), channel_id=1, source_target_pairs={{0,0},{1,1},{2,4},{3,5},{4,2},{5,3},{6,6},{7,7},{8,8},{9,9},{10,12... | collective-permute-start | bytes 2359304 | tf_op jit(solution)/shard_map/ppermute | solution.py:432
  55.4 21.9 %collective-permute-start.17 = (bf16[4,64,1536]{2,1,0:T(8,128)(2,1)S(1)}, bf16[4,64,1536]{2,1,0:T(8,128)(2,1)}, u32[]{:S(2)}, u32[]{:S(2)}) collective-permute-start(bf16[4,64,1536]{2,1,0:T(8,128)(2,1)S(1)} %pad_maximum_fusion.2.refs_11_), channel_id=1, source_target_pairs={{0,16},{8,24},{16,0},{24,8},{1,17},{9,25},{17,1},{25,9},{2,18},{10... | collective-permute-start | bytes 2359304 | tf_op jit(solution)/shard_map/ppermute | solution.py:435
  57.0 20.4 %collective-permute-start.16 = (bf16[4,64,1536]{2,1,0:T(8,128)(2,1)S(1)}, bf16[4,64,1536]{2,1,0:T(8,128)(2,1)}, u32[]{:S(2)}, u32[]{:S(2)}) collective-permute-start(bf16[4,64,1536]{2,1,0:T(8,128)(2,1)S(1)} %pad_maximum_fusion.2.refs_11_), channel_id=1, source_target_pairs={{0,8},{8,0},{16,24},{24,16},{1,9},{9,1},{17,25},{25,17},{2,10},{10... | collective-permute-start | bytes 2359304 | tf_op jit(solution)/shard_map/ppermute | solution.py:435
  58.1 18.5 %collective-permute-start.18 = (f32[32,1536]{1,0:T(8,128)S(1)}, f32[32,1536]{1,0:T(8,128)S(1)}, u32[]{:S(2)}, u32[]{:S(2)}) collective-permute-start(f32[32,1536]{1,0:T(8,128)S(1)} %broadcast_select_fusion.1), channel_id=1, source_target_pairs={{0,16},{1,17},{8,24},{9,25},{2,18},{3,19},{10,26},{11,27},{20,4},{... | collective-permute-start | bytes 589832 | tf_op jit(solution)/shard_map/ppermute | solution.py:476
  77.4 18.4 %collective-permute-start.21 = (bf16[256,1536]{1,0:T(8,128)(2,1)}, bf16[256,1536]{1,0:T(8,128)(2,1)}, u32[]{:S(2)}, u32[]{:S(2)}) collective-permute-start(bf16[256,1536]{1,0:T(8,128)(2,1)} %collective-permute-done.19.refs_10_), channel_id=1, source_target_pairs={{0,2},{1,3},{2,0},{3,1},{4,6},{5,7},{6,4},{7,5},{8,10},{9,11},{10,... | collective-permute-start | bytes 2359304 | tf_op jit(solution)/shard_map/ppermute | solution.py:432
  80.2 18.8 %collective-permute-start.22 = (bf16[4,64,1536]{2,1,0:T(8,128)(2,1)S(1)}, bf16[4,64,1536]{2,1,0:T(8,128)(2,1)}, u32[]{:S(2)}, u32[]{:S(2)}) collective-permute-start(bf16[4,64,1536]{2,1,0:T(8,128)(2,1)S(1)} %pad_maximum_fusion.2.refs_11_), channel_id=1, source_target_pairs={{0,24},{8,16},{16,8},{24,0},{1,25},{9,17},{17,9},{25,1},{2,26},{10... | collective-permute-start | bytes 2359304 | tf_op jit(solution)/shard_map/ppermute | solution.py:435
  104.5 10.2 %collective-permute-start.23 = (bf16[2,1536,512]{2,1,0:T(8,128)(2,1)}, bf16[2,1536,512]{2,1,0:T(8,128)(2,1)}, u32[]{:S(2)}, u32[]{:S(2)}) collective-permute-start(bf16[2,1536,512]{2,1,0:T(8,128)(2,1)} %get-tuple-element.87.row_ref), channel_id=1, source_target_pairs={{0,1},{1,0},{2,3},{3,2},{4,5},{5,4},{6,7},{7,6},{8,9},{9,8},{10,11... | collective-permute-start | bytes 9437192 | tf_op jit(solution)/shard_map/ppermute | solution.py:427
  (11 other events, 283.1 us)

commit v12 on v11

--- a/solution.py
+++ b/solution.py
@@ -304,68 +304,79 @@
     early_kernel(rows, near, *refs)
 
 
-def late_kernel(rows, group_ref, row_fit, col_fit, even_ref, odd_ref, piece_ref, *refs):
-    row_out, col_out, block, sem = refs[2:]
+def late_kernel(rows, group_ref, row_fit, col_fit, piece_ref, even_ref, odd_ref, *refs):
+    row_out, col_out, block, row_part, col_part, block_sem, row_sems, col_sems = refs[2:]
     plane = lax.axis_index("cols") // (lax.axis_size("cols") // rows)
-    step = pl.program_id(0)
     last = by_even(rows - 1, plane, rows)
 
-    @pl.when((step == 0) & last)
+    @pl.when(last)
     def _():
-        pltpu.make_async_copy(even_ref, block, sem).start()
-
-    @pl.when((step == 0) & jnp.logical_not(last))
+        pltpu.make_async_copy(even_ref, block, block_sem).start()
+
+    @pl.when(jnp.logical_not(last))
     def _():
-        pltpu.make_async_copy(odd_ref, block, sem).start()
-
-    resid, sdev = weigh(col_fit[0], *parted(piece_ref[0], 1))
-    col_out[0, 0] = resid.astype(BF16)
-    col_out[1, 0] = sdev.astype(BF16)
-
-    @pl.when(step == rows - 1)
-    def _():
-        pltpu.make_async_copy(odd_ref, block, sem).wait()
-        resid, sdev = weigh(row_fit[...], *parted(block[...], rows))
-        chip = row_fit.shape[0]
-        if row_out.shape[2] != chip:
-            row_out[...] = jnp.zeros(row_out.shape, BF16)
-        row_out[0, :, 0:chip] = resid.T.astype(BF16)
-        row_out[1, :, 0:chip] = sdev.T.astype(BF16)
+        pltpu.make_async_copy(odd_ref, block, block_sem).start()
+
+    copies = []
+    for e in range(rows):
+        resid, sdev = weigh(col_fit[e], *parted(piece_ref[e], 1))
+        col_part[e, 0] = resid.astype(BF16)
+        col_part[e, 1] = sdev.astype(BF16)
+        for i in range(2):
+            copies.append(
+                pltpu.make_async_copy(col_part.at[e, i], col_out.at[i, group_ref[e]], col_sems.at[2 * e + i])
+            )
+            copies[-1].start()
+    chip, width = row_fit.shape
+    space = row_part.shape[2]
+    if space != chip:
+        row_part[...] = jnp.zeros(row_part.shape, BF16)
+    pltpu.make_async_copy(odd_ref, block, block_sem).wait()
+    wide = width // row_sems.shape[0]
+    for at in range(0, width, wide):
+        span = slice(at, at + wide)
+        resid, sdev = weigh(row_fit[:, span], *parted(block[:, span], rows))
+        row_part[0, span, 0:chip] = resid.astype(BF16).T
+        row_part[1, span, 0:chip] = sdev.astype(BF16).T
+        copies.append(
+            pltpu.make_async_copy(
+                row_part.at[:, span, :],
+                row_out.at[:, span, (rows - 1) * space : rows * space],
+                row_sems.at[at // wide],
+            )
+        )
+        copies[-1].start()
+    for copy in copies:
+        copy.wait()
 
 
 def late_call(rows, groups, row_fit, col_fit, even, odd, piece, row_panel, col_panel):
     chip, width = row_fit.shape
     height = chip // rows
     space = row_panel.shape[2] // rows
+    wide = 256 if width % 256 == 0 else width
     anywhere = pl.BlockSpec(memory_space=pl.ANY)
+    here = pl.BlockSpec(memory_space=pltpu.VMEM)
     return pl.pallas_call(
         functools.partial(late_kernel, rows),
-        grid_spec=pltpu.PrefetchScalarGridSpec(
-            num_scalar_prefetch=1,
-            grid=(rows,),
-            in_specs=[
-                pl.BlockSpec((chip, width), lambda e, at: (0, 0)),
-                pl.BlockSpec((1, height, width), lambda e, at: (e, 0, 0)),
-                anywhere,
-                anywhere,
-                pl.BlockSpec((1, 2 * height, width), lambda e, at: (e, 0, 0)),
-                anywhere,
-                anywhere,
-            ],
-            out_specs=(
-                pl.BlockSpec((2, width, space), lambda e, at: (0, 0, rows - 1)),
-                pl.BlockSpec((2, 1, height, width), lambda e, at: (0, at[e], 0, 0)),
-            ),
-            scratch_shapes=[pltpu.VMEM((2 * chip, width), BF16), pltpu.SemaphoreType.DMA],
-        ),
+        in_specs=[pl.BlockSpec(memory_space=pltpu.SMEM), here, here, here] + [anywhere] * 4,
+        out_specs=(anywhere, anywhere),
         out_shape=(
             jax.ShapeDtypeStruct(row_panel.shape, BF16),
             jax.ShapeDtypeStruct(col_panel.shape, BF16),
         ),
+        scratch_shapes=[
+            pltpu.VMEM((2 * chip, width), BF16),
+            pltpu.VMEM((2, width, space), BF16),
+            pltpu.VMEM((rows, 2, height, width), BF16),
+            pltpu.SemaphoreType.DMA,
+            pltpu.SemaphoreType.DMA((width // wide,)),
+            pltpu.SemaphoreType.DMA((2 * rows,)),
+        ],
         input_output_aliases={6: 0, 7: 1},
         compiler_params=pltpu.CompilerParams(vmem_limit_bytes=VMEM_ALL),
         name="late",
-    )(groups, row_fit, col_fit, even, odd, piece, row_panel, col_panel)
+    )(groups, row_fit, col_fit, piece, even, odd, row_panel, col_panel)
 
 
 def quotient(numer, denom):
@@ -476,9 +487,10 @@
         return jnp.where((row ^ plane) < hop, x, lax.ppermute(x, ("rows", "cols"), moves))
 
     gram = gram_call(dosage, present, components)
-    quarters, gram = lax.optimization_barrier((quarters, gram))
+    col_comps = lax.dynamic_slice_in_dim(components, core * width, width, 1)
+    quarters, gram, col_comps = lax.optimization_barrier((quarters, gram, col_comps))
     gram = gram + beside(gram, hops[0])
-    col_comps = lax.dynamic_slice_in_dim(components, core * width, width, 1)
+    col_comps = doubled(col_comps, hops[0])
     quarters, gram, col_comps, held, odd, even = lax.optimization_barrier(
         (jnp.stack(quarters), gram, col_comps, held, odd, even)
     )
@@ -489,13 +501,12 @@
         gram = gram + beside(gram, hop)
     coef = solve_call([gram, beside(gram, hops[-1])], comps, markers)
     coef = by_core([swap(coef, k) for k in range(ratio)])
-    col_comps = doubled(col_comps, hops[0])
+    for hop in hops[1:]:
+        col_comps = doubled(col_comps, hop)
     coefs = [across(coef, e) for e in range(rows)]
     moved, coefs, col_comps, held, odd, even = lax.optimization_barrier(
         (jnp.stack(moved), coefs, col_comps, held, odd, even)
     )
-    for hop in hops[1:]:
-        col_comps = doubled(col_comps, hop)
     near = [moved]
     for step in range(rows - 3):
         odd, even = odd + [exchange(even[-1], 1)], even + [exchange(odd[-1], 0)]

time: 125 us -> 125 us (level)
  starting transfers between devices: 37.1 us -> 34.7 us
    ppermute x5, waiting for transfers between devices: 1.93 us -> 18.2 us  [exchange(): return lax.ppermute(x, 'cols', pairs(lambda z, c: (other[z], c)))]
    ppermute x2, waiting for transfers between devices: 14.4 us -> 2.09 us  [doubled(): lax.ppermute(x, ('rows', 'cols'), moves)]
    ppermute x8, starting transfers between devices: 12.7 us -> 7.87 us  [beside(): lax.ppermute(x, 'rows', [(i, i ^ d) for i in range(rows)])]
    ppermute x6, starting transfers between devices: 9.15 us -> 11 us  [across(): return lax.ppermute(x, 'cols', pairs(lambda z, c: (z ^ e, c))) if e else x]
    ppermute x8, waiting for transfers between devices: 11.2 us -> 9.74 us  [beside(): lax.ppermute(x, 'rows', [(i, i ^ d) for i in range(rows)])]
  transfers between devices with their start and end apart: 24 -> 24, of which waited for: 11 -> 14; matrix products, arithmetic and copies ran while one was open for 3% -> 4% of each run, Pallas kernels for 26% -> 26%
where the time goes in v12:
time: 125 us
  Pallas kernels  47.2 us (38%)
  waiting for transfers between devices  35 us (28%)
  starting transfers between devices  34.7 us (28%)
  other arithmetic  5.83 us (5%)
  local copies, waits for them, and re-layouts  1.66 us (1%)
    pallas_call x2, Pallas kernels, kin_call(): pl.pallas_call(kin_kernel, grid_spec=pltpu.PrefetchScalarGridSpec(num_sca...  20.3 us
    ppermute x5, waiting for transfers between devices, exchange(): return lax.ppermute(x, 'cols', pairs(lambda z, c: (other[z], c)))  18.2 us
    ppermute x6, starting transfers between devices, across(): return lax.ppermute(x, 'cols', pairs(lambda z, c: (z ^ e, c))) if e else x  11 us
    ppermute x8, waiting for transfers between devices, beside(): lax.ppermute(x, 'rows', [(i, i ^ d) for i in range(rows)])  9.74 us
    pallas_call x1, Pallas kernels, early_call(): pl.pallas_call(functools.partial(early_kernel_at, rows, len(pieces)), gri...  9.57 us
    ppermute x5, starting transfers between devices, exchange(): return lax.ppermute(x, 'cols', pairs(lambda z, c: (other[z], c)))  8.9 us
    ppermute x8, starting transfers between devices, beside(): lax.ppermute(x, 'rows', [(i, i ^ d) for i in range(rows)])  7.87 us
    pallas_call x1, Pallas kernels, solve_call(): pl.pallas_call(functools.partial(solve_kernel, comps, markers), out_shape...  7.09 us
  transfers between devices with their start and end apart: 24, of which 14 were waited for; matrix products, arithmetic and copies ran while one was open for 4% of the time, Pallas kernels for 26%

profile of v12, /device:TPU:0, one launch (start us, length us, event | category | flops | bytes accessed | tf_op | source)
XLA Modules:
  0.0 124.7 jit_solution(7440074076989115433)
XLA Ops:
  3.5 3.0 %collective-permute-start.7 = (bf16[256,1536]{1,0:T(8,128)(2,1)S(1)}, bf16[256,1536]{1,0:T(8,128)(2,1)S(1)}, u32[]{:S(2)}, u32[]{:S(2)}) collective-permute-start(bf16[256,1536]{1,0:T(8,128)(2,1)S(1)} %pad_maximum_fusion.refs_6_), channel_id=1, source_target_pairs={{0,2},{1,3},{2,0},{3,1},{4,6},{5,7},{6,4},{7,5},{8,10},{9,11},{10,... | collective-permute-start | bytes 2359304 | tf_op jit(solution)/shard_map/ppermute | solution.py:443
  8.1 2.4 %collective-permute-start.3 = (bf16[64,1536]{1,0:T(8,128)(2,1)}, bf16[64,1536]{1,0:T(8,128)(2,1)S(1)}, u32[]{:S(2)}, u32[]{:S(2)}) collective-permute-start(bf16[64,1536]{1,0:T(8,128)(2,1)} %get-tuple-element.95), channel_id=1, source_target_pairs={{0,24},{8,16},{16,8},{24,0},{1,25},{9,17},{17,9},{25,1},{2,26},{10... | collective-permute-start | bytes 589832 | tf_op jit(solution)/shard_map/ppermute | solution.py:446
  11.7 5.6 %gram.1 = f32[360,128]{1,0:T(8,128)} custom-call(s32[64,3072]{1,0:T(8,128)} %dosage_ref, s32[64,3072]{1,0:T(8,128)} %present_ref, f32[32,3072]{1,0:T(8,128)} %refs_0_.1), custom_call_target="tpu_custom_call" | custom-call | tf_op jit(solution)/shard_map/gram/pallas_call | solution.py:63
  17.3 2.8 %collective-permute-done.2 = bf16[64,1536]{1,0:T(8,128)(2,1)S(1)} collective-permute-done((bf16[64,1536]{1,0:T(8,128)(2,1)}, bf16[64,1536]{1,0:T(8,128)(2,1)S(1)}, u32[]{:S(2)}, u32[]{:S(2)}) %collective-permute-start.2) | collective-permute-done | bytes 196640 | tf_op jit(solution)/shard_map/ppermute | solution.py:446
  21.8 2.4 %collective-permute-start.5 = (f32[32,1536]{1,0:T(8,128)S(1)}, f32[32,1536]{1,0:T(8,128)S(1)}, u32[]{:S(2)}, u32[]{:S(2)}) collective-permute-start(f32[32,1536]{1,0:T(8,128)S(1)} %constant_dynamic-slice_fusion.1), channel_id=1, source_target_pairs={{0,8},{1,9},{10,2},{11,3},{20,28},{21,29},{30,22},{31,23}} | collective-permute-start | bytes 589832 | tf_op jit(solution)/shard_map/ppermute | solution.py:487
  25.3 1.9 %collective-permute-done.4 = f32[360,128]{1,0:T(8,128)S(1)} collective-permute-done((f32[360,128]{1,0:T(8,128)}, f32[360,128]{1,0:T(8,128)S(1)}, u32[]{:S(2)}, u32[]{:S(2)}) %collective-permute-start.4) | collective-permute-done | bytes 184352 | tf_op jit(solution)/shard_map/ppermute | solution.py:446
  28.1 2.1 %collective-permute-done.5 = f32[32,1536]{1,0:T(8,128)S(1)} collective-permute-done((f32[32,1536]{1,0:T(8,128)S(1)}, f32[32,1536]{1,0:T(8,128)S(1)}, u32[]{:S(2)}, u32[]{:S(2)}) %collective-permute-start.5) | collective-permute-done | bytes 196640 | tf_op jit(solution)/shard_map/ppermute | solution.py:487
  30.3 3.9 %collective-permute-start.16 = (f32[32,1536]{1,0:T(8,128)S(1)}, f32[32,1536]{1,0:T(8,128)S(1)}, u32[]{:S(2)}, u32[]{:S(2)}) collective-permute-start(f32[32,1536]{1,0:T(8,128)S(1)} %broadcast_select_fusion.1), channel_id=1, source_target_pairs={{0,16},{1,17},{8,24},{9,25},{2,18},{3,19},{10,26},{11,27},{20,4},{... | collective-permute-start | bytes 589832 | tf_op jit(solution)/shard_map/ppermute | solution.py:487
  34.3 2.3 %collective-permute-start.10 = (bf16[64,1536]{1,0:T(8,128)(2,1)S(1)}, bf16[64,1536]{1,0:T(8,128)(2,1)S(1)}, u32[]{:S(2)}, u32[]{:S(2)}) collective-permute-start(bf16[64,1536]{1,0:T(8,128)(2,1)S(1)} %get-tuple-element.92), channel_id=1, source_target_pairs={{0,6},{1,7},{2,4},{3,5},{4,2},{5,3},{6,0},{7,1},{8,14},{9,15},{10,... | collective-permute-start | bytes 589832 | tf_op jit(solution)/shard_map/ppermute | solution.py:449
  36.6 4.3 %collective-permute-start.9 = (bf16[64,1536]{1,0:T(8,128)(2,1)S(1)}, bf16[64,1536]{1,0:T(8,128)(2,1)S(1)}, u32[]{:S(2)}, u32[]{:S(2)}) collective-permute-start(bf16[64,1536]{1,0:T(8,128)(2,1)S(1)} %get-tuple-element.93), channel_id=1, source_target_pairs={{0,4},{1,5},{2,6},{3,7},{4,0},{5,1},{6,2},{7,3},{8,12},{9,13},{10,... | collective-permute-start | bytes 589832 | tf_op jit(solution)/shard_map/ppermute | solution.py:449
  41.6 7.1 %solve.1 = bf16[64,128]{1,0:T(8,128)(2,1)} custom-call(f32[360,128]{1,0:T(8,128)} %copy-done.8, f32[360,128]{1,0:T(8,128)} %copy-done.9), custom_call_target="tpu_custom_call" | custom-call | tf_op jit(solution)/shard_map/solve/pallas_call | solution.py:152
  50.8 1.5 %collective-permute-start.15 = (bf16[128,128]{1,0:T(8,128)(2,1)S(1)}, bf16[128,128]{1,0:T(8,128)(2,1)S(1)}, u32[]{:S(2)}, u32[]{:S(2)}) collective-permute-start(bf16[128,128]{1,0:T(8,128)(2,1)S(1)} %pad_maximum_fusion.5.refs_2_), channel_id=1, source_target_pairs={{0,6},{1,7},{2,4},{3,5},{4,2},{5,3},{6,0},{7,1},{8,14},{9,15},{10,... | collective-permute-start | bytes 98312 | tf_op jit(solution)/shard_map/ppermute | solution.py:449
  52.4 2.0 %collective-permute-start.14 = (bf16[128,128]{1,0:T(8,128)(2,1)S(1)}, bf16[128,128]{1,0:T(8,128)(2,1)S(1)}, u32[]{:S(2)}, u32[]{:S(2)}) collective-permute-start(bf16[128,128]{1,0:T(8,128)(2,1)S(1)} %pad_maximum_fusion.5.refs_2_), channel_id=1, source_target_pairs={{0,4},{1,5},{2,6},{3,7},{4,0},{5,1},{6,2},{7,3},{8,12},{9,13},{10,... | collective-permute-start | bytes 98312 | tf_op jit(solution)/shard_map/ppermute | solution.py:449
  59.2 1.6 %collective-permute-start.19 = (bf16[256,1536]{1,0:T(8,128)(2,1)S(1)}, bf16[256,1536]{1,0:T(8,128)(2,1)}, u32[]{:S(2)}, u32[]{:S(2)}) collective-permute-start(bf16[256,1536]{1,0:T(8,128)(2,1)S(1)} %collective-permute-done.7.refs_7_), channel_id=1, source_target_pairs={{0,0},{1,1},{2,4},{3,5},{4,2},{5,3},{6,6},{7,7},{8,8},{9,9},{10,12... | collective-permute-start | bytes 2359304 | tf_op jit(solution)/shard_map/ppermute | solution.py:443
  61.4 15.3 %collective-permute-done.20.refs_8_ = bf16[256,1536]{1,0:T(8,128)(2,1)S(1)} collective-permute-done((bf16[256,1536]{1,0:T(8,128)(2,1)S(1)}, bf16[256,1536]{1,0:T(8,128)(2,1)S(1)}, u32[]{:S(2)}, u32[]{:S(2)}) %collective-permute-start.20) | collective-permute-done | bytes 786464 | tf_op jit(solution)/shard_map/ppermute | solution.py:443
  76.7 2.0 %collective-permute-done.18.refs_13_ = bf16[4,64,1536]{2,1,0:T(8,128)(2,1)S(1)} collective-permute-done((bf16[4,64,1536]{2,1,0:T(8,128)(2,1)S(1)}, bf16[4,64,1536]{2,1,0:T(8,128)(2,1)S(1)}, u32[]{:S(2)}, u32[]{:S(2)}) %collective-permute-start.18) | collective-permute-done | bytes 786464 | tf_op jit(solution)/shard_map/ppermute | solution.py:446
  78.9 2.7 %collective-permute-start.22 = (bf16[256,1536]{1,0:T(8,128)(2,1)}, bf16[256,1536]{1,0:T(8,128)(2,1)}, u32[]{:S(2)}, u32[]{:S(2)}) collective-permute-start(bf16[256,1536]{1,0:T(8,128)(2,1)} %collective-permute-done.19.refs_10_), channel_id=1, source_target_pairs={{0,2},{1,3},{2,0},{3,1},{4,6},{5,7},{6,4},{7,5},{8,10},{9,11},{10,... | collective-permute-start | bytes 2359304 | tf_op jit(solution)/shard_map/ppermute | solution.py:443
  81.6 2.2 %collective-permute-start.21 = (bf16[4,64,1536]{2,1,0:T(8,128)(2,1)S(1)}, bf16[4,64,1536]{2,1,0:T(8,128)(2,1)}, u32[]{:S(2)}, u32[]{:S(2)}) collective-permute-start(bf16[4,64,1536]{2,1,0:T(8,128)(2,1)S(1)} %pad_maximum_fusion.2.refs_11_), channel_id=1, source_target_pairs={{0,24},{8,16},{16,8},{24,0},{1,25},{9,17},{17,9},{25,1},{2,26},{10... | collective-permute-start | bytes 2359304 | tf_op jit(solution)/shard_map/ppermute | solution.py:446
  84.5 9.6 %early.1 = (bf16[2,1536,512]{2,1,0:T(8,128)(2,1)}, bf16[2,16,32,1536]{3,2,1,0:T(8,128)(2,1)}, f32[128,1536]{1,0:T(8,128)}, f32[4,32,1536]{2,1,0:T(8,128)}) custom-call(s32[1]{0:T(128)} %bitcast.5.part_ref, f32[32,3072]{1,0:T(8,128)} %refs_0_.1, f32[32,1536]{1,0:T(8,128)} %broadcast_select_fusion.refs_1_, bf16[128,128]{1,0:T(8,128)(2,1)} %copy-done.10, ...), custom_call_target="tpu_custom_call" | custom-call | tf_op jit(solution)/shard_map/early/pallas_call | solution.py:269
  94.0 2.9 %collective-permute-done.22.even_ref = bf16[256,1536]{1,0:T(8,128)(2,1)} collective-permute-done((bf16[256,1536]{1,0:T(8,128)(2,1)}, bf16[256,1536]{1,0:T(8,128)(2,1)}, u32[]{:S(2)}, u32[]{:S(2)}) %collective-permute-start.22) | collective-permute-done | bytes 786464 | tf_op jit(solution)/shard_map/ppermute | solution.py:443
  97.0 2.7 %collective-permute-done.21.piece_ref = bf16[4,64,1536]{2,1,0:T(8,128)(2,1)} collective-permute-done((bf16[4,64,1536]{2,1,0:T(8,128)(2,1)S(1)}, bf16[4,64,1536]{2,1,0:T(8,128)(2,1)}, u32[]{:S(2)}, u32[]{:S(2)}) %collective-permute-start.21) | collective-permute-done | bytes 786464 | tf_op jit(solution)/shard_map/ppermute | solution.py:446
  99.7 4.6 %late.1 = (bf16[2,1536,512]{2,1,0:T(8,128)(2,1)}, bf16[2,16,32,1536]{3,2,1,0:T(8,128)(2,1)}) custom-call(s32[4]{0:T(128)} %pad_add_fusion.group_ref, f32[128,1536]{1,0:T(8,128)} %get-tuple-element.85.row_fit, f32[4,32,1536]{2,1,0:T(8,128)} %get-tuple-element.86.col_fit, ...), custom_call_target="tpu_custom_call", output_to_operand_aliasing={{0}: (6, {}), {1}: (7, {})} | custom-call | tf_op jit(solution)/shard_map/late/pallas_call | solution.py:360
  104.4 10.1 %kinship.2.refs_0_ = f32[3072,1536]{1,0:T(8,128)} custom-call(s32[1]{0:T(128)} %bitcast.27.part_ref, bf16[2,1536,512]{2,1,0:T(8,128)(2,1)} %get-tuple-element.89.row_ref, bf16[2,512,1536]{2,1,0:T(8,128)(2,1)} %bitcast.37), custom_call_target="tpu_custom_call" | custom-call | tf_op jit(solution)/shard_map/kinship/pallas_call | solution.py:408
  114.6 10.1 %kinship.3 = f32[3072,1536]{1,0:T(8,128)} custom-call(s32[1]{0:T(128)} %bitcast.part_ref, bf16[2,1536,512]{2,1,0:T(8,128)(2,1)} %collective-permute-done.23.row_ref, bf16[2,512,1536]{2,1,0:T(8,128)(2,1)} %bitcast.38, f32[3072,1536]{1,0:T(8,128)} %kinship.2.refs_0_), custom_call_target="tpu_custom_call", output_to_operand_aliasing={{}: (3, {})} | custom-call | tf_op jit(solution)/shard_map/kinship/pallas_call | solution.py:408
  (74 shorter events, 19.1 us)
Async XLA Ops:
  1.5 1.9 %collective-permute-start = (bf16[128,1536]{1,0:T(8,128)(2,1)S(1)}, bf16[128,1536]{1,0:T(8,128)(2,1)S(1)}, u32[]{:S(2)}, u32[]{:S(2)}) collective-permute-start(bf16[128,1536]{1,0:T(8,128)(2,1)S(1)} %bitcast.44), channel_id=1, source_target_pairs={{0,1},{1,0},{2,3},{3,2},{4,5},{5,4},{6,7},{7,6},{8,9},{9,8},{10,11... | collective-permute-start | bytes 1179656 | tf_op jit(solution)/shard_map/ppermute | solution.py:438
  3.5 26.7 %collective-permute-start.7 = (bf16[256,1536]{1,0:T(8,128)(2,1)S(1)}, bf16[256,1536]{1,0:T(8,128)(2,1)S(1)}, u32[]{:S(2)}, u32[]{:S(2)}) collective-permute-start(bf16[256,1536]{1,0:T(8,128)(2,1)S(1)} %pad_maximum_fusion.refs_6_), channel_id=1, source_target_pairs={{0,2},{1,3},{2,0},{3,1},{4,6},{5,7},{6,4},{7,5},{8,10},{9,11},{10,... | collective-permute-start | bytes 2359304 | tf_op jit(solution)/shard_map/ppermute | solution.py:443
  6.5 23.7 %collective-permute-start.6 = (bf16[256,1536]{1,0:T(8,128)(2,1)S(1)}, bf16[256,1536]{1,0:T(8,128)(2,1)S(1)}, u32[]{:S(2)}, u32[]{:S(2)}) collective-permute-start(bf16[256,1536]{1,0:T(8,128)(2,1)S(1)} %pad_maximum_fusion.refs_6_), channel_id=1, source_target_pairs={{0,0},{1,1},{2,4},{3,5},{4,2},{5,3},{6,6},{7,7},{8,8},{9,9},{10,12... | collective-permute-start | bytes 2359304 | tf_op jit(solution)/shard_map/ppermute | solution.py:443
  8.1 9.2 %collective-permute-start.3 = (bf16[64,1536]{1,0:T(8,128)(2,1)}, bf16[64,1536]{1,0:T(8,128)(2,1)S(1)}, u32[]{:S(2)}, u32[]{:S(2)}) collective-permute-start(bf16[64,1536]{1,0:T(8,128)(2,1)} %get-tuple-element.95), channel_id=1, source_target_pairs={{0,24},{8,16},{16,8},{24,0},{1,25},{9,17},{17,9},{25,1},{2,26},{10... | collective-permute-start | bytes 589832 | tf_op jit(solution)/shard_map/ppermute | solution.py:446
  10.6 9.5 %collective-permute-start.2 = (bf16[64,1536]{1,0:T(8,128)(2,1)}, bf16[64,1536]{1,0:T(8,128)(2,1)S(1)}, u32[]{:S(2)}, u32[]{:S(2)}) collective-permute-start(bf16[64,1536]{1,0:T(8,128)(2,1)} %get-tuple-element.96), channel_id=1, source_target_pairs={{0,16},{8,24},{16,0},{24,8},{1,17},{9,25},{17,1},{25,9},{2,18},{10... | collective-permute-start | bytes 589832 | tf_op jit(solution)/shard_map/ppermute | solution.py:446
  11.1 9.2 %collective-permute-start.1 = (bf16[64,1536]{1,0:T(8,128)(2,1)}, bf16[64,1536]{1,0:T(8,128)(2,1)}, u32[]{:S(2)}, u32[]{:S(2)}) collective-permute-start(bf16[64,1536]{1,0:T(8,128)(2,1)} %get-tuple-element.97), channel_id=1, source_target_pairs={{0,8},{8,0},{16,24},{24,16},{1,9},{9,1},{17,25},{25,17},{2,10},{10... | collective-permute-start | bytes 589832 | tf_op jit(solution)/shard_map/ppermute | solution.py:446
  20.3 6.8 %collective-permute-start.4 = (f32[360,128]{1,0:T(8,128)}, f32[360,128]{1,0:T(8,128)S(1)}, u32[]{:S(2)}, u32[]{:S(2)}) collective-permute-start(f32[360,128]{1,0:T(8,128)} %gram.1), channel_id=1, source_target_pairs={{0,8},{8,0},{16,24},{24,16},{1,9},{9,1},{17,25},{25,17},{2,10},{10... | collective-permute-start | bytes 552968 | tf_op jit(solution)/shard_map/ppermute | solution.py:446
  21.8 8.4 %collective-permute-start.5 = (f32[32,1536]{1,0:T(8,128)S(1)}, f32[32,1536]{1,0:T(8,128)S(1)}, u32[]{:S(2)}, u32[]{:S(2)}) collective-permute-start(f32[32,1536]{1,0:T(8,128)S(1)} %constant_dynamic-slice_fusion.1), channel_id=1, source_target_pairs={{0,8},{1,9},{10,2},{11,3},{20,28},{21,29},{30,22},{31,23}} | collective-permute-start | bytes 589832 | tf_op jit(solution)/shard_map/ppermute | solution.py:487
  30.3 10.7 %collective-permute-start.11 = (f32[360,128]{1,0:T(8,128)S(1)}, f32[360,128]{1,0:T(8,128)S(1)}, u32[]{:S(2)}, u32[]{:S(2)}) collective-permute-start(f32[360,128]{1,0:T(8,128)S(1)} %add.105.refs_0_), channel_id=1, source_target_pairs={{0,16},{8,24},{16,0},{24,8},{1,17},{9,25},{17,1},{25,9},{2,18},{10... | collective-permute-start | bytes 552968 | tf_op jit(solution)/shard_map/ppermute | solution.py:446
  30.3 18.4 %collective-permute-start.16 = (f32[32,1536]{1,0:T(8,128)S(1)}, f32[32,1536]{1,0:T(8,128)S(1)}, u32[]{:S(2)}, u32[]{:S(2)}) collective-permute-start(f32[32,1536]{1,0:T(8,128)S(1)} %broadcast_select_fusion.1), channel_id=1, source_target_pairs={{0,16},{1,17},{8,24},{9,25},{2,18},{3,19},{10,26},{11,27},{20,4},{... | collective-permute-start | bytes 589832 | tf_op jit(solution)/shard_map/ppermute | solution.py:487
  34.3 20.0 %collective-permute-start.10 = (bf16[64,1536]{1,0:T(8,128)(2,1)S(1)}, bf16[64,1536]{1,0:T(8,128)(2,1)S(1)}, u32[]{:S(2)}, u32[]{:S(2)}) collective-permute-start(bf16[64,1536]{1,0:T(8,128)(2,1)S(1)} %get-tuple-element.92), channel_id=1, source_target_pairs={{0,6},{1,7},{2,4},{3,5},{4,2},{5,3},{6,0},{7,1},{8,14},{9,15},{10,... | collective-permute-start | bytes 589832 | tf_op jit(solution)/shard_map/ppermute | solution.py:449
  36.6 18.7 %collective-permute-start.9 = (bf16[64,1536]{1,0:T(8,128)(2,1)S(1)}, bf16[64,1536]{1,0:T(8,128)(2,1)S(1)}, u32[]{:S(2)}, u32[]{:S(2)}) collective-permute-start(bf16[64,1536]{1,0:T(8,128)(2,1)S(1)} %get-tuple-element.93), channel_id=1, source_target_pairs={{0,4},{1,5},{2,6},{3,7},{4,0},{5,1},{6,2},{7,3},{8,12},{9,13},{10,... | collective-permute-start | bytes 589832 | tf_op jit(solution)/shard_map/ppermute | solution.py:449
  40.9 14.4 %collective-permute-start.8 = (bf16[64,1536]{1,0:T(8,128)(2,1)S(1)}, bf16[64,1536]{1,0:T(8,128)(2,1)S(1)}, u32[]{:S(2)}, u32[]{:S(2)}) collective-permute-start(bf16[64,1536]{1,0:T(8,128)(2,1)S(1)} %get-tuple-element.94), channel_id=1, source_target_pairs={{0,2},{1,3},{2,0},{3,1},{4,6},{5,7},{6,4},{7,5},{8,10},{9,11},{10,... | collective-permute-start | bytes 589832 | tf_op jit(solution)/shard_map/ppermute | solution.py:449
  48.7 1.4 %collective-permute-start.12 = (bf16[64,128]{1,0:T(8,128)(2,1)}, bf16[64,128]{1,0:T(8,128)(2,1)S(1)}, u32[]{:S(2)}, u32[]{:S(2)}) collective-permute-start(bf16[64,128]{1,0:T(8,128)(2,1)} %solve.1), channel_id=1, source_target_pairs={{0,1},{1,0},{2,3},{3,2},{4,5},{5,4},{6,7},{7,6},{8,9},{9,8},{10,11... | collective-permute-start | bytes 49160 | tf_op jit(solution)/shard_map/ppermute | solution.py:438
  50.8 6.1 %collective-permute-start.15 = (bf16[128,128]{1,0:T(8,128)(2,1)S(1)}, bf16[128,128]{1,0:T(8,128)(2,1)S(1)}, u32[]{:S(2)}, u32[]{:S(2)}) collective-permute-start(bf16[128,128]{1,0:T(8,128)(2,1)S(1)} %pad_maximum_fusion.5.refs_2_), channel_id=1, source_target_pairs={{0,6},{1,7},{2,4},{3,5},{4,2},{5,3},{6,0},{7,1},{8,14},{9,15},{10,... | collective-permute-start | bytes 98312 | tf_op jit(solution)/shard_map/ppermute | solution.py:449
  52.4 5.6 %collective-permute-start.14 = (bf16[128,128]{1,0:T(8,128)(2,1)S(1)}, bf16[128,128]{1,0:T(8,128)(2,1)S(1)}, u32[]{:S(2)}, u32[]{:S(2)}) collective-permute-start(bf16[128,128]{1,0:T(8,128)(2,1)S(1)} %pad_maximum_fusion.5.refs_2_), channel_id=1, source_target_pairs={{0,4},{1,5},{2,6},{3,7},{4,0},{5,1},{6,2},{7,3},{8,12},{9,13},{10,... | collective-permute-start | bytes 98312 | tf_op jit(solution)/shard_map/ppermute | solution.py:449
  54.4 3.9 %collective-permute-start.13 = (bf16[128,128]{1,0:T(8,128)(2,1)S(1)}, bf16[128,128]{1,0:T(8,128)(2,1)S(1)}, u32[]{:S(2)}, u32[]{:S(2)}) collective-permute-start(bf16[128,128]{1,0:T(8,128)(2,1)S(1)} %pad_maximum_fusion.5.refs_2_), channel_id=1, source_target_pairs={{0,2},{1,3},{2,0},{3,1},{4,6},{5,7},{6,4},{7,5},{8,10},{9,11},{10,... | collective-permute-start | bytes 98312 | tf_op jit(solution)/shard_map/ppermute | solution.py:449
  58.3 18.4 %collective-permute-start.20 = (bf16[256,1536]{1,0:T(8,128)(2,1)S(1)}, bf16[256,1536]{1,0:T(8,128)(2,1)S(1)}, u32[]{:S(2)}, u32[]{:S(2)}) collective-permute-start(bf16[256,1536]{1,0:T(8,128)(2,1)S(1)} %collective-permute-done.6.refs_9_.odd_ref), channel_id=1, source_target_pairs={{0,2},{1,3},{2,0},{3,1},{4,6},{5,7},{6,4},{7,5},{8,10},{9,11},{10,... | collective-permute-start | bytes 2359304 | tf_op jit(solution)/shard_map/ppermute | solution.py:443
  59.2 17.5 %collective-permute-start.19 = (bf16[256,1536]{1,0:T(8,128)(2,1)S(1)}, bf16[256,1536]{1,0:T(8,128)(2,1)}, u32[]{:S(2)}, u32[]{:S(2)}) collective-permute-start(bf16[256,1536]{1,0:T(8,128)(2,1)S(1)} %collective-permute-done.7.refs_7_), channel_id=1, source_target_pairs={{0,0},{1,1},{2,4},{3,5},{4,2},{5,3},{6,6},{7,7},{8,8},{9,9},{10,12... | collective-permute-start | bytes 2359304 | tf_op jit(solution)/shard_map/ppermute | solution.py:443
  60.8 17.9 %collective-permute-start.18 = (bf16[4,64,1536]{2,1,0:T(8,128)(2,1)S(1)}, bf16[4,64,1536]{2,1,0:T(8,128)(2,1)S(1)}, u32[]{:S(2)}, u32[]{:S(2)}) collective-permute-start(bf16[4,64,1536]{2,1,0:T(8,128)(2,1)S(1)} %pad_maximum_fusion.2.refs_11_), channel_id=1, source_target_pairs={{0,16},{8,24},{16,0},{24,8},{1,17},{9,25},{17,1},{25,9},{2,18},{10... | collective-permute-start | bytes 2359304 | tf_op jit(solution)/shard_map/ppermute | solution.py:446
  60.8 18.1 %collective-permute-start.17 = (bf16[4,64,1536]{2,1,0:T(8,128)(2,1)S(1)}, bf16[4,64,1536]{2,1,0:T(8,128)(2,1)S(1)}, u32[]{:S(2)}, u32[]{:S(2)}) collective-permute-start(bf16[4,64,1536]{2,1,0:T(8,128)(2,1)S(1)} %pad_maximum_fusion.2.refs_11_), channel_id=1, source_target_pairs={{0,8},{8,0},{16,24},{24,16},{1,9},{9,1},{17,25},{25,17},{2,10},{10... | collective-permute-start | bytes 2359304 | tf_op jit(solution)/shard_map/ppermute | solution.py:446
  78.9 18.1 %collective-permute-start.22 = (bf16[256,1536]{1,0:T(8,128)(2,1)}, bf16[256,1536]{1,0:T(8,128)(2,1)}, u32[]{:S(2)}, u32[]{:S(2)}) collective-permute-start(bf16[256,1536]{1,0:T(8,128)(2,1)} %collective-permute-done.19.refs_10_), channel_id=1, source_target_pairs={{0,2},{1,3},{2,0},{3,1},{4,6},{5,7},{6,4},{7,5},{8,10},{9,11},{10,... | collective-permute-start | bytes 2359304 | tf_op jit(solution)/shard_map/ppermute | solution.py:443
  81.6 18.1 %collective-permute-start.21 = (bf16[4,64,1536]{2,1,0:T(8,128)(2,1)S(1)}, bf16[4,64,1536]{2,1,0:T(8,128)(2,1)}, u32[]{:S(2)}, u32[]{:S(2)}) collective-permute-start(bf16[4,64,1536]{2,1,0:T(8,128)(2,1)S(1)} %pad_maximum_fusion.2.refs_11_), channel_id=1, source_target_pairs={{0,24},{8,16},{16,8},{24,0},{1,25},{9,17},{17,9},{25,1},{2,26},{10... | collective-permute-start | bytes 2359304 | tf_op jit(solution)/shard_map/ppermute | solution.py:446
  104.3 10.2 %collective-permute-start.23 = (bf16[2,1536,512]{2,1,0:T(8,128)(2,1)}, bf16[2,1536,512]{2,1,0:T(8,128)(2,1)}, u32[]{:S(2)}, u32[]{:S(2)}) collective-permute-start(bf16[2,1536,512]{2,1,0:T(8,128)(2,1)} %get-tuple-element.89.row_ref), channel_id=1, source_target_pairs={{0,1},{1,0},{2,3},{3,2},{4,5},{5,4},{6,7},{7,6},{8,9},{9,8},{10,11... | collective-permute-start | bytes 9437192 | tf_op jit(solution)/shard_map/ppermute | solution.py:438
  (14 other events, 278.2 us)

commit v13 on v12

--- a/solution.py
+++ b/solution.py
@@ -477,14 +477,7 @@
     hops = [1 << i for i in range(rows.bit_length() - 1)]
 
     def doubled(x, hop):
-        moves = [
-            (r * cols + z * ratio + c, (r ^ hop) * cols + z * ratio + c)
-            for z in range(rows)
-            for r in range(rows)
-            if (r ^ z) < hop
-            for c in range(ratio)
-        ]
-        return jnp.where((row ^ plane) < hop, x, lax.ppermute(x, ("rows", "cols"), moves))
+        return jnp.where((row ^ plane) < hop, x, beside(x, hop))
 
     gram = gram_call(dosage, present, components)
     col_comps = lax.dynamic_slice_in_dim(components, core * width, width, 1)

time: 125 us -> 125 us (level)
  starting transfers between devices: 34.7 us -> 30.5 us
  waiting for transfers between devices: 35 us -> 38.5 us
    ppermute x2 -> x0, starting transfers between devices: 6.35 us -> none  [doubled(): lax.ppermute(x, ('rows', 'cols'), moves)]
    ppermute x8 -> x10, waiting for transfers between devices: 9.74 us -> 14.8 us  [beside(): lax.ppermute(x, 'rows', [(i, i ^ d) for i in range(rows)])]
    ppermute x8 -> x10, starting transfers between devices: 7.87 us -> 10.9 us  [beside(): lax.ppermute(x, 'rows', [(i, i ^ d) for i in range(rows)])]
    ppermute x2 -> x0, waiting for transfers between devices: 2.09 us -> none  [doubled(): lax.ppermute(x, ('rows', 'cols'), moves)]
where the time goes in v13:
time: 125 us; the launch traced here: 124 us
  Pallas kernels  47.2 us (38%)
  waiting for transfers between devices  38.5 us (31%)
  starting transfers between devices  30.5 us (24%)
  other arithmetic  5.83 us (5%)
  local copies, waits for them, and re-layouts  1.65 us (1%)
    pallas_call x2, Pallas kernels, kin_call(): pl.pallas_call(kin_kernel, grid_spec=pltpu.PrefetchScalarGridSpec(num_sca...  20.3 us
    ppermute x5, waiting for transfers between devices, exchange(): return lax.ppermute(x, 'cols', pairs(lambda z, c: (other[z], c)))  17.9 us
    ppermute x10, waiting for transfers between devices, beside(): lax.ppermute(x, 'rows', [(i, i ^ d) for i in range(rows)])  14.8 us
    ppermute x6, starting transfers between devices, across(): return lax.ppermute(x, 'cols', pairs(lambda z, c: (z ^ e, c))) if e else x  11.1 us
    ppermute x10, starting transfers between devices, beside(): lax.ppermute(x, 'rows', [(i, i ^ d) for i in range(rows)])  10.9 us
    pallas_call x1, Pallas kernels, early_call(): pl.pallas_call(functools.partial(early_kernel_at, rows, len(pieces)), gri...  9.56 us
    ppermute x5, starting transfers between devices, exchange(): return lax.ppermute(x, 'cols', pairs(lambda z, c: (other[z], c)))  7.95 us
    pallas_call x1, Pallas kernels, solve_call(): pl.pallas_call(functools.partial(solve_kernel, comps, markers), out_shape...  7.09 us
  transfers between devices with their start and end apart: 24, of which 14 were waited for; matrix products, arithmetic and copies ran while one was open for 4% of the time, Pallas kernels for 26%

profile of v13, /device:TPU:0, one launch (start us, length us, event | category | flops | bytes accessed | tf_op | source)
XLA Modules:
  0.0 124.0 jit_solution(14683991776748598127)
XLA Ops:
  3.5 3.0 %collective-permute-start.7 = (bf16[256,1536]{1,0:T(8,128)(2,1)S(1)}, bf16[256,1536]{1,0:T(8,128)(2,1)S(1)}, u32[]{:S(2)}, u32[]{:S(2)}) collective-permute-start(bf16[256,1536]{1,0:T(8,128)(2,1)S(1)} %pad_maximum_fusion.refs_6_), channel_id=1, source_target_pairs={{0,2},{1,3},{2,0},{3,1},{4,6},{5,7},{6,4},{7,5},{8,10},{9,11},{10,... | collective-permute-start | bytes 2359304 | tf_op jit(solution)/shard_map/ppermute | solution.py:443
  8.1 2.4 %collective-permute-start.3 = (bf16[64,1536]{1,0:T(8,128)(2,1)}, bf16[64,1536]{1,0:T(8,128)(2,1)S(1)}, u32[]{:S(2)}, u32[]{:S(2)}) collective-permute-start(bf16[64,1536]{1,0:T(8,128)(2,1)} %get-tuple-element.95), channel_id=1, source_target_pairs={{0,24},{8,16},{16,8},{24,0},{1,25},{9,17},{17,9},{25,1},{2,26},{10... | collective-permute-start | bytes 589832 | tf_op jit(solution)/shard_map/ppermute | solution.py:446
  11.7 5.6 %gram.1 = f32[360,128]{1,0:T(8,128)} custom-call(s32[64,3072]{1,0:T(8,128)} %dosage_ref, s32[64,3072]{1,0:T(8,128)} %present_ref, f32[32,3072]{1,0:T(8,128)} %refs_0_.1), custom_call_target="tpu_custom_call" | custom-call | tf_op jit(solution)/shard_map/gram/pallas_call | solution.py:63
  17.3 2.8 %collective-permute-done.2 = bf16[64,1536]{1,0:T(8,128)(2,1)S(1)} collective-permute-done((bf16[64,1536]{1,0:T(8,128)(2,1)}, bf16[64,1536]{1,0:T(8,128)(2,1)S(1)}, u32[]{:S(2)}, u32[]{:S(2)}) %collective-permute-start.2) | collective-permute-done | bytes 196640 | tf_op jit(solution)/shard_map/ppermute | solution.py:446
  20.3 1.5 %collective-permute-start.4 = (f32[360,128]{1,0:T(8,128)}, f32[360,128]{1,0:T(8,128)S(1)}, u32[]{:S(2)}, u32[]{:S(2)}) collective-permute-start(f32[360,128]{1,0:T(8,128)} %gram.1), channel_id=1, source_target_pairs={{0,8},{8,0},{16,24},{24,16},{1,9},{9,1},{17,25},{25,17},{2,10},{10... | collective-permute-start | bytes 552968 | tf_op jit(solution)/shard_map/ppermute | solution.py:446
  23.4 4.7 %collective-permute-done.4 = f32[360,128]{1,0:T(8,128)S(1)} collective-permute-done((f32[360,128]{1,0:T(8,128)}, f32[360,128]{1,0:T(8,128)S(1)}, u32[]{:S(2)}, u32[]{:S(2)}) %collective-permute-start.4) | collective-permute-done | bytes 184352 | tf_op jit(solution)/shard_map/ppermute | solution.py:446
  29.0 2.2 %collective-permute-done.5 = f32[32,1536]{1,0:T(8,128)S(1)} collective-permute-done((f32[32,1536]{1,0:T(8,128)S(1)}, f32[32,1536]{1,0:T(8,128)S(1)}, u32[]{:S(2)}, u32[]{:S(2)}) %collective-permute-start.5) | collective-permute-done | bytes 196640 | tf_op jit(solution)/shard_map/ppermute | solution.py:446
  33.4 2.5 %collective-permute-start.10 = (bf16[64,1536]{1,0:T(8,128)(2,1)S(1)}, bf16[64,1536]{1,0:T(8,128)(2,1)S(1)}, u32[]{:S(2)}, u32[]{:S(2)}) collective-permute-start(bf16[64,1536]{1,0:T(8,128)(2,1)S(1)} %get-tuple-element.92), channel_id=1, source_target_pairs={{0,6},{1,7},{2,4},{3,5},{4,2},{5,3},{6,0},{7,1},{8,14},{9,15},{10,... | collective-permute-start | bytes 589832 | tf_op jit(solution)/shard_map/ppermute | solution.py:449
  36.0 3.1 %collective-permute-start.9 = (bf16[64,1536]{1,0:T(8,128)(2,1)S(1)}, bf16[64,1536]{1,0:T(8,128)(2,1)S(1)}, u32[]{:S(2)}, u32[]{:S(2)}) collective-permute-start(bf16[64,1536]{1,0:T(8,128)(2,1)S(1)} %get-tuple-element.93), channel_id=1, source_target_pairs={{0,4},{1,5},{2,6},{3,7},{4,0},{5,1},{6,2},{7,3},{8,12},{9,13},{10,... | collective-permute-start | bytes 589832 | tf_op jit(solution)/shard_map/ppermute | solution.py:449
  39.7 7.1 %solve.1 = bf16[64,128]{1,0:T(8,128)(2,1)} custom-call(f32[360,128]{1,0:T(8,128)} %copy-done.8, f32[360,128]{1,0:T(8,128)} %copy-done.9), custom_call_target="tpu_custom_call" | custom-call | tf_op jit(solution)/shard_map/solve/pallas_call | solution.py:152
  48.9 2.4 %collective-permute-start.15 = (bf16[128,128]{1,0:T(8,128)(2,1)S(1)}, bf16[128,128]{1,0:T(8,128)(2,1)S(1)}, u32[]{:S(2)}, u32[]{:S(2)}) collective-permute-start(bf16[128,128]{1,0:T(8,128)(2,1)S(1)} %pad_maximum_fusion.5.refs_2_), channel_id=1, source_target_pairs={{0,6},{1,7},{2,4},{3,5},{4,2},{5,3},{6,0},{7,1},{8,14},{9,15},{10,... | collective-permute-start | bytes 98312 | tf_op jit(solution)/shard_map/ppermute | solution.py:449
  51.3 3.1 %collective-permute-start.14 = (bf16[128,128]{1,0:T(8,128)(2,1)S(1)}, bf16[128,128]{1,0:T(8,128)(2,1)S(1)}, u32[]{:S(2)}, u32[]{:S(2)}) collective-permute-start(bf16[128,128]{1,0:T(8,128)(2,1)S(1)} %pad_maximum_fusion.5.refs_2_), channel_id=1, source_target_pairs={{0,4},{1,5},{2,6},{3,7},{4,0},{5,1},{6,2},{7,3},{8,12},{9,13},{10,... | collective-permute-start | bytes 98312 | tf_op jit(solution)/shard_map/ppermute | solution.py:449
  54.7 2.4 %collective-permute-done.14.refs_4_ = bf16[128,128]{1,0:T(8,128)(2,1)S(1)} collective-permute-done((bf16[128,128]{1,0:T(8,128)(2,1)S(1)}, bf16[128,128]{1,0:T(8,128)(2,1)S(1)}, u32[]{:S(2)}, u32[]{:S(2)}) %collective-permute-start.14) | collective-permute-done | bytes 32800 | tf_op jit(solution)/shard_map/ppermute | solution.py:449
  58.7 1.6 %collective-permute-start.19 = (bf16[256,1536]{1,0:T(8,128)(2,1)S(1)}, bf16[256,1536]{1,0:T(8,128)(2,1)}, u32[]{:S(2)}, u32[]{:S(2)}) collective-permute-start(bf16[256,1536]{1,0:T(8,128)(2,1)S(1)} %collective-permute-done.7.refs_7_), channel_id=1, source_target_pairs={{0,0},{1,1},{2,4},{3,5},{4,2},{5,3},{6,6},{7,7},{8,8},{9,9},{10,12... | collective-permute-start | bytes 2359304 | tf_op jit(solution)/shard_map/ppermute | solution.py:443
  62.0 14.6 %collective-permute-done.20.refs_8_ = bf16[256,1536]{1,0:T(8,128)(2,1)S(1)} collective-permute-done((bf16[256,1536]{1,0:T(8,128)(2,1)S(1)}, bf16[256,1536]{1,0:T(8,128)(2,1)S(1)}, u32[]{:S(2)}, u32[]{:S(2)}) %collective-permute-start.20) | collective-permute-done | bytes 786464 | tf_op jit(solution)/shard_map/ppermute | solution.py:443
  76.6 1.6 %collective-permute-done.18.refs_13_ = bf16[4,64,1536]{2,1,0:T(8,128)(2,1)S(1)} collective-permute-done((bf16[4,64,1536]{2,1,0:T(8,128)(2,1)S(1)}, bf16[4,64,1536]{2,1,0:T(8,128)(2,1)S(1)}, u32[]{:S(2)}, u32[]{:S(2)}) %collective-permute-start.18) | collective-permute-done | bytes 786464 | tf_op jit(solution)/shard_map/ppermute | solution.py:446
  79.3 2.3 %collective-permute-start.22 = (bf16[256,1536]{1,0:T(8,128)(2,1)}, bf16[256,1536]{1,0:T(8,128)(2,1)}, u32[]{:S(2)}, u32[]{:S(2)}) collective-permute-start(bf16[256,1536]{1,0:T(8,128)(2,1)} %collective-permute-done.19.refs_10_), channel_id=1, source_target_pairs={{0,2},{1,3},{2,0},{3,1},{4,6},{5,7},{6,4},{7,5},{8,10},{9,11},{10,... | collective-permute-start | bytes 2359304 | tf_op jit(solution)/shard_map/ppermute | solution.py:443
  81.6 1.6 %collective-permute-start.21 = (bf16[4,64,1536]{2,1,0:T(8,128)(2,1)S(1)}, bf16[4,64,1536]{2,1,0:T(8,128)(2,1)}, u32[]{:S(2)}, u32[]{:S(2)}) collective-permute-start(bf16[4,64,1536]{2,1,0:T(8,128)(2,1)S(1)} %pad_maximum_fusion.2.refs_11_), channel_id=1, source_target_pairs={{0,24},{8,16},{16,8},{24,0},{1,25},{9,17},{17,9},{25,1},{2,26},{10... | collective-permute-start | bytes 2359304 | tf_op jit(solution)/shard_map/ppermute | solution.py:446
  83.9 9.6 %early.1 = (bf16[2,1536,512]{2,1,0:T(8,128)(2,1)}, bf16[2,16,32,1536]{3,2,1,0:T(8,128)(2,1)}, f32[128,1536]{1,0:T(8,128)}, f32[4,32,1536]{2,1,0:T(8,128)}) custom-call(s32[1]{0:T(128)} %bitcast.5.part_ref, f32[32,3072]{1,0:T(8,128)} %refs_0_.1, f32[32,1536]{1,0:T(8,128)} %broadcast_select_fusion.refs_1_, bf16[128,128]{1,0:T(8,128)(2,1)} %copy-done.10, ...), custom_call_target="tpu_custom_call" | custom-call | tf_op jit(solution)/shard_map/early/pallas_call | solution.py:269
  93.5 3.3 %collective-permute-done.22.even_ref = bf16[256,1536]{1,0:T(8,128)(2,1)} collective-permute-done((bf16[256,1536]{1,0:T(8,128)(2,1)}, bf16[256,1536]{1,0:T(8,128)(2,1)}, u32[]{:S(2)}, u32[]{:S(2)}) %collective-permute-start.22) | collective-permute-done | bytes 786464 | tf_op jit(solution)/shard_map/ppermute | solution.py:443
  96.8 2.2 %collective-permute-done.21.piece_ref = bf16[4,64,1536]{2,1,0:T(8,128)(2,1)} collective-permute-done((bf16[4,64,1536]{2,1,0:T(8,128)(2,1)S(1)}, bf16[4,64,1536]{2,1,0:T(8,128)(2,1)}, u32[]{:S(2)}, u32[]{:S(2)}) %collective-permute-start.21) | collective-permute-done | bytes 786464 | tf_op jit(solution)/shard_map/ppermute | solution.py:446
  99.0 4.6 %late.1 = (bf16[2,1536,512]{2,1,0:T(8,128)(2,1)}, bf16[2,16,32,1536]{3,2,1,0:T(8,128)(2,1)}) custom-call(s32[4]{0:T(128)} %pad_add_fusion.group_ref, f32[128,1536]{1,0:T(8,128)} %get-tuple-element.85.row_fit, f32[4,32,1536]{2,1,0:T(8,128)} %get-tuple-element.86.col_fit, ...), custom_call_target="tpu_custom_call", output_to_operand_aliasing={{0}: (6, {}), {1}: (7, {})} | custom-call | tf_op jit(solution)/shard_map/late/pallas_call | solution.py:360
  103.8 10.1 %kinship.2.refs_0_ = f32[3072,1536]{1,0:T(8,128)} custom-call(s32[1]{0:T(128)} %bitcast.27.part_ref, bf16[2,1536,512]{2,1,0:T(8,128)(2,1)} %get-tuple-element.89.row_ref, bf16[2,512,1536]{2,1,0:T(8,128)(2,1)} %bitcast.37), custom_call_target="tpu_custom_call" | custom-call | tf_op jit(solution)/shard_map/kinship/pallas_call | solution.py:408
  113.9 10.1 %kinship.3 = f32[3072,1536]{1,0:T(8,128)} custom-call(s32[1]{0:T(128)} %bitcast.part_ref, bf16[2,1536,512]{2,1,0:T(8,128)(2,1)} %collective-permute-done.23.row_ref, bf16[2,512,1536]{2,1,0:T(8,128)(2,1)} %bitcast.38, f32[3072,1536]{1,0:T(8,128)} %kinship.2.refs_0_), custom_call_target="tpu_custom_call", output_to_operand_aliasing={{}: (3, {})} | custom-call | tf_op jit(solution)/shard_map/kinship/pallas_call | solution.py:408
  (74 shorter events, 19.2 us)
Async XLA Ops:
  1.5 1.9 %collective-permute-start = (bf16[128,1536]{1,0:T(8,128)(2,1)S(1)}, bf16[128,1536]{1,0:T(8,128)(2,1)S(1)}, u32[]{:S(2)}, u32[]{:S(2)}) collective-permute-start(bf16[128,1536]{1,0:T(8,128)(2,1)S(1)} %bitcast.44), channel_id=1, source_target_pairs={{0,1},{1,0},{2,3},{3,2},{4,5},{5,4},{6,7},{7,6},{8,9},{9,8},{10,11... | collective-permute-start | bytes 1179656 | tf_op jit(solution)/shard_map/ppermute | solution.py:438
  3.5 27.7 %collective-permute-start.7 = (bf16[256,1536]{1,0:T(8,128)(2,1)S(1)}, bf16[256,1536]{1,0:T(8,128)(2,1)S(1)}, u32[]{:S(2)}, u32[]{:S(2)}) collective-permute-start(bf16[256,1536]{1,0:T(8,128)(2,1)S(1)} %pad_maximum_fusion.refs_6_), channel_id=1, source_target_pairs={{0,2},{1,3},{2,0},{3,1},{4,6},{5,7},{6,4},{7,5},{8,10},{9,11},{10,... | collective-permute-start | bytes 2359304 | tf_op jit(solution)/shard_map/ppermute | solution.py:443
  6.5 24.7 %collective-permute-start.6 = (bf16[256,1536]{1,0:T(8,128)(2,1)S(1)}, bf16[256,1536]{1,0:T(8,128)(2,1)S(1)}, u32[]{:S(2)}, u32[]{:S(2)}) collective-permute-start(bf16[256,1536]{1,0:T(8,128)(2,1)S(1)} %pad_maximum_fusion.refs_6_), channel_id=1, source_target_pairs={{0,0},{1,1},{2,4},{3,5},{4,2},{5,3},{6,6},{7,7},{8,8},{9,9},{10,12... | collective-permute-start | bytes 2359304 | tf_op jit(solution)/shard_map/ppermute | solution.py:443
  8.1 9.2 %collective-permute-start.3 = (bf16[64,1536]{1,0:T(8,128)(2,1)}, bf16[64,1536]{1,0:T(8,128)(2,1)S(1)}, u32[]{:S(2)}, u32[]{:S(2)}) collective-permute-start(bf16[64,1536]{1,0:T(8,128)(2,1)} %get-tuple-element.95), channel_id=1, source_target_pairs={{0,24},{8,16},{16,8},{24,0},{1,25},{9,17},{17,9},{25,1},{2,26},{10... | collective-permute-start | bytes 589832 | tf_op jit(solution)/shard_map/ppermute | solution.py:446
  10.6 9.5 %collective-permute-start.2 = (bf16[64,1536]{1,0:T(8,128)(2,1)}, bf16[64,1536]{1,0:T(8,128)(2,1)S(1)}, u32[]{:S(2)}, u32[]{:S(2)}) collective-permute-start(bf16[64,1536]{1,0:T(8,128)(2,1)} %get-tuple-element.96), channel_id=1, source_target_pairs={{0,16},{8,24},{16,0},{24,8},{1,17},{9,25},{17,1},{25,9},{2,18},{10... | collective-permute-start | bytes 589832 | tf_op jit(solution)/shard_map/ppermute | solution.py:446
  11.1 9.2 %collective-permute-start.1 = (bf16[64,1536]{1,0:T(8,128)(2,1)}, bf16[64,1536]{1,0:T(8,128)(2,1)}, u32[]{:S(2)}, u32[]{:S(2)}) collective-permute-start(bf16[64,1536]{1,0:T(8,128)(2,1)} %get-tuple-element.97), channel_id=1, source_target_pairs={{0,8},{8,0},{16,24},{24,16},{1,9},{9,1},{17,25},{25,17},{2,10},{10... | collective-permute-start | bytes 589832 | tf_op jit(solution)/shard_map/ppermute | solution.py:446
  20.3 7.7 %collective-permute-start.4 = (f32[360,128]{1,0:T(8,128)}, f32[360,128]{1,0:T(8,128)S(1)}, u32[]{:S(2)}, u32[]{:S(2)}) collective-permute-start(f32[360,128]{1,0:T(8,128)} %gram.1), channel_id=1, source_target_pairs={{0,8},{8,0},{16,24},{24,16},{1,9},{9,1},{17,25},{25,17},{2,10},{10... | collective-permute-start | bytes 552968 | tf_op jit(solution)/shard_map/ppermute | solution.py:446
  21.8 9.4 %collective-permute-start.5 = (f32[32,1536]{1,0:T(8,128)S(1)}, f32[32,1536]{1,0:T(8,128)S(1)}, u32[]{:S(2)}, u32[]{:S(2)}) collective-permute-start(f32[32,1536]{1,0:T(8,128)S(1)} %constant_dynamic-slice_fusion.1), channel_id=1, source_target_pairs={{0,8},{8,0},{16,24},{24,16},{1,9},{9,1},{17,25},{25,17},{2,10},{10... | collective-permute-start | bytes 589832 | tf_op jit(solution)/shard_map/ppermute | solution.py:446
  31.3 7.8 %collective-permute-start.11 = (f32[360,128]{1,0:T(8,128)S(1)}, f32[360,128]{1,0:T(8,128)S(1)}, u32[]{:S(2)}, u32[]{:S(2)}) collective-permute-start(f32[360,128]{1,0:T(8,128)S(1)} %add.105.refs_0_), channel_id=1, source_target_pairs={{0,16},{8,24},{16,0},{24,8},{1,17},{9,25},{17,1},{25,9},{2,18},{10... | collective-permute-start | bytes 552968 | tf_op jit(solution)/shard_map/ppermute | solution.py:446
  32.7 14.0 %collective-permute-start.16 = (f32[32,1536]{1,0:T(8,128)S(1)}, f32[32,1536]{1,0:T(8,128)S(1)}, u32[]{:S(2)}, u32[]{:S(2)}) collective-permute-start(f32[32,1536]{1,0:T(8,128)S(1)} %broadcast_select_fusion.1), channel_id=1, source_target_pairs={{0,16},{8,24},{16,0},{24,8},{1,17},{9,25},{17,1},{25,9},{2,18},{10... | collective-permute-start | bytes 589832 | tf_op jit(solution)/shard_map/ppermute | solution.py:446
  33.4 21.0 %collective-permute-start.10 = (bf16[64,1536]{1,0:T(8,128)(2,1)S(1)}, bf16[64,1536]{1,0:T(8,128)(2,1)S(1)}, u32[]{:S(2)}, u32[]{:S(2)}) collective-permute-start(bf16[64,1536]{1,0:T(8,128)(2,1)S(1)} %get-tuple-element.92), channel_id=1, source_target_pairs={{0,6},{1,7},{2,4},{3,5},{4,2},{5,3},{6,0},{7,1},{8,14},{9,15},{10,... | collective-permute-start | bytes 589832 | tf_op jit(solution)/shard_map/ppermute | solution.py:449
  36.0 18.5 %collective-permute-start.9 = (bf16[64,1536]{1,0:T(8,128)(2,1)S(1)}, bf16[64,1536]{1,0:T(8,128)(2,1)S(1)}, u32[]{:S(2)}, u32[]{:S(2)}) collective-permute-start(bf16[64,1536]{1,0:T(8,128)(2,1)S(1)} %get-tuple-element.93), channel_id=1, source_target_pairs={{0,4},{1,5},{2,6},{3,7},{4,0},{5,1},{6,2},{7,3},{8,12},{9,13},{10,... | collective-permute-start | bytes 589832 | tf_op jit(solution)/shard_map/ppermute | solution.py:449
  39.0 15.4 %collective-permute-start.8 = (bf16[64,1536]{1,0:T(8,128)(2,1)S(1)}, bf16[64,1536]{1,0:T(8,128)(2,1)S(1)}, u32[]{:S(2)}, u32[]{:S(2)}) collective-permute-start(bf16[64,1536]{1,0:T(8,128)(2,1)S(1)} %get-tuple-element.94), channel_id=1, source_target_pairs={{0,2},{1,3},{2,0},{3,1},{4,6},{5,7},{6,4},{7,5},{8,10},{9,11},{10,... | collective-permute-start | bytes 589832 | tf_op jit(solution)/shard_map/ppermute | solution.py:449
  46.8 1.4 %collective-permute-start.12 = (bf16[64,128]{1,0:T(8,128)(2,1)}, bf16[64,128]{1,0:T(8,128)(2,1)S(1)}, u32[]{:S(2)}, u32[]{:S(2)}) collective-permute-start(bf16[64,128]{1,0:T(8,128)(2,1)} %solve.1), channel_id=1, source_target_pairs={{0,1},{1,0},{2,3},{3,2},{4,5},{5,4},{6,7},{7,6},{8,9},{9,8},{10,11... | collective-permute-start | bytes 49160 | tf_op jit(solution)/shard_map/ppermute | solution.py:438
  48.9 5.8 %collective-permute-start.15 = (bf16[128,128]{1,0:T(8,128)(2,1)S(1)}, bf16[128,128]{1,0:T(8,128)(2,1)S(1)}, u32[]{:S(2)}, u32[]{:S(2)}) collective-permute-start(bf16[128,128]{1,0:T(8,128)(2,1)S(1)} %pad_maximum_fusion.5.refs_2_), channel_id=1, source_target_pairs={{0,6},{1,7},{2,4},{3,5},{4,2},{5,3},{6,0},{7,1},{8,14},{9,15},{10,... | collective-permute-start | bytes 98312 | tf_op jit(solution)/shard_map/ppermute | solution.py:449
  51.3 5.7 %collective-permute-start.14 = (bf16[128,128]{1,0:T(8,128)(2,1)S(1)}, bf16[128,128]{1,0:T(8,128)(2,1)S(1)}, u32[]{:S(2)}, u32[]{:S(2)}) collective-permute-start(bf16[128,128]{1,0:T(8,128)(2,1)S(1)} %pad_maximum_fusion.5.refs_2_), channel_id=1, source_target_pairs={{0,4},{1,5},{2,6},{3,7},{4,0},{5,1},{6,2},{7,3},{8,12},{9,13},{10,... | collective-permute-start | bytes 98312 | tf_op jit(solution)/shard_map/ppermute | solution.py:449
  54.4 3.9 %collective-permute-start.13 = (bf16[128,128]{1,0:T(8,128)(2,1)S(1)}, bf16[128,128]{1,0:T(8,128)(2,1)S(1)}, u32[]{:S(2)}, u32[]{:S(2)}) collective-permute-start(bf16[128,128]{1,0:T(8,128)(2,1)S(1)} %pad_maximum_fusion.5.refs_2_), channel_id=1, source_target_pairs={{0,2},{1,3},{2,0},{3,1},{4,6},{5,7},{6,4},{7,5},{8,10},{9,11},{10,... | collective-permute-start | bytes 98312 | tf_op jit(solution)/shard_map/ppermute | solution.py:449
  58.3 18.3 %collective-permute-start.20 = (bf16[256,1536]{1,0:T(8,128)(2,1)S(1)}, bf16[256,1536]{1,0:T(8,128)(2,1)S(1)}, u32[]{:S(2)}, u32[]{:S(2)}) collective-permute-start(bf16[256,1536]{1,0:T(8,128)(2,1)S(1)} %collective-permute-done.6.refs_9_.odd_ref), channel_id=1, source_target_pairs={{0,2},{1,3},{2,0},{3,1},{4,6},{5,7},{6,4},{7,5},{8,10},{9,11},{10,... | collective-permute-start | bytes 2359304 | tf_op jit(solution)/shard_map/ppermute | solution.py:443
  58.7 17.9 %collective-permute-start.19 = (bf16[256,1536]{1,0:T(8,128)(2,1)S(1)}, bf16[256,1536]{1,0:T(8,128)(2,1)}, u32[]{:S(2)}, u32[]{:S(2)}) collective-permute-start(bf16[256,1536]{1,0:T(8,128)(2,1)S(1)} %collective-permute-done.7.refs_7_), channel_id=1, source_target_pairs={{0,0},{1,1},{2,4},{3,5},{4,2},{5,3},{6,6},{7,7},{8,8},{9,9},{10,12... | collective-permute-start | bytes 2359304 | tf_op jit(solution)/shard_map/ppermute | solution.py:443
  60.3 17.9 %collective-permute-start.18 = (bf16[4,64,1536]{2,1,0:T(8,128)(2,1)S(1)}, bf16[4,64,1536]{2,1,0:T(8,128)(2,1)S(1)}, u32[]{:S(2)}, u32[]{:S(2)}) collective-permute-start(bf16[4,64,1536]{2,1,0:T(8,128)(2,1)S(1)} %pad_maximum_fusion.2.refs_11_), channel_id=1, source_target_pairs={{0,16},{8,24},{16,0},{24,8},{1,17},{9,25},{17,1},{25,9},{2,18},{10... | collective-permute-start | bytes 2359304 | tf_op jit(solution)/shard_map/ppermute | solution.py:446
  61.7 17.6 %collective-permute-start.17 = (bf16[4,64,1536]{2,1,0:T(8,128)(2,1)S(1)}, bf16[4,64,1536]{2,1,0:T(8,128)(2,1)S(1)}, u32[]{:S(2)}, u32[]{:S(2)}) collective-permute-start(bf16[4,64,1536]{2,1,0:T(8,128)(2,1)S(1)} %pad_maximum_fusion.2.refs_11_), channel_id=1, source_target_pairs={{0,8},{8,0},{16,24},{24,16},{1,9},{9,1},{17,25},{25,17},{2,10},{10... | collective-permute-start | bytes 2359304 | tf_op jit(solution)/shard_map/ppermute | solution.py:446
  79.3 17.5 %collective-permute-start.22 = (bf16[256,1536]{1,0:T(8,128)(2,1)}, bf16[256,1536]{1,0:T(8,128)(2,1)}, u32[]{:S(2)}, u32[]{:S(2)}) collective-permute-start(bf16[256,1536]{1,0:T(8,128)(2,1)} %collective-permute-done.19.refs_10_), channel_id=1, source_target_pairs={{0,2},{1,3},{2,0},{3,1},{4,6},{5,7},{6,4},{7,5},{8,10},{9,11},{10,... | collective-permute-start | bytes 2359304 | tf_op jit(solution)/shard_map/ppermute | solution.py:443
  81.6 17.4 %collective-permute-start.21 = (bf16[4,64,1536]{2,1,0:T(8,128)(2,1)S(1)}, bf16[4,64,1536]{2,1,0:T(8,128)(2,1)}, u32[]{:S(2)}, u32[]{:S(2)}) collective-permute-start(bf16[4,64,1536]{2,1,0:T(8,128)(2,1)S(1)} %pad_maximum_fusion.2.refs_11_), channel_id=1, source_target_pairs={{0,24},{8,16},{16,8},{24,0},{1,25},{9,17},{17,9},{25,1},{2,26},{10... | collective-permute-start | bytes 2359304 | tf_op jit(solution)/shard_map/ppermute | solution.py:446
  103.7 10.2 %collective-permute-start.23 = (bf16[2,1536,512]{2,1,0:T(8,128)(2,1)}, bf16[2,1536,512]{2,1,0:T(8,128)(2,1)}, u32[]{:S(2)}, u32[]{:S(2)}) collective-permute-start(bf16[2,1536,512]{2,1,0:T(8,128)(2,1)} %get-tuple-element.89.row_ref), channel_id=1, source_target_pairs={{0,1},{1,0},{2,3},{3,2},{4,5},{5,4},{6,7},{7,6},{8,9},{9,8},{10,11... | collective-permute-start | bytes 9437192 | tf_op jit(solution)/shard_map/ppermute | solution.py:438
  (14 other events, 278.2 us)

commit v14 on v13

--- a/solution.py
+++ b/solution.py
@@ -477,13 +477,13 @@
     hops = [1 << i for i in range(rows.bit_length() - 1)]
 
     def doubled(x, hop):
-        return jnp.where((row ^ plane) < hop, x, beside(x, hop))
+        return jnp.where(((row ^ plane) & hop) == 0, x, beside(x, hop))
 
     gram = gram_call(dosage, present, components)
     col_comps = lax.dynamic_slice_in_dim(components, core * width, width, 1)
     quarters, gram, col_comps = lax.optimization_barrier((quarters, gram, col_comps))
     gram = gram + beside(gram, hops[0])
-    col_comps = doubled(col_comps, hops[0])
+    col_comps = doubled(col_comps, hops[-1])
     quarters, gram, col_comps, held, odd, even = lax.optimization_barrier(
         (jnp.stack(quarters), gram, col_comps, held, odd, even)
     )
@@ -494,7 +494,7 @@
         gram = gram + beside(gram, hop)
     coef = solve_call([gram, beside(gram, hops[-1])], comps, markers)
     coef = by_core([swap(coef, k) for k in range(ratio)])
-    for hop in hops[1:]:
+    for hop in hops[:-1]:
         col_comps = doubled(col_comps, hop)
     coefs = [across(coef, e) for e in range(rows)]
     moved, coefs, col_comps, held, odd, even = lax.optimization_barrier(

time: 125 us -> 121 us (0.968)
  waiting for transfers between devices: 38.5 us -> 33.9 us
  starting transfers between devices: 30.5 us -> 31.9 us
    ppermute x10, waiting for transfers between devices: 14.8 us -> 12.6 us  [beside(): lax.ppermute(x, 'rows', [(i, i ^ d) for i in range(rows)])]
    ppermute x5, waiting for transfers between devices: 17.9 us -> 16.4 us  [exchange(): return lax.ppermute(x, 'cols', pairs(lambda z, c: (other[z], c)))]
  transfers between devices with their start and end apart: 24 -> 24, of which waited for: 14 -> 14; matrix products, arithmetic and copies ran while one was open for 4% -> 4% of each run, Pallas kernels for 26% -> 27%
where the time goes in v14:
time: 121 us
  Pallas kernels  47.2 us (39%)
  waiting for transfers between devices  33.9 us (28%)
  starting transfers between devices  31.9 us (26%)
  other arithmetic  5.83 us (5%)
  local copies, waits for them, and re-layouts  1.65 us (1%)
    pallas_call x2, Pallas kernels, kin_call(): pl.pallas_call(kin_kernel, grid_spec=pltpu.PrefetchScalarGridSpec(num_sca...  20.3 us
    ppermute x5, waiting for transfers between devices, exchange(): return lax.ppermute(x, 'cols', pairs(lambda z, c: (other[z], c)))  16.4 us
    ppermute x10, waiting for transfers between devices, beside(): lax.ppermute(x, 'rows', [(i, i ^ d) for i in range(rows)])  12.6 us
    ppermute x10, starting transfers between devices, beside(): lax.ppermute(x, 'rows', [(i, i ^ d) for i in range(rows)])  12.1 us
    ppermute x6, starting transfers between devices, across(): return lax.ppermute(x, 'cols', pairs(lambda z, c: (z ^ e, c))) if e else x  10.1 us
    pallas_call x1, Pallas kernels, early_call(): pl.pallas_call(functools.partial(early_kernel_at, rows, len(pieces)), gri...  9.56 us
    ppermute x5, starting transfers between devices, exchange(): return lax.ppermute(x, 'cols', pairs(lambda z, c: (other[z], c)))  9.15 us
    pallas_call x1, Pallas kernels, solve_call(): pl.pallas_call(functools.partial(solve_kernel, comps, markers), out_shape...  7.09 us
  transfers between devices with their start and end apart: 24, of which 14 were waited for; matrix products, arithmetic and copies ran while one was open for 4% of the time, Pallas kernels for 27%

profile of v14, /device:TPU:0, one launch (start us, length us, event | category | flops | bytes accessed | tf_op | source)
XLA Modules:
  0.0 120.7 jit_solution(7202928473038775614)
XLA Ops:
  0.0 1.4 %dynamic-slice_convert_fusion = (bf16[64,1536]{1,0:T(8,128)(2,1)S(1)}, bf16[64,1536]{1,0:T(8,128)(2,1)S(1)}, bf16[64,1536]{1,0:T(8,128)(2,1)S(1)}, bf16[64,1536]{1,0:T(8,128)(2,1)S(1)}) fusion(s32[64,3072]{1,0:T(8,128)} %present_ref, s32[]{:T(128)S(6)} %select_n.132, s32[]{:T(128)S(6)} %select_n.131, s32[64,3072]{1,0:T(8,128)} %dosage_ref), kind=kLoop, calls=%fused_computation.7 | loop fusion | flops 393216 | bytes 2359304 | tf_op jit(solution)/shard_map/convert_element_type | solution.py:466
  3.5 3.0 %collective-permute-start.7 = (bf16[256,1536]{1,0:T(8,128)(2,1)S(1)}, bf16[256,1536]{1,0:T(8,128)(2,1)S(1)}, u32[]{:S(2)}, u32[]{:S(2)}) collective-permute-start(bf16[256,1536]{1,0:T(8,128)(2,1)S(1)} %pad_maximum_fusion.refs_6_), channel_id=1, source_target_pairs={{0,2},{1,3},{2,0},{3,1},{4,6},{5,7},{6,4},{7,5},{8,10},{9,11},{10,... | collective-permute-start | bytes 2359304 | tf_op jit(solution)/shard_map/ppermute | solution.py:443
  8.1 2.4 %collective-permute-start.3 = (bf16[64,1536]{1,0:T(8,128)(2,1)}, bf16[64,1536]{1,0:T(8,128)(2,1)S(1)}, u32[]{:S(2)}, u32[]{:S(2)}) collective-permute-start(bf16[64,1536]{1,0:T(8,128)(2,1)} %get-tuple-element.95), channel_id=1, source_target_pairs={{0,24},{8,16},{16,8},{24,0},{1,25},{9,17},{17,9},{25,1},{2,26},{10... | collective-permute-start | bytes 589832 | tf_op jit(solution)/shard_map/ppermute | solution.py:446
  11.7 5.6 %gram.1 = f32[360,128]{1,0:T(8,128)} custom-call(s32[64,3072]{1,0:T(8,128)} %dosage_ref, s32[64,3072]{1,0:T(8,128)} %present_ref, f32[32,3072]{1,0:T(8,128)} %refs_0_.1), custom_call_target="tpu_custom_call" | custom-call | tf_op jit(solution)/shard_map/gram/pallas_call | solution.py:63
  17.3 2.8 %collective-permute-done.2 = bf16[64,1536]{1,0:T(8,128)(2,1)S(1)} collective-permute-done((bf16[64,1536]{1,0:T(8,128)(2,1)}, bf16[64,1536]{1,0:T(8,128)(2,1)S(1)}, u32[]{:S(2)}, u32[]{:S(2)}) %collective-permute-start.2) | collective-permute-done | bytes 196640 | tf_op jit(solution)/shard_map/ppermute | solution.py:446
  20.3 1.5 %collective-permute-start.4 = (f32[360,128]{1,0:T(8,128)}, f32[360,128]{1,0:T(8,128)S(1)}, u32[]{:S(2)}, u32[]{:S(2)}) collective-permute-start(f32[360,128]{1,0:T(8,128)} %gram.1), channel_id=1, source_target_pairs={{0,8},{8,0},{16,24},{24,16},{1,9},{9,1},{17,25},{25,17},{2,10},{10... | collective-permute-start | bytes 552968 | tf_op jit(solution)/shard_map/ppermute | solution.py:446
  23.4 3.5 %collective-permute-done.4 = f32[360,128]{1,0:T(8,128)S(1)} collective-permute-done((f32[360,128]{1,0:T(8,128)}, f32[360,128]{1,0:T(8,128)S(1)}, u32[]{:S(2)}, u32[]{:S(2)}) %collective-permute-start.4) | collective-permute-done | bytes 184352 | tf_op jit(solution)/shard_map/ppermute | solution.py:446
  30.4 2.5 %collective-permute-start.10 = (bf16[64,1536]{1,0:T(8,128)(2,1)S(1)}, bf16[64,1536]{1,0:T(8,128)(2,1)S(1)}, u32[]{:S(2)}, u32[]{:S(2)}) collective-permute-start(bf16[64,1536]{1,0:T(8,128)(2,1)S(1)} %get-tuple-element.92), channel_id=1, source_target_pairs={{0,6},{1,7},{2,4},{3,5},{4,2},{5,3},{6,0},{7,1},{8,14},{9,15},{10,... | collective-permute-start | bytes 589832 | tf_op jit(solution)/shard_map/ppermute | solution.py:449
  32.9 3.1 %collective-permute-start.9 = (bf16[64,1536]{1,0:T(8,128)(2,1)S(1)}, bf16[64,1536]{1,0:T(8,128)(2,1)S(1)}, u32[]{:S(2)}, u32[]{:S(2)}) collective-permute-start(bf16[64,1536]{1,0:T(8,128)(2,1)S(1)} %get-tuple-element.93), channel_id=1, source_target_pairs={{0,4},{1,5},{2,6},{3,7},{4,0},{5,1},{6,2},{7,3},{8,12},{9,13},{10,... | collective-permute-start | bytes 589832 | tf_op jit(solution)/shard_map/ppermute | solution.py:449
  36.7 7.1 %solve.1 = bf16[64,128]{1,0:T(8,128)(2,1)} custom-call(f32[360,128]{1,0:T(8,128)} %copy-done.8, f32[360,128]{1,0:T(8,128)} %copy-done.9), custom_call_target="tpu_custom_call" | custom-call | tf_op jit(solution)/shard_map/solve/pallas_call | solution.py:152
  45.9 1.5 %collective-permute-start.15 = (bf16[128,128]{1,0:T(8,128)(2,1)S(1)}, bf16[128,128]{1,0:T(8,128)(2,1)S(1)}, u32[]{:S(2)}, u32[]{:S(2)}) collective-permute-start(bf16[128,128]{1,0:T(8,128)(2,1)S(1)} %pad_maximum_fusion.5.refs_2_), channel_id=1, source_target_pairs={{0,6},{1,7},{2,4},{3,5},{4,2},{5,3},{6,0},{7,1},{8,14},{9,15},{10,... | collective-permute-start | bytes 98312 | tf_op jit(solution)/shard_map/ppermute | solution.py:449
  47.4 2.0 %collective-permute-start.14 = (bf16[128,128]{1,0:T(8,128)(2,1)S(1)}, bf16[128,128]{1,0:T(8,128)(2,1)S(1)}, u32[]{:S(2)}, u32[]{:S(2)}) collective-permute-start(bf16[128,128]{1,0:T(8,128)(2,1)S(1)} %pad_maximum_fusion.5.refs_2_), channel_id=1, source_target_pairs={{0,4},{1,5},{2,6},{3,7},{4,0},{5,1},{6,2},{7,3},{8,12},{9,13},{10,... | collective-permute-start | bytes 98312 | tf_op jit(solution)/shard_map/ppermute | solution.py:449
  50.5 1.5 %collective-permute-done.15.refs_5_ = bf16[128,128]{1,0:T(8,128)(2,1)S(1)} collective-permute-done((bf16[128,128]{1,0:T(8,128)(2,1)S(1)}, bf16[128,128]{1,0:T(8,128)(2,1)S(1)}, u32[]{:S(2)}, u32[]{:S(2)}) %collective-permute-start.15) | collective-permute-done | bytes 32800 | tf_op jit(solution)/shard_map/ppermute | solution.py:449
  54.3 1.6 %collective-permute-start.19 = (bf16[256,1536]{1,0:T(8,128)(2,1)S(1)}, bf16[256,1536]{1,0:T(8,128)(2,1)}, u32[]{:S(2)}, u32[]{:S(2)}) collective-permute-start(bf16[256,1536]{1,0:T(8,128)(2,1)S(1)} %collective-permute-done.7.refs_7_), channel_id=1, source_target_pairs={{0,0},{1,1},{2,4},{3,5},{4,2},{5,3},{6,6},{7,7},{8,8},{9,9},{10,12... | collective-permute-start | bytes 2359304 | tf_op jit(solution)/shard_map/ppermute | solution.py:443
  58.0 13.6 %collective-permute-done.20.refs_8_ = bf16[256,1536]{1,0:T(8,128)(2,1)S(1)} collective-permute-done((bf16[256,1536]{1,0:T(8,128)(2,1)S(1)}, bf16[256,1536]{1,0:T(8,128)(2,1)S(1)}, u32[]{:S(2)}, u32[]{:S(2)}) %collective-permute-start.20) | collective-permute-done | bytes 786464 | tf_op jit(solution)/shard_map/ppermute | solution.py:443
  71.6 2.2 %collective-permute-done.18.refs_13_ = bf16[4,64,1536]{2,1,0:T(8,128)(2,1)S(1)} collective-permute-done((bf16[4,64,1536]{2,1,0:T(8,128)(2,1)S(1)}, bf16[4,64,1536]{2,1,0:T(8,128)(2,1)S(1)}, u32[]{:S(2)}, u32[]{:S(2)}) %collective-permute-start.18) | collective-permute-done | bytes 786464 | tf_op jit(solution)/shard_map/ppermute | solution.py:446
  74.8 2.9 %collective-permute-start.22 = (bf16[256,1536]{1,0:T(8,128)(2,1)}, bf16[256,1536]{1,0:T(8,128)(2,1)}, u32[]{:S(2)}, u32[]{:S(2)}) collective-permute-start(bf16[256,1536]{1,0:T(8,128)(2,1)} %collective-permute-done.19.refs_10_), channel_id=1, source_target_pairs={{0,2},{1,3},{2,0},{3,1},{4,6},{5,7},{6,4},{7,5},{8,10},{9,11},{10,... | collective-permute-start | bytes 2359304 | tf_op jit(solution)/shard_map/ppermute | solution.py:443
  77.8 2.4 %collective-permute-start.21 = (bf16[4,64,1536]{2,1,0:T(8,128)(2,1)S(1)}, bf16[4,64,1536]{2,1,0:T(8,128)(2,1)}, u32[]{:S(2)}, u32[]{:S(2)}) collective-permute-start(bf16[4,64,1536]{2,1,0:T(8,128)(2,1)S(1)} %pad_maximum_fusion.2.refs_11_), channel_id=1, source_target_pairs={{0,24},{8,16},{16,8},{24,0},{1,25},{9,17},{17,9},{25,1},{2,26},{10... | collective-permute-start | bytes 2359304 | tf_op jit(solution)/shard_map/ppermute | solution.py:446
  80.8 9.6 %early.1 = (bf16[2,1536,512]{2,1,0:T(8,128)(2,1)}, bf16[2,16,32,1536]{3,2,1,0:T(8,128)(2,1)}, f32[128,1536]{1,0:T(8,128)}, f32[4,32,1536]{2,1,0:T(8,128)}) custom-call(s32[1]{0:T(128)} %bitcast.5.part_ref, f32[32,3072]{1,0:T(8,128)} %refs_0_.1, f32[32,1536]{1,0:T(8,128)} %broadcast_select_fusion.refs_1_, bf16[128,128]{1,0:T(8,128)(2,1)} %copy-done.10, ...), custom_call_target="tpu_custom_call" | custom-call | tf_op jit(solution)/shard_map/early/pallas_call | solution.py:269
  90.4 2.7 %collective-permute-done.22.even_ref = bf16[256,1536]{1,0:T(8,128)(2,1)} collective-permute-done((bf16[256,1536]{1,0:T(8,128)(2,1)}, bf16[256,1536]{1,0:T(8,128)(2,1)}, u32[]{:S(2)}, u32[]{:S(2)}) %collective-permute-start.22) | collective-permute-done | bytes 786464 | tf_op jit(solution)/shard_map/ppermute | solution.py:443
  93.1 2.6 %collective-permute-done.21.piece_ref = bf16[4,64,1536]{2,1,0:T(8,128)(2,1)} collective-permute-done((bf16[4,64,1536]{2,1,0:T(8,128)(2,1)S(1)}, bf16[4,64,1536]{2,1,0:T(8,128)(2,1)}, u32[]{:S(2)}, u32[]{:S(2)}) %collective-permute-start.21) | collective-permute-done | bytes 786464 | tf_op jit(solution)/shard_map/ppermute | solution.py:446
  95.7 4.6 %late.1 = (bf16[2,1536,512]{2,1,0:T(8,128)(2,1)}, bf16[2,16,32,1536]{3,2,1,0:T(8,128)(2,1)}) custom-call(s32[4]{0:T(128)} %pad_add_fusion.group_ref, f32[128,1536]{1,0:T(8,128)} %get-tuple-element.85.row_fit, f32[4,32,1536]{2,1,0:T(8,128)} %get-tuple-element.86.col_fit, ...), custom_call_target="tpu_custom_call", output_to_operand_aliasing={{0}: (6, {}), {1}: (7, {})} | custom-call | tf_op jit(solution)/shard_map/late/pallas_call | solution.py:360
  100.5 10.1 %kinship.2.refs_0_ = f32[3072,1536]{1,0:T(8,128)} custom-call(s32[1]{0:T(128)} %bitcast.27.part_ref, bf16[2,1536,512]{2,1,0:T(8,128)(2,1)} %get-tuple-element.89.row_ref, bf16[2,512,1536]{2,1,0:T(8,128)(2,1)} %bitcast.37), custom_call_target="tpu_custom_call" | custom-call | tf_op jit(solution)/shard_map/kinship/pallas_call | solution.py:408
  110.6 10.1 %kinship.3 = f32[3072,1536]{1,0:T(8,128)} custom-call(s32[1]{0:T(128)} %bitcast.part_ref, bf16[2,1536,512]{2,1,0:T(8,128)(2,1)} %collective-permute-done.23.row_ref, bf16[2,512,1536]{2,1,0:T(8,128)(2,1)} %bitcast.38, f32[3072,1536]{1,0:T(8,128)} %kinship.2.refs_0_), custom_call_target="tpu_custom_call", output_to_operand_aliasing={{}: (3, {})} | custom-call | tf_op jit(solution)/shard_map/kinship/pallas_call | solution.py:408
  (74 shorter events, 19.8 us)
Async XLA Ops:
  1.5 1.9 %collective-permute-start = (bf16[128,1536]{1,0:T(8,128)(2,1)S(1)}, bf16[128,1536]{1,0:T(8,128)(2,1)S(1)}, u32[]{:S(2)}, u32[]{:S(2)}) collective-permute-start(bf16[128,1536]{1,0:T(8,128)(2,1)S(1)} %bitcast.44), channel_id=1, source_target_pairs={{0,1},{1,0},{2,3},{3,2},{4,5},{5,4},{6,7},{7,6},{8,9},{9,8},{10,11... | collective-permute-start | bytes 1179656 | tf_op jit(solution)/shard_map/ppermute | solution.py:438
  3.5 24.7 %collective-permute-start.7 = (bf16[256,1536]{1,0:T(8,128)(2,1)S(1)}, bf16[256,1536]{1,0:T(8,128)(2,1)S(1)}, u32[]{:S(2)}, u32[]{:S(2)}) collective-permute-start(bf16[256,1536]{1,0:T(8,128)(2,1)S(1)} %pad_maximum_fusion.refs_6_), channel_id=1, source_target_pairs={{0,2},{1,3},{2,0},{3,1},{4,6},{5,7},{6,4},{7,5},{8,10},{9,11},{10,... | collective-permute-start | bytes 2359304 | tf_op jit(solution)/shard_map/ppermute | solution.py:443
  6.5 21.8 %collective-permute-start.6 = (bf16[256,1536]{1,0:T(8,128)(2,1)S(1)}, bf16[256,1536]{1,0:T(8,128)(2,1)S(1)}, u32[]{:S(2)}, u32[]{:S(2)}) collective-permute-start(bf16[256,1536]{1,0:T(8,128)(2,1)S(1)} %pad_maximum_fusion.refs_6_), channel_id=1, source_target_pairs={{0,0},{1,1},{2,4},{3,5},{4,2},{5,3},{6,6},{7,7},{8,8},{9,9},{10,12... | collective-permute-start | bytes 2359304 | tf_op jit(solution)/shard_map/ppermute | solution.py:443
  8.1 9.2 %collective-permute-start.3 = (bf16[64,1536]{1,0:T(8,128)(2,1)}, bf16[64,1536]{1,0:T(8,128)(2,1)S(1)}, u32[]{:S(2)}, u32[]{:S(2)}) collective-permute-start(bf16[64,1536]{1,0:T(8,128)(2,1)} %get-tuple-element.95), channel_id=1, source_target_pairs={{0,24},{8,16},{16,8},{24,0},{1,25},{9,17},{17,9},{25,1},{2,26},{10... | collective-permute-start | bytes 589832 | tf_op jit(solution)/shard_map/ppermute | solution.py:446
  10.6 9.5 %collective-permute-start.2 = (bf16[64,1536]{1,0:T(8,128)(2,1)}, bf16[64,1536]{1,0:T(8,128)(2,1)S(1)}, u32[]{:S(2)}, u32[]{:S(2)}) collective-permute-start(bf16[64,1536]{1,0:T(8,128)(2,1)} %get-tuple-element.96), channel_id=1, source_target_pairs={{0,16},{8,24},{16,0},{24,8},{1,17},{9,25},{17,1},{25,9},{2,18},{10... | collective-permute-start | bytes 589832 | tf_op jit(solution)/shard_map/ppermute | solution.py:446
  11.1 9.2 %collective-permute-start.1 = (bf16[64,1536]{1,0:T(8,128)(2,1)}, bf16[64,1536]{1,0:T(8,128)(2,1)}, u32[]{:S(2)}, u32[]{:S(2)}) collective-permute-start(bf16[64,1536]{1,0:T(8,128)(2,1)} %get-tuple-element.97), channel_id=1, source_target_pairs={{0,8},{8,0},{16,24},{24,16},{1,9},{9,1},{17,25},{25,17},{2,10},{10... | collective-permute-start | bytes 589832 | tf_op jit(solution)/shard_map/ppermute | solution.py:446
  20.3 6.7 %collective-permute-start.4 = (f32[360,128]{1,0:T(8,128)}, f32[360,128]{1,0:T(8,128)S(1)}, u32[]{:S(2)}, u32[]{:S(2)}) collective-permute-start(f32[360,128]{1,0:T(8,128)} %gram.1), channel_id=1, source_target_pairs={{0,8},{8,0},{16,24},{24,16},{1,9},{9,1},{17,25},{25,17},{2,10},{10... | collective-permute-start | bytes 552968 | tf_op jit(solution)/shard_map/ppermute | solution.py:446
  21.8 6.4 %collective-permute-start.5 = (f32[32,1536]{1,0:T(8,128)S(1)}, f32[32,1536]{1,0:T(8,128)S(1)}, u32[]{:S(2)}, u32[]{:S(2)}) collective-permute-start(f32[32,1536]{1,0:T(8,128)S(1)} %constant_dynamic-slice_fusion.1), channel_id=1, source_target_pairs={{0,16},{8,24},{16,0},{24,8},{1,17},{9,25},{17,1},{25,9},{2,18},{10... | collective-permute-start | bytes 589832 | tf_op jit(solution)/shard_map/ppermute | solution.py:446
  28.3 7.7 %collective-permute-start.11 = (f32[360,128]{1,0:T(8,128)S(1)}, f32[360,128]{1,0:T(8,128)S(1)}, u32[]{:S(2)}, u32[]{:S(2)}) collective-permute-start(f32[360,128]{1,0:T(8,128)S(1)} %add.105.refs_0_), channel_id=1, source_target_pairs={{0,16},{8,24},{16,0},{24,8},{1,17},{9,25},{17,1},{25,9},{2,18},{10... | collective-permute-start | bytes 552968 | tf_op jit(solution)/shard_map/ppermute | solution.py:446
  29.5 14.3 %collective-permute-start.16 = (f32[32,1536]{1,0:T(8,128)S(1)}, f32[32,1536]{1,0:T(8,128)S(1)}, u32[]{:S(2)}, u32[]{:S(2)}) collective-permute-start(f32[32,1536]{1,0:T(8,128)S(1)} %broadcast_select_fusion.1), channel_id=1, source_target_pairs={{0,8},{8,0},{16,24},{24,16},{1,9},{9,1},{17,25},{25,17},{2,10},{10... | collective-permute-start | bytes 589832 | tf_op jit(solution)/shard_map/ppermute | solution.py:446
  30.4 19.1 %collective-permute-start.10 = (bf16[64,1536]{1,0:T(8,128)(2,1)S(1)}, bf16[64,1536]{1,0:T(8,128)(2,1)S(1)}, u32[]{:S(2)}, u32[]{:S(2)}) collective-permute-start(bf16[64,1536]{1,0:T(8,128)(2,1)S(1)} %get-tuple-element.92), channel_id=1, source_target_pairs={{0,6},{1,7},{2,4},{3,5},{4,2},{5,3},{6,0},{7,1},{8,14},{9,15},{10,... | collective-permute-start | bytes 589832 | tf_op jit(solution)/shard_map/ppermute | solution.py:449
  32.9 17.4 %collective-permute-start.9 = (bf16[64,1536]{1,0:T(8,128)(2,1)S(1)}, bf16[64,1536]{1,0:T(8,128)(2,1)S(1)}, u32[]{:S(2)}, u32[]{:S(2)}) collective-permute-start(bf16[64,1536]{1,0:T(8,128)(2,1)S(1)} %get-tuple-element.93), channel_id=1, source_target_pairs={{0,4},{1,5},{2,6},{3,7},{4,0},{5,1},{6,2},{7,3},{8,12},{9,13},{10,... | collective-permute-start | bytes 589832 | tf_op jit(solution)/shard_map/ppermute | solution.py:449
  36.0 14.4 %collective-permute-start.8 = (bf16[64,1536]{1,0:T(8,128)(2,1)S(1)}, bf16[64,1536]{1,0:T(8,128)(2,1)S(1)}, u32[]{:S(2)}, u32[]{:S(2)}) collective-permute-start(bf16[64,1536]{1,0:T(8,128)(2,1)S(1)} %get-tuple-element.94), channel_id=1, source_target_pairs={{0,2},{1,3},{2,0},{3,1},{4,6},{5,7},{6,4},{7,5},{8,10},{9,11},{10,... | collective-permute-start | bytes 589832 | tf_op jit(solution)/shard_map/ppermute | solution.py:449
  43.8 1.4 %collective-permute-start.12 = (bf16[64,128]{1,0:T(8,128)(2,1)}, bf16[64,128]{1,0:T(8,128)(2,1)S(1)}, u32[]{:S(2)}, u32[]{:S(2)}) collective-permute-start(bf16[64,128]{1,0:T(8,128)(2,1)} %solve.1), channel_id=1, source_target_pairs={{0,1},{1,0},{2,3},{3,2},{4,5},{5,4},{6,7},{7,6},{8,9},{9,8},{10,11... | collective-permute-start | bytes 49160 | tf_op jit(solution)/shard_map/ppermute | solution.py:438
  45.9 6.1 %collective-permute-start.15 = (bf16[128,128]{1,0:T(8,128)(2,1)S(1)}, bf16[128,128]{1,0:T(8,128)(2,1)S(1)}, u32[]{:S(2)}, u32[]{:S(2)}) collective-permute-start(bf16[128,128]{1,0:T(8,128)(2,1)S(1)} %pad_maximum_fusion.5.refs_2_), channel_id=1, source_target_pairs={{0,6},{1,7},{2,4},{3,5},{4,2},{5,3},{6,0},{7,1},{8,14},{9,15},{10,... | collective-permute-start | bytes 98312 | tf_op jit(solution)/shard_map/ppermute | solution.py:449
  47.4 5.6 %collective-permute-start.14 = (bf16[128,128]{1,0:T(8,128)(2,1)S(1)}, bf16[128,128]{1,0:T(8,128)(2,1)S(1)}, u32[]{:S(2)}, u32[]{:S(2)}) collective-permute-start(bf16[128,128]{1,0:T(8,128)(2,1)S(1)} %pad_maximum_fusion.5.refs_2_), channel_id=1, source_target_pairs={{0,4},{1,5},{2,6},{3,7},{4,0},{5,1},{6,2},{7,3},{8,12},{9,13},{10,... | collective-permute-start | bytes 98312 | tf_op jit(solution)/shard_map/ppermute | solution.py:449
  49.4 3.9 %collective-permute-start.13 = (bf16[128,128]{1,0:T(8,128)(2,1)S(1)}, bf16[128,128]{1,0:T(8,128)(2,1)S(1)}, u32[]{:S(2)}, u32[]{:S(2)}) collective-permute-start(bf16[128,128]{1,0:T(8,128)(2,1)S(1)} %pad_maximum_fusion.5.refs_2_), channel_id=1, source_target_pairs={{0,2},{1,3},{2,0},{3,1},{4,6},{5,7},{6,4},{7,5},{8,10},{9,11},{10,... | collective-permute-start | bytes 98312 | tf_op jit(solution)/shard_map/ppermute | solution.py:449
  53.4 18.3 %collective-permute-start.20 = (bf16[256,1536]{1,0:T(8,128)(2,1)S(1)}, bf16[256,1536]{1,0:T(8,128)(2,1)S(1)}, u32[]{:S(2)}, u32[]{:S(2)}) collective-permute-start(bf16[256,1536]{1,0:T(8,128)(2,1)S(1)} %collective-permute-done.6.refs_9_.odd_ref), channel_id=1, source_target_pairs={{0,2},{1,3},{2,0},{3,1},{4,6},{5,7},{6,4},{7,5},{8,10},{9,11},{10,... | collective-permute-start | bytes 2359304 | tf_op jit(solution)/shard_map/ppermute | solution.py:443
  54.3 17.4 %collective-permute-start.19 = (bf16[256,1536]{1,0:T(8,128)(2,1)S(1)}, bf16[256,1536]{1,0:T(8,128)(2,1)}, u32[]{:S(2)}, u32[]{:S(2)}) collective-permute-start(bf16[256,1536]{1,0:T(8,128)(2,1)S(1)} %collective-permute-done.7.refs_7_), channel_id=1, source_target_pairs={{0,0},{1,1},{2,4},{3,5},{4,2},{5,3},{6,6},{7,7},{8,8},{9,9},{10,12... | collective-permute-start | bytes 2359304 | tf_op jit(solution)/shard_map/ppermute | solution.py:443
  55.9 17.9 %collective-permute-start.18 = (bf16[4,64,1536]{2,1,0:T(8,128)(2,1)S(1)}, bf16[4,64,1536]{2,1,0:T(8,128)(2,1)S(1)}, u32[]{:S(2)}, u32[]{:S(2)}) collective-permute-start(bf16[4,64,1536]{2,1,0:T(8,128)(2,1)S(1)} %pad_maximum_fusion.2.refs_11_), channel_id=1, source_target_pairs={{0,16},{8,24},{16,0},{24,8},{1,17},{9,25},{17,1},{25,9},{2,18},{10... | collective-permute-start | bytes 2359304 | tf_op jit(solution)/shard_map/ppermute | solution.py:446
  57.2 17.6 %collective-permute-start.17 = (bf16[4,64,1536]{2,1,0:T(8,128)(2,1)S(1)}, bf16[4,64,1536]{2,1,0:T(8,128)(2,1)S(1)}, u32[]{:S(2)}, u32[]{:S(2)}) collective-permute-start(bf16[4,64,1536]{2,1,0:T(8,128)(2,1)S(1)} %pad_maximum_fusion.2.refs_11_), channel_id=1, source_target_pairs={{0,8},{8,0},{16,24},{24,16},{1,9},{9,1},{17,25},{25,17},{2,10},{10... | collective-permute-start | bytes 2359304 | tf_op jit(solution)/shard_map/ppermute | solution.py:446
  74.8 18.3 %collective-permute-start.22 = (bf16[256,1536]{1,0:T(8,128)(2,1)}, bf16[256,1536]{1,0:T(8,128)(2,1)}, u32[]{:S(2)}, u32[]{:S(2)}) collective-permute-start(bf16[256,1536]{1,0:T(8,128)(2,1)} %collective-permute-done.19.refs_10_), channel_id=1, source_target_pairs={{0,2},{1,3},{2,0},{3,1},{4,6},{5,7},{6,4},{7,5},{8,10},{9,11},{10,... | collective-permute-start | bytes 2359304 | tf_op jit(solution)/shard_map/ppermute | solution.py:443
  77.8 18.0 %collective-permute-start.21 = (bf16[4,64,1536]{2,1,0:T(8,128)(2,1)S(1)}, bf16[4,64,1536]{2,1,0:T(8,128)(2,1)}, u32[]{:S(2)}, u32[]{:S(2)}) collective-permute-start(bf16[4,64,1536]{2,1,0:T(8,128)(2,1)S(1)} %pad_maximum_fusion.2.refs_11_), channel_id=1, source_target_pairs={{0,24},{8,16},{16,8},{24,0},{1,25},{9,17},{17,9},{25,1},{2,26},{10... | collective-permute-start | bytes 2359304 | tf_op jit(solution)/shard_map/ppermute | solution.py:446
  100.4 10.2 %collective-permute-start.23 = (bf16[2,1536,512]{2,1,0:T(8,128)(2,1)}, bf16[2,1536,512]{2,1,0:T(8,128)(2,1)}, u32[]{:S(2)}, u32[]{:S(2)}) collective-permute-start(bf16[2,1536,512]{2,1,0:T(8,128)(2,1)} %get-tuple-element.89.row_ref), channel_id=1, source_target_pairs={{0,1},{1,0},{2,3},{3,2},{4,5},{5,4},{6,7},{7,6},{8,9},{9,8},{10,11... | collective-permute-start | bytes 9437192 | tf_op jit(solution)/shard_map/ppermute | solution.py:438
  (14 other events, 277.2 us)

commit v15 on v14

--- a/solution.py
+++ b/solution.py
@@ -481,7 +481,7 @@
 
     gram = gram_call(dosage, present, components)
     col_comps = lax.dynamic_slice_in_dim(components, core * width, width, 1)
-    quarters, gram, col_comps = lax.optimization_barrier((quarters, gram, col_comps))
+    quarters[1], gram, col_comps = lax.optimization_barrier((quarters[1], gram, col_comps))
     gram = gram + beside(gram, hops[0])
     col_comps = doubled(col_comps, hops[-1])
     quarters, gram, col_comps, held, odd, even = lax.optimization_barrier(

time: 121 us -> 120 us (level)
  starting transfers between devices: 31.9 us -> 29.7 us
    ppermute x5, waiting for transfers between devices: 16.4 us -> 18 us  [exchange(): return lax.ppermute(x, 'cols', pairs(lambda z, c: (other[z], c)))]
    ppermute x10, waiting for transfers between devices: 12.6 us -> 11.4 us  [beside(): lax.ppermute(x, 'rows', [(i, i ^ d) for i in range(rows)])]
  transfers between devices with their start and end apart: 24 -> 24, of which waited for: 14 -> 13; matrix products, arithmetic and copies ran while one was open for 4% -> 4% of each run, Pallas kernels for 27% -> 27%
where the time goes in v15:
time: 120 us; the launch traced here: 119 us
  Pallas kernels  47.2 us (39%)
  waiting for transfers between devices  34.7 us (29%)
  starting transfers between devices  29.7 us (25%)
  other arithmetic  5.92 us (5%)
  local copies, waits for them, and re-layouts  1.61 us (1%)
    pallas_call x2, Pallas kernels, kin_call(): pl.pallas_call(kin_kernel, grid_spec=pltpu.PrefetchScalarGridSpec(num_sca...  20.3 us
    ppermute x5, waiting for transfers between devices, exchange(): return lax.ppermute(x, 'cols', pairs(lambda z, c: (other[z], c)))  18 us
    ppermute x10, waiting for transfers between devices, beside(): lax.ppermute(x, 'rows', [(i, i ^ d) for i in range(rows)])  11.4 us
    ppermute x10, starting transfers between devices, beside(): lax.ppermute(x, 'rows', [(i, i ^ d) for i in range(rows)])  11 us
    ppermute x6, starting transfers between devices, across(): return lax.ppermute(x, 'cols', pairs(lambda z, c: (z ^ e, c))) if e else x  10.1 us
    pallas_call x1, Pallas kernels, early_call(): pl.pallas_call(functools.partial(early_kernel_at, rows, len(pieces)), gri...  9.56 us
    ppermute x5, starting transfers between devices, exchange(): return lax.ppermute(x, 'cols', pairs(lambda z, c: (other[z], c)))  7.96 us
    pallas_call x1, Pallas kernels, solve_call(): pl.pallas_call(functools.partial(solve_kernel, comps, markers), out_shape...  7.09 us
  transfers between devices with their start and end apart: 24, of which 13 were waited for; matrix products, arithmetic and copies ran while one was open for 4% of the time, Pallas kernels for 27%

profile of v15, /device:TPU:0, one launch (start us, length us, event | category | flops | bytes accessed | tf_op | source)
XLA Modules:
  0.0 119.4 jit_solution(882127256777377871)
XLA Ops:
  0.0 1.4 %dynamic-slice_convert_fusion = (bf16[64,1536]{1,0:T(8,128)(2,1)S(1)}, bf16[64,1536]{1,0:T(8,128)(2,1)S(1)}, bf16[64,1536]{1,0:T(8,128)(2,1)S(1)}, bf16[64,1536]{1,0:T(8,128)(2,1)S(1)}) fusion(s32[64,3072]{1,0:T(8,128)} %present_ref, s32[]{:T(128)S(6)} %select_n.132, s32[]{:T(128)S(6)} %select_n.131, s32[64,3072]{1,0:T(8,128)} %dosage_ref), kind=kLoop, calls=%fused_computation.7 | loop fusion | flops 393216 | bytes 2359304 | tf_op jit(solution)/shard_map/convert_element_type | solution.py:466
  3.5 3.0 %collective-permute-start.7 = (bf16[256,1536]{1,0:T(8,128)(2,1)S(1)}, bf16[256,1536]{1,0:T(8,128)(2,1)S(1)}, u32[]{:S(2)}, u32[]{:S(2)}) collective-permute-start(bf16[256,1536]{1,0:T(8,128)(2,1)S(1)} %pad_maximum_fusion.refs_6_), channel_id=1, source_target_pairs={{0,2},{1,3},{2,0},{3,1},{4,6},{5,7},{6,4},{7,5},{8,10},{9,11},{10,... | collective-permute-start | bytes 2359304 | tf_op jit(solution)/shard_map/ppermute | solution.py:443
  8.1 2.4 %collective-permute-start.3 = (bf16[64,1536]{1,0:T(8,128)(2,1)}, bf16[64,1536]{1,0:T(8,128)(2,1)S(1)}, u32[]{:S(2)}, u32[]{:S(2)}) collective-permute-start(bf16[64,1536]{1,0:T(8,128)(2,1)} %get-tuple-element.90), channel_id=1, source_target_pairs={{0,24},{8,16},{16,8},{24,0},{1,25},{9,17},{17,9},{25,1},{2,26},{10... | collective-permute-start | bytes 589832 | tf_op jit(solution)/shard_map/ppermute | solution.py:446
  11.6 5.6 %gram.1 = f32[360,128]{1,0:T(8,128)} custom-call(s32[64,3072]{1,0:T(8,128)} %dosage_ref, s32[64,3072]{1,0:T(8,128)} %present_ref, f32[32,3072]{1,0:T(8,128)} %refs_0_.1), custom_call_target="tpu_custom_call" | custom-call | tf_op jit(solution)/shard_map/gram/pallas_call | solution.py:63
  17.3 3.0 %collective-permute-done.1 = bf16[64,1536]{1,0:T(8,128)(2,1)} collective-permute-done((bf16[64,1536]{1,0:T(8,128)(2,1)}, bf16[64,1536]{1,0:T(8,128)(2,1)}, u32[]{:S(2)}, u32[]{:S(2)}) %collective-permute-start.1) | collective-permute-done | bytes 196640 | tf_op jit(solution)/shard_map/ppermute | solution.py:446
  20.3 1.5 %collective-permute-start.4 = (f32[360,128]{1,0:T(8,128)}, f32[360,128]{1,0:T(8,128)S(1)}, u32[]{:S(2)}, u32[]{:S(2)}) collective-permute-start(f32[360,128]{1,0:T(8,128)} %gram.1), channel_id=1, source_target_pairs={{0,8},{8,0},{16,24},{24,16},{1,9},{9,1},{17,25},{25,17},{2,10},{10... | collective-permute-start | bytes 552968 | tf_op jit(solution)/shard_map/ppermute | solution.py:446
  23.4 2.6 %collective-permute-done.4 = f32[360,128]{1,0:T(8,128)S(1)} collective-permute-done((f32[360,128]{1,0:T(8,128)}, f32[360,128]{1,0:T(8,128)S(1)}, u32[]{:S(2)}, u32[]{:S(2)}) %collective-permute-start.4) | collective-permute-done | bytes 184352 | tf_op jit(solution)/shard_map/ppermute | solution.py:446
  29.2 2.5 %collective-permute-start.10 = (bf16[64,1536]{1,0:T(8,128)(2,1)S(1)}, bf16[64,1536]{1,0:T(8,128)(2,1)S(1)}, u32[]{:S(2)}, u32[]{:S(2)}) collective-permute-start(bf16[64,1536]{1,0:T(8,128)(2,1)S(1)} %get-tuple-element.86), channel_id=1, source_target_pairs={{0,6},{1,7},{2,4},{3,5},{4,2},{5,3},{6,0},{7,1},{8,14},{9,15},{10,... | collective-permute-start | bytes 589832 | tf_op jit(solution)/shard_map/ppermute | solution.py:449
  31.7 3.1 %collective-permute-start.9 = (bf16[64,1536]{1,0:T(8,128)(2,1)S(1)}, bf16[64,1536]{1,0:T(8,128)(2,1)S(1)}, u32[]{:S(2)}, u32[]{:S(2)}) collective-permute-start(bf16[64,1536]{1,0:T(8,128)(2,1)S(1)} %get-tuple-element.87), channel_id=1, source_target_pairs={{0,4},{1,5},{2,6},{3,7},{4,0},{5,1},{6,2},{7,3},{8,12},{9,13},{10,... | collective-permute-start | bytes 589832 | tf_op jit(solution)/shard_map/ppermute | solution.py:449
  35.5 7.1 %solve.1 = bf16[64,128]{1,0:T(8,128)(2,1)} custom-call(f32[360,128]{1,0:T(8,128)} %copy-done.8, f32[360,128]{1,0:T(8,128)} %copy-done.9), custom_call_target="tpu_custom_call" | custom-call | tf_op jit(solution)/shard_map/solve/pallas_call | solution.py:152
  44.7 1.7 %collective-permute-start.15 = (bf16[128,128]{1,0:T(8,128)(2,1)S(1)}, bf16[128,128]{1,0:T(8,128)(2,1)S(1)}, u32[]{:S(2)}, u32[]{:S(2)}) collective-permute-start(bf16[128,128]{1,0:T(8,128)(2,1)S(1)} %pad_maximum_fusion.5.refs_2_), channel_id=1, source_target_pairs={{0,6},{1,7},{2,4},{3,5},{4,2},{5,3},{6,0},{7,1},{8,14},{9,15},{10,... | collective-permute-start | bytes 98312 | tf_op jit(solution)/shard_map/ppermute | solution.py:449
  46.4 2.3 %collective-permute-start.14 = (bf16[128,128]{1,0:T(8,128)(2,1)S(1)}, bf16[128,128]{1,0:T(8,128)(2,1)S(1)}, u32[]{:S(2)}, u32[]{:S(2)}) collective-permute-start(bf16[128,128]{1,0:T(8,128)(2,1)S(1)} %pad_maximum_fusion.5.refs_2_), channel_id=1, source_target_pairs={{0,4},{1,5},{2,6},{3,7},{4,0},{5,1},{6,2},{7,3},{8,12},{9,13},{10,... | collective-permute-start | bytes 98312 | tf_op jit(solution)/shard_map/ppermute | solution.py:449
  50.6 1.5 %collective-permute-done.14.refs_4_ = bf16[128,128]{1,0:T(8,128)(2,1)S(1)} collective-permute-done((bf16[128,128]{1,0:T(8,128)(2,1)S(1)}, bf16[128,128]{1,0:T(8,128)(2,1)S(1)}, u32[]{:S(2)}, u32[]{:S(2)}) %collective-permute-start.14) | collective-permute-done | bytes 32800 | tf_op jit(solution)/shard_map/ppermute | solution.py:449
  53.1 1.6 %collective-permute-start.19 = (bf16[256,1536]{1,0:T(8,128)(2,1)S(1)}, bf16[256,1536]{1,0:T(8,128)(2,1)}, u32[]{:S(2)}, u32[]{:S(2)}) collective-permute-start(bf16[256,1536]{1,0:T(8,128)(2,1)S(1)} %collective-permute-done.7.refs_7_), channel_id=1, source_target_pairs={{0,0},{1,1},{2,4},{3,5},{4,2},{5,3},{6,6},{7,7},{8,8},{9,9},{10,12... | collective-permute-start | bytes 2359304 | tf_op jit(solution)/shard_map/ppermute | solution.py:443
  54.7 1.5 %collective-permute-start.18 = (bf16[4,64,1536]{2,1,0:T(8,128)(2,1)S(1)}, bf16[4,64,1536]{2,1,0:T(8,128)(2,1)S(1)}, u32[]{:S(2)}, u32[]{:S(2)}) collective-permute-start(bf16[4,64,1536]{2,1,0:T(8,128)(2,1)S(1)} %pad_maximum_fusion.2.refs_11_), channel_id=1, source_target_pairs={{0,16},{8,24},{16,0},{24,8},{1,17},{9,25},{17,1},{25,9},{2,18},{10... | collective-permute-start | bytes 2359304 | tf_op jit(solution)/shard_map/ppermute | solution.py:446
  57.2 13.5 %collective-permute-done.20.refs_8_ = bf16[256,1536]{1,0:T(8,128)(2,1)S(1)} collective-permute-done((bf16[256,1536]{1,0:T(8,128)(2,1)S(1)}, bf16[256,1536]{1,0:T(8,128)(2,1)S(1)}, u32[]{:S(2)}, u32[]{:S(2)}) %collective-permute-start.20) | collective-permute-done | bytes 786464 | tf_op jit(solution)/shard_map/ppermute | solution.py:443
  70.7 2.0 %collective-permute-done.18.refs_13_ = bf16[4,64,1536]{2,1,0:T(8,128)(2,1)S(1)} collective-permute-done((bf16[4,64,1536]{2,1,0:T(8,128)(2,1)S(1)}, bf16[4,64,1536]{2,1,0:T(8,128)(2,1)S(1)}, u32[]{:S(2)}, u32[]{:S(2)}) %collective-permute-start.18) | collective-permute-done | bytes 786464 | tf_op jit(solution)/shard_map/ppermute | solution.py:446
  73.8 2.1 %collective-permute-start.22 = (bf16[256,1536]{1,0:T(8,128)(2,1)}, bf16[256,1536]{1,0:T(8,128)(2,1)}, u32[]{:S(2)}, u32[]{:S(2)}) collective-permute-start(bf16[256,1536]{1,0:T(8,128)(2,1)} %collective-permute-done.19.refs_10_), channel_id=1, source_target_pairs={{0,2},{1,3},{2,0},{3,1},{4,6},{5,7},{6,4},{7,5},{8,10},{9,11},{10,... | collective-permute-start | bytes 2359304 | tf_op jit(solution)/shard_map/ppermute | solution.py:443
  78.1 9.6 %early.1 = (bf16[2,1536,512]{2,1,0:T(8,128)(2,1)}, bf16[2,16,32,1536]{3,2,1,0:T(8,128)(2,1)}, f32[128,1536]{1,0:T(8,128)}, f32[4,32,1536]{2,1,0:T(8,128)}) custom-call(s32[1]{0:T(128)} %bitcast.5.part_ref, f32[32,3072]{1,0:T(8,128)} %refs_0_.1, f32[32,1536]{1,0:T(8,128)} %broadcast_select_fusion.refs_1_, bf16[128,128]{1,0:T(8,128)(2,1)} %copy-done.10, ...), custom_call_target="tpu_custom_call" | custom-call | tf_op jit(solution)/shard_map/early/pallas_call | solution.py:269
  87.7 4.5 %collective-permute-done.22.even_ref = bf16[256,1536]{1,0:T(8,128)(2,1)} collective-permute-done((bf16[256,1536]{1,0:T(8,128)(2,1)}, bf16[256,1536]{1,0:T(8,128)(2,1)}, u32[]{:S(2)}, u32[]{:S(2)}) %collective-permute-start.22) | collective-permute-done | bytes 786464 | tf_op jit(solution)/shard_map/ppermute | solution.py:443
  92.1 2.2 %collective-permute-done.21.piece_ref = bf16[4,64,1536]{2,1,0:T(8,128)(2,1)} collective-permute-done((bf16[4,64,1536]{2,1,0:T(8,128)(2,1)S(1)}, bf16[4,64,1536]{2,1,0:T(8,128)(2,1)}, u32[]{:S(2)}, u32[]{:S(2)}) %collective-permute-start.21) | collective-permute-done | bytes 786464 | tf_op jit(solution)/shard_map/ppermute | solution.py:446
  94.4 4.6 %late.1 = (bf16[2,1536,512]{2,1,0:T(8,128)(2,1)}, bf16[2,16,32,1536]{3,2,1,0:T(8,128)(2,1)}) custom-call(s32[4]{0:T(128)} %pad_add_fusion.group_ref, f32[128,1536]{1,0:T(8,128)} %get-tuple-element.79.row_fit, f32[4,32,1536]{2,1,0:T(8,128)} %get-tuple-element.80.col_fit, ...), custom_call_target="tpu_custom_call", output_to_operand_aliasing={{0}: (6, {}), {1}: (7, {})} | custom-call | tf_op jit(solution)/shard_map/late/pallas_call | solution.py:360
  99.1 10.1 %kinship.2.refs_0_ = f32[3072,1536]{1,0:T(8,128)} custom-call(s32[1]{0:T(128)} %bitcast.27.part_ref, bf16[2,1536,512]{2,1,0:T(8,128)(2,1)} %get-tuple-element.83.row_ref, bf16[2,512,1536]{2,1,0:T(8,128)(2,1)} %bitcast.38), custom_call_target="tpu_custom_call" | custom-call | tf_op jit(solution)/shard_map/kinship/pallas_call | solution.py:408
  109.2 10.1 %kinship.3 = f32[3072,1536]{1,0:T(8,128)} custom-call(s32[1]{0:T(128)} %bitcast.part_ref, bf16[2,1536,512]{2,1,0:T(8,128)(2,1)} %collective-permute-done.23.row_ref, bf16[2,512,1536]{2,1,0:T(8,128)(2,1)} %bitcast.39, f32[3072,1536]{1,0:T(8,128)} %kinship.2.refs_0_), custom_call_target="tpu_custom_call", output_to_operand_aliasing={{}: (3, {})} | custom-call | tf_op jit(solution)/shard_map/kinship/pallas_call | solution.py:408
  (74 shorter events, 19.5 us)
Async XLA Ops:
  1.5 1.9 %collective-permute-start = (bf16[128,1536]{1,0:T(8,128)(2,1)S(1)}, bf16[128,1536]{1,0:T(8,128)(2,1)S(1)}, u32[]{:S(2)}, u32[]{:S(2)}) collective-permute-start(bf16[128,1536]{1,0:T(8,128)(2,1)S(1)} %bitcast.44), channel_id=1, source_target_pairs={{0,1},{1,0},{2,3},{3,2},{4,5},{5,4},{6,7},{7,6},{8,9},{9,8},{10,11... | collective-permute-start | bytes 1179656 | tf_op jit(solution)/shard_map/ppermute | solution.py:438
  3.5 23.9 %collective-permute-start.7 = (bf16[256,1536]{1,0:T(8,128)(2,1)S(1)}, bf16[256,1536]{1,0:T(8,128)(2,1)S(1)}, u32[]{:S(2)}, u32[]{:S(2)}) collective-permute-start(bf16[256,1536]{1,0:T(8,128)(2,1)S(1)} %pad_maximum_fusion.refs_6_), channel_id=1, source_target_pairs={{0,2},{1,3},{2,0},{3,1},{4,6},{5,7},{6,4},{7,5},{8,10},{9,11},{10,... | collective-permute-start | bytes 2359304 | tf_op jit(solution)/shard_map/ppermute | solution.py:443
  6.5 20.9 %collective-permute-start.6 = (bf16[256,1536]{1,0:T(8,128)(2,1)S(1)}, bf16[256,1536]{1,0:T(8,128)(2,1)S(1)}, u32[]{:S(2)}, u32[]{:S(2)}) collective-permute-start(bf16[256,1536]{1,0:T(8,128)(2,1)S(1)} %pad_maximum_fusion.refs_6_), channel_id=1, source_target_pairs={{0,0},{1,1},{2,4},{3,5},{4,2},{5,3},{6,6},{7,7},{8,8},{9,9},{10,12... | collective-permute-start | bytes 2359304 | tf_op jit(solution)/shard_map/ppermute | solution.py:443
  8.1 13.7 %collective-permute-start.3 = (bf16[64,1536]{1,0:T(8,128)(2,1)}, bf16[64,1536]{1,0:T(8,128)(2,1)S(1)}, u32[]{:S(2)}, u32[]{:S(2)}) collective-permute-start(bf16[64,1536]{1,0:T(8,128)(2,1)} %get-tuple-element.90), channel_id=1, source_target_pairs={{0,24},{8,16},{16,8},{24,0},{1,25},{9,17},{17,9},{25,1},{2,26},{10... | collective-permute-start | bytes 589832 | tf_op jit(solution)/shard_map/ppermute | solution.py:446
  10.5 11.7 %collective-permute-start.2 = (bf16[64,1536]{1,0:T(8,128)(2,1)S(1)}, bf16[64,1536]{1,0:T(8,128)(2,1)}, u32[]{:S(2)}, u32[]{:S(2)}) collective-permute-start(bf16[64,1536]{1,0:T(8,128)(2,1)S(1)} %get-tuple-element.91), channel_id=1, source_target_pairs={{0,16},{8,24},{16,0},{24,8},{1,17},{9,25},{17,1},{25,9},{2,18},{10... | collective-permute-start | bytes 589832 | tf_op jit(solution)/shard_map/ppermute | solution.py:446
  11.0 9.2 %collective-permute-start.1 = (bf16[64,1536]{1,0:T(8,128)(2,1)}, bf16[64,1536]{1,0:T(8,128)(2,1)}, u32[]{:S(2)}, u32[]{:S(2)}) collective-permute-start(bf16[64,1536]{1,0:T(8,128)(2,1)} %get-tuple-element.92), channel_id=1, source_target_pairs={{0,8},{8,0},{16,24},{24,16},{1,9},{9,1},{17,25},{25,17},{2,10},{10... | collective-permute-start | bytes 589832 | tf_op jit(solution)/shard_map/ppermute | solution.py:446
  20.3 5.7 %collective-permute-start.4 = (f32[360,128]{1,0:T(8,128)}, f32[360,128]{1,0:T(8,128)S(1)}, u32[]{:S(2)}, u32[]{:S(2)}) collective-permute-start(f32[360,128]{1,0:T(8,128)} %gram.1), channel_id=1, source_target_pairs={{0,8},{8,0},{16,24},{24,16},{1,9},{9,1},{17,25},{25,17},{2,10},{10... | collective-permute-start | bytes 552968 | tf_op jit(solution)/shard_map/ppermute | solution.py:446
  21.8 5.7 %collective-permute-start.5 = (f32[32,1536]{1,0:T(8,128)S(1)}, f32[32,1536]{1,0:T(8,128)S(1)}, u32[]{:S(2)}, u32[]{:S(2)}) collective-permute-start(f32[32,1536]{1,0:T(8,128)S(1)} %constant_dynamic-slice_fusion.3), channel_id=1, source_target_pairs={{0,16},{8,24},{16,0},{24,8},{1,17},{9,25},{17,1},{25,9},{2,18},{10... | collective-permute-start | bytes 589832 | tf_op jit(solution)/shard_map/ppermute | solution.py:446
  27.5 7.3 %collective-permute-start.11 = (f32[360,128]{1,0:T(8,128)S(1)}, f32[360,128]{1,0:T(8,128)S(1)}, u32[]{:S(2)}, u32[]{:S(2)}) collective-permute-start(f32[360,128]{1,0:T(8,128)S(1)} %add.105.refs_0_), channel_id=1, source_target_pairs={{0,16},{8,24},{16,0},{24,8},{1,17},{9,25},{17,1},{25,9},{2,18},{10... | collective-permute-start | bytes 552968 | tf_op jit(solution)/shard_map/ppermute | solution.py:446
  28.1 14.5 %collective-permute-start.16 = (f32[32,1536]{1,0:T(8,128)S(1)}, f32[32,1536]{1,0:T(8,128)S(1)}, u32[]{:S(2)}, u32[]{:S(2)}) collective-permute-start(f32[32,1536]{1,0:T(8,128)S(1)} %broadcast_select_fusion.1), channel_id=1, source_target_pairs={{0,8},{8,0},{16,24},{24,16},{1,9},{9,1},{17,25},{25,17},{2,10},{10... | collective-permute-start | bytes 589832 | tf_op jit(solution)/shard_map/ppermute | solution.py:446
  29.2 19.4 %collective-permute-start.10 = (bf16[64,1536]{1,0:T(8,128)(2,1)S(1)}, bf16[64,1536]{1,0:T(8,128)(2,1)S(1)}, u32[]{:S(2)}, u32[]{:S(2)}) collective-permute-start(bf16[64,1536]{1,0:T(8,128)(2,1)S(1)} %get-tuple-element.86), channel_id=1, source_target_pairs={{0,6},{1,7},{2,4},{3,5},{4,2},{5,3},{6,0},{7,1},{8,14},{9,15},{10,... | collective-permute-start | bytes 589832 | tf_op jit(solution)/shard_map/ppermute | solution.py:449
  31.7 17.4 %collective-permute-start.9 = (bf16[64,1536]{1,0:T(8,128)(2,1)S(1)}, bf16[64,1536]{1,0:T(8,128)(2,1)S(1)}, u32[]{:S(2)}, u32[]{:S(2)}) collective-permute-start(bf16[64,1536]{1,0:T(8,128)(2,1)S(1)} %get-tuple-element.87), channel_id=1, source_target_pairs={{0,4},{1,5},{2,6},{3,7},{4,0},{5,1},{6,2},{7,3},{8,12},{9,13},{10,... | collective-permute-start | bytes 589832 | tf_op jit(solution)/shard_map/ppermute | solution.py:449
  34.8 14.4 %collective-permute-start.8 = (bf16[64,1536]{1,0:T(8,128)(2,1)S(1)}, bf16[64,1536]{1,0:T(8,128)(2,1)S(1)}, u32[]{:S(2)}, u32[]{:S(2)}) collective-permute-start(bf16[64,1536]{1,0:T(8,128)(2,1)S(1)} %get-tuple-element.88), channel_id=1, source_target_pairs={{0,2},{1,3},{2,0},{3,1},{4,6},{5,7},{6,4},{7,5},{8,10},{9,11},{10,... | collective-permute-start | bytes 589832 | tf_op jit(solution)/shard_map/ppermute | solution.py:449
  42.6 1.4 %collective-permute-start.12 = (bf16[64,128]{1,0:T(8,128)(2,1)}, bf16[64,128]{1,0:T(8,128)(2,1)S(1)}, u32[]{:S(2)}, u32[]{:S(2)}) collective-permute-start(bf16[64,128]{1,0:T(8,128)(2,1)} %solve.1), channel_id=1, source_target_pairs={{0,1},{1,0},{2,3},{3,2},{4,5},{5,4},{6,7},{7,6},{8,9},{9,8},{10,11... | collective-permute-start | bytes 49160 | tf_op jit(solution)/shard_map/ppermute | solution.py:438
  44.7 5.9 %collective-permute-start.15 = (bf16[128,128]{1,0:T(8,128)(2,1)S(1)}, bf16[128,128]{1,0:T(8,128)(2,1)S(1)}, u32[]{:S(2)}, u32[]{:S(2)}) collective-permute-start(bf16[128,128]{1,0:T(8,128)(2,1)S(1)} %pad_maximum_fusion.5.refs_2_), channel_id=1, source_target_pairs={{0,6},{1,7},{2,4},{3,5},{4,2},{5,3},{6,0},{7,1},{8,14},{9,15},{10,... | collective-permute-start | bytes 98312 | tf_op jit(solution)/shard_map/ppermute | solution.py:449
  46.4 5.8 %collective-permute-start.14 = (bf16[128,128]{1,0:T(8,128)(2,1)S(1)}, bf16[128,128]{1,0:T(8,128)(2,1)S(1)}, u32[]{:S(2)}, u32[]{:S(2)}) collective-permute-start(bf16[128,128]{1,0:T(8,128)(2,1)S(1)} %pad_maximum_fusion.5.refs_2_), channel_id=1, source_target_pairs={{0,4},{1,5},{2,6},{3,7},{4,0},{5,1},{6,2},{7,3},{8,12},{9,13},{10,... | collective-permute-start | bytes 98312 | tf_op jit(solution)/shard_map/ppermute | solution.py:449
  48.6 3.9 %collective-permute-start.13 = (bf16[128,128]{1,0:T(8,128)(2,1)S(1)}, bf16[128,128]{1,0:T(8,128)(2,1)S(1)}, u32[]{:S(2)}, u32[]{:S(2)}) collective-permute-start(bf16[128,128]{1,0:T(8,128)(2,1)S(1)} %pad_maximum_fusion.5.refs_2_), channel_id=1, source_target_pairs={{0,2},{1,3},{2,0},{3,1},{4,6},{5,7},{6,4},{7,5},{8,10},{9,11},{10,... | collective-permute-start | bytes 98312 | tf_op jit(solution)/shard_map/ppermute | solution.py:449
  52.5 18.2 %collective-permute-start.20 = (bf16[256,1536]{1,0:T(8,128)(2,1)S(1)}, bf16[256,1536]{1,0:T(8,128)(2,1)S(1)}, u32[]{:S(2)}, u32[]{:S(2)}) collective-permute-start(bf16[256,1536]{1,0:T(8,128)(2,1)S(1)} %collective-permute-done.6.refs_9_.odd_ref), channel_id=1, source_target_pairs={{0,2},{1,3},{2,0},{3,1},{4,6},{5,7},{6,4},{7,5},{8,10},{9,11},{10,... | collective-permute-start | bytes 2359304 | tf_op jit(solution)/shard_map/ppermute | solution.py:443
  53.1 17.6 %collective-permute-start.19 = (bf16[256,1536]{1,0:T(8,128)(2,1)S(1)}, bf16[256,1536]{1,0:T(8,128)(2,1)}, u32[]{:S(2)}, u32[]{:S(2)}) collective-permute-start(bf16[256,1536]{1,0:T(8,128)(2,1)S(1)} %collective-permute-done.7.refs_7_), channel_id=1, source_target_pairs={{0,0},{1,1},{2,4},{3,5},{4,2},{5,3},{6,6},{7,7},{8,8},{9,9},{10,12... | collective-permute-start | bytes 2359304 | tf_op jit(solution)/shard_map/ppermute | solution.py:443
  54.7 18.0 %collective-permute-start.18 = (bf16[4,64,1536]{2,1,0:T(8,128)(2,1)S(1)}, bf16[4,64,1536]{2,1,0:T(8,128)(2,1)S(1)}, u32[]{:S(2)}, u32[]{:S(2)}) collective-permute-start(bf16[4,64,1536]{2,1,0:T(8,128)(2,1)S(1)} %pad_maximum_fusion.2.refs_11_), channel_id=1, source_target_pairs={{0,16},{8,24},{16,0},{24,8},{1,17},{9,25},{17,1},{25,9},{2,18},{10... | collective-permute-start | bytes 2359304 | tf_op jit(solution)/shard_map/ppermute | solution.py:446
  56.2 17.6 %collective-permute-start.17 = (bf16[4,64,1536]{2,1,0:T(8,128)(2,1)S(1)}, bf16[4,64,1536]{2,1,0:T(8,128)(2,1)S(1)}, u32[]{:S(2)}, u32[]{:S(2)}) collective-permute-start(bf16[4,64,1536]{2,1,0:T(8,128)(2,1)S(1)} %pad_maximum_fusion.2.refs_11_), channel_id=1, source_target_pairs={{0,8},{8,0},{16,24},{24,16},{1,9},{9,1},{17,25},{25,17},{2,10},{10... | collective-permute-start | bytes 2359304 | tf_op jit(solution)/shard_map/ppermute | solution.py:446
  73.8 18.3 %collective-permute-start.22 = (bf16[256,1536]{1,0:T(8,128)(2,1)}, bf16[256,1536]{1,0:T(8,128)(2,1)}, u32[]{:S(2)}, u32[]{:S(2)}) collective-permute-start(bf16[256,1536]{1,0:T(8,128)(2,1)} %collective-permute-done.19.refs_10_), channel_id=1, source_target_pairs={{0,2},{1,3},{2,0},{3,1},{4,6},{5,7},{6,4},{7,5},{8,10},{9,11},{10,... | collective-permute-start | bytes 2359304 | tf_op jit(solution)/shard_map/ppermute | solution.py:443
  76.0 18.4 %collective-permute-start.21 = (bf16[4,64,1536]{2,1,0:T(8,128)(2,1)S(1)}, bf16[4,64,1536]{2,1,0:T(8,128)(2,1)}, u32[]{:S(2)}, u32[]{:S(2)}) collective-permute-start(bf16[4,64,1536]{2,1,0:T(8,128)(2,1)S(1)} %pad_maximum_fusion.2.refs_11_), channel_id=1, source_target_pairs={{0,24},{8,16},{16,8},{24,0},{1,25},{9,17},{17,9},{25,1},{2,26},{10... | collective-permute-start | bytes 2359304 | tf_op jit(solution)/shard_map/ppermute | solution.py:446
  99.0 10.2 %collective-permute-start.23 = (bf16[2,1536,512]{2,1,0:T(8,128)(2,1)}, bf16[2,1536,512]{2,1,0:T(8,128)(2,1)}, u32[]{:S(2)}, u32[]{:S(2)}) collective-permute-start(bf16[2,1536,512]{2,1,0:T(8,128)(2,1)} %get-tuple-element.83.row_ref), channel_id=1, source_target_pairs={{0,1},{1,0},{2,3},{3,2},{4,5},{5,4},{6,7},{7,6},{8,9},{9,8},{10,11... | collective-permute-start | bytes 9437192 | tf_op jit(solution)/shard_map/ppermute | solution.py:438
  (14 other events, 265.2 us)

commit v16 on v15

--- a/solution.py
+++ b/solution.py
@@ -493,13 +493,15 @@
     for hop in hops[1:-1]:
         gram = gram + beside(gram, hop)
     coef = solve_call([gram, beside(gram, hops[-1])], comps, markers)
-    coef = by_core([swap(coef, k) for k in range(ratio)])
     for hop in hops[:-1]:
         col_comps = doubled(col_comps, hop)
-    coefs = [across(coef, e) for e in range(rows)]
-    moved, coefs, col_comps, held, odd, even = lax.optimization_barrier(
-        (jnp.stack(moved), coefs, col_comps, held, odd, even)
+    shares = [across(coef, e) for e in range(rows)]
+    moved, shares, col_comps, held, odd, even = lax.optimization_barrier(
+        (jnp.stack(moved), shares, col_comps, held, odd, even)
     )
+    shares = jnp.concatenate(shares, axis=0)
+    shares = [swap(shares, k) for k in range(ratio)]
+    coefs = [by_core([x[e * markers : (e + 1) * markers] for x in shares]) for e in range(rows)]
     near = [moved]
     for step in range(rows - 3):
         odd, even = odd + [exchange(even[-1], 1)], even + [exchange(odd[-1], 0)]

time: 120 us -> 117 us (0.975)
  waiting for transfers between devices: 34.7 us -> 25.5 us
  other arithmetic: 5.92 us -> 9.03 us
  starting transfers between devices: 29.7 us -> 32.7 us
    ppermute x5, waiting for transfers between devices: 18 us -> 10.8 us  [exchange(): return lax.ppermute(x, 'cols', pairs(lambda z, c: (other[z], c)))]
    ppermute x10, waiting for transfers between devices: 11.4 us -> 8.9 us  [beside(): lax.ppermute(x, 'rows', [(i, i ^ d) for i in range(rows)])]
    concatenate x2 -> x5, other arithmetic: 0.06 us -> 2.49 us  [by_core(): return jnp.concatenate(placed, axis=0)]
    ppermute x5, starting transfers between devices: 7.96 us -> 10.3 us  [exchange(): return lax.ppermute(x, 'cols', pairs(lambda z, c: (other[z], c)))]
  transfers between devices with their start and end apart: 24 -> 24, of which waited for: 13 -> 11; matrix products, arithmetic and copies ran while one was open for 4% -> 7% of each run, Pallas kernels for 27% -> 28%
where the time goes in v16:
time: 117 us; the launch traced here: 116 us
  Pallas kernels  47.3 us (40%)
  starting transfers between devices  32.7 us (28%)
  waiting for transfers between devices  25.5 us (22%)
  other arithmetic  9.03 us (8%)
  local copies, waits for them, and re-layouts  1.6 us (1%)
    pallas_call x2, Pallas kernels, kin_call(): pl.pallas_call(kin_kernel, grid_spec=pltpu.PrefetchScalarGridSpec(num_sca...  20.3 us
    ppermute x10, starting transfers between devices, beside(): lax.ppermute(x, 'rows', [(i, i ^ d) for i in range(rows)])  11.9 us
    ppermute x5, waiting for transfers between devices, exchange(): return lax.ppermute(x, 'cols', pairs(lambda z, c: (other[z], c)))  10.8 us
    ppermute x5, starting transfers between devices, exchange(): return lax.ppermute(x, 'cols', pairs(lambda z, c: (other[z], c)))  10.3 us
    ppermute x6, starting transfers between devices, across(): return lax.ppermute(x, 'cols', pairs(lambda z, c: (z ^ e, c))) if e else x  9.99 us
    pallas_call x1, Pallas kernels, early_call(): pl.pallas_call(functools.partial(early_kernel_at, rows, len(pieces)), gri...  9.58 us
    ppermute x10, waiting for transfers between devices, beside(): lax.ppermute(x, 'rows', [(i, i ^ d) for i in range(rows)])  8.9 us
    pallas_call x1, Pallas kernels, solve_call(): pl.pallas_call(functools.partial(solve_kernel, comps, markers), out_shape...  7.09 us
  transfers between devices with their start and end apart: 24, of which 11 were waited for; matrix products, arithmetic and copies ran while one was open for 7% of the time, Pallas kernels for 28%

profile of v16, /device:TPU:0, one launch (start us, length us, event | category | flops | bytes accessed | tf_op | source)
XLA Modules:
  0.0 116.4 jit_solution(4842672648602950468)
XLA Ops:
  0.0 1.4 %dynamic-slice_convert_fusion = (bf16[64,1536]{1,0:T(8,128)(2,1)S(1)}, bf16[64,1536]{1,0:T(8,128)(2,1)S(1)}, bf16[64,1536]{1,0:T(8,128)(2,1)S(1)}, bf16[64,1536]{1,0:T(8,128)(2,1)S(1)}) fusion(s32[64,3072]{1,0:T(8,128)} %present_ref, s32[]{:T(128)S(6)} %select_n.168, s32[]{:T(128)S(6)} %select_n.167, s32[64,3072]{1,0:T(8,128)} %dosage_ref), kind=kLoop, calls=%fused_computation.7 | loop fusion | flops 393216 | bytes 2359304 | tf_op jit(solution)/shard_map/convert_element_type | solution.py:466
  2.1 1.3 %collective-permute-done = bf16[128,1536]{1,0:T(8,128)(2,1)S(1)} collective-permute-done((bf16[128,1536]{1,0:T(8,128)(2,1)S(1)}, bf16[128,1536]{1,0:T(8,128)(2,1)S(1)}, u32[]{:S(2)}, u32[]{:S(2)}) %collective-permute-start) | collective-permute-done | bytes 393248 | tf_op jit(solution)/shard_map/ppermute | solution.py:438
  3.5 3.0 %collective-permute-start.7 = (bf16[256,1536]{1,0:T(8,128)(2,1)S(1)}, bf16[256,1536]{1,0:T(8,128)(2,1)S(1)}, u32[]{:S(2)}, u32[]{:S(2)}) collective-permute-start(bf16[256,1536]{1,0:T(8,128)(2,1)S(1)} %pad_maximum_fusion.refs_6_), channel_id=1, source_target_pairs={{0,2},{1,3},{2,0},{3,1},{4,6},{5,7},{6,4},{7,5},{8,10},{9,11},{10,... | collective-permute-start | bytes 2359304 | tf_op jit(solution)/shard_map/ppermute | solution.py:443
  8.1 2.4 %collective-permute-start.3 = (bf16[64,1536]{1,0:T(8,128)(2,1)}, bf16[64,1536]{1,0:T(8,128)(2,1)S(1)}, u32[]{:S(2)}, u32[]{:S(2)}) collective-permute-start(bf16[64,1536]{1,0:T(8,128)(2,1)} %get-tuple-element.90), channel_id=1, source_target_pairs={{0,24},{8,16},{16,8},{24,0},{1,25},{9,17},{17,9},{25,1},{2,26},{10... | collective-permute-start | bytes 589832 | tf_op jit(solution)/shard_map/ppermute | solution.py:446
  11.6 5.7 %gram.1 = f32[360,128]{1,0:T(8,128)} custom-call(s32[64,3072]{1,0:T(8,128)} %dosage_ref, s32[64,3072]{1,0:T(8,128)} %present_ref, f32[32,3072]{1,0:T(8,128)} %refs_0_.1), custom_call_target="tpu_custom_call" | custom-call | tf_op jit(solution)/shard_map/gram/pallas_call | solution.py:63
  17.3 3.0 %collective-permute-done.1 = bf16[64,1536]{1,0:T(8,128)(2,1)} collective-permute-done((bf16[64,1536]{1,0:T(8,128)(2,1)}, bf16[64,1536]{1,0:T(8,128)(2,1)}, u32[]{:S(2)}, u32[]{:S(2)}) %collective-permute-start.1) | collective-permute-done | bytes 196640 | tf_op jit(solution)/shard_map/ppermute | solution.py:446
  20.3 1.5 %collective-permute-start.4 = (f32[360,128]{1,0:T(8,128)}, f32[360,128]{1,0:T(8,128)S(1)}, u32[]{:S(2)}, u32[]{:S(2)}) collective-permute-start(f32[360,128]{1,0:T(8,128)} %gram.1), channel_id=1, source_target_pairs={{0,8},{8,0},{16,24},{24,16},{1,9},{9,1},{17,25},{25,17},{2,10},{10... | collective-permute-start | bytes 552968 | tf_op jit(solution)/shard_map/ppermute | solution.py:446
  23.4 2.6 %collective-permute-done.4 = f32[360,128]{1,0:T(8,128)S(1)} collective-permute-done((f32[360,128]{1,0:T(8,128)}, f32[360,128]{1,0:T(8,128)S(1)}, u32[]{:S(2)}, u32[]{:S(2)}) %collective-permute-start.4) | collective-permute-done | bytes 184352 | tf_op jit(solution)/shard_map/ppermute | solution.py:446
  29.2 2.5 %collective-permute-start.10 = (bf16[64,1536]{1,0:T(8,128)(2,1)S(1)}, bf16[64,1536]{1,0:T(8,128)(2,1)S(1)}, u32[]{:S(2)}, u32[]{:S(2)}) collective-permute-start(bf16[64,1536]{1,0:T(8,128)(2,1)S(1)} %get-tuple-element.86), channel_id=1, source_target_pairs={{0,6},{1,7},{2,4},{3,5},{4,2},{5,3},{6,0},{7,1},{8,14},{9,15},{10,... | collective-permute-start | bytes 589832 | tf_op jit(solution)/shard_map/ppermute | solution.py:449
  31.7 3.1 %collective-permute-start.9 = (bf16[64,1536]{1,0:T(8,128)(2,1)S(1)}, bf16[64,1536]{1,0:T(8,128)(2,1)S(1)}, u32[]{:S(2)}, u32[]{:S(2)}) collective-permute-start(bf16[64,1536]{1,0:T(8,128)(2,1)S(1)} %get-tuple-element.87), channel_id=1, source_target_pairs={{0,4},{1,5},{2,6},{3,7},{4,0},{5,1},{6,2},{7,3},{8,12},{9,13},{10,... | collective-permute-start | bytes 589832 | tf_op jit(solution)/shard_map/ppermute | solution.py:449
  35.5 7.1 %solve.1 = bf16[64,128]{1,0:T(8,128)(2,1)} custom-call(f32[360,128]{1,0:T(8,128)} %copy-done.8, f32[360,128]{1,0:T(8,128)} %copy-done.9), custom_call_target="tpu_custom_call" | custom-call | tf_op jit(solution)/shard_map/solve/pallas_call | solution.py:152
  42.6 1.6 %collective-permute-start.14 = (bf16[64,128]{1,0:T(8,128)(2,1)}, bf16[64,128]{1,0:T(8,128)(2,1)S(1)}, u32[]{:S(2)}, u32[]{:S(2)}) collective-permute-start(bf16[64,128]{1,0:T(8,128)(2,1)} %solve.1), channel_id=1, source_target_pairs={{0,6},{1,7},{2,4},{3,5},{4,2},{5,3},{6,0},{7,1},{8,14},{9,15},{10,... | collective-permute-start | bytes 49160 | tf_op jit(solution)/shard_map/ppermute | solution.py:449
  44.2 2.3 %collective-permute-start.13 = (bf16[64,128]{1,0:T(8,128)(2,1)}, bf16[64,128]{1,0:T(8,128)(2,1)S(1)}, u32[]{:S(2)}, u32[]{:S(2)}) collective-permute-start(bf16[64,128]{1,0:T(8,128)(2,1)} %solve.1), channel_id=1, source_target_pairs={{0,4},{1,5},{2,6},{3,7},{4,0},{5,1},{6,2},{7,3},{8,12},{9,13},{10,... | collective-permute-start | bytes 49160 | tf_op jit(solution)/shard_map/ppermute | solution.py:449
  49.3 1.8 %collective-permute-done.12 = bf16[64,128]{1,0:T(8,128)(2,1)S(1)} collective-permute-done((bf16[64,128]{1,0:T(8,128)(2,1)}, bf16[64,128]{1,0:T(8,128)(2,1)S(1)}, u32[]{:S(2)}, u32[]{:S(2)}) %collective-permute-start.12) | collective-permute-done | bytes 16416 | tf_op jit(solution)/shard_map/ppermute | solution.py:449
  54.1 1.6 %collective-permute-start.19 = (bf16[256,1536]{1,0:T(8,128)(2,1)S(1)}, bf16[256,1536]{1,0:T(8,128)(2,1)}, u32[]{:S(2)}, u32[]{:S(2)}) collective-permute-start(bf16[256,1536]{1,0:T(8,128)(2,1)S(1)} %collective-permute-done.7.refs_7_), channel_id=1, source_target_pairs={{0,0},{1,1},{2,4},{3,5},{4,2},{5,3},{6,6},{7,7},{8,8},{9,9},{10,12... | collective-permute-start | bytes 2359304 | tf_op jit(solution)/shard_map/ppermute | solution.py:443
  60.9 8.9 %collective-permute-done.20.refs_8_ = bf16[256,1536]{1,0:T(8,128)(2,1)S(1)} collective-permute-done((bf16[256,1536]{1,0:T(8,128)(2,1)S(1)}, bf16[256,1536]{1,0:T(8,128)(2,1)S(1)}, u32[]{:S(2)}, u32[]{:S(2)}) %collective-permute-start.20) | collective-permute-done | bytes 786464 | tf_op jit(solution)/shard_map/ppermute | solution.py:443
  69.8 4.1 %collective-permute-start.22 = (bf16[256,1536]{1,0:T(8,128)(2,1)}, bf16[256,1536]{1,0:T(8,128)(2,1)}, u32[]{:S(2)}, u32[]{:S(2)}) collective-permute-start(bf16[256,1536]{1,0:T(8,128)(2,1)} %collective-permute-done.19.refs_10_), channel_id=1, source_target_pairs={{0,2},{1,3},{2,0},{3,1},{4,6},{5,7},{6,4},{7,5},{8,10},{9,11},{10,... | collective-permute-start | bytes 2359304 | tf_op jit(solution)/shard_map/ppermute | solution.py:443
  73.8 2.6 %collective-permute-start.21 = (bf16[4,64,1536]{2,1,0:T(8,128)(2,1)S(1)}, bf16[4,64,1536]{2,1,0:T(8,128)(2,1)}, u32[]{:S(2)}, u32[]{:S(2)}) collective-permute-start(bf16[4,64,1536]{2,1,0:T(8,128)(2,1)S(1)} %pad_maximum_fusion.2.refs_11_), channel_id=1, source_target_pairs={{0,24},{8,16},{16,8},{24,0},{1,25},{9,17},{17,9},{25,1},{2,26},{10... | collective-permute-start | bytes 2359304 | tf_op jit(solution)/shard_map/ppermute | solution.py:446
  77.1 9.6 %early.1 = (bf16[2,1536,512]{2,1,0:T(8,128)(2,1)}, bf16[2,16,32,1536]{3,2,1,0:T(8,128)(2,1)}, f32[128,1536]{1,0:T(8,128)}, f32[4,32,1536]{2,1,0:T(8,128)}) custom-call(s32[1]{0:T(128)} %bitcast.5.part_ref, f32[32,3072]{1,0:T(8,128)} %refs_0_.1, f32[32,1536]{1,0:T(8,128)} %broadcast_select_fusion.refs_1_, bf16[128,128]{1,0:T(8,128)(2,1)} %pad_maximum_fusion.6.refs_2_, ...), custom_call_target="tpu_custom_call" | custom-call | tf_op jit(solution)/shard_map/early/pallas_call | solution.py:269
  86.6 1.9 %collective-permute-done.22.even_ref = bf16[256,1536]{1,0:T(8,128)(2,1)} collective-permute-done((bf16[256,1536]{1,0:T(8,128)(2,1)}, bf16[256,1536]{1,0:T(8,128)(2,1)}, u32[]{:S(2)}, u32[]{:S(2)}) %collective-permute-start.22) | collective-permute-done | bytes 786464 | tf_op jit(solution)/shard_map/ppermute | solution.py:443
  88.6 2.8 %collective-permute-done.21.piece_ref = bf16[4,64,1536]{2,1,0:T(8,128)(2,1)} collective-permute-done((bf16[4,64,1536]{2,1,0:T(8,128)(2,1)S(1)}, bf16[4,64,1536]{2,1,0:T(8,128)(2,1)}, u32[]{:S(2)}, u32[]{:S(2)}) %collective-permute-start.21) | collective-permute-done | bytes 786464 | tf_op jit(solution)/shard_map/ppermute | solution.py:446
  91.4 4.6 %late.1 = (bf16[2,1536,512]{2,1,0:T(8,128)(2,1)}, bf16[2,16,32,1536]{3,2,1,0:T(8,128)(2,1)}) custom-call(s32[4]{0:T(128)} %pad_add_fusion.group_ref, f32[128,1536]{1,0:T(8,128)} %get-tuple-element.79.row_fit, f32[4,32,1536]{2,1,0:T(8,128)} %get-tuple-element.80.col_fit, ...), custom_call_target="tpu_custom_call", output_to_operand_aliasing={{0}: (6, {}), {1}: (7, {})} | custom-call | tf_op jit(solution)/shard_map/late/pallas_call | solution.py:360
  96.1 10.1 %kinship.2.refs_0_ = f32[3072,1536]{1,0:T(8,128)} custom-call(s32[1]{0:T(128)} %bitcast.27.part_ref, bf16[2,1536,512]{2,1,0:T(8,128)(2,1)} %get-tuple-element.83.row_ref, bf16[2,512,1536]{2,1,0:T(8,128)(2,1)} %bitcast.38), custom_call_target="tpu_custom_call" | custom-call | tf_op jit(solution)/shard_map/kinship/pallas_call | solution.py:408
  106.3 10.1 %kinship.3 = f32[3072,1536]{1,0:T(8,128)} custom-call(s32[1]{0:T(128)} %bitcast.part_ref, bf16[2,1536,512]{2,1,0:T(8,128)(2,1)} %collective-permute-done.23.row_ref, bf16[2,512,1536]{2,1,0:T(8,128)(2,1)} %bitcast.39, f32[3072,1536]{1,0:T(8,128)} %kinship.2.refs_0_), custom_call_target="tpu_custom_call", output_to_operand_aliasing={{}: (3, {})} | custom-call | tf_op jit(solution)/shard_map/kinship/pallas_call | solution.py:408
  (70 shorter events, 20.5 us)
Async XLA Ops:
  1.5 1.9 %collective-permute-start = (bf16[128,1536]{1,0:T(8,128)(2,1)S(1)}, bf16[128,1536]{1,0:T(8,128)(2,1)S(1)}, u32[]{:S(2)}, u32[]{:S(2)}) collective-permute-start(bf16[128,1536]{1,0:T(8,128)(2,1)S(1)} %bitcast.44), channel_id=1, source_target_pairs={{0,1},{1,0},{2,3},{3,2},{4,5},{5,4},{6,7},{7,6},{8,9},{9,8},{10,11... | collective-permute-start | bytes 1179656 | tf_op jit(solution)/shard_map/ppermute | solution.py:438
  3.5 23.9 %collective-permute-start.7 = (bf16[256,1536]{1,0:T(8,128)(2,1)S(1)}, bf16[256,1536]{1,0:T(8,128)(2,1)S(1)}, u32[]{:S(2)}, u32[]{:S(2)}) collective-permute-start(bf16[256,1536]{1,0:T(8,128)(2,1)S(1)} %pad_maximum_fusion.refs_6_), channel_id=1, source_target_pairs={{0,2},{1,3},{2,0},{3,1},{4,6},{5,7},{6,4},{7,5},{8,10},{9,11},{10,... | collective-permute-start | bytes 2359304 | tf_op jit(solution)/shard_map/ppermute | solution.py:443
  6.5 21.0 %collective-permute-start.6 = (bf16[256,1536]{1,0:T(8,128)(2,1)S(1)}, bf16[256,1536]{1,0:T(8,128)(2,1)S(1)}, u32[]{:S(2)}, u32[]{:S(2)}) collective-permute-start(bf16[256,1536]{1,0:T(8,128)(2,1)S(1)} %pad_maximum_fusion.refs_6_), channel_id=1, source_target_pairs={{0,0},{1,1},{2,4},{3,5},{4,2},{5,3},{6,6},{7,7},{8,8},{9,9},{10,12... | collective-permute-start | bytes 2359304 | tf_op jit(solution)/shard_map/ppermute | solution.py:443
  8.1 13.7 %collective-permute-start.3 = (bf16[64,1536]{1,0:T(8,128)(2,1)}, bf16[64,1536]{1,0:T(8,128)(2,1)S(1)}, u32[]{:S(2)}, u32[]{:S(2)}) collective-permute-start(bf16[64,1536]{1,0:T(8,128)(2,1)} %get-tuple-element.90), channel_id=1, source_target_pairs={{0,24},{8,16},{16,8},{24,0},{1,25},{9,17},{17,9},{25,1},{2,26},{10... | collective-permute-start | bytes 589832 | tf_op jit(solution)/shard_map/ppermute | solution.py:446
  10.5 11.7 %collective-permute-start.2 = (bf16[64,1536]{1,0:T(8,128)(2,1)S(1)}, bf16[64,1536]{1,0:T(8,128)(2,1)}, u32[]{:S(2)}, u32[]{:S(2)}) collective-permute-start(bf16[64,1536]{1,0:T(8,128)(2,1)S(1)} %get-tuple-element.91), channel_id=1, source_target_pairs={{0,16},{8,24},{16,0},{24,8},{1,17},{9,25},{17,1},{25,9},{2,18},{10... | collective-permute-start | bytes 589832 | tf_op jit(solution)/shard_map/ppermute | solution.py:446
  11.0 9.2 %collective-permute-start.1 = (bf16[64,1536]{1,0:T(8,128)(2,1)}, bf16[64,1536]{1,0:T(8,128)(2,1)}, u32[]{:S(2)}, u32[]{:S(2)}) collective-permute-start(bf16[64,1536]{1,0:T(8,128)(2,1)} %get-tuple-element.92), channel_id=1, source_target_pairs={{0,8},{8,0},{16,24},{24,16},{1,9},{9,1},{17,25},{25,17},{2,10},{10... | collective-permute-start | bytes 589832 | tf_op jit(solution)/shard_map/ppermute | solution.py:446
  20.3 5.7 %collective-permute-start.4 = (f32[360,128]{1,0:T(8,128)}, f32[360,128]{1,0:T(8,128)S(1)}, u32[]{:S(2)}, u32[]{:S(2)}) collective-permute-start(f32[360,128]{1,0:T(8,128)} %gram.1), channel_id=1, source_target_pairs={{0,8},{8,0},{16,24},{24,16},{1,9},{9,1},{17,25},{25,17},{2,10},{10... | collective-permute-start | bytes 552968 | tf_op jit(solution)/shard_map/ppermute | solution.py:446
  21.8 5.7 %collective-permute-start.5 = (f32[32,1536]{1,0:T(8,128)S(1)}, f32[32,1536]{1,0:T(8,128)S(1)}, u32[]{:S(2)}, u32[]{:S(2)}) collective-permute-start(f32[32,1536]{1,0:T(8,128)S(1)} %constant_dynamic-slice_fusion.3), channel_id=1, source_target_pairs={{0,16},{8,24},{16,0},{24,8},{1,17},{9,25},{17,1},{25,9},{2,18},{10... | collective-permute-start | bytes 589832 | tf_op jit(solution)/shard_map/ppermute | solution.py:446
  27.5 7.3 %collective-permute-start.11 = (f32[360,128]{1,0:T(8,128)S(1)}, f32[360,128]{1,0:T(8,128)S(1)}, u32[]{:S(2)}, u32[]{:S(2)}) collective-permute-start(f32[360,128]{1,0:T(8,128)S(1)} %add.111.refs_0_), channel_id=1, source_target_pairs={{0,16},{8,24},{16,0},{24,8},{1,17},{9,25},{17,1},{25,9},{2,18},{10... | collective-permute-start | bytes 552968 | tf_op jit(solution)/shard_map/ppermute | solution.py:446
  28.1 16.1 %collective-permute-start.15 = (f32[32,1536]{1,0:T(8,128)S(1)}, f32[32,1536]{1,0:T(8,128)S(1)}, u32[]{:S(2)}, u32[]{:S(2)}) collective-permute-start(f32[32,1536]{1,0:T(8,128)S(1)} %broadcast_select_fusion.1), channel_id=1, source_target_pairs={{0,8},{8,0},{16,24},{24,16},{1,9},{9,1},{17,25},{25,17},{2,10},{10... | collective-permute-start | bytes 589832 | tf_op jit(solution)/shard_map/ppermute | solution.py:446
  29.2 17.9 %collective-permute-start.10 = (bf16[64,1536]{1,0:T(8,128)(2,1)S(1)}, bf16[64,1536]{1,0:T(8,128)(2,1)S(1)}, u32[]{:S(2)}, u32[]{:S(2)}) collective-permute-start(bf16[64,1536]{1,0:T(8,128)(2,1)S(1)} %get-tuple-element.86), channel_id=1, source_target_pairs={{0,6},{1,7},{2,4},{3,5},{4,2},{5,3},{6,0},{7,1},{8,14},{9,15},{10,... | collective-permute-start | bytes 589832 | tf_op jit(solution)/shard_map/ppermute | solution.py:449
  31.7 17.2 %collective-permute-start.9 = (bf16[64,1536]{1,0:T(8,128)(2,1)S(1)}, bf16[64,1536]{1,0:T(8,128)(2,1)S(1)}, u32[]{:S(2)}, u32[]{:S(2)}) collective-permute-start(bf16[64,1536]{1,0:T(8,128)(2,1)S(1)} %get-tuple-element.87), channel_id=1, source_target_pairs={{0,4},{1,5},{2,6},{3,7},{4,0},{5,1},{6,2},{7,3},{8,12},{9,13},{10,... | collective-permute-start | bytes 589832 | tf_op jit(solution)/shard_map/ppermute | solution.py:449
  34.8 14.2 %collective-permute-start.8 = (bf16[64,1536]{1,0:T(8,128)(2,1)S(1)}, bf16[64,1536]{1,0:T(8,128)(2,1)S(1)}, u32[]{:S(2)}, u32[]{:S(2)}) collective-permute-start(bf16[64,1536]{1,0:T(8,128)(2,1)S(1)} %get-tuple-element.88), channel_id=1, source_target_pairs={{0,2},{1,3},{2,0},{3,1},{4,6},{5,7},{6,4},{7,5},{8,10},{9,11},{10,... | collective-permute-start | bytes 589832 | tf_op jit(solution)/shard_map/ppermute | solution.py:449
  42.6 6.5 %collective-permute-start.14 = (bf16[64,128]{1,0:T(8,128)(2,1)}, bf16[64,128]{1,0:T(8,128)(2,1)S(1)}, u32[]{:S(2)}, u32[]{:S(2)}) collective-permute-start(bf16[64,128]{1,0:T(8,128)(2,1)} %solve.1), channel_id=1, source_target_pairs={{0,6},{1,7},{2,4},{3,5},{4,2},{5,3},{6,0},{7,1},{8,14},{9,15},{10,... | collective-permute-start | bytes 49160 | tf_op jit(solution)/shard_map/ppermute | solution.py:449
  44.2 5.1 %collective-permute-start.13 = (bf16[64,128]{1,0:T(8,128)(2,1)}, bf16[64,128]{1,0:T(8,128)(2,1)S(1)}, u32[]{:S(2)}, u32[]{:S(2)}) collective-permute-start(bf16[64,128]{1,0:T(8,128)(2,1)} %solve.1), channel_id=1, source_target_pairs={{0,4},{1,5},{2,6},{3,7},{4,0},{5,1},{6,2},{7,3},{8,12},{9,13},{10,... | collective-permute-start | bytes 49160 | tf_op jit(solution)/shard_map/ppermute | solution.py:449
  47.1 4.0 %collective-permute-start.12 = (bf16[64,128]{1,0:T(8,128)(2,1)}, bf16[64,128]{1,0:T(8,128)(2,1)S(1)}, u32[]{:S(2)}, u32[]{:S(2)}) collective-permute-start(bf16[64,128]{1,0:T(8,128)(2,1)} %solve.1), channel_id=1, source_target_pairs={{0,2},{1,3},{2,0},{3,1},{4,6},{5,7},{6,4},{7,5},{8,10},{9,11},{10,... | collective-permute-start | bytes 49160 | tf_op jit(solution)/shard_map/ppermute | solution.py:449
  51.1 18.6 %collective-permute-start.17 = (bf16[4,64,1536]{2,1,0:T(8,128)(2,1)S(1)}, bf16[4,64,1536]{2,1,0:T(8,128)(2,1)S(1)}, u32[]{:S(2)}, u32[]{:S(2)}) collective-permute-start(bf16[4,64,1536]{2,1,0:T(8,128)(2,1)S(1)} %pad_maximum_fusion.2.refs_11_), channel_id=1, source_target_pairs={{0,16},{8,24},{16,0},{24,8},{1,17},{9,25},{17,1},{25,9},{2,18},{10... | collective-permute-start | bytes 2359304 | tf_op jit(solution)/shard_map/ppermute | solution.py:446
  52.2 17.5 %collective-permute-start.16 = (bf16[4,64,1536]{2,1,0:T(8,128)(2,1)S(1)}, bf16[4,64,1536]{2,1,0:T(8,128)(2,1)S(1)}, u32[]{:S(2)}, u32[]{:S(2)}) collective-permute-start(bf16[4,64,1536]{2,1,0:T(8,128)(2,1)S(1)} %pad_maximum_fusion.2.refs_11_), channel_id=1, source_target_pairs={{0,8},{8,0},{16,24},{24,16},{1,9},{9,1},{17,25},{25,17},{2,10},{10... | collective-permute-start | bytes 2359304 | tf_op jit(solution)/shard_map/ppermute | solution.py:446
  53.2 16.5 %collective-permute-start.20 = (bf16[256,1536]{1,0:T(8,128)(2,1)S(1)}, bf16[256,1536]{1,0:T(8,128)(2,1)S(1)}, u32[]{:S(2)}, u32[]{:S(2)}) collective-permute-start(bf16[256,1536]{1,0:T(8,128)(2,1)S(1)} %collective-permute-done.6.refs_9_.odd_ref), channel_id=1, source_target_pairs={{0,2},{1,3},{2,0},{3,1},{4,6},{5,7},{6,4},{7,5},{8,10},{9,11},{10,... | collective-permute-start | bytes 2359304 | tf_op jit(solution)/shard_map/ppermute | solution.py:443
  54.1 15.6 %collective-permute-start.19 = (bf16[256,1536]{1,0:T(8,128)(2,1)S(1)}, bf16[256,1536]{1,0:T(8,128)(2,1)}, u32[]{:S(2)}, u32[]{:S(2)}) collective-permute-start(bf16[256,1536]{1,0:T(8,128)(2,1)S(1)} %collective-permute-done.7.refs_7_), channel_id=1, source_target_pairs={{0,0},{1,1},{2,4},{3,5},{4,2},{5,3},{6,6},{7,7},{8,8},{9,9},{10,12... | collective-permute-start | bytes 2359304 | tf_op jit(solution)/shard_map/ppermute | solution.py:443
  56.4 1.3 %collective-permute-start.18 = (bf16[256,128]{1,0:T(8,128)(2,1)S(1)}, bf16[256,128]{1,0:T(8,128)(2,1)S(1)}, u32[]{:S(2)}, u32[]{:S(2)}) collective-permute-start(bf16[256,128]{1,0:T(8,128)(2,1)S(1)} %pad_maximum_fusion.5), channel_id=1, source_target_pairs={{0,1},{1,0},{2,3},{3,2},{4,5},{5,4},{6,7},{7,6},{8,9},{9,8},{10,11... | collective-permute-start | bytes 196616 | tf_op jit(solution)/shard_map/ppermute | solution.py:438
  69.8 18.8 %collective-permute-start.22 = (bf16[256,1536]{1,0:T(8,128)(2,1)}, bf16[256,1536]{1,0:T(8,128)(2,1)}, u32[]{:S(2)}, u32[]{:S(2)}) collective-permute-start(bf16[256,1536]{1,0:T(8,128)(2,1)} %collective-permute-done.19.refs_10_), channel_id=1, source_target_pairs={{0,2},{1,3},{2,0},{3,1},{4,6},{5,7},{6,4},{7,5},{8,10},{9,11},{10,... | collective-permute-start | bytes 2359304 | tf_op jit(solution)/shard_map/ppermute | solution.py:443
  73.8 17.6 %collective-permute-start.21 = (bf16[4,64,1536]{2,1,0:T(8,128)(2,1)S(1)}, bf16[4,64,1536]{2,1,0:T(8,128)(2,1)}, u32[]{:S(2)}, u32[]{:S(2)}) collective-permute-start(bf16[4,64,1536]{2,1,0:T(8,128)(2,1)S(1)} %pad_maximum_fusion.2.refs_11_), channel_id=1, source_target_pairs={{0,24},{8,16},{16,8},{24,0},{1,25},{9,17},{17,9},{25,1},{2,26},{10... | collective-permute-start | bytes 2359304 | tf_op jit(solution)/shard_map/ppermute | solution.py:446
  96.0 10.2 %collective-permute-start.23 = (bf16[2,1536,512]{2,1,0:T(8,128)(2,1)}, bf16[2,1536,512]{2,1,0:T(8,128)(2,1)}, u32[]{:S(2)}, u32[]{:S(2)}) collective-permute-start(bf16[2,1536,512]{2,1,0:T(8,128)(2,1)} %get-tuple-element.83.row_ref), channel_id=1, source_target_pairs={{0,1},{1,0},{2,3},{3,2},{4,5},{5,4},{6,7},{7,6},{8,9},{9,8},{10,11... | collective-permute-start | bytes 9437192 | tf_op jit(solution)/shard_map/ppermute | solution.py:438
  (10 other events, 150.4 us)

commit v17 on v16

--- a/solution.py
+++ b/solution.py
@@ -394,7 +394,7 @@
 def kin_call(part, people, row_panel, col_panel, before):
     _, count, depth = row_panel.shape
     width = col_panel.shape[2]
-    wide = 512 if width % 512 == 0 else width
+    wide = 768 if width % 768 == 0 else width
     in_specs = [
         pl.BlockSpec((2, count, depth), lambda i, at: (0, 0, 0)),
         pl.BlockSpec((2, depth, wide), lambda i, at: (0, 0, i)),

time: 117 us -> 118 us (level)
  no operation moved by 1% of the time
where the time goes in v17:
time: 118 us; the launch traced here: 117 us
  Pallas kernels  47.7 us (40%)
  starting transfers between devices  32.7 us (28%)
  waiting for transfers between devices  25.5 us (22%)
  other arithmetic  9.03 us (8%)
  local copies, waits for them, and re-layouts  1.6 us (1%)
    pallas_call x2, Pallas kernels, kin_call(): pl.pallas_call(kin_kernel, grid_spec=pltpu.PrefetchScalarGridSpec(num_sca...  20.8 us
    ppermute x10, starting transfers between devices, beside(): lax.ppermute(x, 'rows', [(i, i ^ d) for i in range(rows)])  11.9 us
    ppermute x5, waiting for transfers between devices, exchange(): return lax.ppermute(x, 'cols', pairs(lambda z, c: (other[z], c)))  10.8 us
    ppermute x5, starting transfers between devices, exchange(): return lax.ppermute(x, 'cols', pairs(lambda z, c: (other[z], c)))  10.3 us
    ppermute x6, starting transfers between devices, across(): return lax.ppermute(x, 'cols', pairs(lambda z, c: (z ^ e, c))) if e else x  9.99 us
    pallas_call x1, Pallas kernels, early_call(): pl.pallas_call(functools.partial(early_kernel_at, rows, len(pieces)), gri...  9.58 us
    ppermute x10, waiting for transfers between devices, beside(): lax.ppermute(x, 'rows', [(i, i ^ d) for i in range(rows)])  8.9 us
    pallas_call x1, Pallas kernels, solve_call(): pl.pallas_call(functools.partial(solve_kernel, comps, markers), out_shape...  7.09 us
  transfers between devices with their start and end apart: 24, of which 11 were waited for; matrix products, arithmetic and copies ran while one was open for 7% of the time, Pallas kernels for 28%

profile of v17, /device:TPU:0, one launch (start us, length us, event | category | flops | bytes accessed | tf_op | source)
XLA Modules:
  0.0 116.9 jit_solution(11244580546800165655)
XLA Ops:
  0.0 1.4 %dynamic-slice_convert_fusion = (bf16[64,1536]{1,0:T(8,128)(2,1)S(1)}, bf16[64,1536]{1,0:T(8,128)(2,1)S(1)}, bf16[64,1536]{1,0:T(8,128)(2,1)S(1)}, bf16[64,1536]{1,0:T(8,128)(2,1)S(1)}) fusion(s32[64,3072]{1,0:T(8,128)} %present_ref, s32[]{:T(128)S(6)} %select_n.168, s32[]{:T(128)S(6)} %select_n.167, s32[64,3072]{1,0:T(8,128)} %dosage_ref), kind=kLoop, calls=%fused_computation.7 | loop fusion | flops 393216 | bytes 2359304 | tf_op jit(solution)/shard_map/convert_element_type | solution.py:466
  2.1 1.3 %collective-permute-done = bf16[128,1536]{1,0:T(8,128)(2,1)S(1)} collective-permute-done((bf16[128,1536]{1,0:T(8,128)(2,1)S(1)}, bf16[128,1536]{1,0:T(8,128)(2,1)S(1)}, u32[]{:S(2)}, u32[]{:S(2)}) %collective-permute-start) | collective-permute-done | bytes 393248 | tf_op jit(solution)/shard_map/ppermute | solution.py:438
  3.5 3.0 %collective-permute-start.7 = (bf16[256,1536]{1,0:T(8,128)(2,1)S(1)}, bf16[256,1536]{1,0:T(8,128)(2,1)S(1)}, u32[]{:S(2)}, u32[]{:S(2)}) collective-permute-start(bf16[256,1536]{1,0:T(8,128)(2,1)S(1)} %pad_maximum_fusion.refs_6_), channel_id=1, source_target_pairs={{0,2},{1,3},{2,0},{3,1},{4,6},{5,7},{6,4},{7,5},{8,10},{9,11},{10,... | collective-permute-start | bytes 2359304 | tf_op jit(solution)/shard_map/ppermute | solution.py:443
  8.1 2.4 %collective-permute-start.3 = (bf16[64,1536]{1,0:T(8,128)(2,1)}, bf16[64,1536]{1,0:T(8,128)(2,1)S(1)}, u32[]{:S(2)}, u32[]{:S(2)}) collective-permute-start(bf16[64,1536]{1,0:T(8,128)(2,1)} %get-tuple-element.90), channel_id=1, source_target_pairs={{0,24},{8,16},{16,8},{24,0},{1,25},{9,17},{17,9},{25,1},{2,26},{10... | collective-permute-start | bytes 589832 | tf_op jit(solution)/shard_map/ppermute | solution.py:446
  11.6 5.7 %gram.1 = f32[360,128]{1,0:T(8,128)} custom-call(s32[64,3072]{1,0:T(8,128)} %dosage_ref, s32[64,3072]{1,0:T(8,128)} %present_ref, f32[32,3072]{1,0:T(8,128)} %refs_0_.1), custom_call_target="tpu_custom_call" | custom-call | tf_op jit(solution)/shard_map/gram/pallas_call | solution.py:63
  17.3 3.0 %collective-permute-done.1 = bf16[64,1536]{1,0:T(8,128)(2,1)} collective-permute-done((bf16[64,1536]{1,0:T(8,128)(2,1)}, bf16[64,1536]{1,0:T(8,128)(2,1)}, u32[]{:S(2)}, u32[]{:S(2)}) %collective-permute-start.1) | collective-permute-done | bytes 196640 | tf_op jit(solution)/shard_map/ppermute | solution.py:446
  20.3 1.5 %collective-permute-start.4 = (f32[360,128]{1,0:T(8,128)}, f32[360,128]{1,0:T(8,128)S(1)}, u32[]{:S(2)}, u32[]{:S(2)}) collective-permute-start(f32[360,128]{1,0:T(8,128)} %gram.1), channel_id=1, source_target_pairs={{0,8},{8,0},{16,24},{24,16},{1,9},{9,1},{17,25},{25,17},{2,10},{10... | collective-permute-start | bytes 552968 | tf_op jit(solution)/shard_map/ppermute | solution.py:446
  23.4 2.6 %collective-permute-done.4 = f32[360,128]{1,0:T(8,128)S(1)} collective-permute-done((f32[360,128]{1,0:T(8,128)}, f32[360,128]{1,0:T(8,128)S(1)}, u32[]{:S(2)}, u32[]{:S(2)}) %collective-permute-start.4) | collective-permute-done | bytes 184352 | tf_op jit(solution)/shard_map/ppermute | solution.py:446
  29.2 2.5 %collective-permute-start.10 = (bf16[64,1536]{1,0:T(8,128)(2,1)S(1)}, bf16[64,1536]{1,0:T(8,128)(2,1)S(1)}, u32[]{:S(2)}, u32[]{:S(2)}) collective-permute-start(bf16[64,1536]{1,0:T(8,128)(2,1)S(1)} %get-tuple-element.86), channel_id=1, source_target_pairs={{0,6},{1,7},{2,4},{3,5},{4,2},{5,3},{6,0},{7,1},{8,14},{9,15},{10,... | collective-permute-start | bytes 589832 | tf_op jit(solution)/shard_map/ppermute | solution.py:449
  31.7 3.1 %collective-permute-start.9 = (bf16[64,1536]{1,0:T(8,128)(2,1)S(1)}, bf16[64,1536]{1,0:T(8,128)(2,1)S(1)}, u32[]{:S(2)}, u32[]{:S(2)}) collective-permute-start(bf16[64,1536]{1,0:T(8,128)(2,1)S(1)} %get-tuple-element.87), channel_id=1, source_target_pairs={{0,4},{1,5},{2,6},{3,7},{4,0},{5,1},{6,2},{7,3},{8,12},{9,13},{10,... | collective-permute-start | bytes 589832 | tf_op jit(solution)/shard_map/ppermute | solution.py:449
  35.5 7.1 %solve.1 = bf16[64,128]{1,0:T(8,128)(2,1)} custom-call(f32[360,128]{1,0:T(8,128)} %copy-done.8, f32[360,128]{1,0:T(8,128)} %copy-done.9), custom_call_target="tpu_custom_call" | custom-call | tf_op jit(solution)/shard_map/solve/pallas_call | solution.py:152
  42.6 1.6 %collective-permute-start.14 = (bf16[64,128]{1,0:T(8,128)(2,1)}, bf16[64,128]{1,0:T(8,128)(2,1)S(1)}, u32[]{:S(2)}, u32[]{:S(2)}) collective-permute-start(bf16[64,128]{1,0:T(8,128)(2,1)} %solve.1), channel_id=1, source_target_pairs={{0,6},{1,7},{2,4},{3,5},{4,2},{5,3},{6,0},{7,1},{8,14},{9,15},{10,... | collective-permute-start | bytes 49160 | tf_op jit(solution)/shard_map/ppermute | solution.py:449
  44.2 2.3 %collective-permute-start.13 = (bf16[64,128]{1,0:T(8,128)(2,1)}, bf16[64,128]{1,0:T(8,128)(2,1)S(1)}, u32[]{:S(2)}, u32[]{:S(2)}) collective-permute-start(bf16[64,128]{1,0:T(8,128)(2,1)} %solve.1), channel_id=1, source_target_pairs={{0,4},{1,5},{2,6},{3,7},{4,0},{5,1},{6,2},{7,3},{8,12},{9,13},{10,... | collective-permute-start | bytes 49160 | tf_op jit(solution)/shard_map/ppermute | solution.py:449
  49.3 1.8 %collective-permute-done.12 = bf16[64,128]{1,0:T(8,128)(2,1)S(1)} collective-permute-done((bf16[64,128]{1,0:T(8,128)(2,1)}, bf16[64,128]{1,0:T(8,128)(2,1)S(1)}, u32[]{:S(2)}, u32[]{:S(2)}) %collective-permute-start.12) | collective-permute-done | bytes 16416 | tf_op jit(solution)/shard_map/ppermute | solution.py:449
  54.1 1.6 %collective-permute-start.19 = (bf16[256,1536]{1,0:T(8,128)(2,1)S(1)}, bf16[256,1536]{1,0:T(8,128)(2,1)}, u32[]{:S(2)}, u32[]{:S(2)}) collective-permute-start(bf16[256,1536]{1,0:T(8,128)(2,1)S(1)} %collective-permute-done.7.refs_7_), channel_id=1, source_target_pairs={{0,0},{1,1},{2,4},{3,5},{4,2},{5,3},{6,6},{7,7},{8,8},{9,9},{10,12... | collective-permute-start | bytes 2359304 | tf_op jit(solution)/shard_map/ppermute | solution.py:443
  60.9 8.9 %collective-permute-done.20.refs_8_ = bf16[256,1536]{1,0:T(8,128)(2,1)S(1)} collective-permute-done((bf16[256,1536]{1,0:T(8,128)(2,1)S(1)}, bf16[256,1536]{1,0:T(8,128)(2,1)S(1)}, u32[]{:S(2)}, u32[]{:S(2)}) %collective-permute-start.20) | collective-permute-done | bytes 786464 | tf_op jit(solution)/shard_map/ppermute | solution.py:443
  69.8 4.1 %collective-permute-start.22 = (bf16[256,1536]{1,0:T(8,128)(2,1)}, bf16[256,1536]{1,0:T(8,128)(2,1)}, u32[]{:S(2)}, u32[]{:S(2)}) collective-permute-start(bf16[256,1536]{1,0:T(8,128)(2,1)} %collective-permute-done.19.refs_10_), channel_id=1, source_target_pairs={{0,2},{1,3},{2,0},{3,1},{4,6},{5,7},{6,4},{7,5},{8,10},{9,11},{10,... | collective-permute-start | bytes 2359304 | tf_op jit(solution)/shard_map/ppermute | solution.py:443
  73.8 2.6 %collective-permute-start.21 = (bf16[4,64,1536]{2,1,0:T(8,128)(2,1)S(1)}, bf16[4,64,1536]{2,1,0:T(8,128)(2,1)}, u32[]{:S(2)}, u32[]{:S(2)}) collective-permute-start(bf16[4,64,1536]{2,1,0:T(8,128)(2,1)S(1)} %pad_maximum_fusion.2.refs_11_), channel_id=1, source_target_pairs={{0,24},{8,16},{16,8},{24,0},{1,25},{9,17},{17,9},{25,1},{2,26},{10... | collective-permute-start | bytes 2359304 | tf_op jit(solution)/shard_map/ppermute | solution.py:446
  77.1 9.6 %early.1 = (bf16[2,1536,512]{2,1,0:T(8,128)(2,1)}, bf16[2,16,32,1536]{3,2,1,0:T(8,128)(2,1)}, f32[128,1536]{1,0:T(8,128)}, f32[4,32,1536]{2,1,0:T(8,128)}) custom-call(s32[1]{0:T(128)} %bitcast.5.part_ref, f32[32,3072]{1,0:T(8,128)} %refs_0_.1, f32[32,1536]{1,0:T(8,128)} %broadcast_select_fusion.refs_1_, bf16[128,128]{1,0:T(8,128)(2,1)} %pad_maximum_fusion.6.refs_2_, ...), custom_call_target="tpu_custom_call" | custom-call | tf_op jit(solution)/shard_map/early/pallas_call | solution.py:269
  86.6 1.9 %collective-permute-done.22.even_ref = bf16[256,1536]{1,0:T(8,128)(2,1)} collective-permute-done((bf16[256,1536]{1,0:T(8,128)(2,1)}, bf16[256,1536]{1,0:T(8,128)(2,1)}, u32[]{:S(2)}, u32[]{:S(2)}) %collective-permute-start.22) | collective-permute-done | bytes 786464 | tf_op jit(solution)/shard_map/ppermute | solution.py:443
  88.6 2.8 %collective-permute-done.21.piece_ref = bf16[4,64,1536]{2,1,0:T(8,128)(2,1)} collective-permute-done((bf16[4,64,1536]{2,1,0:T(8,128)(2,1)S(1)}, bf16[4,64,1536]{2,1,0:T(8,128)(2,1)}, u32[]{:S(2)}, u32[]{:S(2)}) %collective-permute-start.21) | collective-permute-done | bytes 786464 | tf_op jit(solution)/shard_map/ppermute | solution.py:446
  91.4 4.6 %late.1 = (bf16[2,1536,512]{2,1,0:T(8,128)(2,1)}, bf16[2,16,32,1536]{3,2,1,0:T(8,128)(2,1)}) custom-call(s32[4]{0:T(128)} %pad_add_fusion.group_ref, f32[128,1536]{1,0:T(8,128)} %get-tuple-element.79.row_fit, f32[4,32,1536]{2,1,0:T(8,128)} %get-tuple-element.80.col_fit, ...), custom_call_target="tpu_custom_call", output_to_operand_aliasing={{0}: (6, {}), {1}: (7, {})} | custom-call | tf_op jit(solution)/shard_map/late/pallas_call | solution.py:360
  96.1 10.4 %kinship.2.refs_0_ = f32[3072,1536]{1,0:T(8,128)} custom-call(s32[1]{0:T(128)} %bitcast.27.part_ref, bf16[2,1536,512]{2,1,0:T(8,128)(2,1)} %get-tuple-element.83.row_ref, bf16[2,512,1536]{2,1,0:T(8,128)(2,1)} %bitcast.38), custom_call_target="tpu_custom_call" | custom-call | tf_op jit(solution)/shard_map/kinship/pallas_call | solution.py:408
  106.5 10.4 %kinship.3 = f32[3072,1536]{1,0:T(8,128)} custom-call(s32[1]{0:T(128)} %bitcast.part_ref, bf16[2,1536,512]{2,1,0:T(8,128)(2,1)} %collective-permute-done.23.row_ref, bf16[2,512,1536]{2,1,0:T(8,128)(2,1)} %bitcast.39, f32[3072,1536]{1,0:T(8,128)} %kinship.2.refs_0_), custom_call_target="tpu_custom_call", output_to_operand_aliasing={{}: (3, {})} | custom-call | tf_op jit(solution)/shard_map/kinship/pallas_call | solution.py:408
  (70 shorter events, 20.5 us)
Async XLA Ops:
  1.5 1.9 %collective-permute-start = (bf16[128,1536]{1,0:T(8,128)(2,1)S(1)}, bf16[128,1536]{1,0:T(8,128)(2,1)S(1)}, u32[]{:S(2)}, u32[]{:S(2)}) collective-permute-start(bf16[128,1536]{1,0:T(8,128)(2,1)S(1)} %bitcast.44), channel_id=1, source_target_pairs={{0,1},{1,0},{2,3},{3,2},{4,5},{5,4},{6,7},{7,6},{8,9},{9,8},{10,11... | collective-permute-start | bytes 1179656 | tf_op jit(solution)/shard_map/ppermute | solution.py:438
  3.5 23.9 %collective-permute-start.7 = (bf16[256,1536]{1,0:T(8,128)(2,1)S(1)}, bf16[256,1536]{1,0:T(8,128)(2,1)S(1)}, u32[]{:S(2)}, u32[]{:S(2)}) collective-permute-start(bf16[256,1536]{1,0:T(8,128)(2,1)S(1)} %pad_maximum_fusion.refs_6_), channel_id=1, source_target_pairs={{0,2},{1,3},{2,0},{3,1},{4,6},{5,7},{6,4},{7,5},{8,10},{9,11},{10,... | collective-permute-start | bytes 2359304 | tf_op jit(solution)/shard_map/ppermute | solution.py:443
  6.5 21.0 %collective-permute-start.6 = (bf16[256,1536]{1,0:T(8,128)(2,1)S(1)}, bf16[256,1536]{1,0:T(8,128)(2,1)S(1)}, u32[]{:S(2)}, u32[]{:S(2)}) collective-permute-start(bf16[256,1536]{1,0:T(8,128)(2,1)S(1)} %pad_maximum_fusion.refs_6_), channel_id=1, source_target_pairs={{0,0},{1,1},{2,4},{3,5},{4,2},{5,3},{6,6},{7,7},{8,8},{9,9},{10,12... | collective-permute-start | bytes 2359304 | tf_op jit(solution)/shard_map/ppermute | solution.py:443
  8.1 13.7 %collective-permute-start.3 = (bf16[64,1536]{1,0:T(8,128)(2,1)}, bf16[64,1536]{1,0:T(8,128)(2,1)S(1)}, u32[]{:S(2)}, u32[]{:S(2)}) collective-permute-start(bf16[64,1536]{1,0:T(8,128)(2,1)} %get-tuple-element.90), channel_id=1, source_target_pairs={{0,24},{8,16},{16,8},{24,0},{1,25},{9,17},{17,9},{25,1},{2,26},{10... | collective-permute-start | bytes 589832 | tf_op jit(solution)/shard_map/ppermute | solution.py:446
  10.5 11.7 %collective-permute-start.2 = (bf16[64,1536]{1,0:T(8,128)(2,1)S(1)}, bf16[64,1536]{1,0:T(8,128)(2,1)}, u32[]{:S(2)}, u32[]{:S(2)}) collective-permute-start(bf16[64,1536]{1,0:T(8,128)(2,1)S(1)} %get-tuple-element.91), channel_id=1, source_target_pairs={{0,16},{8,24},{16,0},{24,8},{1,17},{9,25},{17,1},{25,9},{2,18},{10... | collective-permute-start | bytes 589832 | tf_op jit(solution)/shard_map/ppermute | solution.py:446
  11.0 9.2 %collective-permute-start.1 = (bf16[64,1536]{1,0:T(8,128)(2,1)}, bf16[64,1536]{1,0:T(8,128)(2,1)}, u32[]{:S(2)}, u32[]{:S(2)}) collective-permute-start(bf16[64,1536]{1,0:T(8,128)(2,1)} %get-tuple-element.92), channel_id=1, source_target_pairs={{0,8},{8,0},{16,24},{24,16},{1,9},{9,1},{17,25},{25,17},{2,10},{10... | collective-permute-start | bytes 589832 | tf_op jit(solution)/shard_map/ppermute | solution.py:446
  20.3 5.7 %collective-permute-start.4 = (f32[360,128]{1,0:T(8,128)}, f32[360,128]{1,0:T(8,128)S(1)}, u32[]{:S(2)}, u32[]{:S(2)}) collective-permute-start(f32[360,128]{1,0:T(8,128)} %gram.1), channel_id=1, source_target_pairs={{0,8},{8,0},{16,24},{24,16},{1,9},{9,1},{17,25},{25,17},{2,10},{10... | collective-permute-start | bytes 552968 | tf_op jit(solution)/shard_map/ppermute | solution.py:446
  21.8 5.7 %collective-permute-start.5 = (f32[32,1536]{1,0:T(8,128)S(1)}, f32[32,1536]{1,0:T(8,128)S(1)}, u32[]{:S(2)}, u32[]{:S(2)}) collective-permute-start(f32[32,1536]{1,0:T(8,128)S(1)} %constant_dynamic-slice_fusion.3), channel_id=1, source_target_pairs={{0,16},{8,24},{16,0},{24,8},{1,17},{9,25},{17,1},{25,9},{2,18},{10... | collective-permute-start | bytes 589832 | tf_op jit(solution)/shard_map/ppermute | solution.py:446
  27.5 7.3 %collective-permute-start.11 = (f32[360,128]{1,0:T(8,128)S(1)}, f32[360,128]{1,0:T(8,128)S(1)}, u32[]{:S(2)}, u32[]{:S(2)}) collective-permute-start(f32[360,128]{1,0:T(8,128)S(1)} %add.111.refs_0_), channel_id=1, source_target_pairs={{0,16},{8,24},{16,0},{24,8},{1,17},{9,25},{17,1},{25,9},{2,18},{10... | collective-permute-start | bytes 552968 | tf_op jit(solution)/shard_map/ppermute | solution.py:446
  28.1 16.1 %collective-permute-start.15 = (f32[32,1536]{1,0:T(8,128)S(1)}, f32[32,1536]{1,0:T(8,128)S(1)}, u32[]{:S(2)}, u32[]{:S(2)}) collective-permute-start(f32[32,1536]{1,0:T(8,128)S(1)} %broadcast_select_fusion.1), channel_id=1, source_target_pairs={{0,8},{8,0},{16,24},{24,16},{1,9},{9,1},{17,25},{25,17},{2,10},{10... | collective-permute-start | bytes 589832 | tf_op jit(solution)/shard_map/ppermute | solution.py:446
  29.2 17.9 %collective-permute-start.10 = (bf16[64,1536]{1,0:T(8,128)(2,1)S(1)}, bf16[64,1536]{1,0:T(8,128)(2,1)S(1)}, u32[]{:S(2)}, u32[]{:S(2)}) collective-permute-start(bf16[64,1536]{1,0:T(8,128)(2,1)S(1)} %get-tuple-element.86), channel_id=1, source_target_pairs={{0,6},{1,7},{2,4},{3,5},{4,2},{5,3},{6,0},{7,1},{8,14},{9,15},{10,... | collective-permute-start | bytes 589832 | tf_op jit(solution)/shard_map/ppermute | solution.py:449
  31.7 17.2 %collective-permute-start.9 = (bf16[64,1536]{1,0:T(8,128)(2,1)S(1)}, bf16[64,1536]{1,0:T(8,128)(2,1)S(1)}, u32[]{:S(2)}, u32[]{:S(2)}) collective-permute-start(bf16[64,1536]{1,0:T(8,128)(2,1)S(1)} %get-tuple-element.87), channel_id=1, source_target_pairs={{0,4},{1,5},{2,6},{3,7},{4,0},{5,1},{6,2},{7,3},{8,12},{9,13},{10,... | collective-permute-start | bytes 589832 | tf_op jit(solution)/shard_map/ppermute | solution.py:449
  34.8 14.2 %collective-permute-start.8 = (bf16[64,1536]{1,0:T(8,128)(2,1)S(1)}, bf16[64,1536]{1,0:T(8,128)(2,1)S(1)}, u32[]{:S(2)}, u32[]{:S(2)}) collective-permute-start(bf16[64,1536]{1,0:T(8,128)(2,1)S(1)} %get-tuple-element.88), channel_id=1, source_target_pairs={{0,2},{1,3},{2,0},{3,1},{4,6},{5,7},{6,4},{7,5},{8,10},{9,11},{10,... | collective-permute-start | bytes 589832 | tf_op jit(solution)/shard_map/ppermute | solution.py:449
  42.6 6.5 %collective-permute-start.14 = (bf16[64,128]{1,0:T(8,128)(2,1)}, bf16[64,128]{1,0:T(8,128)(2,1)S(1)}, u32[]{:S(2)}, u32[]{:S(2)}) collective-permute-start(bf16[64,128]{1,0:T(8,128)(2,1)} %solve.1), channel_id=1, source_target_pairs={{0,6},{1,7},{2,4},{3,5},{4,2},{5,3},{6,0},{7,1},{8,14},{9,15},{10,... | collective-permute-start | bytes 49160 | tf_op jit(solution)/shard_map/ppermute | solution.py:449
  44.2 5.1 %collective-permute-start.13 = (bf16[64,128]{1,0:T(8,128)(2,1)}, bf16[64,128]{1,0:T(8,128)(2,1)S(1)}, u32[]{:S(2)}, u32[]{:S(2)}) collective-permute-start(bf16[64,128]{1,0:T(8,128)(2,1)} %solve.1), channel_id=1, source_target_pairs={{0,4},{1,5},{2,6},{3,7},{4,0},{5,1},{6,2},{7,3},{8,12},{9,13},{10,... | collective-permute-start | bytes 49160 | tf_op jit(solution)/shard_map/ppermute | solution.py:449
  47.1 4.0 %collective-permute-start.12 = (bf16[64,128]{1,0:T(8,128)(2,1)}, bf16[64,128]{1,0:T(8,128)(2,1)S(1)}, u32[]{:S(2)}, u32[]{:S(2)}) collective-permute-start(bf16[64,128]{1,0:T(8,128)(2,1)} %solve.1), channel_id=1, source_target_pairs={{0,2},{1,3},{2,0},{3,1},{4,6},{5,7},{6,4},{7,5},{8,10},{9,11},{10,... | collective-permute-start | bytes 49160 | tf_op jit(solution)/shard_map/ppermute | solution.py:449
  51.1 18.6 %collective-permute-start.17 = (bf16[4,64,1536]{2,1,0:T(8,128)(2,1)S(1)}, bf16[4,64,1536]{2,1,0:T(8,128)(2,1)S(1)}, u32[]{:S(2)}, u32[]{:S(2)}) collective-permute-start(bf16[4,64,1536]{2,1,0:T(8,128)(2,1)S(1)} %pad_maximum_fusion.2.refs_11_), channel_id=1, source_target_pairs={{0,16},{8,24},{16,0},{24,8},{1,17},{9,25},{17,1},{25,9},{2,18},{10... | collective-permute-start | bytes 2359304 | tf_op jit(solution)/shard_map/ppermute | solution.py:446
  52.2 17.5 %collective-permute-start.16 = (bf16[4,64,1536]{2,1,0:T(8,128)(2,1)S(1)}, bf16[4,64,1536]{2,1,0:T(8,128)(2,1)S(1)}, u32[]{:S(2)}, u32[]{:S(2)}) collective-permute-start(bf16[4,64,1536]{2,1,0:T(8,128)(2,1)S(1)} %pad_maximum_fusion.2.refs_11_), channel_id=1, source_target_pairs={{0,8},{8,0},{16,24},{24,16},{1,9},{9,1},{17,25},{25,17},{2,10},{10... | collective-permute-start | bytes 2359304 | tf_op jit(solution)/shard_map/ppermute | solution.py:446
  53.2 16.5 %collective-permute-start.20 = (bf16[256,1536]{1,0:T(8,128)(2,1)S(1)}, bf16[256,1536]{1,0:T(8,128)(2,1)S(1)}, u32[]{:S(2)}, u32[]{:S(2)}) collective-permute-start(bf16[256,1536]{1,0:T(8,128)(2,1)S(1)} %collective-permute-done.6.refs_9_.odd_ref), channel_id=1, source_target_pairs={{0,2},{1,3},{2,0},{3,1},{4,6},{5,7},{6,4},{7,5},{8,10},{9,11},{10,... | collective-permute-start | bytes 2359304 | tf_op jit(solution)/shard_map/ppermute | solution.py:443
  54.1 15.6 %collective-permute-start.19 = (bf16[256,1536]{1,0:T(8,128)(2,1)S(1)}, bf16[256,1536]{1,0:T(8,128)(2,1)}, u32[]{:S(2)}, u32[]{:S(2)}) collective-permute-start(bf16[256,1536]{1,0:T(8,128)(2,1)S(1)} %collective-permute-done.7.refs_7_), channel_id=1, source_target_pairs={{0,0},{1,1},{2,4},{3,5},{4,2},{5,3},{6,6},{7,7},{8,8},{9,9},{10,12... | collective-permute-start | bytes 2359304 | tf_op jit(solution)/shard_map/ppermute | solution.py:443
  56.4 1.3 %collective-permute-start.18 = (bf16[256,128]{1,0:T(8,128)(2,1)S(1)}, bf16[256,128]{1,0:T(8,128)(2,1)S(1)}, u32[]{:S(2)}, u32[]{:S(2)}) collective-permute-start(bf16[256,128]{1,0:T(8,128)(2,1)S(1)} %pad_maximum_fusion.5), channel_id=1, source_target_pairs={{0,1},{1,0},{2,3},{3,2},{4,5},{5,4},{6,7},{7,6},{8,9},{9,8},{10,11... | collective-permute-start | bytes 196616 | tf_op jit(solution)/shard_map/ppermute | solution.py:438
  69.8 18.8 %collective-permute-start.22 = (bf16[256,1536]{1,0:T(8,128)(2,1)}, bf16[256,1536]{1,0:T(8,128)(2,1)}, u32[]{:S(2)}, u32[]{:S(2)}) collective-permute-start(bf16[256,1536]{1,0:T(8,128)(2,1)} %collective-permute-done.19.refs_10_), channel_id=1, source_target_pairs={{0,2},{1,3},{2,0},{3,1},{4,6},{5,7},{6,4},{7,5},{8,10},{9,11},{10,... | collective-permute-start | bytes 2359304 | tf_op jit(solution)/shard_map/ppermute | solution.py:443
  73.8 17.6 %collective-permute-start.21 = (bf16[4,64,1536]{2,1,0:T(8,128)(2,1)S(1)}, bf16[4,64,1536]{2,1,0:T(8,128)(2,1)}, u32[]{:S(2)}, u32[]{:S(2)}) collective-permute-start(bf16[4,64,1536]{2,1,0:T(8,128)(2,1)S(1)} %pad_maximum_fusion.2.refs_11_), channel_id=1, source_target_pairs={{0,24},{8,16},{16,8},{24,0},{1,25},{9,17},{17,9},{25,1},{2,26},{10... | collective-permute-start | bytes 2359304 | tf_op jit(solution)/shard_map/ppermute | solution.py:446
  96.0 10.5 %collective-permute-start.23 = (bf16[2,1536,512]{2,1,0:T(8,128)(2,1)}, bf16[2,1536,512]{2,1,0:T(8,128)(2,1)}, u32[]{:S(2)}, u32[]{:S(2)}) collective-permute-start(bf16[2,1536,512]{2,1,0:T(8,128)(2,1)} %get-tuple-element.83.row_ref), channel_id=1, source_target_pairs={{0,1},{1,0},{2,3},{3,2},{4,5},{5,4},{6,7},{7,6},{8,9},{9,8},{10,11... | collective-permute-start | bytes 9437192 | tf_op jit(solution)/shard_map/ppermute | solution.py:438
  (10 other events, 150.4 us)

commit v18 on v16

--- a/solution.py
+++ b/solution.py
@@ -103,7 +103,10 @@
     for j in range(comps):
         first = firsts[j]
         column = columns[j]
-        inv = 1.0 / column[j - first : j - first + 1]
+        pivot = column[j - first : j - first + 1]
+        inv = pl.reciprocal(pivot, approx=True)
+        for _ in range(2):
+            inv = inv * (2.0 - pivot * inv)
         scaled = column * inv
         edge_j = edge[j : j + 1]
         moment_j = moment[j : j + 1]

time: 117 us -> 117 us (level)
  no operation moved by 1% of the time
where the time goes in v18:
time: 117 us; the launch traced here: 116 us
  Pallas kernels  47.4 us (41%)
  starting transfers between devices  32.7 us (28%)
  waiting for transfers between devices  25.4 us (22%)
  other arithmetic  9.03 us (8%)
  local copies, waits for them, and re-layouts  1.6 us (1%)
    pallas_call x2, Pallas kernels, kin_call(): pl.pallas_call(kin_kernel, grid_spec=pltpu.PrefetchScalarGridSpec(num_sca...  20.3 us
    ppermute x10, starting transfers between devices, beside(): lax.ppermute(x, 'rows', [(i, i ^ d) for i in range(rows)])  11.9 us
    ppermute x5, waiting for transfers between devices, exchange(): return lax.ppermute(x, 'cols', pairs(lambda z, c: (other[z], c)))  10.6 us
    ppermute x5, starting transfers between devices, exchange(): return lax.ppermute(x, 'cols', pairs(lambda z, c: (other[z], c)))  10.3 us
    ppermute x6, starting transfers between devices, across(): return lax.ppermute(x, 'cols', pairs(lambda z, c: (z ^ e, c))) if e else x  9.99 us
    pallas_call x1, Pallas kernels, early_call(): pl.pallas_call(functools.partial(early_kernel_at, rows, len(pieces)), gri...  9.58 us
    ppermute x10, waiting for transfers between devices, beside(): lax.ppermute(x, 'rows', [(i, i ^ d) for i in range(rows)])  9 us
    pallas_call x1, Pallas kernels, solve_call(): pl.pallas_call(functools.partial(solve_kernel, comps, markers), out_shape...  7.19 us
  transfers between devices with their start and end apart: 24, of which 11 were waited for; matrix products, arithmetic and copies ran while one was open for 7% of the time, Pallas kernels for 28%

profile of v18, /device:TPU:0, one launch (start us, length us, event | category | flops | bytes accessed | tf_op | source)
XLA Modules:
  0.0 116.4 jit_solution(814246816406723200)
XLA Ops:
  0.0 1.4 %dynamic-slice_convert_fusion = (bf16[64,1536]{1,0:T(8,128)(2,1)S(1)}, bf16[64,1536]{1,0:T(8,128)(2,1)S(1)}, bf16[64,1536]{1,0:T(8,128)(2,1)S(1)}, bf16[64,1536]{1,0:T(8,128)(2,1)S(1)}) fusion(s32[64,3072]{1,0:T(8,128)} %present_ref, s32[]{:T(128)S(6)} %select_n.168, s32[]{:T(128)S(6)} %select_n.167, s32[64,3072]{1,0:T(8,128)} %dosage_ref), kind=kLoop, calls=%fused_computation.7 | loop fusion | flops 393216 | bytes 2359304 | tf_op jit(solution)/shard_map/convert_element_type | solution.py:469
  2.1 1.3 %collective-permute-done = bf16[128,1536]{1,0:T(8,128)(2,1)S(1)} collective-permute-done((bf16[128,1536]{1,0:T(8,128)(2,1)S(1)}, bf16[128,1536]{1,0:T(8,128)(2,1)S(1)}, u32[]{:S(2)}, u32[]{:S(2)}) %collective-permute-start) | collective-permute-done | bytes 393248 | tf_op jit(solution)/shard_map/ppermute | solution.py:441
  3.5 3.0 %collective-permute-start.7 = (bf16[256,1536]{1,0:T(8,128)(2,1)S(1)}, bf16[256,1536]{1,0:T(8,128)(2,1)S(1)}, u32[]{:S(2)}, u32[]{:S(2)}) collective-permute-start(bf16[256,1536]{1,0:T(8,128)(2,1)S(1)} %pad_maximum_fusion.refs_6_), channel_id=1, source_target_pairs={{0,2},{1,3},{2,0},{3,1},{4,6},{5,7},{6,4},{7,5},{8,10},{9,11},{10,... | collective-permute-start | bytes 2359304 | tf_op jit(solution)/shard_map/ppermute | solution.py:446
  8.1 2.4 %collective-permute-start.3 = (bf16[64,1536]{1,0:T(8,128)(2,1)}, bf16[64,1536]{1,0:T(8,128)(2,1)S(1)}, u32[]{:S(2)}, u32[]{:S(2)}) collective-permute-start(bf16[64,1536]{1,0:T(8,128)(2,1)} %get-tuple-element.90), channel_id=1, source_target_pairs={{0,24},{8,16},{16,8},{24,0},{1,25},{9,17},{17,9},{25,1},{2,26},{10... | collective-permute-start | bytes 589832 | tf_op jit(solution)/shard_map/ppermute | solution.py:449
  11.6 5.7 %gram.1 = f32[360,128]{1,0:T(8,128)} custom-call(s32[64,3072]{1,0:T(8,128)} %dosage_ref, s32[64,3072]{1,0:T(8,128)} %present_ref, f32[32,3072]{1,0:T(8,128)} %refs_0_.1), custom_call_target="tpu_custom_call" | custom-call | tf_op jit(solution)/shard_map/gram/pallas_call | solution.py:63
  17.3 3.0 %collective-permute-done.1 = bf16[64,1536]{1,0:T(8,128)(2,1)} collective-permute-done((bf16[64,1536]{1,0:T(8,128)(2,1)}, bf16[64,1536]{1,0:T(8,128)(2,1)}, u32[]{:S(2)}, u32[]{:S(2)}) %collective-permute-start.1) | collective-permute-done | bytes 196640 | tf_op jit(solution)/shard_map/ppermute | solution.py:449
  20.3 1.5 %collective-permute-start.4 = (f32[360,128]{1,0:T(8,128)}, f32[360,128]{1,0:T(8,128)S(1)}, u32[]{:S(2)}, u32[]{:S(2)}) collective-permute-start(f32[360,128]{1,0:T(8,128)} %gram.1), channel_id=1, source_target_pairs={{0,8},{8,0},{16,24},{24,16},{1,9},{9,1},{17,25},{25,17},{2,10},{10... | collective-permute-start | bytes 552968 | tf_op jit(solution)/shard_map/ppermute | solution.py:449
  23.4 2.6 %collective-permute-done.4 = f32[360,128]{1,0:T(8,128)S(1)} collective-permute-done((f32[360,128]{1,0:T(8,128)}, f32[360,128]{1,0:T(8,128)S(1)}, u32[]{:S(2)}, u32[]{:S(2)}) %collective-permute-start.4) | collective-permute-done | bytes 184352 | tf_op jit(solution)/shard_map/ppermute | solution.py:449
  29.2 2.5 %collective-permute-start.10 = (bf16[64,1536]{1,0:T(8,128)(2,1)S(1)}, bf16[64,1536]{1,0:T(8,128)(2,1)S(1)}, u32[]{:S(2)}, u32[]{:S(2)}) collective-permute-start(bf16[64,1536]{1,0:T(8,128)(2,1)S(1)} %get-tuple-element.86), channel_id=1, source_target_pairs={{0,6},{1,7},{2,4},{3,5},{4,2},{5,3},{6,0},{7,1},{8,14},{9,15},{10,... | collective-permute-start | bytes 589832 | tf_op jit(solution)/shard_map/ppermute | solution.py:452
  31.7 3.1 %collective-permute-start.9 = (bf16[64,1536]{1,0:T(8,128)(2,1)S(1)}, bf16[64,1536]{1,0:T(8,128)(2,1)S(1)}, u32[]{:S(2)}, u32[]{:S(2)}) collective-permute-start(bf16[64,1536]{1,0:T(8,128)(2,1)S(1)} %get-tuple-element.87), channel_id=1, source_target_pairs={{0,4},{1,5},{2,6},{3,7},{4,0},{5,1},{6,2},{7,3},{8,12},{9,13},{10,... | collective-permute-start | bytes 589832 | tf_op jit(solution)/shard_map/ppermute | solution.py:452
  35.5 7.2 %solve.1 = bf16[64,128]{1,0:T(8,128)(2,1)} custom-call(f32[360,128]{1,0:T(8,128)} %copy-done.8, f32[360,128]{1,0:T(8,128)} %copy-done.9), custom_call_target="tpu_custom_call" | custom-call | tf_op jit(solution)/shard_map/solve/pallas_call | solution.py:155
  42.7 1.6 %collective-permute-start.14 = (bf16[64,128]{1,0:T(8,128)(2,1)}, bf16[64,128]{1,0:T(8,128)(2,1)S(1)}, u32[]{:S(2)}, u32[]{:S(2)}) collective-permute-start(bf16[64,128]{1,0:T(8,128)(2,1)} %solve.1), channel_id=1, source_target_pairs={{0,6},{1,7},{2,4},{3,5},{4,2},{5,3},{6,0},{7,1},{8,14},{9,15},{10,... | collective-permute-start | bytes 49160 | tf_op jit(solution)/shard_map/ppermute | solution.py:452
  44.3 2.3 %collective-permute-start.13 = (bf16[64,128]{1,0:T(8,128)(2,1)}, bf16[64,128]{1,0:T(8,128)(2,1)S(1)}, u32[]{:S(2)}, u32[]{:S(2)}) collective-permute-start(bf16[64,128]{1,0:T(8,128)(2,1)} %solve.1), channel_id=1, source_target_pairs={{0,4},{1,5},{2,6},{3,7},{4,0},{5,1},{6,2},{7,3},{8,12},{9,13},{10,... | collective-permute-start | bytes 49160 | tf_op jit(solution)/shard_map/ppermute | solution.py:452
  49.3 1.9 %collective-permute-done.12 = bf16[64,128]{1,0:T(8,128)(2,1)S(1)} collective-permute-done((bf16[64,128]{1,0:T(8,128)(2,1)}, bf16[64,128]{1,0:T(8,128)(2,1)S(1)}, u32[]{:S(2)}, u32[]{:S(2)}) %collective-permute-start.12) | collective-permute-done | bytes 16416 | tf_op jit(solution)/shard_map/ppermute | solution.py:452
  54.2 1.6 %collective-permute-start.19 = (bf16[256,1536]{1,0:T(8,128)(2,1)S(1)}, bf16[256,1536]{1,0:T(8,128)(2,1)}, u32[]{:S(2)}, u32[]{:S(2)}) collective-permute-start(bf16[256,1536]{1,0:T(8,128)(2,1)S(1)} %collective-permute-done.7.refs_7_), channel_id=1, source_target_pairs={{0,0},{1,1},{2,4},{3,5},{4,2},{5,3},{6,6},{7,7},{8,8},{9,9},{10,12... | collective-permute-start | bytes 2359304 | tf_op jit(solution)/shard_map/ppermute | solution.py:446
  61.0 8.7 %collective-permute-done.20.refs_8_ = bf16[256,1536]{1,0:T(8,128)(2,1)S(1)} collective-permute-done((bf16[256,1536]{1,0:T(8,128)(2,1)S(1)}, bf16[256,1536]{1,0:T(8,128)(2,1)S(1)}, u32[]{:S(2)}, u32[]{:S(2)}) %collective-permute-start.20) | collective-permute-done | bytes 786464 | tf_op jit(solution)/shard_map/ppermute | solution.py:446
  69.7 4.1 %collective-permute-start.22 = (bf16[256,1536]{1,0:T(8,128)(2,1)}, bf16[256,1536]{1,0:T(8,128)(2,1)}, u32[]{:S(2)}, u32[]{:S(2)}) collective-permute-start(bf16[256,1536]{1,0:T(8,128)(2,1)} %collective-permute-done.19.refs_10_), channel_id=1, source_target_pairs={{0,2},{1,3},{2,0},{3,1},{4,6},{5,7},{6,4},{7,5},{8,10},{9,11},{10,... | collective-permute-start | bytes 2359304 | tf_op jit(solution)/shard_map/ppermute | solution.py:446
  73.8 2.6 %collective-permute-start.21 = (bf16[4,64,1536]{2,1,0:T(8,128)(2,1)S(1)}, bf16[4,64,1536]{2,1,0:T(8,128)(2,1)}, u32[]{:S(2)}, u32[]{:S(2)}) collective-permute-start(bf16[4,64,1536]{2,1,0:T(8,128)(2,1)S(1)} %pad_maximum_fusion.2.refs_11_), channel_id=1, source_target_pairs={{0,24},{8,16},{16,8},{24,0},{1,25},{9,17},{17,9},{25,1},{2,26},{10... | collective-permute-start | bytes 2359304 | tf_op jit(solution)/shard_map/ppermute | solution.py:449
  77.1 9.6 %early.1 = (bf16[2,1536,512]{2,1,0:T(8,128)(2,1)}, bf16[2,16,32,1536]{3,2,1,0:T(8,128)(2,1)}, f32[128,1536]{1,0:T(8,128)}, f32[4,32,1536]{2,1,0:T(8,128)}) custom-call(s32[1]{0:T(128)} %bitcast.5.part_ref, f32[32,3072]{1,0:T(8,128)} %refs_0_.1, f32[32,1536]{1,0:T(8,128)} %broadcast_select_fusion.refs_1_, bf16[128,128]{1,0:T(8,128)(2,1)} %pad_maximum_fusion.6.refs_2_, ...), custom_call_target="tpu_custom_call" | custom-call | tf_op jit(solution)/shard_map/early/pallas_call | solution.py:272
  86.6 1.8 %collective-permute-done.22.even_ref = bf16[256,1536]{1,0:T(8,128)(2,1)} collective-permute-done((bf16[256,1536]{1,0:T(8,128)(2,1)}, bf16[256,1536]{1,0:T(8,128)(2,1)}, u32[]{:S(2)}, u32[]{:S(2)}) %collective-permute-start.22) | collective-permute-done | bytes 786464 | tf_op jit(solution)/shard_map/ppermute | solution.py:446
  88.5 2.9 %collective-permute-done.21.piece_ref = bf16[4,64,1536]{2,1,0:T(8,128)(2,1)} collective-permute-done((bf16[4,64,1536]{2,1,0:T(8,128)(2,1)S(1)}, bf16[4,64,1536]{2,1,0:T(8,128)(2,1)}, u32[]{:S(2)}, u32[]{:S(2)}) %collective-permute-start.21) | collective-permute-done | bytes 786464 | tf_op jit(solution)/shard_map/ppermute | solution.py:449
  91.4 4.6 %late.1 = (bf16[2,1536,512]{2,1,0:T(8,128)(2,1)}, bf16[2,16,32,1536]{3,2,1,0:T(8,128)(2,1)}) custom-call(s32[4]{0:T(128)} %pad_add_fusion.group_ref, f32[128,1536]{1,0:T(8,128)} %get-tuple-element.79.row_fit, f32[4,32,1536]{2,1,0:T(8,128)} %get-tuple-element.80.col_fit, ...), custom_call_target="tpu_custom_call", output_to_operand_aliasing={{0}: (6, {}), {1}: (7, {})} | custom-call | tf_op jit(solution)/shard_map/late/pallas_call | solution.py:363
  96.1 10.1 %kinship.2.refs_0_ = f32[3072,1536]{1,0:T(8,128)} custom-call(s32[1]{0:T(128)} %bitcast.27.part_ref, bf16[2,1536,512]{2,1,0:T(8,128)(2,1)} %get-tuple-element.83.row_ref, bf16[2,512,1536]{2,1,0:T(8,128)(2,1)} %bitcast.38), custom_call_target="tpu_custom_call" | custom-call | tf_op jit(solution)/shard_map/kinship/pallas_call | solution.py:411
  106.3 10.1 %kinship.3 = f32[3072,1536]{1,0:T(8,128)} custom-call(s32[1]{0:T(128)} %bitcast.part_ref, bf16[2,1536,512]{2,1,0:T(8,128)(2,1)} %collective-permute-done.23.row_ref, bf16[2,512,1536]{2,1,0:T(8,128)(2,1)} %bitcast.39, f32[3072,1536]{1,0:T(8,128)} %kinship.2.refs_0_), custom_call_target="tpu_custom_call", output_to_operand_aliasing={{}: (3, {})} | custom-call | tf_op jit(solution)/shard_map/kinship/pallas_call | solution.py:411
  (70 shorter events, 20.4 us)
Async XLA Ops:
  1.5 1.9 %collective-permute-start = (bf16[128,1536]{1,0:T(8,128)(2,1)S(1)}, bf16[128,1536]{1,0:T(8,128)(2,1)S(1)}, u32[]{:S(2)}, u32[]{:S(2)}) collective-permute-start(bf16[128,1536]{1,0:T(8,128)(2,1)S(1)} %bitcast.44), channel_id=1, source_target_pairs={{0,1},{1,0},{2,3},{3,2},{4,5},{5,4},{6,7},{7,6},{8,9},{9,8},{10,11... | collective-permute-start | bytes 1179656 | tf_op jit(solution)/shard_map/ppermute | solution.py:441
  3.5 23.9 %collective-permute-start.7 = (bf16[256,1536]{1,0:T(8,128)(2,1)S(1)}, bf16[256,1536]{1,0:T(8,128)(2,1)S(1)}, u32[]{:S(2)}, u32[]{:S(2)}) collective-permute-start(bf16[256,1536]{1,0:T(8,128)(2,1)S(1)} %pad_maximum_fusion.refs_6_), channel_id=1, source_target_pairs={{0,2},{1,3},{2,0},{3,1},{4,6},{5,7},{6,4},{7,5},{8,10},{9,11},{10,... | collective-permute-start | bytes 2359304 | tf_op jit(solution)/shard_map/ppermute | solution.py:446
  6.5 21.0 %collective-permute-start.6 = (bf16[256,1536]{1,0:T(8,128)(2,1)S(1)}, bf16[256,1536]{1,0:T(8,128)(2,1)S(1)}, u32[]{:S(2)}, u32[]{:S(2)}) collective-permute-start(bf16[256,1536]{1,0:T(8,128)(2,1)S(1)} %pad_maximum_fusion.refs_6_), channel_id=1, source_target_pairs={{0,0},{1,1},{2,4},{3,5},{4,2},{5,3},{6,6},{7,7},{8,8},{9,9},{10,12... | collective-permute-start | bytes 2359304 | tf_op jit(solution)/shard_map/ppermute | solution.py:446
  8.1 13.7 %collective-permute-start.3 = (bf16[64,1536]{1,0:T(8,128)(2,1)}, bf16[64,1536]{1,0:T(8,128)(2,1)S(1)}, u32[]{:S(2)}, u32[]{:S(2)}) collective-permute-start(bf16[64,1536]{1,0:T(8,128)(2,1)} %get-tuple-element.90), channel_id=1, source_target_pairs={{0,24},{8,16},{16,8},{24,0},{1,25},{9,17},{17,9},{25,1},{2,26},{10... | collective-permute-start | bytes 589832 | tf_op jit(solution)/shard_map/ppermute | solution.py:449
  10.5 11.7 %collective-permute-start.2 = (bf16[64,1536]{1,0:T(8,128)(2,1)S(1)}, bf16[64,1536]{1,0:T(8,128)(2,1)}, u32[]{:S(2)}, u32[]{:S(2)}) collective-permute-start(bf16[64,1536]{1,0:T(8,128)(2,1)S(1)} %get-tuple-element.91), channel_id=1, source_target_pairs={{0,16},{8,24},{16,0},{24,8},{1,17},{9,25},{17,1},{25,9},{2,18},{10... | collective-permute-start | bytes 589832 | tf_op jit(solution)/shard_map/ppermute | solution.py:449
  11.0 9.2 %collective-permute-start.1 = (bf16[64,1536]{1,0:T(8,128)(2,1)}, bf16[64,1536]{1,0:T(8,128)(2,1)}, u32[]{:S(2)}, u32[]{:S(2)}) collective-permute-start(bf16[64,1536]{1,0:T(8,128)(2,1)} %get-tuple-element.92), channel_id=1, source_target_pairs={{0,8},{8,0},{16,24},{24,16},{1,9},{9,1},{17,25},{25,17},{2,10},{10... | collective-permute-start | bytes 589832 | tf_op jit(solution)/shard_map/ppermute | solution.py:449
  20.3 5.7 %collective-permute-start.4 = (f32[360,128]{1,0:T(8,128)}, f32[360,128]{1,0:T(8,128)S(1)}, u32[]{:S(2)}, u32[]{:S(2)}) collective-permute-start(f32[360,128]{1,0:T(8,128)} %gram.1), channel_id=1, source_target_pairs={{0,8},{8,0},{16,24},{24,16},{1,9},{9,1},{17,25},{25,17},{2,10},{10... | collective-permute-start | bytes 552968 | tf_op jit(solution)/shard_map/ppermute | solution.py:449
  21.8 5.7 %collective-permute-start.5 = (f32[32,1536]{1,0:T(8,128)S(1)}, f32[32,1536]{1,0:T(8,128)S(1)}, u32[]{:S(2)}, u32[]{:S(2)}) collective-permute-start(f32[32,1536]{1,0:T(8,128)S(1)} %constant_dynamic-slice_fusion.3), channel_id=1, source_target_pairs={{0,16},{8,24},{16,0},{24,8},{1,17},{9,25},{17,1},{25,9},{2,18},{10... | collective-permute-start | bytes 589832 | tf_op jit(solution)/shard_map/ppermute | solution.py:449
  27.5 7.3 %collective-permute-start.11 = (f32[360,128]{1,0:T(8,128)S(1)}, f32[360,128]{1,0:T(8,128)S(1)}, u32[]{:S(2)}, u32[]{:S(2)}) collective-permute-start(f32[360,128]{1,0:T(8,128)S(1)} %add.111.refs_0_), channel_id=1, source_target_pairs={{0,16},{8,24},{16,0},{24,8},{1,17},{9,25},{17,1},{25,9},{2,18},{10... | collective-permute-start | bytes 552968 | tf_op jit(solution)/shard_map/ppermute | solution.py:449
  28.1 16.2 %collective-permute-start.15 = (f32[32,1536]{1,0:T(8,128)S(1)}, f32[32,1536]{1,0:T(8,128)S(1)}, u32[]{:S(2)}, u32[]{:S(2)}) collective-permute-start(f32[32,1536]{1,0:T(8,128)S(1)} %broadcast_select_fusion.1), channel_id=1, source_target_pairs={{0,8},{8,0},{16,24},{24,16},{1,9},{9,1},{17,25},{25,17},{2,10},{10... | collective-permute-start | bytes 589832 | tf_op jit(solution)/shard_map/ppermute | solution.py:449
  29.2 18.0 %collective-permute-start.10 = (bf16[64,1536]{1,0:T(8,128)(2,1)S(1)}, bf16[64,1536]{1,0:T(8,128)(2,1)S(1)}, u32[]{:S(2)}, u32[]{:S(2)}) collective-permute-start(bf16[64,1536]{1,0:T(8,128)(2,1)S(1)} %get-tuple-element.86), channel_id=1, source_target_pairs={{0,6},{1,7},{2,4},{3,5},{4,2},{5,3},{6,0},{7,1},{8,14},{9,15},{10,... | collective-permute-start | bytes 589832 | tf_op jit(solution)/shard_map/ppermute | solution.py:452
  31.7 17.2 %collective-permute-start.9 = (bf16[64,1536]{1,0:T(8,128)(2,1)S(1)}, bf16[64,1536]{1,0:T(8,128)(2,1)S(1)}, u32[]{:S(2)}, u32[]{:S(2)}) collective-permute-start(bf16[64,1536]{1,0:T(8,128)(2,1)S(1)} %get-tuple-element.87), channel_id=1, source_target_pairs={{0,4},{1,5},{2,6},{3,7},{4,0},{5,1},{6,2},{7,3},{8,12},{9,13},{10,... | collective-permute-start | bytes 589832 | tf_op jit(solution)/shard_map/ppermute | solution.py:452
  34.8 14.2 %collective-permute-start.8 = (bf16[64,1536]{1,0:T(8,128)(2,1)S(1)}, bf16[64,1536]{1,0:T(8,128)(2,1)S(1)}, u32[]{:S(2)}, u32[]{:S(2)}) collective-permute-start(bf16[64,1536]{1,0:T(8,128)(2,1)S(1)} %get-tuple-element.88), channel_id=1, source_target_pairs={{0,2},{1,3},{2,0},{3,1},{4,6},{5,7},{6,4},{7,5},{8,10},{9,11},{10,... | collective-permute-start | bytes 589832 | tf_op jit(solution)/shard_map/ppermute | solution.py:452
  42.7 6.4 %collective-permute-start.14 = (bf16[64,128]{1,0:T(8,128)(2,1)}, bf16[64,128]{1,0:T(8,128)(2,1)S(1)}, u32[]{:S(2)}, u32[]{:S(2)}) collective-permute-start(bf16[64,128]{1,0:T(8,128)(2,1)} %solve.1), channel_id=1, source_target_pairs={{0,6},{1,7},{2,4},{3,5},{4,2},{5,3},{6,0},{7,1},{8,14},{9,15},{10,... | collective-permute-start | bytes 49160 | tf_op jit(solution)/shard_map/ppermute | solution.py:452
  44.3 5.0 %collective-permute-start.13 = (bf16[64,128]{1,0:T(8,128)(2,1)}, bf16[64,128]{1,0:T(8,128)(2,1)S(1)}, u32[]{:S(2)}, u32[]{:S(2)}) collective-permute-start(bf16[64,128]{1,0:T(8,128)(2,1)} %solve.1), channel_id=1, source_target_pairs={{0,4},{1,5},{2,6},{3,7},{4,0},{5,1},{6,2},{7,3},{8,12},{9,13},{10,... | collective-permute-start | bytes 49160 | tf_op jit(solution)/shard_map/ppermute | solution.py:452
  47.2 4.0 %collective-permute-start.12 = (bf16[64,128]{1,0:T(8,128)(2,1)}, bf16[64,128]{1,0:T(8,128)(2,1)S(1)}, u32[]{:S(2)}, u32[]{:S(2)}) collective-permute-start(bf16[64,128]{1,0:T(8,128)(2,1)} %solve.1), channel_id=1, source_target_pairs={{0,2},{1,3},{2,0},{3,1},{4,6},{5,7},{6,4},{7,5},{8,10},{9,11},{10,... | collective-permute-start | bytes 49160 | tf_op jit(solution)/shard_map/ppermute | solution.py:452
  51.2 18.5 %collective-permute-start.17 = (bf16[4,64,1536]{2,1,0:T(8,128)(2,1)S(1)}, bf16[4,64,1536]{2,1,0:T(8,128)(2,1)S(1)}, u32[]{:S(2)}, u32[]{:S(2)}) collective-permute-start(bf16[4,64,1536]{2,1,0:T(8,128)(2,1)S(1)} %pad_maximum_fusion.2.refs_11_), channel_id=1, source_target_pairs={{0,16},{8,24},{16,0},{24,8},{1,17},{9,25},{17,1},{25,9},{2,18},{10... | collective-permute-start | bytes 2359304 | tf_op jit(solution)/shard_map/ppermute | solution.py:449
  52.4 17.4 %collective-permute-start.16 = (bf16[4,64,1536]{2,1,0:T(8,128)(2,1)S(1)}, bf16[4,64,1536]{2,1,0:T(8,128)(2,1)S(1)}, u32[]{:S(2)}, u32[]{:S(2)}) collective-permute-start(bf16[4,64,1536]{2,1,0:T(8,128)(2,1)S(1)} %pad_maximum_fusion.2.refs_11_), channel_id=1, source_target_pairs={{0,8},{8,0},{16,24},{24,16},{1,9},{9,1},{17,25},{25,17},{2,10},{10... | collective-permute-start | bytes 2359304 | tf_op jit(solution)/shard_map/ppermute | solution.py:449
  53.3 16.4 %collective-permute-start.20 = (bf16[256,1536]{1,0:T(8,128)(2,1)S(1)}, bf16[256,1536]{1,0:T(8,128)(2,1)S(1)}, u32[]{:S(2)}, u32[]{:S(2)}) collective-permute-start(bf16[256,1536]{1,0:T(8,128)(2,1)S(1)} %collective-permute-done.6.refs_9_.odd_ref), channel_id=1, source_target_pairs={{0,2},{1,3},{2,0},{3,1},{4,6},{5,7},{6,4},{7,5},{8,10},{9,11},{10,... | collective-permute-start | bytes 2359304 | tf_op jit(solution)/shard_map/ppermute | solution.py:446
  54.2 15.5 %collective-permute-start.19 = (bf16[256,1536]{1,0:T(8,128)(2,1)S(1)}, bf16[256,1536]{1,0:T(8,128)(2,1)}, u32[]{:S(2)}, u32[]{:S(2)}) collective-permute-start(bf16[256,1536]{1,0:T(8,128)(2,1)S(1)} %collective-permute-done.7.refs_7_), channel_id=1, source_target_pairs={{0,0},{1,1},{2,4},{3,5},{4,2},{5,3},{6,6},{7,7},{8,8},{9,9},{10,12... | collective-permute-start | bytes 2359304 | tf_op jit(solution)/shard_map/ppermute | solution.py:446
  56.5 1.3 %collective-permute-start.18 = (bf16[256,128]{1,0:T(8,128)(2,1)S(1)}, bf16[256,128]{1,0:T(8,128)(2,1)S(1)}, u32[]{:S(2)}, u32[]{:S(2)}) collective-permute-start(bf16[256,128]{1,0:T(8,128)(2,1)S(1)} %pad_maximum_fusion.5), channel_id=1, source_target_pairs={{0,1},{1,0},{2,3},{3,2},{4,5},{5,4},{6,7},{7,6},{8,9},{9,8},{10,11... | collective-permute-start | bytes 196616 | tf_op jit(solution)/shard_map/ppermute | solution.py:441
  69.7 18.7 %collective-permute-start.22 = (bf16[256,1536]{1,0:T(8,128)(2,1)}, bf16[256,1536]{1,0:T(8,128)(2,1)}, u32[]{:S(2)}, u32[]{:S(2)}) collective-permute-start(bf16[256,1536]{1,0:T(8,128)(2,1)} %collective-permute-done.19.refs_10_), channel_id=1, source_target_pairs={{0,2},{1,3},{2,0},{3,1},{4,6},{5,7},{6,4},{7,5},{8,10},{9,11},{10,... | collective-permute-start | bytes 2359304 | tf_op jit(solution)/shard_map/ppermute | solution.py:446
  73.8 17.6 %collective-permute-start.21 = (bf16[4,64,1536]{2,1,0:T(8,128)(2,1)S(1)}, bf16[4,64,1536]{2,1,0:T(8,128)(2,1)}, u32[]{:S(2)}, u32[]{:S(2)}) collective-permute-start(bf16[4,64,1536]{2,1,0:T(8,128)(2,1)S(1)} %pad_maximum_fusion.2.refs_11_), channel_id=1, source_target_pairs={{0,24},{8,16},{16,8},{24,0},{1,25},{9,17},{17,9},{25,1},{2,26},{10... | collective-permute-start | bytes 2359304 | tf_op jit(solution)/shard_map/ppermute | solution.py:449
  96.0 10.2 %collective-permute-start.23 = (bf16[2,1536,512]{2,1,0:T(8,128)(2,1)}, bf16[2,1536,512]{2,1,0:T(8,128)(2,1)}, u32[]{:S(2)}, u32[]{:S(2)}) collective-permute-start(bf16[2,1536,512]{2,1,0:T(8,128)(2,1)} %get-tuple-element.83.row_ref), channel_id=1, source_target_pairs={{0,1},{1,0},{2,3},{3,2},{4,5},{5,4},{6,7},{7,6},{8,9},{9,8},{10,11... | collective-permute-start | bytes 9437192 | tf_op jit(solution)/shard_map/ppermute | solution.py:441
  (10 other events, 150.5 us)
